TPU v7x, 32 devices: a whole 2x2x4 slice. The times are simulated.
32 devices in a mesh: dp: 8 (over z, core), tensor: 4 (over y, x).
Axes of the slice: x: 2, y: 2, z: 4, core: 2. Of those that a mesh axis runs over, the one named last changes fastest.
Arguments:
- tokens: bfloat16 [16384, 2048], P(('dp', 'tensor')), may hold values from -6 to 6
- segments: int32 [16384], P('dp'), may hold values from 0 to 287, as said below
- positions: int32 [16384], P('dp'), may hold values from 0 to 2397, as said below
- w_query: bfloat16 [2048, 2048], P('dp', 'tensor'), may hold values from -0.125 to 0.125
- w_key: bfloat16 [2048, 512], P('dp', 'tensor'), may hold values from -0.125 to 0.125
- w_value: bfloat16 [2048, 512], P('dp', 'tensor'), may hold values from -0.125 to 0.125
- w_out: bfloat16 [2048, 2048], P('dp', 'tensor'), may hold values from -1 to 1
- w_gate: bfloat16 [2048, 8192], P('dp', 'tensor'), may hold values from -0.125 to 0.125
- w_up: bfloat16 [2048, 8192], P('dp', 'tensor'), may hold values from -0.125 to 0.125
- w_down: bfloat16 [2048, 8192], P('dp', 'tensor'), may hold values from -0.0625 to 0.0625
- norm_attn: float32 [2048], replicated, may hold values from 0.1 to 1.9
- norm_mlp: float32 [2048], replicated, may hold values from 0.1 to 1.9
- query_gain: float32 [64], replicated, may hold values from 0.1 to 1.9
- key_gain: float32 [64], replicated, may hold values from 0.1 to 1.9
- out_grad: bfloat16 [16384, 2048], P(('dp', 'tensor')), may hold values from -6 to 6
Outputs:
- output: bfloat16 [16384, 2048], P(('dp', 'tensor'))
- grad_tokens: float32 [16384, 2048], P(('dp', 'tensor'))
- grad_w_query: float32 [2048, 2048], P('dp', 'tensor')
- grad_w_key: float32 [2048, 512], P('dp', 'tensor')
- grad_w_value: float32 [2048, 512], P('dp', 'tensor')
- grad_w_out: float32 [2048, 2048], P('dp', 'tensor')
- grad_w_gate: float32 [2048, 8192], P('dp', 'tensor')
- grad_w_up: float32 [2048, 8192], P('dp', 'tensor')
- grad_w_down: float32 [2048, 8192], P('dp', 'tensor')
- grad_norm_attn: float32 [2048], replicated
- grad_norm_mlp: float32 [2048], replicated
- grad_query_gain: float32 [64], replicated
- grad_key_gain: float32 [64], replicated
Inputs may be any that keep to these rules, and one draw needn't show every extreme that they name: `segments`: document numbers never fall along a sequence of 1024 tokens, and no number stands in two sequences; every document has 60 to 800 tokens, except that the last one of a sequence may be cut short. `positions`: 0 at a document's first token, then rising by 1 to 3 from each token of the document to the next.
All inputs are finite; a program needn't handle non-finite values.
Results may differ from a plain program's by a relative error of at most 0.019.
Values may be sent and summed in bfloat16 or wider, within the bound.
A program may use at most 224 MiB of HBM per device.

v0:
```python
import jax
import jax.numpy as jnp
from jax import lax
from jax.sharding import PartitionSpec as P

EPS = 1e-05
THETA = 1000000.0


def rms_scale(values):
    return lax.rsqrt(jnp.mean(values * values, axis=-1, keepdims=True) + EPS)


def norm_back(grad_normed, normed, inverse):
    return inverse * (grad_normed - normed * jnp.mean(grad_normed * normed, axis=-1, keepdims=True))


def rotary_tables(places, width):
    half_width = width // 2
    frequency = THETA ** (-jnp.arange(half_width, dtype=jnp.float32) * 2.0 / width)
    angles = places.astype(jnp.float32)[:, None] * frequency[None, :]
    cosine_table = jnp.concatenate([jnp.cos(angles), jnp.cos(angles)], axis=-1)[:, None, :]
    sine_table = jnp.concatenate([jnp.sin(angles), jnp.sin(angles)], axis=-1)[:, None, :]
    return (cosine_table, sine_table)


def rotate(values, cosine_table, sine_table):
    half_width = values.shape[-1] // 2
    turned = jnp.concatenate([-values[..., half_width:], values[..., :half_width]], axis=-1)
    return values * cosine_table + turned * sine_table


def rotate_back(grads_in, cosine_table, sine_table):
    half_width = grads_in.shape[-1] // 2
    scaled = grads_in * sine_table
    turned = jnp.concatenate([scaled[..., half_width:], -scaled[..., :half_width]], axis=-1)
    return grads_in * cosine_table + turned


def contract_rows(left, right):
    return lax.dot_general(
        left, right, (((0,), (0,)), ((), ())), preferred_element_type=jnp.float32
    )


def contract_cols(left, right):
    return lax.dot_general(
        left, right, (((1,), (1,)), ((), ())), preferred_element_type=jnp.float32
    )


def per_device(
    tokens,
    segments,
    positions,
    w_query,
    w_key,
    w_value,
    w_out,
    w_gate,
    w_up,
    w_down,
    norm_attn,
    norm_mlp,
    query_gain,
    key_gain,
    out_grad,
):
    head_dim = query_gain.shape[0]
    group_rows = segments.shape[0]
    local_heads = w_query.shape[1] // head_dim
    local_kv = w_key.shape[1] // head_dim
    repeat = local_heads // local_kv
    score_scale = head_dim ** (-0.5)
    block_rows = min(512, group_rows)
    block_count = group_rows // block_rows
    row_ids = jnp.arange(group_rows)

    def block_mask(first_row):
        block_ids = first_row + jnp.arange(block_rows)
        block_segs = lax.dynamic_slice_in_dim(segments, first_row, block_rows, 0)
        return (block_segs[:, None] == segments[None, :]) & (row_ids[None, :] <= block_ids[:, None])

    inputs = tokens.astype(jnp.float32)
    inv_one = rms_scale(inputs)
    normed_one = inputs * inv_one
    hidden_one = (normed_one * norm_attn).astype(jnp.bfloat16)
    rows_one = lax.all_gather(hidden_one, "tensor", axis=0, tiled=True)
    wq_all, wk_all, wv_all, wo_all = (
        lax.all_gather(w_query, "dp", axis=0, tiled=True),
        lax.all_gather(w_key, "dp", axis=0, tiled=True),
        lax.all_gather(w_value, "dp", axis=0, tiled=True),
        lax.all_gather(w_out, "dp", axis=0, tiled=True),
    )
    query_raw = jnp.dot(rows_one, wq_all, preferred_element_type=jnp.float32).reshape(
        group_rows, local_heads, head_dim
    )
    key_raw = jnp.dot(rows_one, wk_all, preferred_element_type=jnp.float32).reshape(
        group_rows, local_kv, head_dim
    )
    values = (
        jnp.dot(rows_one, wv_all, preferred_element_type=jnp.float32)
        .astype(jnp.bfloat16)
        .reshape(group_rows, local_kv, head_dim)
    )
    cosine_table, sine_table = rotary_tables(positions, head_dim)
    inv_query = rms_scale(query_raw)
    query_normed = query_raw * inv_query
    inv_key = rms_scale(key_raw)
    key_normed = key_raw * inv_key
    queries = rotate(query_normed * query_gain, cosine_table, sine_table).astype(jnp.bfloat16)
    keys = rotate(key_normed * key_gain, cosine_table, sine_table).astype(jnp.bfloat16)
    grouped = queries.reshape(group_rows, local_kv, repeat, head_dim)

    def block_scores(first_row):
        query_block = lax.dynamic_slice_in_dim(grouped, first_row, block_rows, 0)
        scores = (
            jnp.einsum("bkrd,ckd->krbc", query_block, keys, preferred_element_type=jnp.float32)
            * score_scale
        )
        return (query_block, jnp.where(block_mask(first_row), scores, -jnp.inf))

    def attend_block(block_index):
        first_row = block_index * block_rows
        query_block, scores = block_scores(first_row)
        row_max = jnp.max(scores, axis=-1, keepdims=True)
        weights = jnp.exp(scores - row_max)
        row_total = jnp.sum(weights, axis=-1, keepdims=True)
        probabilities = (weights / row_total).astype(jnp.bfloat16)
        mixture = jnp.einsum(
            "krbc,ckd->bkrd", probabilities, values, preferred_element_type=jnp.float32
        )
        return (
            mixture.astype(jnp.bfloat16).reshape(block_rows, local_heads * head_dim),
            (row_max + jnp.log(row_total))[..., 0],
        )

    attended, log_sums = lax.map(attend_block, jnp.arange(block_count))
    attended = attended.reshape(group_rows, local_heads * head_dim)
    branch = lax.psum_scatter(
        contract_cols(attended, wo_all), "tensor", scatter_dimension=0, tiled=True
    )
    resid = inputs + branch
    inv_two = rms_scale(resid)
    normed_two = resid * inv_two
    hidden_two = (normed_two * norm_mlp).astype(jnp.bfloat16)
    rows_two = lax.all_gather(hidden_two, "tensor", axis=0, tiled=True)
    wg_all, wu_all, wd_all = (
        lax.all_gather(w_gate, "dp", axis=0, tiled=True),
        lax.all_gather(w_up, "dp", axis=0, tiled=True),
        lax.all_gather(w_down, "dp", axis=0, tiled=True),
    )
    gate_raw = jnp.dot(rows_two, wg_all, preferred_element_type=jnp.float32)
    up_raw = jnp.dot(rows_two, wu_all, preferred_element_type=jnp.float32)
    sigmoid_gate = jax.nn.sigmoid(gate_raw)
    act = (gate_raw * sigmoid_gate * up_raw).astype(jnp.bfloat16)
    mlp_out = lax.psum_scatter(
        contract_cols(act, wd_all).astype(jnp.bfloat16), "tensor", scatter_dimension=0, tiled=True
    ).astype(jnp.float32)
    output = (resid + mlp_out).astype(jnp.bfloat16)
    grad_out = out_grad.astype(jnp.float32)
    grad_rows = lax.all_gather(out_grad, "tensor", axis=0, tiled=True)
    grad_hidden = jnp.dot(grad_rows, wd_all, preferred_element_type=jnp.float32)
    grad_wd = contract_rows(grad_rows, act)
    grad_up = (grad_hidden * gate_raw * sigmoid_gate).astype(jnp.bfloat16)
    grad_gate = (
        grad_hidden * up_raw * sigmoid_gate * (1.0 + gate_raw * (1.0 - sigmoid_gate))
    ).astype(jnp.bfloat16)
    grad_wg = contract_rows(rows_two, grad_gate)
    grad_wu = contract_rows(rows_two, grad_up)
    grad_two = lax.psum_scatter(
        contract_cols(grad_gate, wg_all) + contract_cols(grad_up, wu_all),
        "tensor",
        scatter_dimension=0,
        tiled=True,
    )
    mlp_grads = (
        lax.psum_scatter(
            grad_wg.astype(jnp.bfloat16), "dp", scatter_dimension=0, tiled=True
        ).astype(jnp.float32),
        lax.psum_scatter(
            grad_wu.astype(jnp.bfloat16), "dp", scatter_dimension=0, tiled=True
        ).astype(jnp.float32),
        lax.psum_scatter(
            grad_wd.astype(jnp.bfloat16), "dp", scatter_dimension=0, tiled=True
        ).astype(jnp.float32),
    )
    gain_mlp_part = jnp.sum(grad_two * normed_two, axis=0)
    grad_resid = grad_out + norm_back(grad_two * norm_mlp, normed_two, inv_two)
    grad_branch = grad_resid.astype(jnp.bfloat16)
    branch_rows = lax.all_gather(grad_branch, "tensor", axis=0, tiled=True)
    grad_attended = jnp.dot(branch_rows, wo_all, preferred_element_type=jnp.float32).astype(
        jnp.bfloat16
    )
    grad_wo = contract_rows(branch_rows, attended)
    grad_grouped = grad_attended.reshape(group_rows, local_kv, repeat, head_dim)

    def back_block(carry, pieces):
        grad_keys, grad_values = carry
        block_index, block_lse = pieces
        first_row = block_index * block_rows
        query_block, scores = block_scores(first_row)
        probabilities = jnp.exp(scores - block_lse[..., None])
        grad_block = lax.dynamic_slice_in_dim(grad_grouped, first_row, block_rows, 0)
        grad_probs = jnp.einsum(
            "bkrd,ckd->krbc", grad_block, values, preferred_element_type=jnp.float32
        )
        row_delta = jnp.sum(probabilities * grad_probs, axis=-1, keepdims=True)
        grad_scores = (probabilities * (grad_probs - row_delta)).astype(jnp.bfloat16)
        grad_query = (
            jnp.einsum("krbc,ckd->bkrd", grad_scores, keys, preferred_element_type=jnp.float32)
            * score_scale
        )
        grad_keys = (
            grad_keys
            + jnp.einsum(
                "krbc,bkrd->ckd", grad_scores, query_block, preferred_element_type=jnp.float32
            )
            * score_scale
        )
        grad_values = grad_values + jnp.einsum(
            "krbc,bkrd->ckd",
            probabilities.astype(jnp.bfloat16),
            grad_block,
            preferred_element_type=jnp.float32,
        )
        return ((grad_keys, grad_values), grad_query.reshape(block_rows, local_heads, head_dim))

    empty_kv = jnp.zeros((group_rows, local_kv, head_dim), jnp.float32)
    (grad_krot, grad_vals), grad_qrot = lax.scan(
        back_block, (empty_kv, empty_kv), (jnp.arange(block_count), log_sums)
    )
    grad_qrot = grad_qrot.reshape(group_rows, local_heads, head_dim)
    turned_query = rotate_back(grad_qrot, cosine_table, sine_table)
    turned_key = rotate_back(grad_krot, cosine_table, sine_table)
    query_gain_part = jnp.sum(turned_query * query_normed, axis=(0, 1))
    key_gain_part = jnp.sum(turned_key * key_normed, axis=(0, 1))
    grad_query_raw = (
        norm_back(turned_query * query_gain, query_normed, inv_query)
        .astype(jnp.bfloat16)
        .reshape(group_rows, local_heads * head_dim)
    )
    grad_key_raw = (
        norm_back(turned_key * key_gain, key_normed, inv_key)
        .astype(jnp.bfloat16)
        .reshape(group_rows, local_kv * head_dim)
    )
    grad_value_raw = grad_vals.astype(jnp.bfloat16).reshape(group_rows, local_kv * head_dim)
    grad_wq = contract_rows(rows_one, grad_query_raw)
    grad_wk = contract_rows(rows_one, grad_key_raw)
    grad_wv = contract_rows(rows_one, grad_value_raw)
    back_terms = (
        contract_cols(grad_query_raw, wq_all)
        + contract_cols(grad_key_raw, wk_all)
        + contract_cols(grad_value_raw, wv_all)
    )
    grad_one = lax.psum_scatter(
        back_terms.astype(jnp.bfloat16), "tensor", scatter_dimension=0, tiled=True
    ).astype(jnp.float32)
    attn_grads = (
        lax.psum_scatter(
            grad_wq.astype(jnp.bfloat16), "dp", scatter_dimension=0, tiled=True
        ).astype(jnp.float32),
        lax.psum_scatter(
            grad_wk.astype(jnp.bfloat16), "dp", scatter_dimension=0, tiled=True
        ).astype(jnp.float32),
        lax.psum_scatter(
            grad_wv.astype(jnp.bfloat16), "dp", scatter_dimension=0, tiled=True
        ).astype(jnp.float32),
        lax.psum_scatter(
            grad_wo.astype(jnp.bfloat16), "dp", scatter_dimension=0, tiled=True
        ).astype(jnp.float32),
    )
    gain_attn_part = jnp.sum(grad_one * normed_one, axis=0)
    grad_input = grad_resid + norm_back(grad_one * norm_attn, normed_one, inv_one)
    gain_totals = lax.psum(
        (gain_attn_part, gain_mlp_part, query_gain_part, key_gain_part), ("dp", "tensor")
    )
    return (
        output,
        grad_input,
        attn_grads[0],
        attn_grads[1],
        attn_grads[2],
        attn_grads[3],
        mlp_grads[0],
        mlp_grads[1],
        mlp_grads[2],
        gain_totals[0],
        gain_totals[1],
        gain_totals[2],
        gain_totals[3],
    )


def solution(mesh):
    return jax.shard_map(
        per_device,
        mesh=mesh,
        in_specs=(
            P(("dp", "tensor"), None),
            P("dp"),
            P("dp"),
            P("dp", "tensor"),
            P("dp", "tensor"),
            P("dp", "tensor"),
            P("dp", "tensor"),
            P("dp", "tensor"),
            P("dp", "tensor"),
            P("dp", "tensor"),
            P(),
            P(),
            P(),
            P(),
            P(("dp", "tensor"), None),
        ),
        out_specs=(
            P(("dp", "tensor"), None),
            P(("dp", "tensor"), None),
            P("dp", "tensor"),
            P("dp", "tensor"),
            P("dp", "tensor"),
            P("dp", "tensor"),
            P("dp", "tensor"),
            P("dp", "tensor"),
            P("dp", "tensor"),
            P(),
            P(),
            P(),
            P(),
        ),
        check_vma=False,
    )
```

profile of v0, /device:TPU:0, one launch (start us, length us, event | category | flops | bytes accessed | tf_op | source)
XLA Modules:
  0.0 2158.2 jit_solution(3576122960468910912)
XLA Ops:
  16.2 16.6 all_gather.35
  32.8 16.0 all_gather.36
  48.7 55.2 %all-gather.10.cloned.1.call-done = bf16[2048,2048]{1,0:T(8,128)(2,1)} async-done(((bf16[512,2048]{1,0:T(8,128)(2,1)}), bf16[2048,2048]{1,0:T(8,128)(2,1)}) %all-gather.10.cloned.1.call-update) | async-done | bytes 8388624 | tf_op jit(solution)/shard_map/all_gather | solution.py:88
  110.6 24.0 %all-gather.12.cloned.1.call-done = bf16[2048,512]{1,0:T(8,128)(2,1)} async-done(((bf16[256,512]{1,0:T(8,128)(2,1)}), bf16[2048,512]{1,0:T(8,128)(2,1)}) %all-gather.12.cloned.1.call-update) | async-done | bytes 2097168 | tf_op jit(solution)/shard_map/all_gather | solution.py:90
  159.0 199.3 %while.28 = (s32[]{:T(128)}, bf16[4,512,512]{2,1,0:T(8,128)(2,1)}, f32[4,2,4,512]{3,2,1,0:T(4,128)}, s32[4]{0:T(128)S(1)}, s32[2048]{0:T(1024)S(1)}, /*index=5*/...) while((s32[]{:T(128)}, bf16[4,512,512]{2,1,0:T(8,128)(2,1)}, ...), condition=%wide.region_6.7_spmd.clone, body=%wide.region_3.6_spmd.clone.sunk | while | flops 2251551232 | bytes 109201608 | solution.py:138
  176.3 15.0 fusion.141
  226.1 15.0 fusion.141
  275.9 15.0 fusion.141
  325.7 15.0 fusion.141
  372.7 152.5 %reduce-scatter.12.cloned.1.call-done = f32[512,2048]{1,0:T(8,128)} async-done(((f32[2048,2048]{1,0:T(8,128)}), f32[512,2048]{1,0:T(8,128)}) %reduce-scatter.12.cloned.1.call-update) | async-done | bytes 4194320 | tf_op jit(solution)/shard_map/reduce_scatter | solution.py:140
  534.1 74.6 %all-gather.20.cloned.1.call-done = bf16[2048,2048]{1,0:T(8,128)(2,1)} async-done(((bf16[256,2048]{1,0:T(8,128)(2,1)}), bf16[2048,2048]{1,0:T(8,128)(2,1)}) %all-gather.20.cloned.1.call-update) | async-done | bytes 8388624 | tf_op jit(solution)/shard_map/all_gather | solution.py:150
  608.7 88.4 %all-gather.16.cloned.1.call-done = bf16[2048,2048]{1,0:T(8,128)(2,1)} async-done(((bf16[512,2048]{1,0:T(8,128)(2,1)}), bf16[2048,2048]{1,0:T(8,128)(2,1)}) %all-gather.16.cloned.1.call-update) | async-done | bytes 8388624 | tf_op jit(solution)/shard_map/all_gather | solution.py:147
  697.1 24.2 %fusion.73 = f32[2048,2048]{1,0:T(8,128)} fusion(bf16[2048,2048]{1,0:T(8,128)(2,1)} %all-gather.16.cloned.1.call-done, bf16[2048,2048]{1,0:T(8,128)(2,1)} %all-gather.20.cloned.1.call-done), kind=kOutput, calls=%fused_computation.147 | convolution fusion | flops 17179869184 | bytes 33554432 | tf_op jit(solution)/shard_map/dot_general | solution.py:154
  721.3 59.5 %all-gather.18.cloned.1.call-done = bf16[2048,2048]{1,0:T(8,128)(2,1)} async-done(((bf16[256,2048]{1,0:T(8,128)(2,1)}), bf16[2048,2048]{1,0:T(8,128)(2,1)}) %all-gather.18.cloned.1.call-update) | async-done | bytes 8388624 | tf_op jit(solution)/shard_map/all_gather | solution.py:149
  780.8 24.1 %fusion.72 = f32[2048,2048]{1,0:T(8,128)} fusion(bf16[2048,2048]{1,0:T(8,128)(2,1)} %all-gather.16.cloned.1.call-done, bf16[2048,2048]{1,0:T(8,128)(2,1)} %all-gather.18.cloned.1.call-done), kind=kOutput, calls=%fused_computation.146 | convolution fusion | flops 17179869184 | bytes 33554432 | tf_op jit(solution)/shard_map/dot_general | solution.py:153
  805.0 63.9 %all-gather.24.cloned.1.call-done = bf16[2048,2048]{1,0:T(8,128)(2,1)} async-done(((bf16[512,2048]{1,0:T(8,128)(2,1)}), bf16[2048,2048]{1,0:T(8,128)(2,1)}) %all-gather.24.cloned.1.call-update) | async-done | bytes 8388624 | tf_op jit(solution)/shard_map/all_gather | solution.py:162
  868.9 83.7 %all-gather.22.cloned.1.call-done = bf16[2048,2048]{1,0:T(8,128)(2,1)} async-done(((bf16[256,2048]{1,0:T(8,128)(2,1)}), bf16[2048,2048]{1,0:T(8,128)(2,1)}) %all-gather.22.cloned.1.call-update) | async-done | bytes 8388624 | tf_op jit(solution)/shard_map/all_gather | solution.py:151
  952.6 34.7 %multiply_convert_fusion = (bf16[2048,2048]{1,0:T(8,128)(2,1)}, bf16[2048,2048]{1,0:T(8,128)(2,1)}, bf16[2048,2048]{1,0:T(8,128)(2,1)}) fusion(f32[2048,2048]{1,0:T(8,128)} %fusion.72, f32[2048,2048]{1,0:T(8,128)} %fusion.73, bf16[2048,2048]{1,0:T(8,128)(2,1)} %all-gather.24.cloned.1.call-done, bf16[2048,2048]{1,0:T(8,128)(2,1)} %all-gather.22.cloned.1.call-done), kind=kOutput, calls=%fused_computation.59 | convolution fusion | flops 17246978048 | bytes 75497472 | tf_op jit(solution)/shard_map/dot_general | solution.py:163
  987.3 24.3 %fusion.74 = f32[2048,2048]{1,0:T(8,128)} fusion(bf16[2048,2048]{1,0:T(8,128)(2,1)} %get-tuple-element.283, bf16[2048,2048]{1,0:T(8,128)(2,1)} %all-gather.18.cloned.1.call-done), kind=kOutput, calls=%fused_computation.148 | convolution fusion | flops 17179869184 | bytes 33554432 | tf_op jit(solution)/shard_map/dot_general | solution.py:47
  1011.6 26.7 %convolution_add_fusion = f32[2048,2048]{1,0:T(8,128)} fusion(f32[2048,2048]{1,0:T(8,128)} %fusion.74, bf16[2048,2048]{1,0:T(8,128)(2,1)} %get-tuple-element.282, bf16[2048,2048]{1,0:T(8,128)(2,1)} %all-gather.20.cloned.1.call-done), kind=kOutput, calls=%fused_computation.63 | convolution fusion | flops 17184063488 | bytes 50331648 | tf_op jit(solution)/shard_map/dot_general | solution.py:47
  1038.4 152.5 %reduce-scatter.16.cloned.1.call-done = f32[512,2048]{1,0:T(8,128)} async-done(((f32[2048,2048]{1,0:T(8,128)}), f32[512,2048]{1,0:T(8,128)}) %reduce-scatter.16.cloned.1.call-update) | async-done | bytes 4194320 | tf_op jit(solution)/shard_map/reduce_scatter | solution.py:171
  1199.3 23.7 %convert_bitcast_fusion = bf16[2048,2048]{0,1:T(8,128)(2,1)} fusion(bf16[2048,2048]{1,0:T(8,128)(2,1)} %get-tuple-element.284, bf16[2048,2048]{1,0:T(8,128)(2,1)} %all-gather.24.cloned.1.call-done), kind=kOutput, calls=%fused_computation.64 | convolution fusion | flops 17184063488 | bytes 25165824 | tf_op jit(solution)/shard_map/dot_general | solution.py:41
  1223.1 24.0 %convolution_convert_fusion = bf16[2048,2048]{1,0:T(8,128)(2,1)} fusion(bf16[2048,2048]{1,0:T(8,128)(2,1)} %all-gather.16.cloned.1.call-done, bf16[2048,2048]{1,0:T(8,128)(2,1)} %get-tuple-element.282), kind=kOutput, calls=%fused_computation.65 | convolution fusion | flops 17184063488 | bytes 25165824 | tf_op jit(solution)/shard_map/dot_general | solution.py:41
  1257.9 23.7 %convolution_convert_fusion.1 = bf16[2048,2048]{1,0:T(8,128)(2,1)} fusion(bf16[2048,2048]{1,0:T(8,128)(2,1)} %all-gather.16.cloned.1.call-done, bf16[2048,2048]{1,0:T(8,128)(2,1)} %get-tuple-element.283), kind=kOutput, calls=%fused_computation.66 | convolution fusion | flops 17184063488 | bytes 25165824 | tf_op jit(solution)/shard_map/dot_general | solution.py:41
  1296.9 509.0 %while.29 = (s32[]{:T(128)}, f32[2048,2,64]{0,2,1:T(8,128)S(1)}, f32[2048,2,64]{0,2,1:T(8,128)}, f32[4,512,8,64]{1,0,3,2:T(4,128)}, s32[4]{0:T(128)S(1)}, /*inde...) while((s32[]{:T(128)}, f32[2048,2,64]{0,2,1:T(8,128)S(1)}, ...), condition=%wide.region_14.15_spmd.clone, body=%wide.region_12.14_spmd.clone.sunk | while | flops 5499253248 | bytes 352979296 | solution.py:230
  1300.6 17.3 fusion.151
  1317.9 15.2 fusion.156
  1333.2 24.4 %fusion.153 = (f32[2,4,512]{2,1,0:T(4,128)S(1)}, f32[2,512,4,2048]{3,1,2,0:T(8,128)}) fusion(f32[2,512,4,2048]{3,1,2,0:T(8,128)} %fusion.151, f32[2,4,512]{2,1,0:T(4,128)S(1)} %dynamic-slice_bitcast_fusion.2, pred[512,2048]{1,0:T(8,128)(4,1)S(1)} %fusion.152, bf16[2048,2,64]{0,2,1:T(8,128)(2,1)} %get-tuple-element.501, ...), kind=kOutput, calls=%fused_computation.24.clone.1 | convolution fusion | flops 1115680768 | bytes 69238784 | tf_op jit(solution)/shard_map/while/body/eval_jaxpr/bkrd,ckd->krbc/dot_general | solution.py:205
  1357.6 28.1 %fusion.154 = bf16[2,4,512,2048]{3,2,1,0:T(8,128)(2,1)} fusion(f32[2,512,4,2048]{3,1,2,0:T(8,128)} %get-tuple-element.423, f32[2,512,4,2048]{3,1,2,0:T(8,128)} %fusion.151, f32[2,4,512]{2,1,0:T(4,128)S(1)} %get-tuple-element.424, f32[2,4,512]{2,1,0:T(4,128)S(1)} %dynamic-slice_bitcast_fusion.2, pred[512,2048]{1,0:T(8,128)(4,1)S(1)} %fusion.152), kind=kLoop, calls=%fused_computation.26.clone.1 | loop fusion | flops 50331648 | bytes 84967424 | tf_op jit(solution)/shard_map/while/body/eval_jaxpr/convert_element_type | solution.py:209
  1404.0 21.1 dynamic_update_slice.22
  1428.3 17.3 fusion.151
  1445.7 15.3 fusion.156
  1461.0 24.5 %fusion.153 = (f32[2,4,512]{2,1,0:T(4,128)S(1)}, f32[2,512,4,2048]{3,1,2,0:T(8,128)}) fusion(f32[2,512,4,2048]{3,1,2,0:T(8,128)} %fusion.151, f32[2,4,512]{2,1,0:T(4,128)S(1)} %dynamic-slice_bitcast_fusion.2, pred[512,2048]{1,0:T(8,128)(4,1)S(1)} %fusion.152, bf16[2048,2,64]{0,2,1:T(8,128)(2,1)} %get-tuple-element.501, ...), kind=kOutput, calls=%fused_computation.24.clone.1 | convolution fusion | flops 1115680768 | bytes 69238784 | tf_op jit(solution)/shard_map/while/body/eval_jaxpr/bkrd,ckd->krbc/dot_general | solution.py:205
  1485.5 28.5 %fusion.154 = bf16[2,4,512,2048]{3,2,1,0:T(8,128)(2,1)} fusion(f32[2,512,4,2048]{3,1,2,0:T(8,128)} %get-tuple-element.423, f32[2,512,4,2048]{3,1,2,0:T(8,128)} %fusion.151, f32[2,4,512]{2,1,0:T(4,128)S(1)} %get-tuple-element.424, f32[2,4,512]{2,1,0:T(4,128)S(1)} %dynamic-slice_bitcast_fusion.2, pred[512,2048]{1,0:T(8,128)(4,1)S(1)} %fusion.152), kind=kLoop, calls=%fused_computation.26.clone.1 | loop fusion | flops 50331648 | bytes 84967424 | tf_op jit(solution)/shard_map/while/body/eval_jaxpr/convert_element_type | solution.py:209
  1532.3 21.0 dynamic_update_slice.22
  1556.7 17.0 fusion.151
  1588.6 24.2 %fusion.153 = (f32[2,4,512]{2,1,0:T(4,128)S(1)}, f32[2,512,4,2048]{3,1,2,0:T(8,128)}) fusion(f32[2,512,4,2048]{3,1,2,0:T(8,128)} %fusion.151, f32[2,4,512]{2,1,0:T(4,128)S(1)} %dynamic-slice_bitcast_fusion.2, pred[512,2048]{1,0:T(8,128)(4,1)S(1)} %fusion.152, bf16[2048,2,64]{0,2,1:T(8,128)(2,1)} %get-tuple-element.501, ...), kind=kOutput, calls=%fused_computation.24.clone.1 | convolution fusion | flops 1115680768 | bytes 69238784 | tf_op jit(solution)/shard_map/while/body/eval_jaxpr/bkrd,ckd->krbc/dot_general | solution.py:205
  1612.8 27.8 %fusion.154 = bf16[2,4,512,2048]{3,2,1,0:T(8,128)(2,1)} fusion(f32[2,512,4,2048]{3,1,2,0:T(8,128)} %get-tuple-element.423, f32[2,512,4,2048]{3,1,2,0:T(8,128)} %fusion.151, f32[2,4,512]{2,1,0:T(4,128)S(1)} %get-tuple-element.424, f32[2,4,512]{2,1,0:T(4,128)S(1)} %dynamic-slice_bitcast_fusion.2, pred[512,2048]{1,0:T(8,128)(4,1)S(1)} %fusion.152), kind=kLoop, calls=%fused_computation.26.clone.1 | loop fusion | flops 50331648 | bytes 84967424 | tf_op jit(solution)/shard_map/while/body/eval_jaxpr/convert_element_type | solution.py:209
  1658.6 21.0 dynamic_update_slice.22
  1682.9 17.0 fusion.151
  1714.8 24.2 %fusion.153 = (f32[2,4,512]{2,1,0:T(4,128)S(1)}, f32[2,512,4,2048]{3,1,2,0:T(8,128)}) fusion(f32[2,512,4,2048]{3,1,2,0:T(8,128)} %fusion.151, f32[2,4,512]{2,1,0:T(4,128)S(1)} %dynamic-slice_bitcast_fusion.2, pred[512,2048]{1,0:T(8,128)(4,1)S(1)} %fusion.152, bf16[2048,2,64]{0,2,1:T(8,128)(2,1)} %get-tuple-element.501, ...), kind=kOutput, calls=%fused_computation.24.clone.1 | convolution fusion | flops 1115680768 | bytes 69238784 | tf_op jit(solution)/shard_map/while/body/eval_jaxpr/bkrd,ckd->krbc/dot_general | solution.py:205
  1739.0 27.8 %fusion.154 = bf16[2,4,512,2048]{3,2,1,0:T(8,128)(2,1)} fusion(f32[2,512,4,2048]{3,1,2,0:T(8,128)} %get-tuple-element.423, f32[2,512,4,2048]{3,1,2,0:T(8,128)} %fusion.151, f32[2,4,512]{2,1,0:T(4,128)S(1)} %get-tuple-element.424, f32[2,4,512]{2,1,0:T(4,128)S(1)} %dynamic-slice_bitcast_fusion.2, pred[512,2048]{1,0:T(8,128)(4,1)S(1)} %fusion.152), kind=kLoop, calls=%fused_computation.26.clone.1 | loop fusion | flops 50331648 | bytes 84967424 | tf_op jit(solution)/shard_map/while/body/eval_jaxpr/convert_element_type | solution.py:209
  1784.8 21.0 dynamic_update_slice.22
  1896.2 15.7 add_convert_fusion
  1912.2 23.9 %convolution_convert_fusion.2 = bf16[2048,2048]{1,0:T(8,128)(2,1)} fusion(bf16[2048,2048]{1,0:T(8,128)(2,1)} %get-tuple-element.284, bf16[2048,2048]{1,0:T(8,128)(2,1)} %all-gather.22.cloned.1.call-done), kind=kOutput, calls=%fused_computation.67 | convolution fusion | flops 17184063488 | bytes 25165824 | tf_op jit(solution)/shard_map/dot_general | solution.py:47
  1965.9 86.5 %reduce-scatter.18.cloned.1.call-done = bf16[512,2048]{1,0:T(8,128)(2,1)} async-done(((bf16[2048,2048]{1,0:T(8,128)(2,1)}), bf16[512,2048]{1,0:T(8,128)(2,1)}) %reduce-scatter.18.cloned.1.call-update) | async-done | bytes 2097168 | tf_op jit(solution)/shard_map/reduce_scatter | solution.py:257
  2055.3 40.2 %all-reduce = (f32[2048]{0:T(1024)}, f32[2048]{0:T(1024)}, f32[64]{0:T(128)}, f32[64]{0:T(128)}) all-reduce(f32[2048]{0:T(1024)S(1)} %get-tuple-element.229, f32[2048]{0:T(1024)S(1)} %copy-done.54, f32[64]{0:T(128)S(1)} %get-tuple-element.225, f32[64]{0:T(128)S(1)} %get-tuple-element.231), channel_id=1, replica_groups=mesh['dp'=8,'tensor'=4] {'dp','tensor'}, use_global_device_ids=true, to_apply=%region_27.28 | all-reduce | flops 4224 | bytes 33792 | tf_op jit(solution)/shard_map/psum | solution.py:276
  2095.5 47.5 %reduce-scatter.14.cloned.1.call-done = bf16[512,2048]{1,0:T(8,128)(2,1)} async-done(((bf16[2048,2048]{1,0:T(8,128)(2,1)}), bf16[512,2048]{1,0:T(8,128)(2,1)}) %reduce-scatter.14.cloned.1.call-update) | async-done | bytes 2097168 | tf_op jit(solution)/shard_map/reduce_scatter | solution.py:157
  (369 shorter events, 478.1 us)
Async XLA Ops:
  7.2 96.7 %all-gather.10.cloned.1.call-start = ((), (), s32[]{:S(2)}) async-start(), calls=%async_computation.11 | async-start | bytes 10485760 | tf_op jit(solution)/shard_map/all_gather | solution.py:88
  9.9 22.8 %copy-start.48 = (bf16[256,128]{1,0:T(8,128)(2,1)S(1)}, bf16[256,128]{1,0:T(8,128)(2,1)}, u32[]{:S(2)}) copy-start(bf16[256,128]{1,0:T(8,128)(2,1)} %param.24) | copy-start | bytes 196612
  13.4 121.2 %all-gather.12.cloned.1.call-start = ((), (), s32[]{:S(2)}) async-start(), calls=%async_computation.12 | async-start | bytes 2359296 | tf_op jit(solution)/shard_map/all_gather | solution.py:90
  14.2 344.1 %all-gather.14.cloned.1.call-start = ((), (), s32[]{:S(2)}) async-start(), calls=%async_computation.13 | async-start | bytes 2359296 | tf_op jit(solution)/shard_map/all_gather | solution.py:93
  14.9 510.2 %reduce-scatter.12.cloned.1.call-start = ((), (), s32[]{:S(2)}) async-start(), calls=%async_computation.14 | async-start | bytes 20971520 | tf_op jit(solution)/shard_map/reduce_scatter | solution.py:140
  15.0 33.7 %copy-start.64 = (f32[32]{0:T(128)}, f32[32]{0:T(128)S(1)}, u32[]{:S(2)}) copy-start(f32[32]{0:T(128)S(1)} %multiply_power_fusion) | copy-start | bytes 388
  16.1 133.9 %copy-start.13 = (f32[2048,64]{0,1:T(8,128)}, f32[2048,64]{0,1:T(8,128)S(1)}, u32[]{:S(2)}) copy-start(f32[2048,64]{0,1:T(8,128)S(1)} %pad_maximum_fusion.1) | copy-start | bytes 1572868
  16.2 133.9 %copy-start.15 = (f32[2048,64]{0,1:T(8,128)}, f32[2048,64]{0,1:T(8,128)S(1)}, u32[]{:S(2)}) copy-start(f32[2048,64]{0,1:T(8,128)S(1)} %pad_maximum_fusion.2) | copy-start | bytes 1572868
  32.8 77.5 %copy-start.20 = (bf16[2048,128]{1,0:T(8,128)(2,1)}, bf16[2048,128]{1,0:T(8,128)(2,1)S(1)}, u32[]{:S(2)}) copy-start(bf16[2048,128]{1,0:T(8,128)(2,1)S(1)} %all_gather.35) | copy-start | bytes 1572868
  48.7 61.5 %copy-start.59 = (f32[64]{0:T(128)S(1)}, f32[64]{0:T(128)}, u32[]{:S(2)}) copy-start(f32[64]{0:T(128)} %param.32) | copy-start | bytes 772
  110.2 39.8 %copy-start.7 = (f32[2048,128]{0,1:T(8,128)}, f32[2048,128]{0,1:T(8,128)S(1)}, u32[]{:S(2)}) copy-start(f32[2048,128]{0,1:T(8,128)S(1)} %get-tuple-element.300) | copy-start | bytes 3145732
  110.3 39.8 %copy-start.38 = (f32[2048,2]{0,1:T(2,128)}, f32[2048,2]{0,1:T(2,128)S(1)}, u32[]{:S(2)}) copy-start(f32[2048,2]{0,1:T(2,128)S(1)} %add_rsqrt_fusion.1) | copy-start | bytes 49156
  110.6 34.7 %copy-start.61 = (f32[64]{0:T(128)S(1)}, f32[64]{0:T(128)}, u32[]{:S(2)}) copy-start(f32[64]{0:T(128)} %param.31) | copy-start | bytes 772
  371.6 153.6 %copy-start.5 = (bf16[512,2048]{1,0:T(8,128)(2,1)S(1)}, bf16[512,2048]{1,0:T(8,128)(2,1)}, u32[]{:S(2)}) copy-start(bf16[512,2048]{1,0:T(8,128)(2,1)} %param.19) | copy-start | bytes 6291460
  371.6 237.1 %all-gather.20.cloned.1.call-start = ((), (), s32[]{:S(2)}) async-start(), calls=%async_computation.17 | async-start | bytes 9437184 | tf_op jit(solution)/shard_map/all_gather | solution.py:150
  372.2 157.9 %copy-start.41 = (f32[2048]{0:T(1024)S(1)}, f32[2048]{0:T(1024)}, u32[]{:S(2)}) copy-start(f32[2048]{0:T(1024)} %param.30) | copy-start | bytes 24580
  372.2 324.9 %all-gather.16.cloned.1.call-start = ((), (), s32[]{:S(2)}) async-start(), calls=%async_computation.15 | async-start | bytes 10485760 | tf_op jit(solution)/shard_map/all_gather | solution.py:147
  531.8 249.0 %all-gather.18.cloned.1.call-start = ((), (), s32[]{:S(2)}) async-start(), calls=%async_computation.16 | async-start | bytes 9437184 | tf_op jit(solution)/shard_map/all_gather | solution.py:149
  532.6 336.3 %all-gather.24.cloned.1.call-start = ((), (), s32[]{:S(2)}) async-start(), calls=%async_computation.20 | async-start | bytes 10485760 | tf_op jit(solution)/shard_map/all_gather | solution.py:162
  533.3 419.2 %all-gather.22.cloned.1.call-start = ((), (), s32[]{:S(2)}) async-start(), calls=%async_computation.18 | async-start | bytes 9437184 | tf_op jit(solution)/shard_map/all_gather | solution.py:151
  534.1 656.8 %reduce-scatter.16.cloned.1.call-start = ((), (), s32[]{:S(2)}) async-start(), calls=%async_computation.21 | async-start | bytes 20971520 | tf_op jit(solution)/shard_map/reduce_scatter | solution.py:171
  1038.3 152.5 %copy-start.42 = (f32[2048]{0:T(1024)S(1)}, f32[2048]{0:T(1024)}, u32[]{:S(2)}) copy-start(f32[2048]{0:T(1024)} %param.30) | copy-start | bytes 24580
  1038.3 152.5 %copy-start.50 = (f32[512]{0:T(512)S(1)}, f32[512]{0:T(512)}, u32[]{:S(2)}) copy-start(f32[512]{0:T(512)} %copy-done.49) | copy-start | bytes 6148
  1038.3 158.3 %copy-start.11 = (bf16[512,2048]{1,0:T(8,128)(2,1)S(1)}, bf16[512,2048]{1,0:T(8,128)(2,1)}, u32[]{:S(2)}) copy-start(bf16[512,2048]{1,0:T(8,128)(2,1)} %param.33) | copy-start | bytes 6291460
  1038.3 248.7 %all-gather.26.cloned.1.call-start = ((), (), s32[]{:S(2)}) async-start(), calls=%async_computation.22 | async-start | bytes 10485760 | tf_op jit(solution)/shard_map/all_gather | solution.py:191
  1199.3 736.8 %reduce-scatter.32.cloned.1.call-start = ((), (), s32[]{:S(2)}) async-start(), calls=%async_computation.30 | async-start | bytes 9437184 | tf_op jit(solution)/shard_map/reduce_scatter | solution.py:184
  1223.1 715.6 %reduce-scatter.30.cloned.1.call-start = ((), (), s32[]{:S(2)}) async-start(), calls=%async_computation.29 | async-start | bytes 9437184 | tf_op jit(solution)/shard_map/reduce_scatter | solution.py:181
  1247.1 694.6 %reduce-scatter.28.cloned.1.call-start = ((), (), s32[]{:S(2)}) async-start(), calls=%async_computation.28 | async-start | bytes 9437184 | tf_op jit(solution)/shard_map/reduce_scatter | solution.py:178
  1281.7 662.8 %reduce-scatter.24.cloned.1.call-start = ((), (), s32[]{:S(2)}) async-start(), calls=%async_computation.26 | async-start | bytes 589824 | tf_op jit(solution)/shard_map/reduce_scatter | solution.py:267
  1300.6 17.4 copy-start.23
  1333.2 24.4 %copy-start.37 = (f32[2048,2,64]{0,2,1:T(8,128)}, f32[2048,2,64]{0,2,1:T(8,128)S(1)}, u32[]{:S(2)}) copy-start(f32[2048,2,64]{0,2,1:T(8,128)S(1)} %fusion.156) | copy-start | bytes 3145732 | tf_op jit(solution)/shard_map/while
  1428.3 17.4 copy-start.23
  1428.3 17.3 copy-start.36
  1461.0 24.5 %copy-start.37 = (f32[2048,2,64]{0,2,1:T(8,128)}, f32[2048,2,64]{0,2,1:T(8,128)S(1)}, u32[]{:S(2)}) copy-start(f32[2048,2,64]{0,2,1:T(8,128)S(1)} %fusion.156) | copy-start | bytes 3145732 | tf_op jit(solution)/shard_map/while
  1588.6 24.3 %copy-start.37 = (f32[2048,2,64]{0,2,1:T(8,128)}, f32[2048,2,64]{0,2,1:T(8,128)S(1)}, u32[]{:S(2)}) copy-start(f32[2048,2,64]{0,2,1:T(8,128)S(1)} %fusion.156) | copy-start | bytes 3145732 | tf_op jit(solution)/shard_map/while
  1714.8 24.3 %copy-start.37 = (f32[2048,2,64]{0,2,1:T(8,128)}, f32[2048,2,64]{0,2,1:T(8,128)S(1)}, u32[]{:S(2)}) copy-start(f32[2048,2,64]{0,2,1:T(8,128)S(1)} %fusion.156) | copy-start | bytes 3145732 | tf_op jit(solution)/shard_map/while
  1826.9 119.1 %reduce-scatter.22.cloned.1.call-start = ((), (), s32[]{:S(2)}) async-start(), calls=%async_computation.25 | async-start | bytes 589824 | tf_op jit(solution)/shard_map/reduce_scatter | solution.py:264
  1834.8 112.7 %reduce-scatter.26.cloned.1.call-start = ((), (), s32[]{:S(2)}) async-start(), calls=%async_computation.27 | async-start | bytes 2359296 | tf_op jit(solution)/shard_map/reduce_scatter | solution.py:270
  1844.3 119.8 %reduce-scatter.20.cloned.1.call-start = ((), (), s32[]{:S(2)}) async-start(), calls=%async_computation.24 | async-start | bytes 2359296 | tf_op jit(solution)/shard_map/reduce_scatter | solution.py:261
  1879.7 172.7 %reduce-scatter.18.cloned.1.call-start = ((), (), s32[]{:S(2)}) async-start(), calls=%async_computation.23 | async-start | bytes 10485760 | tf_op jit(solution)/shard_map/reduce_scatter | solution.py:257
  1911.9 231.0 %reduce-scatter.14.cloned.1.call-start = ((), (), s32[]{:S(2)}) async-start(), calls=%async_computation.19 | async-start | bytes 10485760 | tf_op jit(solution)/shard_map/reduce_scatter | solution.py:157
  1938.7 113.7 %copy-start.6 = (bf16[512,2048]{1,0:T(8,128)(2,1)S(1)}, bf16[512,2048]{1,0:T(8,128)(2,1)}, u32[]{:S(2)}) copy-start(bf16[512,2048]{1,0:T(8,128)(2,1)} %param.19) | copy-start | bytes 6291460
  1938.7 113.7 %copy-start.44 = (f32[2048]{0:T(1024)S(1)}, f32[2048]{0:T(1024)}, u32[]{:S(2)}) copy-start(f32[2048]{0:T(1024)} %param.29) | copy-start | bytes 24580
  1938.7 113.7 %copy-start.53 = (f32[512]{0:T(512)S(1)}, f32[512]{0:T(512)}, u32[]{:S(2)}) copy-start(f32[512]{0:T(512)} %copy-done.52) | copy-start | bytes 6148
  1941.6 113.7 %copy-start.54 = (f32[2048]{0:T(1024)S(1)}, f32[2048]{0:T(1024)}, u32[]{:S(2)}) copy-start(f32[2048]{0:T(1024)} %get-tuple-element.227) | copy-start | bytes 24580
  1941.7 201.3 %copy-start.43 = (f32[2048]{0:T(1024)S(1)}, f32[2048]{0:T(1024)}, u32[]{:S(2)}) copy-start(f32[2048]{0:T(1024)} %param.30) | copy-start | bytes 24580
  1941.7 201.3 %copy-start.51 = (f32[512]{0:T(512)S(1)}, f32[512]{0:T(512)}, u32[]{:S(2)}) copy-start(f32[512]{0:T(512)} %copy-done.49) | copy-start | bytes 6148
  1941.7 201.3 %copy-start.56 = (f32[512]{0:T(512)S(1)}, f32[512]{0:T(512)}, u32[]{:S(2)}) copy-start(f32[512]{0:T(512)} %copy-done.55) | copy-start | bytes 6148
  (58 other events, 364.0 us)
Sparse Core Ops, SparseCore 0:
  13.6 90.2 all-gather.9
  105.5 29.0 all-gather.11
  136.2 28.5 all-gather.13
  371.7 153.3 reduce-scatter.11
  526.6 82.0 all-gather.19
  611.0 86.1 all-gather.15
  698.7 82.0 all-gather.17
  782.7 86.1 all-gather.23
  870.5 82.0 all-gather.21
  1038.4 152.3 reduce-scatter.15
  1199.4 87.6 all-gather.25
  1289.2 89.5 reduce-scatter.31
  1381.1 87.9 reduce-scatter.29
  1471.3 87.9 reduce-scatter.27
  1827.0 31.7 reduce-scatter.23
  1861.6 29.1 reduce-scatter.21
  1892.9 33.9 reduce-scatter.25
  1929.6 34.4 reduce-scatter.19
  1967.2 85.1 reduce-scatter.17
  2055.6 87.3 reduce-scatter.13
where the time goes:
time: 2170 us; the launch traced here: 2160 us
  waiting for transfers between devices  913 us (42%)
  matrix products  738 us (34%)
  other arithmetic  262 us (12%)
  local copies, waits for them, and re-layouts  150 us (7%)
  blocking collectives  72.7 us (3%)
    reduce_scatter x1, waiting for transfers between devices, per_device(): lax.psum_scatter(contract_cols(attended, wo_all), 'tensor', scatter_dimen...  152 us
    reduce_scatter x1, waiting for transfers between devices, per_device(): lax.psum_scatter(contract_cols(grad_gate, wg_all) + contract_cols(grad_up...  152 us
    dot_general x8, matrix products, block_scores(): jnp.einsum('bkrd,ckd->krbc', query_block, keys, preferred_element_type=jn...  128 us
    dot_general x7, matrix products, contract_cols(): lax.dot_general(left, right, (((1,), (1,)), ((), ())), preferred_element_...  120 us
    convert_element_type x4, other arithmetic, back_block(): (probabilities * (grad_probs - row_delta)).astype(jnp.bfloat16)  112 us
    dot_general x4, matrix products, back_block(): jnp.einsum('bkrd,ckd->krbc', grad_block, values, preferred_element_type=j...  97.4 us
    dot_general x7, matrix products, contract_rows(): lax.dot_general(left, right, (((0,), (0,)), ((), ())), preferred_element_...  97.2 us
    all_gather x1, waiting for transfers between devices, per_device(): rows_two = lax.all_gather(hidden_two, 'tensor', axis=0, tiled=True)  88.4 us
  transfers between devices with their start and end apart: 20, of which 13 were waited for; matrix products, arithmetic and copies ran while one was open for 47% of the time, Pallas kernels for 0%

commit v1 on v0

v1 whole, which is shorter than its diff:
```python
import functools

import jax
import jax.numpy as jnp
from jax import lax
from jax.experimental import pallas as pl
from jax.experimental.pallas import tpu as pltpu
from jax.sharding import PartitionSpec as P

EPS = 1e-05
THETA = 1000000.0
SEQ = 1024
TILE = 256
LOG2E = 1.4426950408889634
MASKED = -1e30
NT = (((1,), (1,)), ((), ()))
TN = (((0,), (0,)), ((), ()))


def rms_scale(values):
    return lax.rsqrt(jnp.mean(values * values, axis=-1, keepdims=True) + EPS)


def norm_back(grad_normed, normed, inverse):
    return inverse * (grad_normed - normed * jnp.mean(grad_normed * normed, axis=-1, keepdims=True))


def rotary_tables(places):
    lane = jnp.arange(128)
    frequency = THETA ** (-(lane % 32).astype(jnp.float32) * 2.0 / 64)
    angles = places.astype(jnp.float32)[:, None] * frequency[None, :]
    sine = jnp.sin(angles)
    upper = (lane % 64 >= 32)[None, :]
    return jnp.cos(angles), jnp.where(upper, 0.0, -sine), jnp.where(upper, sine, 0.0)


def contract_rows(left, right):
    return lax.dot_general(
        left, right, (((0,), (0,)), ((), ())), preferred_element_type=jnp.float32
    )


def half_lanes(rows):
    return lax.broadcasted_iota(jnp.int32, (rows, 128), 1) < 64


def ones_side(side, rows):
    low = half_lanes(rows)
    return jnp.where(low if side == 0 else ~low, 1.0, 0.0).astype(jnp.bfloat16)


def attend_kernel(q_ref, k_ref, v_ref, segc_ref, segr_ref, out_ref, inv_ref, bias_ref, total_ref):
    coef = LOG2E * 64 ** (-0.5)

    @pl.when(pl.program_id(1) == 0)
    def _():
        for at in range(0, SEQ, TILE):
            end = at + TILE
            rows = lax.broadcasted_iota(jnp.int32, (TILE, end), 0) + at
            cols = lax.broadcasted_iota(jnp.int32, (TILE, end), 1)
            allowed = (segc_ref[at:end, :] == segr_ref[0, :, :end]) & (cols <= rows)
            bias_ref[at:end, :end] = jnp.where(allowed, 0.0, MASKED)

    for side in range(2):
        lanes = slice(side * 128, side * 128 + 128)
        for key_at in range(0, SEQ, TILE):
            keys, rows = slice(key_at, key_at + TILE), slice(key_at, SEQ)
            scores = lax.dot_general(
                q_ref[rows, :], k_ref[keys, lanes], NT, preferred_element_type=jnp.float32
            )
            weights = jnp.exp2(scores * coef + bias_ref[rows, keys]).astype(jnp.bfloat16)
            mixed = jnp.concatenate([v_ref[keys, lanes], ones_side(side, TILE)], axis=1)
            part = jnp.dot(weights, mixed, preferred_element_type=jnp.float32)
            if side == 0 and key_at == 0:
                total_ref[...] = part
            else:
                total_ref[rows, :] += part
    inverse = 1.0 / total_ref[:, 128:]
    out_ref[...] = (total_ref[:, :128] * inverse).astype(jnp.bfloat16)
    inv_ref[...] = inverse


def unrotated(grads, raw, cosine, sine_low, sine_high, gain):
    grads = grads * 0.125
    turned = (
        grads * cosine
        - pltpu.roll(grads, 96, 1) * sine_low
        - pltpu.roll(grads, 32, 1) * sine_high
    )
    inverse = head_inverse(raw)
    normed = raw * inverse
    scaled = turned * gain
    change = inverse * (scaled - normed * head_mean(scaled * normed))
    return change, jnp.sum((turned * normed).reshape(-1, 8, 128), axis=0)


def attend_back_kernel(
    chunks, inner_ref, q_ref, k_ref, v_ref, segc_ref, segr_ref, out_ref, inv_ref,
    qraw_ref, kraw_ref, cos_ref, low_ref, high_ref, qgain_ref, kgain_ref, *refs,
):
    pieces, results = refs[:chunks], refs[chunks : 2 * chunks]
    (
        qsum_ref, ksum_ref, bias_ref, mix_ref, qside_ref, gside_ref,
        dq_ref, dk_ref, dv_ref, kpair_ref, vpair_ref, grad_ref,
    ) = refs[2 * chunks :]
    chunk_rows = SEQ // chunks
    q_width = 128 * pl.num_programs(1)
    kv_width = (results[0].shape[1] - q_width) // 2

    def rows_of(k):
        return pl.ds(pl.multiple_of((inner_ref[0] ^ k) * chunk_rows, chunk_rows), chunk_rows)

    def put(values, place):
        dq_ref[...] = values
        for k, result_ref in enumerate(results):
            lanes = pl.ds(pl.multiple_of(place, 128), 128)
            result_ref[:, lanes] = dq_ref[rows_of(k), :].astype(jnp.bfloat16)

    coef = LOG2E * 64 ** (-0.5)
    step = pl.program_id(1)

    @pl.when(step == 0)
    def _():
        for key_at in range(0, SEQ, TILE):
            key_end = key_at + TILE
            keys = lax.broadcasted_iota(jnp.int32, (TILE, SEQ - key_at), 0) + key_at
            rows = lax.broadcasted_iota(jnp.int32, (TILE, SEQ - key_at), 1) + key_at
            allowed = (segc_ref[key_at:key_end, :] == segr_ref[0, :, key_at:]) & (keys <= rows)
            bias_ref[key_at:key_end, key_at:] = jnp.where(allowed, 0.0, MASKED)

    @pl.when((step == 0) & (pl.program_id(0) == 0))
    def _():
        qsum_ref[...] = jnp.zeros_like(qsum_ref)
        ksum_ref[...] = jnp.zeros_like(ksum_ref)

    @pl.when(lax.rem(step, 4) == 0)
    def _():
        kpair_ref[...] = jnp.zeros_like(kpair_ref)
        vpair_ref[...] = jnp.zeros_like(vpair_ref)

    @pl.when(lax.rem(step, 2) == 0)
    def _():
        dk_ref[...] = jnp.zeros_like(dk_ref)
        dv_ref[...] = jnp.zeros_like(dv_ref)

    for k, piece_ref in enumerate(pieces):
        grad_ref[rows_of(k), :] = piece_ref[...].astype(jnp.float32)
    low = half_lanes(SEQ)
    scaled = grad_ref[...] * inv_ref[...]
    scaled_low = scaled.astype(jnp.bfloat16)
    mix_ref[:, :128] = scaled_low
    mix_ref[:, 128:] = -(scaled * out_ref[...].astype(jnp.float32)).astype(jnp.bfloat16)
    none = jnp.zeros_like(scaled_low)
    queries = q_ref[...]
    gside_ref[:, :128] = jnp.where(low, scaled_low, none)
    gside_ref[:, 128:] = jnp.where(low, none, scaled_low)
    qside_ref[:, :128] = jnp.where(low, queries, none)
    qside_ref[:, 128:] = jnp.where(low, none, queries)

    for key_at in range(0, SEQ, TILE):
        keys, rows = slice(key_at, key_at + TILE), slice(key_at, SEQ)
        for side in range(2):
            lanes = slice(side * 128, side * 128 + 128)
            key_side = k_ref[keys, lanes]
            value_side = jnp.concatenate([v_ref[keys, lanes], ones_side(side, TILE)], axis=1)
            scores = lax.dot_general(
                key_side, q_ref[rows, :], NT, preferred_element_type=jnp.float32
            )
            weights = jnp.exp2(scores * coef + bias_ref[keys, rows])
            change = lax.dot_general(
                value_side, mix_ref[rows, :], NT, preferred_element_type=jnp.float32
            )
            grads = (weights * change).astype(jnp.bfloat16)
            dv_ref[keys, :] += jnp.dot(
                weights.astype(jnp.bfloat16),
                gside_ref[rows, lanes],
                preferred_element_type=jnp.float32,
            )
            dk_ref[keys, :] += jnp.dot(
                grads, qside_ref[rows, lanes], preferred_element_type=jnp.float32
            )
            dq = lax.dot_general(grads, key_side, TN, preferred_element_type=jnp.float32)
            if key_at == 0 and side == 0:
                dq_ref[...] = dq
            else:
                dq_ref[rows, :] += dq

    cosine, sine_low, sine_high = cos_ref[...], low_ref[...], high_ref[...]
    change, sums = unrotated(
        dq_ref[...], qraw_ref[...], cosine, sine_low, sine_high, qgain_ref[...]
    )
    qsum_ref[...] += sums
    put(change, step * 128)

    @pl.when(lax.rem(step, 2) == 1)
    def _():
        mine = low == (lax.rem(step, 4) == 1)
        for sum_ref, pair_ref in ((dk_ref, kpair_ref), (dv_ref, vpair_ref)):
            sums = sum_ref[...]
            pair_ref[...] = jnp.where(mine, sums + pltpu.roll(sums, 64, 1), pair_ref[...])

    @pl.when((lax.rem(step, 4) == 3) | (step == pl.num_programs(1) - 1))
    def _():
        change, sums = unrotated(
            kpair_ref[...], kraw_ref[...], cosine, sine_low, sine_high, kgain_ref[...]
        )
        ksum_ref[...] += sums
        put(change, q_width + step // 4 * 128)
        put(vpair_ref[...], q_width + kv_width + step // 4 * 128)


def attention_specs():
    pair = pl.BlockSpec((SEQ, 128), lambda s, p, *_: (s, p))
    group = pl.BlockSpec((SEQ, 256), lambda s, p, *_: (s, p // 2))
    seg_col = pl.BlockSpec((SEQ, 1), lambda s, p, *_: (s, 0))
    seg_row = pl.BlockSpec((1, 1, SEQ), lambda s, p, *_: (s, 0, 0))
    return pair, group, seg_col, seg_row


def attend(queries, key_sides, value_sides, segments):
    rows, width = queries.shape
    sequences, pairs = rows // SEQ, width // 128
    pair, group, seg_col, seg_row = attention_specs()
    work = rows * SEQ * width
    return pl.pallas_call(
        attend_kernel,
        grid=(sequences, pairs),
        in_specs=[pair, group, group, seg_col, seg_row],
        out_specs=[pair, pair],
        out_shape=[
            jax.ShapeDtypeStruct((rows, width), jnp.bfloat16),
            jax.ShapeDtypeStruct((rows, width), jnp.float32),
        ],
        scratch_shapes=[pltpu.VMEM((SEQ, SEQ), jnp.float32), pltpu.VMEM((SEQ, 256), jnp.float32)],
        compiler_params=pltpu.CompilerParams(vmem_limit_bytes=60 * 2**20),
        cost_estimate=pl.CostEstimate(
            flops=42 * work // 10, bytes_accessed=rows * width * 12, transcendentals=work // 128
        ),
    )(queries, key_sides, value_sides, segments[:, None], segments.reshape(sequences, 1, SEQ))


def attend_back(
    inner, sequence, queries, key_sides, value_sides, segments, attended, inverse, pieces, raw, tables,
    query_gain, key_gain,
):
    width = queries.shape[1]
    pairs, chunks, chunk_rows = width // 128, len(pieces), pieces[0].shape[0]
    kv_width = key_sides.shape[1] // 4
    pair, group, seg_col, seg_row = attention_specs()
    kv_raw = pl.BlockSpec((SEQ, 128), lambda s, p, *_: (0, width // 128 + p // 4))
    table = pl.BlockSpec((SEQ, 128), lambda s, p, *_: (sequence, 0))
    gain = pl.BlockSpec((1, 128), lambda s, p, *_: (0, 0))
    total = pl.BlockSpec((8, 128), lambda s, p, *_: (0, 0))
    piece = pl.BlockSpec((chunk_rows, 128), lambda s, p, *_: (0, p))
    columns = width + 2 * kv_width
    work = SEQ * SEQ * width
    flat = pltpu.VMEM((SEQ, 128), jnp.float32)
    return pl.pallas_call(
        functools.partial(attend_back_kernel, chunks),
        grid_spec=pltpu.PrefetchScalarGridSpec(
            num_scalar_prefetch=1,
            grid=(1, pairs),
            in_specs=[pair, group, group, seg_col, seg_row, pair, pair]
            + [pair, kv_raw, table, table, table, gain, gain]
            + [piece] * chunks,
            out_specs=[pl.BlockSpec((chunk_rows, columns), lambda s, p, *_: (0, 0))] * chunks
            + [total, total],
            scratch_shapes=[
                pltpu.VMEM((SEQ, SEQ), jnp.float32),
                pltpu.VMEM((SEQ, 256), jnp.bfloat16),
                pltpu.VMEM((SEQ, 256), jnp.bfloat16),
                pltpu.VMEM((SEQ, 256), jnp.bfloat16),
                flat, flat, flat, flat, flat, flat,
            ],
        ),
        out_shape=[jax.ShapeDtypeStruct((chunk_rows, columns), jnp.bfloat16)] * chunks
        + [jax.ShapeDtypeStruct((8, 128), jnp.float32)] * 2,
        compiler_params=pltpu.CompilerParams(vmem_limit_bytes=60 * 2**20),
        cost_estimate=pl.CostEstimate(
            flops=110 * work // 10, bytes_accessed=SEQ * width * 20, transcendentals=work // 128
        ),
    )(
        inner, queries, key_sides, value_sides, segments[:, None], segments.reshape(-1, 1, SEQ),
        attended, inverse, raw, raw, *tables,
        jnp.tile(query_gain, 2)[None, :], jnp.tile(key_gain, 2)[None, :], *pieces,
    )


def cost(flops, moved, share):
    return pl.CostEstimate(
        flops=int(0.2 * flops / share), bytes_accessed=int(0.2 * moved), transcendentals=0
    )


def head_inverse(values):
    squares = values * values
    high = squares.astype(jnp.bfloat16)
    low = (squares - high.astype(jnp.float32)).astype(jnp.bfloat16)
    return lax.rsqrt(head_sum(high, low) * (1.0 / 64) + EPS)


def head_sum(high, low):
    from_head = lax.broadcasted_iota(jnp.int32, (128, 128), 0) // 64
    to_head = lax.broadcasted_iota(jnp.int32, (128, 128), 1) // 64
    same = jnp.where(from_head == to_head, 1.0, 0.0).astype(jnp.bfloat16)
    return jnp.dot(high, same, preferred_element_type=jnp.float32) + jnp.dot(
        low, same, preferred_element_type=jnp.float32
    )


def head_mean(values):
    high = values.astype(jnp.bfloat16)
    low = (values - high.astype(jnp.float32)).astype(jnp.bfloat16)
    return head_sum(high, low) * (1.0 / 64)


def project_kernel(
    pieces, inner_ref, *refs,
):
    norm_ref, w_ref, cos_ref, low_ref, high_ref, qgain_ref, kgain_ref = refs[pieces : pieces + 7]
    inv_ref, q_ref, k_ref, v_ref, raw_ref = refs[pieces + 7 :]
    inputs = refs[0][...].astype(jnp.float32)
    inverse = rms_scale(inputs)
    hidden = (inputs * inverse * norm_ref[...]).astype(jnp.bfloat16)
    inv_ref[...] = jnp.broadcast_to(inverse, inv_ref.shape)
    q_width, kv_width = q_ref.shape[1], k_ref.shape[1] // 4
    cosine, sine_low, sine_high = cos_ref[...], low_ref[...], high_ref[...]
    lower = lax.broadcasted_iota(jnp.int32, cosine.shape, 1) < 64
    none = jnp.zeros_like(cosine)

    def rotated(raw, gain):
        scaled = raw * head_inverse(raw) * gain
        return (
            scaled * cosine
            + pltpu.roll(scaled, 96, 1) * sine_low
            + pltpu.roll(scaled, 32, 1) * sine_high
        )

    def to_sides(pair, out_ref, at):
        first, second = jnp.where(lower, pair, none), jnp.where(lower, none, pair)
        sides = (first, pltpu.roll(first, 64, 1), pltpu.roll(second, 64, 1), second)
        for index, side in enumerate(sides):
            lanes = slice(at * 4 + index * 128, at * 4 + index * 128 + 128)
            out_ref[:, lanes] = side.astype(jnp.bfloat16)

    wide = jnp.dot(hidden, w_ref[:, q_width:], preferred_element_type=jnp.float32)
    raw_ref[...] = wide[:, : q_width + kv_width]
    for at in range(0, q_width, 128):
        q_ref[:, at : at + 128] = rotated(wide[:, at : at + 128], qgain_ref[...]).astype(
            jnp.bfloat16
        )
    for at in range(0, kv_width, 128):
        place = q_width + at
        to_sides(rotated(wide[:, place : place + 128], kgain_ref[...]), k_ref, at)
        place = q_width + kv_width + at
        to_sides(wide[:, place : place + 128], v_ref, at)


def placed(chunk_rows, block):
    per = chunk_rows // block
    here = lambda r, inner: (r, 0)
    there = lambda r, inner: ((r // per ^ inner[0]) * per + r % per, 0)
    return here, there


def project(inner, sequence, inputs, chunk_rows, norm, weights, tables, query_gain, key_gain, q_width, kv_width):
    rows, width = inputs.shape
    block = chunk_rows
    here, there = placed(block, block)
    fixed = lambda r, mine: (0, 0)
    used = q_width + 2 * kv_width
    table = pl.BlockSpec(
        (block, 128), lambda r, inner: (sequence * (rows // block) + there(r, inner)[0], 0)
    )
    gain = pl.BlockSpec((1, 128), fixed)
    return pl.pallas_call(
        functools.partial(project_kernel, 1),
        grid_spec=pltpu.PrefetchScalarGridSpec(
            num_scalar_prefetch=1,
            grid=(rows // block,),
            in_specs=[
                pl.BlockSpec((block, width), here),
                pl.BlockSpec((1, width), fixed),
                pl.BlockSpec(weights.shape, fixed, pipeline_mode=pl.Buffered(1)),
                table, table, table, gain, gain,
            ],
            out_specs=[
                pl.BlockSpec((block, 128), here),
                pl.BlockSpec((block, q_width), there),
                pl.BlockSpec((block, 4 * kv_width), there),
                pl.BlockSpec((block, 4 * kv_width), there),
                pl.BlockSpec((block, q_width + kv_width), there),
            ],
        ),
        out_shape=[
            jax.ShapeDtypeStruct((rows, 128), jnp.float32),
            jax.ShapeDtypeStruct((rows, q_width), jnp.bfloat16),
            jax.ShapeDtypeStruct((rows, 4 * kv_width), jnp.bfloat16),
            jax.ShapeDtypeStruct((rows, 4 * kv_width), jnp.bfloat16),
            jax.ShapeDtypeStruct((rows, q_width + kv_width), jnp.float32),
        ],
        compiler_params=pltpu.CompilerParams(vmem_limit_bytes=60 * 2**20),
        cost_estimate=cost(2 * rows * width * used, rows * width * 6, 0.22),
    )(
        inner, inputs, norm[None, :], weights, *tables,
        jnp.tile(query_gain, 2)[None, :], jnp.tile(key_gain, 2)[None, :],
    )


def heads_kernel(count, core_ref, grads_ref, *refs):
    rights, outs = refs[: 2 * count - 1], refs[2 * count - 1 :]
    outs[0][...] = jnp.dot(
        grads_ref[...], rights[0][...], preferred_element_type=jnp.float32
    ).astype(jnp.bfloat16)
    half = rights[1].shape[0]
    near = grads_ref[:, pl.ds(pl.multiple_of(core_ref[0] * half, half), half)]
    other = grads_ref[:, pl.ds(pl.multiple_of((1 - core_ref[0]) * half, half), half)]
    for k in range(1, count):
        outs[k][...] = (
            jnp.dot(near, rights[k][...], preferred_element_type=jnp.float32)
            + jnp.dot(other, rights[count - 1 + k][...], preferred_element_type=jnp.float32)
        ).astype(jnp.bfloat16)


def grad_heads(core, grads, own, others, q_width, count):
    rows, width = grads.shape
    fixed = lambda i, core: (0, 0)
    return pl.pallas_call(
        functools.partial(heads_kernel, count),
        grid_spec=pltpu.PrefetchScalarGridSpec(
            num_scalar_prefetch=1,
            grid=(1,),
            in_specs=[pl.BlockSpec(grads.shape, fixed), pl.BlockSpec((width, q_width), fixed)]
            + [pl.BlockSpec(piece.shape, fixed) for piece in others],
            out_specs=[pl.BlockSpec((rows, q_width), fixed)] * count,
        ),
        out_shape=[jax.ShapeDtypeStruct((rows, q_width), jnp.bfloat16)] * count,
        compiler_params=pltpu.CompilerParams(vmem_limit_bytes=60 * 2**20),
        cost_estimate=cost(2 * rows * width * q_width * count, rows * width, 2.67),
    )(core, grads, own, *others)


def peer(distance):
    mine = lax.axis_index("tensor")
    if distance == 1:
        return mine + 1 - 2 * (mine % 2)
    return (mine + 2) % 4 if distance == 2 else 3 - mine


def remote(distance):
    return dict(device_id={"tensor": peer(distance)}, device_id_type=pl.DeviceIdType.MESH)


def greet(distances):
    barrier = pltpu.get_barrier_semaphore()
    for distance in distances:
        pl.semaphore_signal(barrier, inc=1, **remote(distance))
    pl.semaphore_wait(barrier, len(distances))


def carry(distances, src_refs, dst_refs, send_sems=None, recv_sems=None):
    if not distances:
        return
    copies = [
        pltpu.make_async_remote_copy(
            src_ref=src_ref, dst_ref=dst_ref, send_sem=send_sems.at[i], recv_sem=recv_sems.at[i],
            **remote(distance),
        )
        for i, (distance, src_ref, dst_ref) in enumerate(zip(distances, src_refs, dst_refs))
    ]

    @pl.when(pl.program_id(0) == 0)
    def _():
        greet(sorted(set(distances)))
        for sent in copies:
            sent.start()

    @pl.when(pl.program_id(0) == pl.num_programs(0) - 1)
    def _():
        for sent in copies:
            sent.wait()


def carried(sends, collective_id):
    place = pl.BlockSpec(memory_space=pl.ANY)
    count = len(sends)
    if not count:
        return [], [], [], [], {}, []
    return (
        [place] * count,
        [place] * count,
        [jax.ShapeDtypeStruct(value.shape, value.dtype) for _, value in sends],
        [pltpu.SemaphoreType.DMA((count,)), pltpu.SemaphoreType.DMA((count,))],
        dict(collective_id=collective_id, has_side_effects=True),
        [value for _, value in sends],
    )


def hidden_kernel(filled, distances, x_ref, dy_ref, w_ref, *refs):
    refs, count = refs[filled:], len(distances)
    act_ref, grads_ref = refs[count : count + 2]
    carry(distances, refs[:count], refs[count + 2 : 2 * count + 2], *refs[2 * count + 2 :])
    units = act_ref.shape[1]
    inputs, cotangent = x_ref[...], dy_ref[...]
    for at in range(0, units, 256):
        lanes = slice(at, at + 256)
        gate = jnp.dot(inputs, w_ref[:, lanes], preferred_element_type=jnp.float32)
        up = jnp.dot(
            inputs, w_ref[:, units + at : units + at + 256], preferred_element_type=jnp.float32
        )
        change = jnp.dot(
            cotangent, w_ref[:, 2 * units + at : 2 * units + at + 256],
            preferred_element_type=jnp.float32,
        )
        sigmoid = 1.0 / (1.0 + jnp.exp(-gate))
        silu = gate * sigmoid
        act_ref[:, lanes] = (silu * up).astype(jnp.bfloat16)
        grads_ref[:, lanes] = (change * up * sigmoid * (1.0 + gate - silu)).astype(jnp.bfloat16)
        grads_ref[:, units + at : units + at + 256] = (change * silu).astype(jnp.bfloat16)


def hidden_units(inputs, cotangent, weights, filled, sends=(), collective_id=None):
    rows, width = inputs.shape
    units = weights.shape[1] // 3
    block = min(512, rows)
    row = lambda r: (r, 0)
    place = 0 if filled is None else 1
    in_more, out_more, shapes, scratch, params, operands = carried(sends, collective_id)
    act, grads, *received = pl.pallas_call(
        functools.partial(hidden_kernel, place, [distance for distance, _ in sends]),
        grid=(rows // block,),
        in_specs=[
            pl.BlockSpec((block, width), row),
            pl.BlockSpec((block, width), row),
            pl.BlockSpec(weights.shape, lambda r: (0, 0), pipeline_mode=pl.Buffered(1)),
        ]
        + [pl.BlockSpec(memory_space=pl.ANY)] * place
        + in_more,
        out_specs=[
            pl.BlockSpec((block, units), lambda r: (r, place)),
            pl.BlockSpec((block, 2 * units), row),
        ]
        + out_more,
        out_shape=[
            jax.ShapeDtypeStruct((rows, 2 * units), jnp.bfloat16),
            jax.ShapeDtypeStruct((rows, 2 * units), jnp.bfloat16),
        ]
        + shapes,
        scratch_shapes=scratch,
        input_output_aliases={3: 0} if place else {},
        compiler_params=pltpu.CompilerParams(vmem_limit_bytes=60 * 2**20, **params),
        cost_estimate=cost(6 * rows * width * units, (rows * width + width * units) * 6, 0.63),
    )(inputs, cotangent, weights, *([filled] * place), *operands)
    return act, grads, received


def half_types(distance):
    if distance == 0:
        return (jnp.float32, jnp.float32)
    if distance == 1:
        return (jnp.bfloat16, jnp.float32)
    if distance == 2:
        return (jnp.float32, jnp.bfloat16)
    return (jnp.bfloat16, jnp.bfloat16)


def rows_out_kernel(terms, halves, distances, *refs):
    count = len(distances)
    at = 2 * terms + count
    outs = refs[at : at + halves]
    carry(distances, refs[2 * terms : at], refs[at + halves : at + halves + count], *refs[at + halves + count :])
    total = None
    for left_ref, right_ref in zip(refs[:terms], refs[terms : 2 * terms]):
        product = lax.dot_general(
            left_ref[...], right_ref[...], NT, preferred_element_type=jnp.float32
        )
        total = product if total is None else total + product
    half = outs[0].shape[0]
    for index, out_ref in enumerate(outs):
        out_ref[...] = total[index * half : (index + 1) * half].astype(out_ref.dtype)


def rows_out(distances, lefts, rights, spans, chunk_rows, sends=(), collective_id=None):
    width, rows = rights[0].shape[0], len(distances) * chunk_rows
    first = distances[0] // len(distances)
    halves = [dtype for k in distances for dtype in half_types(k)]
    in_specs = [
        pl.BlockSpec(
            (rows, left[1]), lambda n, index=left[2]: (first, index), pipeline_mode=pl.Buffered(1)
        )
        for left in lefts
    ] + [
        pl.BlockSpec((256, columns), lambda n, index=index: (n, index)) for columns, index in spans
    ]
    depth = sum(left[1] for left in lefts)
    in_more, out_more, shapes, scratch, params, operands = carried(sends, collective_id)
    outs = pl.pallas_call(
        functools.partial(
            rows_out_kernel, len(lefts), len(halves), [distance for distance, _ in sends]
        ),
        grid=(width // 256,),
        in_specs=in_specs + in_more,
        out_specs=[pl.BlockSpec((chunk_rows // 2, 256), lambda n: (0, n))] * len(halves) + out_more,
        out_shape=[jax.ShapeDtypeStruct((chunk_rows // 2, width), dtype) for dtype in halves] + shapes,
        scratch_shapes=scratch,
        compiler_params=pltpu.CompilerParams(vmem_limit_bytes=60 * 2**20, **params),
        cost_estimate=cost(2 * rows * depth * width, depth * rows // 4, 4.07),
    )(*(left[0] for left in lefts), *rights, *operands)
    parts = {k: (outs[2 * i], outs[2 * i + 1]) for i, k in enumerate(distances)}
    return (parts, outs[len(halves) :]) if sends else parts


def resid_kernel(count, place_ref, *refs):
    inputs, lefts = refs[:2], (refs[2 : 2 + count], refs[2 + count : 2 + 2 * count])
    rights = refs[2 + 2 * count : 1 + 4 * count]
    norm_ref, hidden_ref, resid_ref, sums_ref = refs[1 + 4 * count :]
    half = sums_ref.shape[1] // 2
    blocks = pl.num_programs(0) // 2

    def block(x_ref, left_refs):
        for core, others in (
            (place_ref[1], rights[1:count]), (1 - place_ref[1], rights[count:])
        ):
            start = pl.multiple_of(core * half, half)
            total = lax.dot_general(
                left_refs[0][...], rights[0][pl.ds(start, half), :], NT,
                preferred_element_type=jnp.float32,
            )
            for left_ref, right_ref in zip(left_refs[1:], others):
                total = total + lax.dot_general(
                    left_ref[...], right_ref[...], NT, preferred_element_type=jnp.float32
                )
            sums_ref[:, pl.ds(start, half)] = total
        resid = x_ref[...].astype(jnp.float32) + sums_ref[...]
        hidden_ref[...] = (resid * rms_scale(resid) * norm_ref[...]).astype(jnp.bfloat16)

        @pl.when(pl.program_id(0) < resid_ref.shape[0])
        def _():
            resid_ref[pl.program_id(0)] = resid

    for sequence in range(2):

        @pl.when(pl.program_id(0) // blocks == sequence)
        def _():
            block(inputs[sequence], lefts[sequence])


def residual(place, inputs, heads, own, others, norm, chunk_rows):
    width, count = inputs[0].shape[1], len(heads[0])
    q_width = heads[0][0].shape[1]
    rows, block = 2 * SEQ, min(512, chunk_rows)
    here, there = placed(chunk_rows, block)
    blocks = SEQ // block
    fixed = lambda r, place: (0, 0)
    once = pl.Buffered(1)
    steps = (
        lambda r: jnp.minimum(r, blocks - 1),
        lambda r: jnp.maximum(r - blocks, 0),
    )
    return pl.pallas_call(
        functools.partial(resid_kernel, count),
        grid_spec=pltpu.PrefetchScalarGridSpec(
            num_scalar_prefetch=1,
            grid=(rows // block,),
            in_specs=[
                pl.BlockSpec((block, width), lambda r, place, step=step: here(step(r), place))
                for step in steps
            ]
            + [
                pl.BlockSpec((block, q_width), lambda r, place, step=step: there(step(r), place))
                for step in steps
                for _ in range(count)
            ]
            + [pl.BlockSpec((width, q_width), fixed, pipeline_mode=once)]
            + [pl.BlockSpec(piece.shape, fixed, pipeline_mode=once) for piece in others]
            + [pl.BlockSpec((1, width), fixed)],
            out_specs=[
                pl.BlockSpec((block, width), here),
                pl.BlockSpec((chunk_rows // block, block, width), lambda r, place: (0, 0, 0)),
            ],
            scratch_shapes=[pltpu.VMEM((block, width), jnp.float32)],
        ),
        out_shape=[
            jax.ShapeDtypeStruct((rows, width), jnp.bfloat16),
            jax.ShapeDtypeStruct((chunk_rows // block, block, width), jnp.float32),
        ],
        compiler_params=pltpu.CompilerParams(vmem_limit_bytes=60 * 2**20),
        cost_estimate=cost(2 * rows * width * width, rows * width * 8, 0.46),
    )(place, *inputs, *heads[0], *heads[1], own, *others, norm[None, :])


def input_kernel(count, core_ref, *refs):
    lefts, rights = refs[:count], refs[count : 3 * count - 1]
    x_ref, grad_ref, norm_ref, out_ref, gains_ref, sums_ref = refs[3 * count - 1 :]
    used = lefts[0].shape[1]
    step, steps = pl.program_id(0), pl.num_programs(0)

    def block(others):
        own = rights[0][:, rights[0].shape[1] - used :]
        total = lax.dot_general(lefts[0][...], own, NT, preferred_element_type=jnp.float32)
        for left_ref, right_ref in zip(lefts[1:], others):
            total = total + lax.dot_general(
                left_ref[...], right_ref[...], NT, preferred_element_type=jnp.float32
            )
        sums_ref[:, pl.ds(pl.multiple_of(step * 256, 256), 256)] = total

    for half in range(2):

        @pl.when(step // (steps // 2) == (core_ref[0] if half == 0 else 1 - core_ref[0]))
        def _():
            block(rights[1 + half * (count - 1) : 1 + (half + 1) * (count - 1)])

    @pl.when(step == steps - 1)
    def _():
        gains_ref[...] = jnp.zeros_like(gains_ref)
        for at in range(0, sums_ref.shape[0], 64):
            rows = slice(at, at + 64)
            grads = sums_ref[rows, :]
            inputs = x_ref[rows, :].astype(jnp.float32)
            inverse = rms_scale(inputs)
            normed = inputs * inverse
            gains_ref[...] += jnp.sum((grads * normed).reshape(-1, 8, grads.shape[1]), axis=0)
            out_ref[rows, :] = grad_ref[rows, :] + norm_back(
                grads * norm_ref[...], normed, inverse
            )


def input_back(core, grads, own, others, inputs, grad_resid, norm):
    rows, width = inputs.shape
    count, used = len(grads), grads[0].shape[1]
    steps = width // 256
    whole = lambda n, core: (0, 0)
    near = lambda n, core: (jnp.clip(n - core[0] * (steps // 2), 0, steps // 2 - 1), 0)
    other = lambda n, core: (jnp.clip(n - (1 - core[0]) * (steps // 2), 0, steps // 2 - 1), 0)
    once = pl.Buffered(1)
    return pl.pallas_call(
        functools.partial(input_kernel, count),
        grid_spec=pltpu.PrefetchScalarGridSpec(
            num_scalar_prefetch=1,
            grid=(steps,),
            in_specs=[pl.BlockSpec((rows, used), whole, pipeline_mode=once)] * count
            + [pl.BlockSpec((256, own.shape[1]), lambda n, core: (n, 0))]
            + [pl.BlockSpec((256, used), near)] * (count - 1)
            + [pl.BlockSpec((256, used), other)] * (count - 1)
            + [pl.BlockSpec((rows, width), whole, pipeline_mode=once)] * 2
            + [pl.BlockSpec((1, width), whole)],
            out_specs=[pl.BlockSpec((rows, width), whole), pl.BlockSpec((8, width), whole)],
            scratch_shapes=[pltpu.VMEM((rows, width), jnp.float32)],
        ),
        out_shape=[
            jax.ShapeDtypeStruct((rows, width), jnp.float32),
            jax.ShapeDtypeStruct((8, width), jnp.float32),
        ],
        compiler_params=pltpu.CompilerParams(vmem_limit_bytes=60 * 2**20),
        cost_estimate=cost(2 * rows * used * width * count, rows * width * 20, 0.28),
    )(core, *grads, own, *others, inputs, grad_resid, norm[None, :])


def attention_weights_kernel(inner_ref, *refs):
    out_ref = refs[-1]
    total = jnp.zeros(out_ref.shape, jnp.float32)
    pieces, at = [], 0
    chunk_rows = refs[0].shape[0]
    for ref in refs[:-1]:
        if ref.shape[0] < SEQ:
            pieces.append(ref)
            continue
        at = 0
        for piece in pieces:
            rows = piece.shape[0]
            start = (at // chunk_rows ^ inner_ref[0]) * chunk_rows + at % chunk_rows
            total = total + lax.dot_general(
                piece[...], ref[pl.ds(pl.multiple_of(start, rows), rows), :], TN,
                preferred_element_type=jnp.float32,
            )
            at += rows
        pieces = []
    out_ref[...] = total.astype(jnp.bfloat16)


def out_weights(inner, pieces, attended):
    width, q_width = pieces[0][0].shape[1], attended[0].shape[1]
    whole = lambda n, inner: (0, 0)
    in_specs = []
    for rows in range(2):
        in_specs += [pl.BlockSpec((piece.shape[0], 256), lambda n, inner: (0, n)) for piece in pieces[rows]]
        in_specs.append(pl.BlockSpec((SEQ, q_width), whole))
    return pl.pallas_call(
        attention_weights_kernel,
        grid_spec=pltpu.PrefetchScalarGridSpec(
            num_scalar_prefetch=1,
            grid=(width // 256,),
            in_specs=in_specs,
            out_specs=pl.BlockSpec((256, q_width), lambda n, inner: (n, 0)),
        ),
        out_shape=jax.ShapeDtypeStruct((width, q_width), jnp.bfloat16),
        compiler_params=pltpu.CompilerParams(vmem_limit_bytes=60 * 2**20),
        cost_estimate=cost(4 * SEQ * q_width * width, SEQ * width * 4, 0.35),
    )(inner, *pieces[0], attended[0], *pieces[1], attended[1])


def projection_weights_kernel(norm_ref, *refs):
    inputs, inverses, grads, out_ref = refs[:2], refs[2:4], refs[4:-1], refs[-1]
    total = jnp.zeros(out_ref.shape, jnp.float32)
    chunk_rows = grads[0].shape[0]
    for k, grad_ref in enumerate(grads):
        at = k * chunk_rows
        rows = slice(at % SEQ, at % SEQ + chunk_rows)
        inverse = inverses[at // SEQ][rows, :]
        normed = inputs[at // SEQ][rows, :].astype(jnp.float32) * jnp.concatenate([inverse] * 2, axis=1)
        total = total + lax.dot_general(
            (normed * norm_ref[...]).astype(jnp.bfloat16), grad_ref[...], TN,
            preferred_element_type=jnp.float32,
        )
    out_ref[...] = total.astype(jnp.bfloat16)


def projection_weights(inputs, inverse, norm, grads):
    width, columns = inputs[0].shape[1], grads[0].shape[1]
    whole = lambda n: (0, 0)
    column = lambda n: (0, n)
    return pl.pallas_call(
        projection_weights_kernel,
        grid=(width // 256,),
        in_specs=[pl.BlockSpec((1, 256), column)]
        + [pl.BlockSpec((SEQ, 256), column)] * 2
        + [pl.BlockSpec((SEQ, 128), whole)] * 2
        + [pl.BlockSpec(part.shape, whole) for part in grads],
        out_specs=pl.BlockSpec((256, columns), lambda n: (n, 0)),
        out_shape=jax.ShapeDtypeStruct((width, columns), jnp.bfloat16),
        compiler_params=pltpu.CompilerParams(vmem_limit_bytes=60 * 2**20),
        cost_estimate=cost(4 * SEQ * columns * width, SEQ * width * 4, 0.43),
    )(norm[None, :], *inputs, *inverse, *grads)


def shift(values, distance, count, axis="tensor"):
    return lax.ppermute(values, axis, [(i, i ^ distance) for i in range(count)])


def gather_kernel(src_ref, own_ref, other_ref, send_sems, recv_sems, local_sem):
    rows = src_ref.shape[0]
    half = rows // 2
    x_top, x_bottom = own_ref.at[pl.ds(rows, half)], own_ref.at[pl.ds(rows + half, half)]
    y_top, y_bottom = other_ref.at[pl.ds(0, half)], other_ref.at[pl.ds(half, half)]
    far_top, far_bottom = other_ref.at[pl.ds(rows, half)], other_ref.at[pl.ds(rows + half, half)]
    top, bottom = src_ref.at[pl.ds(0, half)], src_ref.at[pl.ds(half, half)]
    greet([1, 2])

    def copy(index, from_ref, to_ref, distance):
        return pltpu.make_async_remote_copy(
            src_ref=from_ref, dst_ref=to_ref, send_sem=send_sems.at[index],
            recv_sem=recv_sems.at[index], **remote(distance),
        )

    first = [
        copy(0, bottom, x_bottom, 1), copy(1, top, y_top, 2),
        copy(2, top, x_top, 1), copy(3, bottom, y_bottom, 2),
    ]
    for sent in first:
        sent.start()
    local = pltpu.make_async_copy(src_ref, own_ref.at[pl.ds(0, rows)], local_sem.at[0])
    local.start()
    first[1].wait_recv()
    relay_top = copy(4, y_top, far_top, 1)
    relay_top.start()
    first[0].wait_recv()
    relay_bottom = copy(5, x_bottom, far_bottom, 2)
    relay_bottom.start()
    first[2].wait_recv()
    first[3].wait_recv()
    relay_top.wait_recv()
    relay_bottom.wait_recv()
    for sent in first + [relay_top, relay_bottom]:
        sent.wait_send()
    local.wait()


def gather_rows(values, count):
    if count != 4:
        near = gather_near(values, count)
        return [jnp.concatenate(near[i : i + count // 2], axis=0) for i in (0, count // 2)]
    place = pl.BlockSpec(memory_space=pl.ANY)
    rows, width = values.shape
    wide = jax.ShapeDtypeStruct((2 * rows, width), values.dtype)
    return pl.pallas_call(
        gather_kernel,
        in_specs=[place],
        out_specs=[place] * 2,
        out_shape=[wide, wide],
        scratch_shapes=[
            pltpu.SemaphoreType.DMA((6,)), pltpu.SemaphoreType.DMA((6,)),
            pltpu.SemaphoreType.DMA((1,)),
        ],
        compiler_params=pltpu.CompilerParams(collective_id=1, has_side_effects=True),
        cost_estimate=pl.CostEstimate(
            flops=0, bytes_accessed=values.size * 12, transcendentals=0,
            remote_bytes_transferred=values.size * 6,
        ),
    )(values)


def gather_near(values, count):
    if count == 4:
        return [values, shift(values, 1, count), shift(values, 2, count)]
    whole = lax.all_gather(values, "tensor", axis=0)
    mine = lax.axis_index("tensor")
    return [lax.dynamic_index_in_dim(whole, mine ^ k, 0, False) for k in range(count)]


def gather_far(near, count):
    if count != 4:
        return []
    half = near[0].shape[0] // 2
    return [shift(near[2][:half], 1, count), shift(near[1][half:], 2, count)]


def gather_chunks(values, count):
    near = gather_near(values, count)
    far = gather_far(near, count)
    return near + [jnp.concatenate(far, axis=0)] if far else near


def exchange(parts, distances, count):
    return [part if k == 0 else shift(part, k, count) for k, part in zip(distances, parts)]


def column_piece(weights, columns, core):
    half = weights.shape[0] // 2
    return lax.dynamic_slice(
        weights, (core[0] * half, columns[0]), (half, columns[1] - columns[0])
    )


def gather_others(weights, columns, core, sizes):
    piece = column_piece(weights, columns, core)
    pieces = [shift(piece, k, sizes["tensor"]) for k in range(1, sizes["tensor"])]
    return pieces + [shift(piece, 1, sizes["dp"], "dp") for piece in pieces]


def sum_first(parts, count):
    if count != 4:
        return None
    return shift(parts[3][0], 1, count), shift(parts[3][1], 2, count)


def sum_rest(parts, first, count):
    if count != 4:
        mine = lax.axis_index("tensor")
        half, width = parts[0][0].shape
        stacked = jnp.zeros((count, 2 * half, width), jnp.bfloat16)
        for k in range(count):
            term = jnp.concatenate([side.astype(jnp.bfloat16) for side in parts[k]], axis=0)
            stacked = lax.dynamic_update_index_in_dim(stacked, term, mine ^ k, 0)
        total = lax.psum_scatter(
            stacked.reshape(-1, width), "tensor", scatter_dimension=0, tiled=True
        ).astype(jnp.float32)
        none = jnp.zeros((half, width), jnp.bfloat16)
        return [[total[:half], none, none], [total[half:], none, none]]
    far_top, far_bottom = first
    x_top = shift(parts[1][0], 1, count)
    y_bottom = shift(parts[2][1], 2, count)
    y_top = shift((parts[2][0] + far_top.astype(jnp.float32)).astype(jnp.bfloat16), 2, count)
    x_bottom = shift((parts[1][1] + far_bottom.astype(jnp.float32)).astype(jnp.bfloat16), 1, count)
    return [[None, x_top, y_top], [None, x_bottom, y_bottom]]


def added(own_ref, x_ref, y_ref):
    return own_ref[...] + x_ref[...].astype(jnp.float32) + y_ref[...].astype(jnp.float32)


def own_rows_call(kernel, sums, twos, ones, out_shapes, gains):
    half, width = sums[0][0].shape
    block = min(64, half)
    term = pl.BlockSpec((block, width), lambda i: (i, 0))
    both = pl.BlockSpec((2, block, width), lambda i: (0, i, 0))
    out_specs = [both] * len(out_shapes)
    if gains:
        out_specs.append(pl.BlockSpec((8, width), lambda i: (0, 0)))
        out_shapes = out_shapes + [jax.ShapeDtypeStruct((8, width), jnp.float32)]
    return pl.pallas_call(
        kernel,
        grid=(half // block,),
        in_specs=[term] * 6 + [both] * len(twos) + [pl.BlockSpec((1, width), lambda i: (0, 0))] * len(ones),
        out_specs=out_specs,
        out_shape=out_shapes,
        compiler_params=pltpu.CompilerParams(vmem_limit_bytes=60 * 2**20),
        cost_estimate=cost(half * width * 10, half * width * 10, 1.0),
    )(*sums[0], *sums[1], *twos, *ones)


def resid_back_kernel(*refs):
    dy_ref, resid_ref, norm_ref, grad_ref, low_ref, gains_ref = refs[6:]

    @pl.when(pl.program_id(0) == 0)
    def _():
        gains_ref[...] = jnp.zeros_like(gains_ref)

    for side in range(2):
        grads = added(*refs[3 * side : 3 * side + 3])
        resid = resid_ref[side]
        inverse = rms_scale(resid)
        normed = resid * inverse
        gains_ref[...] += jnp.sum((grads * normed).reshape(-1, 8, grads.shape[1]), axis=0)
        total = dy_ref[side].astype(jnp.float32) + norm_back(grads * norm_ref[...], normed, inverse)
        grad_ref[side] = total
        low_ref[side] = total.astype(jnp.bfloat16)


def output_kernel(*refs):
    resid_ref, out_ref = refs[6:]
    for side in range(2):
        out_ref[side] = (resid_ref[side] + added(*refs[3 * side : 3 * side + 3])).astype(jnp.bfloat16)


def total_everywhere(values, sizes):
    for axis, size in sizes.items():
        distance = 1
        while distance < size:
            values = values + shift(values, distance, size, axis)
            distance *= 2
    return values


def after(value, *others):
    return lax.optimization_barrier((value, others))[0]


def pad_columns(values, width):
    return jnp.pad(values, ((0, 0), (0, width - values.shape[1])))


def gather_weights(*parts):
    return lax.all_gather(jnp.concatenate(parts, axis=1), "dp", axis=0, tiled=True)


def scatter_weights(grads):
    return lax.psum_scatter(grads, "dp", scatter_dimension=0, tiled=True)


def per_device(
    sizes,
    tokens,
    segments,
    positions,
    w_query,
    w_key,
    w_value,
    w_out,
    w_gate,
    w_up,
    w_down,
    norm_attn,
    norm_mlp,
    query_gain,
    key_gain,
    out_grad,
):
    count = sizes["tensor"]
    chunk_rows = tokens.shape[0]
    q_width, key_width = w_query.shape[1], w_key.shape[1]
    kv_width = -(-key_width // 128) * 128
    units = w_gate.shape[1] // 2
    mine = lax.axis_index("tensor").astype(jnp.int32).reshape(1)

    half, width = chunk_rows // 2, tokens.shape[1]
    inner_count = count // 2
    inner, flip = mine % inner_count, mine // inner_count
    core = lax.axis_index("dp").astype(jnp.int32).reshape(1) % 2

    def own_first(values):
        pair = values.reshape(2, SEQ)
        return jnp.where(flip == 0, pair, pair[::-1])

    w_attn = gather_weights(
        w_out, w_query, pad_columns(w_key, kv_width), pad_columns(w_value, kv_width)
    )
    rows_in = gather_rows(tokens, count)
    w_mlp = [
        gather_weights(w_gate[:, part], w_up[:, part], w_down[:, part])
        for part in (slice(0, units), slice(units, 2 * units))
    ]
    segments, positions = own_first(segments), own_first(positions)
    out_others = gather_others(after(w_attn, rows_in), (0, q_width), core, sizes)
    inv_rows, queries, key_sides, value_sides, raw = [], [], [], [], []
    tables = rotary_tables(positions.reshape(-1))
    attended, inv_total, heads = [], [], []
    for sequence in range(2):
        rows = rows_in[sequence]
        if sequence == 1:
            rows = after(rows, attended, out_others[: count - 1])
        results = project(
            inner, sequence, rows, chunk_rows, norm_attn, w_attn, tables, query_gain, key_gain, q_width, kv_width
        )
        for kept, result in zip((inv_rows, queries, key_sides, value_sides, raw), results):
            kept.append(result)
        result, inverse = attend(
            queries[sequence], key_sides[sequence], value_sides[sequence], segments[sequence]
        )
        attended.append(result)
        inv_total.append(inverse)
        heads.append(gather_chunks(result, count))
    grad_near = gather_near(after(out_grad, heads), count)
    crossed = [
        heads[sequence][:inner_count] + heads[1 - sequence][inner_count:] for sequence in range(2)
    ]
    rows_two, resid = residual(
        jnp.concatenate([inner, core]), rows_in, crossed, w_attn, out_others, norm_mlp, chunk_rows
    )
    resid = resid.reshape(2, half, width)
    grad_near = after(grad_near, rows_two)
    grad_rows = jnp.concatenate(grad_near + gather_far(grad_near, count), axis=0)

    half_columns = column_piece(after(w_attn, grad_rows), (q_width, w_attn.shape[1]), core)
    in_near = [shift(half_columns, k, count) for k in range(1, count - 1)]
    act_a, grads_a, _ = hidden_units(rows_two, grad_rows, w_mlp[0], None)
    in_near = after(in_near, grads_a)
    grad_a = contract_rows(after(rows_two, in_near), grads_a).astype(jnp.bfloat16)
    if count == 4:
        in_far = [jnp.concatenate(gather_far([half_columns, *in_near], count), axis=0)]
    else:
        in_far = [shift(in_near[0], count - 2, count)]
    act, grads_b, _ = hidden_units(after(rows_two, grad_a, in_far), grad_rows, w_mlp[1], act_a)
    in_others = in_near + in_far
    in_others = in_others + [shift(part, 1, sizes["dp"], "dp") for part in in_others]
    spans = [(2 * units, 0), (2 * units, 0)]

    def two_parts(distances, grads):
        lefts = [(grads, 2 * units, 0), (grads_b, 2 * units, 0)]
        return rows_out(distances, lefts, w_mlp, spans, chunk_rows)

    grad_b = contract_rows(rows_two, grads_b).astype(jnp.bfloat16)
    two = two_parts(list(range(inner_count, count)), after(grads_a, grad_b))
    two_first = sum_first(two, count)
    for k in range(1, inner_count):
        two.update(two_parts([k], after(grads_a, two[count - 1])))
    if count == 4:
        two_rest = sum_rest(two, two_first, count)
        sent = (two_rest[0][1], two_rest[1][2])
        two.update(two_parts([0], after(grads_a, two[1], sent)))
        two_rest[0][0], two_rest[1][0] = two[0]
    else:
        sent = ()
        two.update(two_parts([0], after(grads_a, two[1])))
        two_rest = sum_rest(two, None, count)
    grad_resid, branch_low, gain_mlp = own_rows_call(
        resid_back_kernel,
        two_rest,
        [out_grad.reshape(2, half, width), resid],
        [norm_mlp[None, :]],
        [
            jax.ShapeDtypeStruct((2, half, width), jnp.float32),
            jax.ShapeDtypeStruct((2, half, width), jnp.bfloat16),
        ],
        True,
    )
    branch_low = branch_low.reshape(chunk_rows, width)
    distances = list(range(count))
    heads_out = grad_heads(core, branch_low, w_attn, out_others, q_width, count)
    heads_in = exchange(heads_out, distances, count)
    scattered_a = scatter_weights(after(grad_a, in_far))
    scattered_b = scatter_weights(after(grad_b, scattered_a, two[count - 1]))
    out_act = after(act, heads_out[0])
    out = rows_out(
        distances, [(out_act, units, 0), (out_act, units, 1)], w_mlp, [(units, 2), (units, 2)], chunk_rows
    )
    grad_down = contract_rows(after(grad_rows, out[0], scattered_b, heads_in), act).astype(jnp.bfloat16)
    tops = bottoms = relays = []
    if count == 4:
        top, bottom = after((branch_low[:half], branch_low[half:]), heads_in, out[0])
        tops = [shift(top, 1, count), shift(top, 2, count)]
    sums, raw_grads = [], []
    for sequence in range(2):
        pieces = heads_in[sequence * inner_count : (sequence + 1) * inner_count]
        if sequence == 0:
            pieces = after(pieces, heads_in, grad_down, tops)
            if count == 4:
                bottom = after(bottom, tops)
                bottoms = [shift(bottom, 1, count), shift(bottom, 2, count)]
        else:
            pieces = after(pieces, bottoms, raw_grads)
            if count == 4:
                near_bottom, near_top = after((bottoms[0], tops[1]), bottoms, raw_grads)
                relays = [shift(near_top, 1, count), shift(near_bottom, 2, count)]
        results = attend_back(
            inner, sequence, queries[sequence], key_sides[sequence], value_sides[sequence],
            segments[sequence], attended[sequence], inv_total[sequence], pieces, raw[sequence], tables,
            query_gain, key_gain,
        )
        raw_grads += results[:inner_count]
        sums.append(results[inner_count:])
    raw_in = exchange(raw_grads, distances, count)
    if count == 4:
        branch = (
            [branch_low, tops[0], bottoms[0]],
            [tops[1], bottoms[1], *relays],
        )
    else:
        branch_near = gather_near(branch_low, count)
        branch = (branch_near[:inner_count], branch_near[inner_count:])
    out_first = sum_first(out, count)
    out_rest = sum_rest(out, out_first, count)
    if count == 4:
        out_rest[0][0], out_rest[1][0] = out[0]
    (output,) = own_rows_call(
        output_kernel, out_rest, [resid], [], [jax.ShapeDtypeStruct((2, half, width), jnp.bfloat16)],
        False,
    )
    distances = list(range(count))
    grad_tokens, gain_attn = input_back(
        core, raw_in, w_attn, in_others, tokens, grad_resid.reshape(chunk_rows, width), norm_attn
    )
    grad_w_out = out_weights(inner, after(branch, raw_grads), attended)
    grad_qkv = projection_weights(after(rows_in, raw_grads, relays), inv_rows, norm_attn, raw_grads)

    scattered_down = scatter_weights(after(grad_down, scattered_b, tops))
    scattered_attn = scatter_weights(
        after(
            jnp.concatenate([grad_w_out, grad_qkv], axis=1),
            scattered_down, raw_in,
        )
    )

    gains = [
        jnp.sum(gain_attn, axis=0),
        jnp.sum(gain_mlp, axis=0),
        jnp.sum((sums[0][0] + sums[1][0]).reshape(-1, 64), axis=0),
        jnp.sum((sums[0][1] + sums[1][1]).reshape(-1, 64), axis=0),
    ]
    gains = jnp.concatenate(gains).reshape(-1, 128)
    gains = total_everywhere(gains, sizes).reshape(-1)
    key_at = 2 * q_width
    value_at = key_at + kv_width
    return (
        output.reshape(chunk_rows, width),
        grad_tokens.reshape(chunk_rows, width),
        scattered_attn[:, q_width:key_at].astype(jnp.float32),
        scattered_attn[:, key_at : key_at + key_width].astype(jnp.float32),
        scattered_attn[:, value_at : value_at + key_width].astype(jnp.float32),
        scattered_attn[:, :q_width].astype(jnp.float32),
        jnp.concatenate([scattered_a[:, :units], scattered_b[:, :units]], axis=1).astype(jnp.float32),
        jnp.concatenate([scattered_a[:, units:], scattered_b[:, units:]], axis=1).astype(jnp.float32),
        scattered_down.astype(jnp.float32),
        gains[:width],
        gains[width : 2 * width],
        gains[2 * width : 2 * width + 64],
        gains[2 * width + 64 : 2 * width + 128],
    )


def solution(mesh):
    return jax.shard_map(
        functools.partial(per_device, dict(mesh.shape)),
        mesh=mesh,
        in_specs=(
            P(("dp", "tensor"), None),
            P("dp"),
            P("dp"),
            P("dp", "tensor"),
            P("dp", "tensor"),
            P("dp", "tensor"),
            P("dp", "tensor"),
            P("dp", "tensor"),
            P("dp", "tensor"),
            P("dp", "tensor"),
            P(),
            P(),
            P(),
            P(),
            P(("dp", "tensor"), None),
        ),
        out_specs=(
            P(("dp", "tensor"), None),
            P(("dp", "tensor"), None),
            P("dp", "tensor"),
            P("dp", "tensor"),
            P("dp", "tensor"),
            P("dp", "tensor"),
            P("dp", "tensor"),
            P("dp", "tensor"),
            P("dp", "tensor"),
            P(),
            P(),
            P(),
            P(),
        ),
        check_vma=False,
    )
```

time: 2170 us -> 798 us (0.37)
  waiting for transfers between devices: 913 us -> 149 us
  matrix products: 738 us -> 71.8 us
  Pallas kernels: 0 us -> 417 us
  other arithmetic: 262 us -> 34 us
  local copies, waits for them, and re-layouts: 150 us -> 44.5 us
  blocking collectives: 72.7 us -> 0 us
  starting transfers between devices: 1.79 us -> 56.1 us
    dot_general x42 -> x0, matrix products: 641 us -> none  [the longest x8 128 us: block_scores(): jnp.einsum('bkrd,ckd->krbc', query_block, keys, preferred_element_type=jn...]
    all_gather x9 -> x3, waiting for transfers between devices: 455 us -> 0.04 us  [gather_weights(): lax.all_gather(jnp.concatenate(parts, axis=1), 'dp', axis=0, tiled=True)]
    reduce_scatter x11 -> x4, waiting for transfers between devices: 454 us -> 8.43 us  [scatter_weights(): return lax.psum_scatter(grads, 'dp', scatter_dimension=0, tiled=True)]
    pallas_call x0 -> x20, Pallas kernels: none -> 417 us  [the longest x4 79.4 us: rows_out(): pl.pallas_call(functools.partial(rows_out_kernel, len(lefts), len(halves)...]
    ppermute x0 -> x54, waiting for transfers between devices: none -> 141 us  [shift(): return lax.ppermute(values, axis, [(i, i ^ distance) for i in range(count)])]
    convert_element_type x19 -> x9, other arithmetic: 144 us -> 17.6 us  [the longest x2 5.45 us: sum_rest(): (parts[2][0] + far_top.astype(jnp.float32)).astype(jnp.bfloat16)]
    dynamic_update_slice x16 -> x0, local copies, waits for them, and re-layouts: 96.8 us -> none  [the longest x8 88.4 us: per_device(): lax.scan(back_block, (empty_kv, empty_kv), (jnp.arange(block_count), log_...]
    reduce_sum x10 -> x4, other arithmetic: 81.6 us -> 0.93 us  [the longest x1 0.86 us: per_device(): jnp.sum(gain_attn, axis=0)]
  transfers between devices with their start and end apart: 20 -> 61, of which waited for: 13 -> 24; matrix products, arithmetic and copies ran while one was open for 47% -> 17% of each run, Pallas kernels for 0% -> 53%
where the time goes in v1:
time: 798 us; the launch traced here: 788 us
  Pallas kernels  417 us (52%)
  waiting for transfers between devices  149 us (19%)
  matrix products  71.8 us (9%)
  starting transfers between devices  56.1 us (7%)
  local copies, waits for them, and re-layouts  44.5 us (6%)
  other arithmetic  34 us (4%)
  between operations  15.1 us (2%)
    ppermute x54, waiting for transfers between devices, shift(): return lax.ppermute(values, axis, [(i, i ^ distance) for i in range(count)])  141 us
    pallas_call x4, Pallas kernels, rows_out(): pl.pallas_call(functools.partial(rows_out_kernel, len(lefts), len(halves)...  79.4 us
    pallas_call x1, Pallas kernels, gather_rows(): pl.pallas_call(gather_kernel, in_specs=[place], out_specs=[place] * 2, ou...  72.8 us
    dot_general x3, matrix products, contract_rows(): lax.dot_general(left, right, (((0,), (0,)), ((), ())), preferred_element_...  71.8 us
    pallas_call x2, Pallas kernels, hidden_units(): pl.pallas_call(functools.partial(hidden_kernel, place, [distance for dist...  71 us
    ppermute x54, starting transfers between devices, shift(): return lax.ppermute(values, axis, [(i, i ^ distance) for i in range(count)])  55.9 us
    pallas_call x2, Pallas kernels, attend_back(): pl.pallas_call(functools.partial(attend_back_kernel, chunks), grid_spec=p...  50.8 us
    pallas_call x1, Pallas kernels, residual(): pl.pallas_call(functools.partial(resid_kernel, count), grid_spec=pltpu.Pr...  32.5 us
  transfers between devices with their start and end apart: 61, of which 24 were waited for; matrix products, arithmetic and copies ran while one was open for 17% of the time, Pallas kernels for 53%

profile of v1, /device:TPU:0, one launch (start us, length us, event | category | flops | bytes accessed | tf_op | source)
XLA Modules:
  0.0 788.1 jit_solution(6733701249035794692)
XLA Ops:
  7.2 2.1 pad_maximum_fusion.3
  14.1 72.8 %shard_map.246 = (bf16[1024,2048]{1,0:T(8,128)(2,1)}, bf16[1024,2048]{1,0:T(8,128)(2,1)}) custom-call(bf16[512,2048]{1,0:T(8,128)(2,1)} %refs_11_.1), custom_call_target="tpu_custom_call" | custom-call | bytes 12582912 | tf_op jit(solution)/shard_map/pallas_call | solution.py:885
  87.5 2.3 constant_dynamic-slice_fusion.1
  96.6 5.8 fusion
  102.4 11.1 %shard_map.247 = (f32[1024,128]{1,0:T(8,128)}, bf16[1024,512]{1,0:T(8,128)(2,1)}, bf16[1024,512]{1,0:T(8,128)(2,1)}, bf16[1024,512]{1,0:T(8,128)(2,1)}, f32[1024,640]{1,0:T(8,128)}) custom-call(s32[1]{0:T(128)S(6)} %select_n.55.inner_ref, bf16[1024,2048]{1,0:T(8,128)(2,1)} %get-tuple-element.187.refs_0_, f32[1,2048]{1,0:T(1,128)} %bitcast.51, ...), custom_call_target="tpu_custom_call" | custom-call | flops 2928386816 | bytes 2516582 | tf_op jit(solution)/shard_map/pallas_call | solution.py:376
  113.5 9.5 %shard_map.248 = (bf16[1024,512]{1,0:T(8,128)(2,1)}, f32[1024,512]{1,0:T(8,128)}) custom-call(bf16[1024,512]{1,0:T(8,128)(2,1)} %get-tuple-element.108.q_ref, bf16[1024,512]{1,0:T(8,128)(2,1)} %get-tuple-element.109.k_ref, bf16[1024,512]{1,0:T(8,128)(2,1)} %get-tuple-element.110.v_ref, s32[1024,1]{1,0:T(8,128)} %copy.29.segc_ref, ...), custom_call_target="tpu_custom_call" | custom-call | flops 2254857728 | bytes 6291456 | tf_op jit(solution)/shard_map/pallas_call | solution.py:225
  125.1 12.4 %collective-permute-done.2.refs_12_.refs_2_ = bf16[1024,512]{1,0:T(8,128)(2,1)S(1)} collective-permute-done((bf16[1024,512]{1,0:T(8,128)(2,1)}, bf16[1024,512]{1,0:T(8,128)(2,1)S(1)}, u32[]{:S(2)}, u32[]{:S(2)}) %collective-permute-start.2) | collective-permute-done | bytes 1048608 | tf_op jit(solution)/shard_map/ppermute | solution.py:837
  138.6 11.3 %shard_map.249 = (f32[1024,128]{1,0:T(8,128)}, bf16[1024,512]{1,0:T(8,128)(2,1)}, bf16[1024,512]{1,0:T(8,128)(2,1)}, bf16[1024,512]{1,0:T(8,128)(2,1)}, f32[1024,640]{1,0:T(8,128)}) custom-call(s32[1]{0:T(128)S(6)} %select_n.55.inner_ref, bf16[1024,2048]{1,0:T(8,128)(2,1)} %get-tuple-element.188.refs_0_.refs_1_, f32[1,2048]{1,0:T(1,128)} %bitcast.52, ...), custom_call_target="tpu_custom_call" | custom-call | flops 2928386816 | bytes 2516582 | tf_op jit(solution)/shard_map/pallas_call | solution.py:376
  149.9 9.7 %shard_map.250 = (bf16[1024,512]{1,0:T(8,128)(2,1)}, f32[1024,512]{1,0:T(8,128)}) custom-call(bf16[1024,512]{1,0:T(8,128)(2,1)} %get-tuple-element.114.q_ref, bf16[1024,512]{1,0:T(8,128)(2,1)} %get-tuple-element.115.k_ref, bf16[1024,512]{1,0:T(8,128)(2,1)} %get-tuple-element.116.v_ref, s32[1024,1]{1,0:T(8,128)} %copy.30.segc_ref, ...), custom_call_target="tpu_custom_call" | custom-call | flops 2254857728 | bytes 6291456 | tf_op jit(solution)/shard_map/pallas_call | solution.py:225
  166.0 20.0 %collective-permute-done.4.refs_4_ = bf16[1024,512]{1,0:T(8,128)(2,1)S(1)} collective-permute-done((bf16[1024,512]{1,0:T(8,128)(2,1)}, bf16[1024,512]{1,0:T(8,128)(2,1)S(1)}, u32[]{:S(2)}, u32[]{:S(2)}) %collective-permute-start.4) | collective-permute-done | bytes 1048608 | tf_op jit(solution)/shard_map/ppermute | solution.py:837
  189.3 9.4 %collective-permute-done.9 = bf16[512,512]{1,0:T(8,128)(2,1)S(1)} collective-permute-done((bf16[512,512]{1,0:T(8,128)(2,1)S(1)}, bf16[512,512]{1,0:T(8,128)(2,1)S(1)}, u32[]{:S(2)}, u32[]{:S(2)}) %collective-permute-start.9) | collective-permute-done | bytes 524320 | tf_op jit(solution)/shard_map/ppermute | solution.py:837
  198.8 8.3 %collective-permute-done.5 = bf16[512,512]{1,0:T(8,128)(2,1)S(1)} collective-permute-done((bf16[512,512]{1,0:T(8,128)(2,1)S(1)}, bf16[512,512]{1,0:T(8,128)(2,1)S(1)}, u32[]{:S(2)}, u32[]{:S(2)}) %collective-permute-start.5) | collective-permute-done | bytes 524320 | tf_op jit(solution)/shard_map/ppermute | solution.py:837
  216.5 32.5 %shard_map.251 = (bf16[2048,2048]{1,0:T(8,128)(2,1)}, f32[1,512,2048]{2,1,0:T(8,128)}) custom-call(s32[2]{0:T(128)} %pad_add_fusion.place_ref, bf16[1024,2048]{1,0:T(8,128)(2,1)} %get-tuple-element.187.refs_0_, bf16[1024,2048]{1,0:T(8,128)(2,1)} %get-tuple-element.188.refs_0_.refs_1_, bf16[1024,512]{1,0:T(8,128)(2,1)} %get-tuple-element.111.refs_2_.out_ref.refs_3_, ...), custom_call_target="tpu_custom_call" | custom-call | flops 7469508096 | bytes 6710886 | tf_op jit(solution)/shard_map/pallas_call | solution.py:660
  249.0 4.0 collective-permute-done.15
  260.5 3.3 constant_dynamic-update-slice_fusion.7
  263.8 3.2 constant_dynamic-update-slice_fusion.6
  267.0 10.7 %collective-permute-done.16 = bf16[256,2048]{1,0:T(8,128)(2,1)S(1)} collective-permute-done((bf16[256,2048]{1,0:T(8,128)(2,1)S(1)}, bf16[256,2048]{1,0:T(8,128)(2,1)S(1)}, u32[]{:S(2)}, u32[]{:S(2)}) %collective-permute-start.16) | collective-permute-done | bytes 1048608 | tf_op jit(solution)/shard_map/ppermute | solution.py:837
  280.5 2.7 constant_dynamic-slice_fusion
  285.2 35.7 %shard_map.252 = (bf16[2048,2048]{1,0:T(8,128)(2,1)}, bf16[2048,2048]{1,0:T(8,128)(2,1)}) custom-call(bf16[2048,2048]{1,0:T(8,128)(2,1)} %get-tuple-element.128.x_ref, bf16[2048,2048]{1,0:T(8,128)(2,1)} %constant_dynamic-update-slice_fusion.4.dy_ref, bf16[2048,3072]{1,0:T(8,128)(2,1)} %all-gather.6.cloned.1.call-done.w_ref.refs_2_), custom_call_target="tpu_custom_call" | custom-call | flops 8180890112 | bytes 7549747 | tf_op jit(solution)/shard_map/pallas_call | solution.py:529
  325.0 23.8 %convolution_convert_fusion.2 = bf16[2048,2048]{1,0:T(8,128)(2,1)} fusion(bf16[2048,2048]{1,0:T(8,128)(2,1)} %get-tuple-element.128.x_ref, bf16[2048,2048]{1,0:T(8,128)(2,1)} %get-tuple-element.139.refs_0_), kind=kOutput, calls=%fused_computation.2 | convolution fusion | flops 17184063488 | bytes 25165824 | tf_op jit(solution)/shard_map/dot_general | solution.py:38
  353.1 35.3 %shard_map.253 = (bf16[2048,2048]{1,0:T(8,128)(2,1)}, bf16[2048,2048]{1,0:T(8,128)(2,1)}) custom-call(bf16[2048,2048]{1,0:T(8,128)(2,1)} %get-tuple-element.128.x_ref, bf16[2048,2048]{1,0:T(8,128)(2,1)} %constant_dynamic-update-slice_fusion.4.dy_ref, bf16[2048,3072]{1,0:T(8,128)(2,1)} %all-gather.8.cloned.1.call-done.w_ref.refs_3_, ...), custom_call_target="tpu_custom_call", output_to_operand_aliasing={{0}: (3, {})} | custom-call | flops 8180890112 | bytes 7549747 | tf_op jit(solution)/shard_map/pallas_call | solution.py:529
  388.4 23.8 %convolution_convert_fusion.1 = bf16[2048,2048]{1,0:T(8,128)(2,1)} fusion(bf16[2048,2048]{1,0:T(8,128)(2,1)} %get-tuple-element.128.x_ref, bf16[2048,2048]{1,0:T(8,128)(2,1)} %get-tuple-element.131.refs_1_), kind=kOutput, calls=%fused_computation.1 | convolution fusion | flops 17184063488 | bytes 25165824 | tf_op jit(solution)/shard_map/dot_general | solution.py:38
  412.3 24.0 %shard_map.254 = (f32[256,2048]{1,0:T(8,128)}, bf16[256,2048]{1,0:T(8,128)(2,1)}, bf16[256,2048]{1,0:T(8,128)(2,1)}, bf16[256,2048]{1,0:T(8,128)(2,1)}) custom-call(bf16[2048,2048]{1,0:T(8,128)(2,1)} %get-tuple-element.139.refs_0_, bf16[2048,2048]{1,0:T(8,128)(2,1)} %get-tuple-element.131.refs_1_, ...), custom_call_target="tpu_custom_call" | custom-call | flops 844219584 | bytes 209715 | tf_op jit(solution)/shard_map/pallas_call | solution.py:597
  436.3 6.7 reduce-scatter.5.cloned.1.call-done
  446.6 15.6 %shard_map.255 = (bf16[256,2048]{1,0:T(8,128)(2,1)}, f32[256,2048]{1,0:T(8,128)}) custom-call(bf16[2048,2048]{1,0:T(8,128)(2,1)} %get-tuple-element.139.refs_0_, bf16[2048,2048]{1,0:T(8,128)(2,1)} %get-tuple-element.131.refs_1_, bf16[2048,3072]{1,0:T(8,128)(2,1)} %all-gather.6.cloned.1.call-done.w_ref.refs_2_, ...), custom_call_target="tpu_custom_call" | custom-call | flops 422109792 | bytes 104857 | tf_op jit(solution)/shard_map/pallas_call | solution.py:597
  462.7 6.9 collective-permute-done.24
  469.5 2.5 add_convert_fusion.3
  473.5 2.5 add_convert_fusion.2
  477.5 15.9 %collective-permute-done.23.refs_5_ = bf16[256,2048]{1,0:T(8,128)(2,1)S(1)} collective-permute-done((bf16[256,2048]{1,0:T(8,128)(2,1)}, bf16[256,2048]{1,0:T(8,128)(2,1)S(1)}, u32[]{:S(2)}, u32[]{:S(2)}) %collective-permute-start.23) | collective-permute-done | bytes 1048608 | tf_op jit(solution)/shard_map/ppermute | solution.py:837
  493.4 15.7 %shard_map.256 = (f32[256,2048]{1,0:T(8,128)}, f32[256,2048]{1,0:T(8,128)}) custom-call(bf16[2048,2048]{1,0:T(8,128)(2,1)} %get-tuple-element.139.refs_0_, bf16[2048,2048]{1,0:T(8,128)(2,1)} %get-tuple-element.131.refs_1_, bf16[2048,3072]{1,0:T(8,128)(2,1)} %all-gather.6.cloned.1.call-done.w_ref.refs_2_, ...), custom_call_target="tpu_custom_call" | custom-call | flops 422109792 | bytes 104857 | tf_op jit(solution)/shard_map/pallas_call | solution.py:597
  509.1 3.2 collective-permute-done.25.refs_2_
  513.6 9.5 %shard_map.257 = (f32[2,256,2048]{2,1,0:T(8,128)}, bf16[2,256,2048]{2,1,0:T(8,128)(2,1)}, f32[8,2048]{1,0:T(8,128)}) custom-call(f32[256,2048]{1,0:T(8,128)} %get-tuple-element.140.refs_0_, bf16[256,2048]{1,0:T(8,128)(2,1)} %collective-permute-done.22.refs_1_, bf16[256,2048]{1,0:T(8,128)(2,1)} %copy-done.32, f32[256,2048]{1,0:T(8,128)} %get-tuple-element.142.refs_3_, ...), custom_call_target="tpu_custom_call" | custom-call | flops 1048576 | bytes 1048576 | tf_op jit(solution)/shard_map/pallas_call | solution.py:980
  523.1 9.4 %shard_map.258 = (bf16[512,512]{1,0:T(8,128)(2,1)}, bf16[512,512]{1,0:T(8,128)(2,1)}, bf16[512,512]{1,0:T(8,128)(2,1)}, bf16[512,512]{1,0:T(8,128)(2,1)}) custom-call(s32[1]{0:T(128)S(6)} %select_n.56.core_ref, bf16[512,2048]{1,0:T(8,128)(2,1)} %bitcast.43, bf16[2048,1280]{1,0:T(8,128)(2,1)} %all-gather.4.cloned.1.call-done.refs_2_.refs_10_.refs_0_.refs_4_, ...), custom_call_target="tpu_custom_call" | custom-call | flops 321720384 | bytes 209715 | tf_op jit(solution)/shard_map/pallas_call | solution.py:428
  536.0 24.0 %shard_map.259 = (f32[256,2048]{1,0:T(8,128)}, f32[256,2048]{1,0:T(8,128)}, bf16[256,2048]{1,0:T(8,128)(2,1)}, f32[256,2048]{1,0:T(8,128)}, f32[256,2048]{1,0:T(...) custom-call(bf16[2048,2048]{1,0:T(8,128)(2,1)} %get-tuple-element.146.refs_0_.refs_1_, ...), custom_call_target="tpu_custom_call" | custom-call | flops 844219584 | bytes 209715 | tf_op jit(solution)/shard_map/pallas_call | solution.py:597
  564.1 24.2 %convolution_convert_fusion = bf16[2048,2048]{1,0:T(8,128)(2,1)} fusion(bf16[2048,2048]{1,0:T(8,128)(2,1)} %constant_dynamic-update-slice_fusion.4.dy_ref, bf16[2048,2048]{1,0:T(8,128)(2,1)} %get-tuple-element.146.refs_0_.refs_1_), kind=kOutput, calls=%fused_computation | convolution fusion | flops 17184063488 | bytes 25165824 | tf_op jit(solution)/shard_map/dot_general | solution.py:38
  591.3 25.5 %shard_map.261 = (bf16[512,768]{1,0:T(8,128)(2,1)}, bf16[512,768]{1,0:T(8,128)(2,1)}, f32[8,128]{1,0:T(8,128)}, f32[8,128]{1,0:T(8,128)}) custom-call(s32[1]{0:T(128)S(6)} %select_n.55.inner_ref, bf16[1024,512]{1,0:T(8,128)(2,1)} %get-tuple-element.108.q_ref, bf16[1024,512]{1,0:T(8,128)(2,1)} %get-tuple-element.109.k_ref, ...), custom_call_target="tpu_custom_call" | custom-call | flops 5905580032 | bytes 10485760 | tf_op jit(solution)/shard_map/pallas_call | solution.py:258
  620.1 25.4 %shard_map.262 = (bf16[512,768]{1,0:T(8,128)(2,1)}, bf16[512,768]{1,0:T(8,128)(2,1)}, f32[8,128]{1,0:T(8,128)}, f32[8,128]{1,0:T(8,128)}) custom-call(s32[1]{0:T(128)S(6)} %select_n.55.inner_ref, bf16[1024,512]{1,0:T(8,128)(2,1)} %get-tuple-element.114.q_ref, bf16[1024,512]{1,0:T(8,128)(2,1)} %get-tuple-element.115.k_ref, ...), custom_call_target="tpu_custom_call" | custom-call | flops 5905580032 | bytes 10485760 | tf_op jit(solution)/shard_map/pallas_call | solution.py:258
  647.6 13.1 %shard_map.265 = bf16[2048,768]{1,0:T(8,128)(2,1)} custom-call(f32[1,2048]{1,0:T(1,128)} %bitcast.53, bf16[1024,2048]{1,0:T(8,128)(2,1)} %get-tuple-element.187.refs_0_, bf16[1024,2048]{1,0:T(8,128)(2,1)} %get-tuple-element.188.refs_0_.refs_1_, f32[1024,128]{1,0:T(8,128)} %get-tuple-element.189.refs_2_, f32[1024,128]{1,0:T(8,128)} %get-tuple-element.190.refs_3_, ...), custom_call_target="tpu_custom_call" | custom-call | flops 2996488704 | bytes 1677721 | tf_op jit(solution)/shard_map/pallas_call | solution.py:822
  660.7 10.9 %shard_map.264 = bf16[2048,512]{1,0:T(8,128)(2,1)} custom-call(s32[1]{0:T(128)S(6)} %select_n.55.inner_ref, bf16[512,2048]{1,0:T(8,128)(2,1)} %bitcast.44, bf16[256,2048]{1,0:T(8,128)(2,1)} %copy-done.28, bf16[256,2048]{1,0:T(8,128)(2,1)} %copy-done.30, bf16[1024,512]{1,0:T(8,128)(2,1)} %get-tuple-element.111.refs_2_.out_ref.refs_3_, ...), custom_call_target="tpu_custom_call" | custom-call | flops 2454267136 | bytes 1677721 | tf_op jit(solution)/shard_map/pallas_call | solution.py:788
  671.5 4.3 pad_maximum_fusion
  681.3 19.7 %collective-permute-done.29 = bf16[256,2048]{1,0:T(8,128)(2,1)S(1)} collective-permute-done((bf16[256,2048]{1,0:T(8,128)(2,1)}, bf16[256,2048]{1,0:T(8,128)(2,1)S(1)}, u32[]{:S(2)}, u32[]{:S(2)}) %collective-permute-start.29) | collective-permute-done | bytes 1048608 | tf_op jit(solution)/shard_map/ppermute | solution.py:837
  702.4 3.0 add_convert_fusion.1
  710.8 19.9 %shard_map.263 = (f32[512,2048]{1,0:T(8,128)}, f32[8,2048]{1,0:T(8,128)}) custom-call(s32[1]{0:T(128)S(6)} %select_n.56.core_ref, bf16[512,768]{1,0:T(8,128)(2,1)} %get-tuple-element.166.refs_0_.refs_4_, bf16[512,768]{1,0:T(8,128)(2,1)} %collective-permute-done.39.refs_1_, bf16[512,768]{1,0:T(8,128)(2,1)} %collective-permute-done.42.refs_2_, ...), custom_call_target="tpu_custom_call" | custom-call | flops 4601750528 | bytes 4194304 | tf_op jit(solution)/shard_map/pallas_call | solution.py:736
  731.9 17.7 %collective-permute-done.30.refs_2_ = bf16[256,2048]{1,0:T(8,128)(2,1)S(1)} collective-permute-done((bf16[256,2048]{1,0:T(8,128)(2,1)}, bf16[256,2048]{1,0:T(8,128)(2,1)S(1)}, u32[]{:S(2)}, u32[]{:S(2)}) %collective-permute-start.30) | collective-permute-done | bytes 1048608 | tf_op jit(solution)/shard_map/ppermute | solution.py:837
  751.5 6.4 shard_map.260
  757.9 2.3 collective-permute-start.50
  762.1 3.2 collective-permute-start.51
  778.9 2.1 slice_convert_fusion
  (273 shorter events, 110.1 us)
Async XLA Ops:
  7.2 80.3 %all-gather.4.cloned.1.call-start = ((), (), s32[]{:S(2)}) async-start(), calls=%async_computation.4 | async-start | bytes 5898240 | tf_op jit(solution)/shard_map/all_gather | solution.py:1033
  9.4 275.8 %all-gather.6.cloned.1.call-start = ((), (), s32[]{:S(2)}) async-start(), calls=%async_computation.5 | async-start | bytes 14155776 | tf_op jit(solution)/shard_map/all_gather | solution.py:1033
  12.2 340.9 %all-gather.8.cloned.1.call-start = ((), (), s32[]{:S(2)}) async-start(), calls=%async_computation.6 | async-start | bytes 14155776 | tf_op jit(solution)/shard_map/all_gather | solution.py:1033
  13.5 429.5 %reduce-scatter.5.cloned.1.call-start = ((), (), s32[]{:S(2)}) async-start(), calls=%async_computation.7 | async-start | bytes 9437184 | tf_op jit(solution)/shard_map/reduce_scatter | solution.py:1037
  89.8 35.3 %collective-permute-start.3 = (bf16[1024,512]{1,0:T(8,128)(2,1)}, bf16[1024,512]{1,0:T(8,128)(2,1)S(1)}, u32[]{:S(2)}, u32[]{:S(2)}) collective-permute-start(bf16[1024,512]{1,0:T(8,128)(2,1)} %constant_dynamic-slice_fusion.1), channel_id=1, source_target_pairs={{0,3},{1,2},{2,1},{3,0},{4,7},{5,6},{6,5},{7,4},{8,11},{9,10},{10,... | collective-permute-start | bytes 3145736 | tf_op jit(solution)/shard_map/ppermute | solution.py:837
  91.3 46.2 %collective-permute-start.2 = (bf16[1024,512]{1,0:T(8,128)(2,1)}, bf16[1024,512]{1,0:T(8,128)(2,1)S(1)}, u32[]{:S(2)}, u32[]{:S(2)}) collective-permute-start(bf16[1024,512]{1,0:T(8,128)(2,1)} %constant_dynamic-slice_fusion.1), channel_id=1, source_target_pairs={{0,2},{1,3},{2,0},{3,1},{4,6},{5,7},{6,4},{7,5},{8,10},{9,11},{10,... | collective-permute-start | bytes 3145736 | tf_op jit(solution)/shard_map/ppermute | solution.py:837
  91.9 46.8 %collective-permute-start.1 = (bf16[1024,512]{1,0:T(8,128)(2,1)}, bf16[1024,512]{1,0:T(8,128)(2,1)S(1)}, u32[]{:S(2)}, u32[]{:S(2)}) collective-permute-start(bf16[1024,512]{1,0:T(8,128)(2,1)} %constant_dynamic-slice_fusion.1), channel_id=1, source_target_pairs={{0,1},{1,0},{2,3},{3,2},{4,5},{5,4},{6,7},{7,6},{8,9},{9,8},{10,11... | collective-permute-start | bytes 3145736 | tf_op jit(solution)/shard_map/ppermute | solution.py:837
  123.0 38.8 %collective-permute-start.8 = (bf16[1024,512]{1,0:T(8,128)(2,1)}, bf16[1024,512]{1,0:T(8,128)(2,1)}, u32[]{:S(2)}, u32[]{:S(2)}) collective-permute-start(bf16[1024,512]{1,0:T(8,128)(2,1)} %get-tuple-element.111.refs_2_.out_ref.refs_3_), channel_id=1, source_target_pairs={{0,2},{1,3},{2,0},{3,1},{4,6},{5,7},{6,4},{7,5},{8,10},{9,11},{10,... | collective-permute-start | bytes 3145736 | tf_op jit(solution)/shard_map/ppermute | solution.py:837
  123.6 40.7 %collective-permute-start = (bf16[1024,512]{1,0:T(8,128)(2,1)}, bf16[1024,512]{1,0:T(8,128)(2,1)}, u32[]{:S(2)}, u32[]{:S(2)}) collective-permute-start(bf16[1024,512]{1,0:T(8,128)(2,1)} %get-tuple-element.111.refs_2_.out_ref.refs_3_), channel_id=1, source_target_pairs={{0,1},{1,0},{2,3},{3,2},{4,5},{5,4},{6,7},{7,6},{8,9},{9,8},{10,11... | collective-permute-start | bytes 3145736 | tf_op jit(solution)/shard_map/ppermute | solution.py:837
  159.6 26.4 %collective-permute-start.4 = (bf16[1024,512]{1,0:T(8,128)(2,1)}, bf16[1024,512]{1,0:T(8,128)(2,1)S(1)}, u32[]{:S(2)}, u32[]{:S(2)}) collective-permute-start(bf16[1024,512]{1,0:T(8,128)(2,1)} %get-tuple-element.117.refs_6_.out_ref.refs_8_), channel_id=1, source_target_pairs={{0,2},{1,3},{2,0},{3,1},{4,6},{5,7},{6,4},{7,5},{8,10},{9,11},{10,... | collective-permute-start | bytes 3145736 | tf_op jit(solution)/shard_map/ppermute | solution.py:837
  161.1 27.5 %collective-permute-start.6 = (bf16[1024,512]{1,0:T(8,128)(2,1)}, bf16[1024,512]{1,0:T(8,128)(2,1)S(1)}, u32[]{:S(2)}, u32[]{:S(2)}) collective-permute-start(bf16[1024,512]{1,0:T(8,128)(2,1)} %get-tuple-element.117.refs_6_.out_ref.refs_8_), channel_id=1, source_target_pairs={{0,1},{1,0},{2,3},{3,2},{4,5},{5,4},{6,7},{7,6},{8,9},{9,8},{10,11... | collective-permute-start | bytes 3145736 | tf_op jit(solution)/shard_map/ppermute | solution.py:837
  162.8 35.8 %collective-permute-start.9 = (bf16[512,512]{1,0:T(8,128)(2,1)S(1)}, bf16[512,512]{1,0:T(8,128)(2,1)S(1)}, u32[]{:S(2)}, u32[]{:S(2)}) collective-permute-start(bf16[512,512]{1,0:T(8,128)(2,1)S(1)} %slice.142), channel_id=1, source_target_pairs={{0,1},{1,0},{2,3},{3,2},{4,5},{5,4},{6,7},{7,6},{8,9},{9,8},{10,11... | collective-permute-start | bytes 1572872 | tf_op jit(solution)/shard_map/ppermute | solution.py:837
  165.4 33.3 %collective-permute-start.10 = (bf16[512,512]{1,0:T(8,128)(2,1)S(1)}, bf16[512,512]{1,0:T(8,128)(2,1)S(1)}, u32[]{:S(2)}, u32[]{:S(2)}) collective-permute-start(bf16[512,512]{1,0:T(8,128)(2,1)S(1)} %slice.143), channel_id=1, source_target_pairs={{0,2},{1,3},{2,0},{3,1},{4,6},{5,7},{6,4},{7,5},{8,10},{9,11},{10,... | collective-permute-start | bytes 1572872 | tf_op jit(solution)/shard_map/ppermute | solution.py:837
  207.2 45.8 %collective-permute-start.15 = (bf16[512,2048]{1,0:T(8,128)(2,1)S(1)}, bf16[512,2048]{1,0:T(8,128)(2,1)}, u32[]{:S(2)}, u32[]{:S(2)}) collective-permute-start(bf16[512,2048]{1,0:T(8,128)(2,1)S(1)} %copy-done.2), channel_id=1, source_target_pairs={{0,2},{1,3},{2,0},{3,1},{4,6},{5,7},{6,4},{7,5},{8,10},{9,11},{10,... | collective-permute-start | bytes 6291464 | tf_op jit(solution)/shard_map/ppermute | solution.py:837
  208.7 45.6 %collective-permute-start.14 = (bf16[512,2048]{1,0:T(8,128)(2,1)S(1)}, bf16[512,2048]{1,0:T(8,128)(2,1)}, u32[]{:S(2)}, u32[]{:S(2)}) collective-permute-start(bf16[512,2048]{1,0:T(8,128)(2,1)S(1)} %copy-done.2), channel_id=1, source_target_pairs={{0,1},{1,0},{2,3},{3,2},{4,5},{5,4},{6,7},{7,6},{8,9},{9,8},{10,11... | collective-permute-start | bytes 6291464 | tf_op jit(solution)/shard_map/ppermute | solution.py:837
  283.1 37.7 %collective-permute-start.19 = (bf16[1024,768]{1,0:T(8,128)(2,1)}, bf16[1024,768]{1,0:T(8,128)(2,1)S(1)}, u32[]{:S(2)}, u32[]{:S(2)}) collective-permute-start(bf16[1024,768]{1,0:T(8,128)(2,1)} %constant_dynamic-slice_fusion), channel_id=1, source_target_pairs={{0,2},{1,3},{2,0},{3,1},{4,6},{5,7},{6,4},{7,5},{8,10},{9,11},{10,... | collective-permute-start | bytes 4718600 | tf_op jit(solution)/shard_map/ppermute | solution.py:837
  284.6 36.3 %collective-permute-start.18 = (bf16[1024,768]{1,0:T(8,128)(2,1)}, bf16[1024,768]{1,0:T(8,128)(2,1)S(1)}, u32[]{:S(2)}, u32[]{:S(2)}) collective-permute-start(bf16[1024,768]{1,0:T(8,128)(2,1)} %constant_dynamic-slice_fusion), channel_id=1, source_target_pairs={{0,1},{1,0},{2,3},{3,2},{4,5},{5,4},{6,7},{7,6},{8,9},{9,8},{10,11... | collective-permute-start | bytes 4718600 | tf_op jit(solution)/shard_map/ppermute | solution.py:837
  323.0 25.8 %collective-permute-start.20 = (bf16[512,768]{1,0:T(8,128)(2,1)}, bf16[512,768]{1,0:T(8,128)(2,1)}, u32[]{:S(2)}, u32[]{:S(2)}) collective-permute-start(bf16[512,768]{1,0:T(8,128)(2,1)} %slice.115), channel_id=1, source_target_pairs={{0,1},{1,0},{2,3},{3,2},{4,5},{5,4},{6,7},{7,6},{8,9},{9,8},{10,11... | collective-permute-start | bytes 2359304 | tf_op jit(solution)/shard_map/ppermute | solution.py:837
  324.4 26.4 %collective-permute-start.21 = (bf16[512,768]{1,0:T(8,128)(2,1)}, bf16[512,768]{1,0:T(8,128)(2,1)}, u32[]{:S(2)}, u32[]{:S(2)}) collective-permute-start(bf16[512,768]{1,0:T(8,128)(2,1)} %slice.116), channel_id=1, source_target_pairs={{0,2},{1,3},{2,0},{3,1},{4,6},{5,7},{6,4},{7,5},{8,10},{9,11},{10,... | collective-permute-start | bytes 2359304 | tf_op jit(solution)/shard_map/ppermute | solution.py:837
  353.0 211.1 %reduce-scatter.7.cloned.1.call-start = ((), (), s32[]{:S(2)}) async-start(), calls=%async_computation.8 | async-start | bytes 9437184 | tf_op jit(solution)/shard_map/reduce_scatter | solution.py:1037
  443.0 234.6 %reduce-scatter.9.cloned.1.call-start = ((), (), s32[]{:S(2)}) async-start(), calls=%async_computation.9 | async-start | bytes 9437184 | tf_op jit(solution)/shard_map/reduce_scatter | solution.py:1037
  443.1 26.5 %collective-permute-start.24 = (bf16[256,2048]{1,0:T(8,128)(2,1)}, bf16[256,2048]{1,0:T(8,128)(2,1)}, u32[]{:S(2)}, u32[]{:S(2)}) collective-permute-start(bf16[256,2048]{1,0:T(8,128)(2,1)} %get-tuple-element.133), channel_id=1, source_target_pairs={{0,1},{1,0},{2,3},{3,2},{4,5},{5,4},{6,7},{7,6},{8,9},{9,8},{10,11... | collective-permute-start | bytes 3145736 | tf_op jit(solution)/shard_map/ppermute | solution.py:837
  444.6 28.9 %collective-permute-start.26 = (bf16[256,2048]{1,0:T(8,128)(2,1)}, bf16[256,2048]{1,0:T(8,128)(2,1)}, u32[]{:S(2)}, u32[]{:S(2)}) collective-permute-start(bf16[256,2048]{1,0:T(8,128)(2,1)} %get-tuple-element.134), channel_id=1, source_target_pairs={{0,2},{1,3},{2,0},{3,1},{4,6},{5,7},{6,4},{7,5},{8,10},{9,11},{10,... | collective-permute-start | bytes 3145736 | tf_op jit(solution)/shard_map/ppermute | solution.py:837
  446.1 47.3 %collective-permute-start.23 = (bf16[256,2048]{1,0:T(8,128)(2,1)}, bf16[256,2048]{1,0:T(8,128)(2,1)S(1)}, u32[]{:S(2)}, u32[]{:S(2)}) collective-permute-start(bf16[256,2048]{1,0:T(8,128)(2,1)} %get-tuple-element.138), channel_id=1, source_target_pairs={{0,2},{1,3},{2,0},{3,1},{4,6},{5,7},{6,4},{7,5},{8,10},{9,11},{10,... | collective-permute-start | bytes 3145736 | tf_op jit(solution)/shard_map/ppermute | solution.py:837
  462.3 31.1 %collective-permute-start.22 = (bf16[256,2048]{1,0:T(8,128)(2,1)}, bf16[256,2048]{1,0:T(8,128)(2,1)}, u32[]{:S(2)}, u32[]{:S(2)}) collective-permute-start(bf16[256,2048]{1,0:T(8,128)(2,1)} %get-tuple-element.136), channel_id=1, source_target_pairs={{0,1},{1,0},{2,3},{3,2},{4,5},{5,4},{6,7},{7,6},{8,9},{9,8},{10,11... | collective-permute-start | bytes 3145736 | tf_op jit(solution)/shard_map/ppermute | solution.py:837
  472.0 40.2 %collective-permute-start.25 = (bf16[256,2048]{1,0:T(8,128)(2,1)}, bf16[256,2048]{1,0:T(8,128)(2,1)S(1)}, u32[]{:S(2)}, u32[]{:S(2)}) collective-permute-start(bf16[256,2048]{1,0:T(8,128)(2,1)} %add_convert_fusion.3), channel_id=1, source_target_pairs={{0,2},{1,3},{2,0},{3,1},{4,6},{5,7},{6,4},{7,5},{8,10},{9,11},{10,... | collective-permute-start | bytes 3145736 | tf_op jit(solution)/shard_map/ppermute | solution.py:837
  476.1 36.2 %collective-permute-start.27 = (bf16[256,2048]{1,0:T(8,128)(2,1)}, bf16[256,2048]{1,0:T(8,128)(2,1)S(1)}, u32[]{:S(2)}, u32[]{:S(2)}) collective-permute-start(bf16[256,2048]{1,0:T(8,128)(2,1)} %add_convert_fusion.2), channel_id=1, source_target_pairs={{0,1},{1,0},{2,3},{3,2},{4,5},{5,4},{6,7},{7,6},{8,9},{9,8},{10,11... | collective-permute-start | bytes 3145736 | tf_op jit(solution)/shard_map/ppermute | solution.py:837
  532.5 28.7 %collective-permute-start.34 = (bf16[512,512]{1,0:T(8,128)(2,1)}, bf16[512,512]{1,0:T(8,128)(2,1)}, u32[]{:S(2)}, u32[]{:S(2)}) collective-permute-start(bf16[512,512]{1,0:T(8,128)(2,1)} %get-tuple-element.157), channel_id=1, source_target_pairs={{0,1},{1,0},{2,3},{3,2},{4,5},{5,4},{6,7},{7,6},{8,9},{9,8},{10,11... | collective-permute-start | bytes 1572872 | tf_op jit(solution)/shard_map/ppermute | solution.py:837
  533.1 28.1 %collective-permute-start.35 = (bf16[512,512]{1,0:T(8,128)(2,1)}, bf16[512,512]{1,0:T(8,128)(2,1)S(1)}, u32[]{:S(2)}, u32[]{:S(2)}) collective-permute-start(bf16[512,512]{1,0:T(8,128)(2,1)} %get-tuple-element.158), channel_id=1, source_target_pairs={{0,2},{1,3},{2,0},{3,1},{4,6},{5,7},{6,4},{7,5},{8,10},{9,11},{10,... | collective-permute-start | bytes 1572872 | tf_op jit(solution)/shard_map/ppermute | solution.py:837
  534.6 26.6 %collective-permute-start.36 = (bf16[512,512]{1,0:T(8,128)(2,1)}, bf16[512,512]{1,0:T(8,128)(2,1)}, u32[]{:S(2)}, u32[]{:S(2)}) collective-permute-start(bf16[512,512]{1,0:T(8,128)(2,1)} %get-tuple-element.159), channel_id=1, source_target_pairs={{0,3},{1,2},{2,1},{3,0},{4,7},{5,6},{6,5},{7,4},{8,11},{9,10},{10,... | collective-permute-start | bytes 1572872 | tf_op jit(solution)/shard_map/ppermute | solution.py:837
  562.0 26.3 %collective-permute-start.38 = (bf16[256,2048]{1,0:T(8,128)(2,1)S(1)}, bf16[256,2048]{1,0:T(8,128)(2,1)S(1)}, u32[]{:S(2)}, u32[]{:S(2)}) collective-permute-start(bf16[256,2048]{1,0:T(8,128)(2,1)S(1)} %get-tuple-element.163), channel_id=1, source_target_pairs={{0,2},{1,3},{2,0},{3,1},{4,6},{5,7},{6,4},{7,5},{8,10},{9,11},{10,... | collective-permute-start | bytes 3145736 | tf_op jit(solution)/shard_map/ppermute | solution.py:837
  589.3 188.0 %reduce-scatter.11.cloned.1.call-start = ((), (), s32[]{:S(2)}) async-start(), calls=%async_computation.10 | async-start | bytes 5898240 | tf_op jit(solution)/shard_map/reduce_scatter | solution.py:1037
  589.3 27.4 %collective-permute-start.41 = (bf16[256,2048]{1,0:T(8,128)(2,1)}, bf16[256,2048]{1,0:T(8,128)(2,1)S(1)}, u32[]{:S(2)}, u32[]{:S(2)}) collective-permute-start(bf16[256,2048]{1,0:T(8,128)(2,1)} %get-tuple-element.171), channel_id=1, source_target_pairs={{0,2},{1,3},{2,0},{3,1},{4,6},{5,7},{6,4},{7,5},{8,10},{9,11},{10,... | collective-permute-start | bytes 3145736 | tf_op jit(solution)/shard_map/ppermute | solution.py:837
  589.9 26.9 %collective-permute-start.40 = (bf16[256,2048]{1,0:T(8,128)(2,1)}, bf16[256,2048]{1,0:T(8,128)(2,1)S(1)}, u32[]{:S(2)}, u32[]{:S(2)}) collective-permute-start(bf16[256,2048]{1,0:T(8,128)(2,1)} %get-tuple-element.171), channel_id=1, source_target_pairs={{0,1},{1,0},{2,3},{3,2},{4,5},{5,4},{6,7},{7,6},{8,9},{9,8},{10,11... | collective-permute-start | bytes 3145736 | tf_op jit(solution)/shard_map/ppermute | solution.py:837
  616.8 30.8 %collective-permute-start.47 = (bf16[256,2048]{1,0:T(8,128)(2,1)S(1)}, bf16[256,2048]{1,0:T(8,128)(2,1)}, u32[]{:S(2)}, u32[]{:S(2)}) collective-permute-start(bf16[256,2048]{1,0:T(8,128)(2,1)S(1)} %collective-permute-done.38.refs_4_), channel_id=1, source_target_pairs={{0,1},{1,0},{2,3},{3,2},{4,5},{5,4},{6,7},{7,6},{8,9},{9,8},{10,11... | collective-permute-start | bytes 3145736 | tf_op jit(solution)/shard_map/ppermute | solution.py:837
  617.2 30.4 %collective-permute-start.48 = (bf16[256,2048]{1,0:T(8,128)(2,1)S(1)}, bf16[256,2048]{1,0:T(8,128)(2,1)}, u32[]{:S(2)}, u32[]{:S(2)}) collective-permute-start(bf16[256,2048]{1,0:T(8,128)(2,1)S(1)} %collective-permute-done.40.refs_2_), channel_id=1, source_target_pairs={{0,2},{1,3},{2,0},{3,1},{4,6},{5,7},{6,4},{7,5},{8,10},{9,11},{10,... | collective-permute-start | bytes 3145736 | tf_op jit(solution)/shard_map/ppermute | solution.py:837
  618.6 57.3 %collective-permute-start.39 = (bf16[512,768]{1,0:T(8,128)(2,1)}, bf16[512,768]{1,0:T(8,128)(2,1)}, u32[]{:S(2)}, u32[]{:S(2)}) collective-permute-start(bf16[512,768]{1,0:T(8,128)(2,1)} %get-tuple-element.167.refs_5_), channel_id=1, source_target_pairs={{0,1},{1,0},{2,3},{3,2},{4,5},{5,4},{6,7},{7,6},{8,9},{9,8},{10,11... | collective-permute-start | bytes 2359304 | tf_op jit(solution)/shard_map/ppermute | solution.py:837
  645.5 30.4 %collective-permute-start.42 = (bf16[512,768]{1,0:T(8,128)(2,1)}, bf16[512,768]{1,0:T(8,128)(2,1)}, u32[]{:S(2)}, u32[]{:S(2)}) collective-permute-start(bf16[512,768]{1,0:T(8,128)(2,1)} %get-tuple-element.174.refs_6_), channel_id=1, source_target_pairs={{0,2},{1,3},{2,0},{3,1},{4,6},{5,7},{6,4},{7,5},{8,10},{9,11},{10,... | collective-permute-start | bytes 2359304 | tf_op jit(solution)/shard_map/ppermute | solution.py:837
  646.4 29.5 %collective-permute-start.43 = (bf16[512,768]{1,0:T(8,128)(2,1)}, bf16[512,768]{1,0:T(8,128)(2,1)}, u32[]{:S(2)}, u32[]{:S(2)}) collective-permute-start(bf16[512,768]{1,0:T(8,128)(2,1)} %get-tuple-element.175.refs_7_), channel_id=1, source_target_pairs={{0,3},{1,2},{2,1},{3,0},{4,7},{5,6},{6,5},{7,4},{8,11},{9,10},{10,... | collective-permute-start | bytes 2359304 | tf_op jit(solution)/shard_map/ppermute | solution.py:837
  679.2 26.2 %collective-permute-start.31 = (bf16[256,2048]{1,0:T(8,128)(2,1)}, bf16[256,2048]{1,0:T(8,128)(2,1)S(1)}, u32[]{:S(2)}, u32[]{:S(2)}) collective-permute-start(bf16[256,2048]{1,0:T(8,128)(2,1)} %get-tuple-element.153), channel_id=1, source_target_pairs={{0,2},{1,3},{2,0},{3,1},{4,6},{5,7},{6,4},{7,5},{8,10},{9,11},{10,... | collective-permute-start | bytes 3145736 | tf_op jit(solution)/shard_map/ppermute | solution.py:837
  680.7 27.5 %collective-permute-start.44 = (bf16[1024,768]{1,0:T(8,128)(2,1)S(1)}, bf16[1024,768]{1,0:T(8,128)(2,1)S(1)}, u32[]{:S(2)}, u32[]{:S(2)}) collective-permute-start(bf16[1024,768]{1,0:T(8,128)(2,1)S(1)} %copy-done.14), channel_id=1, source_target_pairs={{0,4},{4,0},{8,12},{12,8},{16,20},{20,16},{24,28},{28,24},{1,5},{5... | collective-permute-start | bytes 4718600 | tf_op jit(solution)/shard_map/ppermute | solution.py:837
  680.7 28.1 %collective-permute-start.45 = (bf16[1024,768]{1,0:T(8,128)(2,1)S(1)}, bf16[1024,768]{1,0:T(8,128)(2,1)S(1)}, u32[]{:S(2)}, u32[]{:S(2)}) collective-permute-start(bf16[1024,768]{1,0:T(8,128)(2,1)S(1)} %copy-done.12), channel_id=1, source_target_pairs={{0,4},{4,0},{8,12},{12,8},{16,20},{20,16},{24,28},{28,24},{1,5},{5... | collective-permute-start | bytes 4718600 | tf_op jit(solution)/shard_map/ppermute | solution.py:837
  681.2 29.6 %collective-permute-start.46 = (bf16[1024,768]{1,0:T(8,128)(2,1)}, bf16[1024,768]{1,0:T(8,128)(2,1)}, u32[]{:S(2)}, u32[]{:S(2)}) collective-permute-start(bf16[1024,768]{1,0:T(8,128)(2,1)} %constant_dynamic-update-slice_fusion.9.refs_7_), channel_id=1, source_target_pairs={{0,4},{4,0},{8,12},{12,8},{16,20},{20,16},{24,28},{28,24},{1,5},{5... | collective-permute-start | bytes 4718600 | tf_op jit(solution)/shard_map/ppermute | solution.py:837
  700.9 30.7 %collective-permute-start.28 = (bf16[256,2048]{1,0:T(8,128)(2,1)}, bf16[256,2048]{1,0:T(8,128)(2,1)}, u32[]{:S(2)}, u32[]{:S(2)}) collective-permute-start(bf16[256,2048]{1,0:T(8,128)(2,1)} %get-tuple-element.148), channel_id=1, source_target_pairs={{0,1},{1,0},{2,3},{3,2},{4,5},{5,4},{6,7},{7,6},{8,9},{9,8},{10,11... | collective-permute-start | bytes 3145736 | tf_op jit(solution)/shard_map/ppermute | solution.py:837
  705.4 26.5 %collective-permute-start.33 = (bf16[256,2048]{1,0:T(8,128)(2,1)}, bf16[256,2048]{1,0:T(8,128)(2,1)}, u32[]{:S(2)}, u32[]{:S(2)}) collective-permute-start(bf16[256,2048]{1,0:T(8,128)(2,1)} %get-tuple-element.154), channel_id=1, source_target_pairs={{0,2},{1,3},{2,0},{3,1},{4,6},{5,7},{6,4},{7,5},{8,10},{9,11},{10,... | collective-permute-start | bytes 3145736 | tf_op jit(solution)/shard_map/ppermute | solution.py:837
  708.2 41.3 %collective-permute-start.30 = (bf16[256,2048]{1,0:T(8,128)(2,1)}, bf16[256,2048]{1,0:T(8,128)(2,1)S(1)}, u32[]{:S(2)}, u32[]{:S(2)}) collective-permute-start(bf16[256,2048]{1,0:T(8,128)(2,1)} %add_convert_fusion.1), channel_id=1, source_target_pairs={{0,2},{1,3},{2,0},{3,1},{4,6},{5,7},{6,4},{7,5},{8,10},{9,11},{10,... | collective-permute-start | bytes 3145736 | tf_op jit(solution)/shard_map/ppermute | solution.py:837
  709.4 40.2 %collective-permute-start.32 = (bf16[256,2048]{1,0:T(8,128)(2,1)}, bf16[256,2048]{1,0:T(8,128)(2,1)S(1)}, u32[]{:S(2)}, u32[]{:S(2)}) collective-permute-start(bf16[256,2048]{1,0:T(8,128)(2,1)} %add_convert_fusion), channel_id=1, source_target_pairs={{0,1},{1,0},{2,3},{3,2},{4,5},{5,4},{6,7},{7,6},{8,9},{9,8},{10,11... | collective-permute-start | bytes 3145736 | tf_op jit(solution)/shard_map/ppermute | solution.py:837
  731.7 26.2 %collective-permute-start.49 = (f32[33,128]{1,0:T(8,128)S(1)}, f32[33,128]{1,0:T(8,128)S(1)}, u32[]{:S(2)}, u32[]{:S(2)}) collective-permute-start(f32[33,128]{1,0:T(8,128)S(1)} %bitcast.50), channel_id=1, source_target_pairs={{0,4},{4,0},{8,12},{12,8},{16,20},{20,16},{24,28},{28,24},{1,5},{5... | collective-permute-start | bytes 50696 | tf_op jit(solution)/shard_map/ppermute | solution.py:837
  (61 other events, 864.0 us)
Sparse Core Ops, SparseCore 0:
  10.2 58.7 all-gather.3
  71.2 115.4 all-gather.5
  189.0 114.9 all-gather.7
  353.1 89.8 reduce-scatter.4
  445.1 87.9 reduce-scatter.6
  588.4 89.1 reduce-scatter.8
  679.9 58.2 reduce-scatter.10

commit v2 on v1

--- a/solution.py
+++ b/solution.py
@@ -458,48 +458,7 @@
     pl.semaphore_wait(barrier, len(distances))
 
 
-def carry(distances, src_refs, dst_refs, send_sems=None, recv_sems=None):
-    if not distances:
-        return
-    copies = [
-        pltpu.make_async_remote_copy(
-            src_ref=src_ref, dst_ref=dst_ref, send_sem=send_sems.at[i], recv_sem=recv_sems.at[i],
-            **remote(distance),
-        )
-        for i, (distance, src_ref, dst_ref) in enumerate(zip(distances, src_refs, dst_refs))
-    ]
-
-    @pl.when(pl.program_id(0) == 0)
-    def _():
-        greet(sorted(set(distances)))
-        for sent in copies:
-            sent.start()
-
-    @pl.when(pl.program_id(0) == pl.num_programs(0) - 1)
-    def _():
-        for sent in copies:
-            sent.wait()
-
-
-def carried(sends, collective_id):
-    place = pl.BlockSpec(memory_space=pl.ANY)
-    count = len(sends)
-    if not count:
-        return [], [], [], [], {}, []
-    return (
-        [place] * count,
-        [place] * count,
-        [jax.ShapeDtypeStruct(value.shape, value.dtype) for _, value in sends],
-        [pltpu.SemaphoreType.DMA((count,)), pltpu.SemaphoreType.DMA((count,))],
-        dict(collective_id=collective_id, has_side_effects=True),
-        [value for _, value in sends],
-    )
-
-
-def hidden_kernel(filled, distances, x_ref, dy_ref, w_ref, *refs):
-    refs, count = refs[filled:], len(distances)
-    act_ref, grads_ref = refs[count : count + 2]
-    carry(distances, refs[:count], refs[count + 2 : 2 * count + 2], *refs[2 * count + 2 :])
+def hidden_kernel(x_ref, dy_ref, w_ref, filled_ref, act_ref, grads_ref):
     units = act_ref.shape[1]
     inputs, cotangent = x_ref[...], dy_ref[...]
     for at in range(0, units, 256):
@@ -519,39 +478,95 @@
         grads_ref[:, units + at : units + at + 256] = (change * silu).astype(jnp.bfloat16)
 
 
-def hidden_units(inputs, cotangent, weights, filled, sends=(), collective_id=None):
+def hidden_units(inputs, cotangent, weights, filled):
     rows, width = inputs.shape
     units = weights.shape[1] // 3
     block = min(512, rows)
     row = lambda r: (r, 0)
-    place = 0 if filled is None else 1
-    in_more, out_more, shapes, scratch, params, operands = carried(sends, collective_id)
-    act, grads, *received = pl.pallas_call(
-        functools.partial(hidden_kernel, place, [distance for distance, _ in sends]),
+    return pl.pallas_call(
+        hidden_kernel,
         grid=(rows // block,),
         in_specs=[
             pl.BlockSpec((block, width), row),
             pl.BlockSpec((block, width), row),
             pl.BlockSpec(weights.shape, lambda r: (0, 0), pipeline_mode=pl.Buffered(1)),
-        ]
-        + [pl.BlockSpec(memory_space=pl.ANY)] * place
-        + in_more,
+            pl.BlockSpec(memory_space=pl.ANY),
+        ],
         out_specs=[
-            pl.BlockSpec((block, units), lambda r: (r, place)),
+            pl.BlockSpec((block, units), lambda r: (r, 1)),
             pl.BlockSpec((block, 2 * units), row),
-        ]
-        + out_more,
-        out_shape=[
-            jax.ShapeDtypeStruct((rows, 2 * units), jnp.bfloat16),
-            jax.ShapeDtypeStruct((rows, 2 * units), jnp.bfloat16),
-        ]
-        + shapes,
-        scratch_shapes=scratch,
-        input_output_aliases={3: 0} if place else {},
-        compiler_params=pltpu.CompilerParams(vmem_limit_bytes=60 * 2**20, **params),
+        ],
+        out_shape=[jax.ShapeDtypeStruct((rows, 2 * units), jnp.bfloat16)] * 2,
+        input_output_aliases={3: 0},
+        compiler_params=pltpu.CompilerParams(vmem_limit_bytes=60 * 2**20),
         cost_estimate=cost(6 * rows * width * units, (rows * width + width * units) * 6, 0.63),
-    )(inputs, cotangent, weights, *([filled] * place), *operands)
-    return act, grads, received
+    )(inputs, cotangent, weights, filled)
+
+
+def hidden_forward_kernel(x_ref, w_ref, act_ref, factors_ref):
+    units = act_ref.shape[1]
+    inputs = x_ref[...]
+    for at in range(0, units, 256):
+        lanes, beside = slice(at, at + 256), slice(units + at, units + at + 256)
+        gate = jnp.dot(inputs, w_ref[:, lanes], preferred_element_type=jnp.float32)
+        up = jnp.dot(inputs, w_ref[:, beside], preferred_element_type=jnp.float32)
+        sigmoid = 1.0 / (1.0 + jnp.exp(-gate))
+        silu = gate * sigmoid
+        act_ref[:, lanes] = (silu * up).astype(jnp.bfloat16)
+        factors_ref[:, lanes] = (up * sigmoid * (1.0 + gate - silu)).astype(jnp.bfloat16)
+        factors_ref[:, beside] = silu.astype(jnp.bfloat16)
+
+
+def hidden_forward(inputs, weights):
+    rows, width = inputs.shape
+    units = weights.shape[1] // 3
+    block = min(512, rows)
+    row = lambda r: (r, 0)
+    return pl.pallas_call(
+        hidden_forward_kernel,
+        grid=(rows // block,),
+        in_specs=[
+            pl.BlockSpec((block, width), row),
+            pl.BlockSpec((width, 2 * units), lambda r: (0, 0), pipeline_mode=pl.Buffered(1)),
+        ],
+        out_specs=[pl.BlockSpec((block, units), row), pl.BlockSpec((block, 2 * units), row)],
+        out_shape=[jax.ShapeDtypeStruct((rows, 2 * units), jnp.bfloat16)] * 2,
+        compiler_params=pltpu.CompilerParams(vmem_limit_bytes=60 * 2**20),
+        cost_estimate=cost(4 * rows * width * units, (rows * width + width * units) * 4, 0.63),
+    )(inputs, weights)
+
+
+def hidden_backward_kernel(dy_ref, factors_ref, w_ref, grads_ref):
+    units = w_ref.shape[1]
+    cotangent = dy_ref[...]
+    for at in range(0, units, 256):
+        change = jnp.dot(
+            cotangent, w_ref[:, at : at + 256], preferred_element_type=jnp.float32
+        )
+        for lanes in (slice(at, at + 256), slice(units + at, units + at + 256)):
+            grads_ref[:, lanes] = (change * factors_ref[:, lanes].astype(jnp.float32)).astype(
+                jnp.bfloat16
+            )
+
+
+def hidden_backward(cotangent, factors, weights):
+    rows, width = cotangent.shape
+    units = weights.shape[1] // 3
+    block = min(512, rows)
+    row = lambda r: (r, 0)
+    return pl.pallas_call(
+        hidden_backward_kernel,
+        grid=(rows // block,),
+        in_specs=[
+            pl.BlockSpec((block, width), row),
+            pl.BlockSpec((block, 2 * units), row),
+            pl.BlockSpec((width, units), lambda r: (0, 2), pipeline_mode=pl.Buffered(1)),
+        ],
+        out_specs=pl.BlockSpec((block, 2 * units), row),
+        out_shape=jax.ShapeDtypeStruct((rows, 2 * units), jnp.bfloat16),
+        compiler_params=pltpu.CompilerParams(vmem_limit_bytes=60 * 2**20),
+        cost_estimate=cost(2 * rows * width * units, (rows * width + width * units) * 4, 0.63),
+    )(cotangent, factors, weights)
 
 
 def half_types(distance):
@@ -564,11 +579,8 @@
     return (jnp.bfloat16, jnp.bfloat16)
 
 
-def rows_out_kernel(terms, halves, distances, *refs):
-    count = len(distances)
-    at = 2 * terms + count
-    outs = refs[at : at + halves]
-    carry(distances, refs[2 * terms : at], refs[at + halves : at + halves + count], *refs[at + halves + count :])
+def rows_out_kernel(terms, *refs):
+    outs = refs[2 * terms :]
     total = None
     for left_ref, right_ref in zip(refs[:terms], refs[terms : 2 * terms]):
         product = lax.dot_general(
@@ -580,7 +592,7 @@
         out_ref[...] = total[index * half : (index + 1) * half].astype(out_ref.dtype)
 
 
-def rows_out(distances, lefts, rights, spans, chunk_rows, sends=(), collective_id=None):
+def rows_out(distances, lefts, rights, spans, chunk_rows):
     width, rows = rights[0].shape[0], len(distances) * chunk_rows
     first = distances[0] // len(distances)
     halves = [dtype for k in distances for dtype in half_types(k)]
@@ -593,21 +605,16 @@
         pl.BlockSpec((256, columns), lambda n, index=index: (n, index)) for columns, index in spans
     ]
     depth = sum(left[1] for left in lefts)
-    in_more, out_more, shapes, scratch, params, operands = carried(sends, collective_id)
     outs = pl.pallas_call(
-        functools.partial(
-            rows_out_kernel, len(lefts), len(halves), [distance for distance, _ in sends]
-        ),
+        functools.partial(rows_out_kernel, len(lefts)),
         grid=(width // 256,),
-        in_specs=in_specs + in_more,
-        out_specs=[pl.BlockSpec((chunk_rows // 2, 256), lambda n: (0, n))] * len(halves) + out_more,
-        out_shape=[jax.ShapeDtypeStruct((chunk_rows // 2, width), dtype) for dtype in halves] + shapes,
-        scratch_shapes=scratch,
-        compiler_params=pltpu.CompilerParams(vmem_limit_bytes=60 * 2**20, **params),
+        in_specs=in_specs,
+        out_specs=[pl.BlockSpec((chunk_rows // 2, 256), lambda n: (0, n))] * len(halves),
+        out_shape=[jax.ShapeDtypeStruct((chunk_rows // 2, width), dtype) for dtype in halves],
+        compiler_params=pltpu.CompilerParams(vmem_limit_bytes=60 * 2**20),
         cost_estimate=cost(2 * rows * depth * width, depth * rows // 4, 4.07),
-    )(*(left[0] for left in lefts), *rights, *operands)
-    parts = {k: (outs[2 * i], outs[2 * i + 1]) for i, k in enumerate(distances)}
-    return (parts, outs[len(halves) :]) if sends else parts
+    )(*(left[0] for left in lefts), *rights)
+    return {k: (outs[2 * i], outs[2 * i + 1]) for i, k in enumerate(distances)}
 
 
 def resid_kernel(count, place_ref, *refs):
@@ -931,12 +938,6 @@
     )
 
 
-def gather_others(weights, columns, core, sizes):
-    piece = column_piece(weights, columns, core)
-    pieces = [shift(piece, k, sizes["tensor"]) for k in range(1, sizes["tensor"])]
-    return pieces + [shift(piece, 1, sizes["dp"], "dp") for piece in pieces]
-
-
 def sum_first(parts, count):
     if count != 4:
         return None
@@ -1080,14 +1081,18 @@
         for part in (slice(0, units), slice(units, 2 * units))
     ]
     segments, positions = own_first(segments), own_first(positions)
-    out_others = gather_others(after(w_attn, rows_in), (0, q_width), core, sizes)
+    out_near = gather_near(column_piece(after(w_attn, rows_in), (0, q_width), core), count)
     inv_rows, queries, key_sides, value_sides, raw = [], [], [], [], []
     tables = rotary_tables(positions.reshape(-1))
     attended, inv_total, heads = [], [], []
     for sequence in range(2):
         rows = rows_in[sequence]
         if sequence == 1:
-            rows = after(rows, attended, out_others[: count - 1])
+            rows = after(rows, attended, out_near)
+            out_near = after(out_near, attended)
+            out_far = gather_far(out_near, count)
+            out_others = out_near[1:] + ([jnp.concatenate(out_far, axis=0)] if out_far else [])
+            out_others = out_others + [shift(part, 1, sizes["dp"], "dp") for part in out_others]
         results = project(
             inner, sequence, rows, chunk_rows, norm_attn, w_attn, tables, query_gain, key_gain, q_width, kv_width
         )
@@ -1108,18 +1113,20 @@
     )
     resid = resid.reshape(2, half, width)
     grad_near = after(grad_near, rows_two)
-    grad_rows = jnp.concatenate(grad_near + gather_far(grad_near, count), axis=0)
-
-    half_columns = column_piece(after(w_attn, grad_rows), (q_width, w_attn.shape[1]), core)
+    grad_far = gather_far(grad_near, count)
+    act_a, factors = hidden_forward(rows_two, w_mlp[0])
+    grad_rows = jnp.concatenate(grad_near + after(grad_far, act_a), axis=0)
+
+    grads_a = hidden_backward(grad_rows, factors, w_mlp[0])
+    grad_a = contract_rows(rows_two, grads_a).astype(jnp.bfloat16)
+    half_columns = column_piece(after(w_attn, grads_a), (q_width, w_attn.shape[1]), core)
     in_near = [shift(half_columns, k, count) for k in range(1, count - 1)]
-    act_a, grads_a, _ = hidden_units(rows_two, grad_rows, w_mlp[0], None)
-    in_near = after(in_near, grads_a)
-    grad_a = contract_rows(after(rows_two, in_near), grads_a).astype(jnp.bfloat16)
     if count == 4:
-        in_far = [jnp.concatenate(gather_far([half_columns, *in_near], count), axis=0)]
+        far_halves = gather_far([half_columns, *in_near], count)
+        in_far = [jnp.concatenate(far_halves, axis=0)]
     else:
-        in_far = [shift(in_near[0], count - 2, count)]
-    act, grads_b, _ = hidden_units(after(rows_two, grad_a, in_far), grad_rows, w_mlp[1], act_a)
+        far_halves = in_far = [shift(half_columns, count - 1, count)]
+    act, grads_b = hidden_units(after(rows_two, grad_a), grad_rows, w_mlp[1], act_a)
     in_others = in_near + in_far
     in_others = in_others + [shift(part, 1, sizes["dp"], "dp") for part in in_others]
     spans = [(2 * units, 0), (2 * units, 0)]
@@ -1128,15 +1135,15 @@
         lefts = [(grads, 2 * units, 0), (grads_b, 2 * units, 0)]
         return rows_out(distances, lefts, w_mlp, spans, chunk_rows)
 
-    grad_b = contract_rows(rows_two, grads_b).astype(jnp.bfloat16)
-    two = two_parts(list(range(inner_count, count)), after(grads_a, grad_b))
+    grad_b = contract_rows(after(rows_two, in_near), grads_b).astype(jnp.bfloat16)
+    two = two_parts(list(range(inner_count, count)), after(grads_a, grad_b, far_halves))
     two_first = sum_first(two, count)
     for k in range(1, inner_count):
         two.update(two_parts([k], after(grads_a, two[count - 1])))
     if count == 4:
         two_rest = sum_rest(two, two_first, count)
         sent = (two_rest[0][1], two_rest[1][2])
-        two.update(two_parts([0], after(grads_a, two[1], sent)))
+        two.update(two_parts([0], after(grads_a, two[1])))
         two_rest[0][0], two_rest[1][0] = two[0]
     else:
         sent = ()
@@ -1157,7 +1164,7 @@
     distances = list(range(count))
     heads_out = grad_heads(core, branch_low, w_attn, out_others, q_width, count)
     heads_in = exchange(heads_out, distances, count)
-    scattered_a = scatter_weights(after(grad_a, in_far))
+    scattered_a = scatter_weights(grad_a)
     scattered_b = scatter_weights(after(grad_b, scattered_a, two[count - 1]))
     out_act = after(act, heads_out[0])
     out = rows_out(
@@ -1198,17 +1205,6 @@
         branch_near = gather_near(branch_low, count)
         branch = (branch_near[:inner_count], branch_near[inner_count:])
     out_first = sum_first(out, count)
-    out_rest = sum_rest(out, out_first, count)
-    if count == 4:
-        out_rest[0][0], out_rest[1][0] = out[0]
-    (output,) = own_rows_call(
-        output_kernel, out_rest, [resid], [], [jax.ShapeDtypeStruct((2, half, width), jnp.bfloat16)],
-        False,
-    )
-    distances = list(range(count))
-    grad_tokens, gain_attn = input_back(
-        core, raw_in, w_attn, in_others, tokens, grad_resid.reshape(chunk_rows, width), norm_attn
-    )
     grad_w_out = out_weights(inner, after(branch, raw_grads), attended)
     grad_qkv = projection_weights(after(rows_in, raw_grads, relays), inv_rows, norm_attn, raw_grads)
 
@@ -1220,6 +1216,19 @@
         )
     )
 
+    grad_w_gate = jnp.concatenate(
+        [scattered_a[:, :units], scattered_b[:, :units]], axis=1
+    ).astype(jnp.float32)
+    grad_w_up = jnp.concatenate(
+        [scattered_a[:, units:], scattered_b[:, units:]], axis=1
+    ).astype(jnp.float32)
+    grad_w_down = scattered_down.astype(jnp.float32)
+    grad_tokens, gain_attn = input_back(
+        core, after(raw_in, grad_w_gate, grad_w_up), w_attn, in_others, tokens, grad_resid.reshape(chunk_rows, width), norm_attn
+    )
+    out_rest = sum_rest(out, after(out_first, gain_attn) if count == 4 else None, count)
+    if count == 4:
+        out_rest[0][0], out_rest[1][0] = out[0]
     gains = [
         jnp.sum(gain_attn, axis=0),
         jnp.sum(gain_mlp, axis=0),
@@ -1228,6 +1237,11 @@
     ]
     gains = jnp.concatenate(gains).reshape(-1, 128)
     gains = total_everywhere(gains, sizes).reshape(-1)
+    (output,) = own_rows_call(
+        output_kernel, after(out_rest, gains), [resid], [], [jax.ShapeDtypeStruct((2, half, width), jnp.bfloat16)],
+        False,
+    )
+    distances = list(range(count))
     key_at = 2 * q_width
     value_at = key_at + kv_width
     return (
@@ -1237,9 +1251,9 @@
         scattered_attn[:, key_at : key_at + key_width].astype(jnp.float32),
         scattered_attn[:, value_at : value_at + key_width].astype(jnp.float32),
         scattered_attn[:, :q_width].astype(jnp.float32),
-        jnp.concatenate([scattered_a[:, :units], scattered_b[:, :units]], axis=1).astype(jnp.float32),
-        jnp.concatenate([scattered_a[:, units:], scattered_b[:, units:]], axis=1).astype(jnp.float32),
-        scattered_down.astype(jnp.float32),
+        grad_w_gate,
+        grad_w_up,
+        grad_w_down,
         gains[:width],
         gains[width : 2 * width],
         gains[2 * width : 2 * width + 64],

time: 798 us -> 767 us (0.961)
  waiting for transfers between devices: 149 us -> 112 us
    ppermute x54 -> x55, waiting for transfers between devices: 141 us -> 110 us  [shift(): return lax.ppermute(values, axis, [(i, i ^ distance) for i in range(count)])]
    pallas_call x6 -> x7, Pallas kernels: 150 us -> 156 us  [the longest x4 79.6 us: rows_out(): pl.pallas_call(functools.partial(rows_out_kernel, len(lefts)), grid=(widt...]
    unnamed x104 -> x109, local copies, waits for them, and re-layouts: 20.7 us -> 18.3 us
    ppermute x54 -> x55, starting transfers between devices: 55.9 us -> 55.3 us  [shift(): return lax.ppermute(values, axis, [(i, i ^ distance) for i in range(count)])]
  transfers between devices with their start and end apart: 61 -> 62, of which waited for: 24 -> 17; matrix products, arithmetic and copies ran while one was open for 17% -> 18% of each run, Pallas kernels for 53% -> 56%
where the time goes in v2:
time: 767 us; the launch traced here: 756 us
  Pallas kernels  423 us (55%)
  waiting for transfers between devices  112 us (15%)
  matrix products  71.6 us (9%)
  starting transfers between devices  55.5 us (7%)
  local copies, waits for them, and re-layouts  43.4 us (6%)
  other arithmetic  35.3 us (5%)
  between operations  15.3 us (2%)
    ppermute x55, waiting for transfers between devices, shift(): return lax.ppermute(values, axis, [(i, i ^ distance) for i in range(count)])  110 us
    pallas_call x4, Pallas kernels, rows_out(): pl.pallas_call(functools.partial(rows_out_kernel, len(lefts)), grid=(widt...  79.6 us
    pallas_call x1, Pallas kernels, gather_rows(): pl.pallas_call(gather_kernel, in_specs=[place], out_specs=[place] * 2, ou...  72.8 us
    dot_general x3, matrix products, contract_rows(): lax.dot_general(left, right, (((0,), (0,)), ((), ())), preferred_element_...  71.6 us
    ppermute x55, starting transfers between devices, shift(): return lax.ppermute(values, axis, [(i, i ^ distance) for i in range(count)])  55.3 us
    pallas_call x2, Pallas kernels, attend_back(): pl.pallas_call(functools.partial(attend_back_kernel, chunks), grid_spec=p...  50.6 us
    pallas_call x1, Pallas kernels, hidden_units(): pl.pallas_call(hidden_kernel, grid=(rows // block,), in_specs=[pl.BlockSp...  36 us
    pallas_call x1, Pallas kernels, residual(): pl.pallas_call(functools.partial(resid_kernel, count), grid_spec=pltpu.Pr...  32.4 us
  transfers between devices with their start and end apart: 62, of which 17 were waited for; matrix products, arithmetic and copies ran while one was open for 18% of the time, Pallas kernels for 56%

profile of v2, /device:TPU:0, one launch (start us, length us, event | category | flops | bytes accessed | tf_op | source)
XLA Modules:
  0.0 756.4 jit_solution(6829790666471380881)
XLA Ops:
  15.2 72.8 %shard_map.246 = (bf16[1024,2048]{1,0:T(8,128)(2,1)}, bf16[1024,2048]{1,0:T(8,128)(2,1)}) custom-call(bf16[512,2048]{1,0:T(8,128)(2,1)} %refs_11_.1), custom_call_target="tpu_custom_call" | custom-call | bytes 12582912 | tf_op jit(solution)/shard_map/pallas_call | solution.py:892
  96.3 5.8 fusion
  102.1 11.1 %shard_map.247 = (f32[1024,128]{1,0:T(8,128)}, bf16[1024,512]{1,0:T(8,128)(2,1)}, bf16[1024,512]{1,0:T(8,128)(2,1)}, bf16[1024,512]{1,0:T(8,128)(2,1)}, f32[1024,640]{1,0:T(8,128)}) custom-call(s32[1]{0:T(128)S(6)} %select_n.55.inner_ref, bf16[1024,2048]{1,0:T(8,128)(2,1)} %get-tuple-element.219.refs_0_, f32[1,2048]{1,0:T(1,128)} %bitcast.51, ...), custom_call_target="tpu_custom_call" | custom-call | flops 2928386816 | bytes 2516582 | tf_op jit(solution)/shard_map/pallas_call | solution.py:376
  113.2 9.5 %shard_map.248 = (bf16[1024,512]{1,0:T(8,128)(2,1)}, f32[1024,512]{1,0:T(8,128)}) custom-call(bf16[1024,512]{1,0:T(8,128)(2,1)} %get-tuple-element.121.q_ref, bf16[1024,512]{1,0:T(8,128)(2,1)} %get-tuple-element.122.k_ref, bf16[1024,512]{1,0:T(8,128)(2,1)} %get-tuple-element.123.v_ref, s32[1024,1]{1,0:T(8,128)} %copy.29.segc_ref, ...), custom_call_target="tpu_custom_call" | custom-call | flops 2254857728 | bytes 6291456 | tf_op jit(solution)/shard_map/pallas_call | solution.py:225
  124.8 11.8 %shard_map.249 = (f32[1024,128]{1,0:T(8,128)}, bf16[1024,512]{1,0:T(8,128)(2,1)}, bf16[1024,512]{1,0:T(8,128)(2,1)}, bf16[1024,512]{1,0:T(8,128)(2,1)}, f32[1024,640]{1,0:T(8,128)}) custom-call(s32[1]{0:T(128)S(6)} %select_n.55.inner_ref, bf16[1024,2048]{1,0:T(8,128)(2,1)} %get-tuple-element.220.refs_0_.refs_1_, f32[1,2048]{1,0:T(1,128)} %bitcast.52, ...), custom_call_target="tpu_custom_call" | custom-call | flops 2928386816 | bytes 2516582 | tf_op jit(solution)/shard_map/pallas_call | solution.py:376
  136.6 9.9 %shard_map.250 = (bf16[1024,512]{1,0:T(8,128)(2,1)}, f32[1024,512]{1,0:T(8,128)}) custom-call(bf16[1024,512]{1,0:T(8,128)(2,1)} %get-tuple-element.127.q_ref, bf16[1024,512]{1,0:T(8,128)(2,1)} %get-tuple-element.128.k_ref, bf16[1024,512]{1,0:T(8,128)(2,1)} %get-tuple-element.129.v_ref, s32[1024,1]{1,0:T(8,128)} %copy.30.segc_ref, ...), custom_call_target="tpu_custom_call" | custom-call | flops 2254857728 | bytes 6291456 | tf_op jit(solution)/shard_map/pallas_call | solution.py:225
  151.9 21.0 %collective-permute-done.3.refs_4_ = bf16[1024,512]{1,0:T(8,128)(2,1)S(1)} collective-permute-done((bf16[1024,512]{1,0:T(8,128)(2,1)}, bf16[1024,512]{1,0:T(8,128)(2,1)S(1)}, u32[]{:S(2)}, u32[]{:S(2)}) %collective-permute-start.3) | collective-permute-done | bytes 1048608 | tf_op jit(solution)/shard_map/ppermute | solution.py:844
  175.8 8.8 %collective-permute-done.8 = bf16[512,512]{1,0:T(8,128)(2,1)S(1)} collective-permute-done((bf16[512,512]{1,0:T(8,128)(2,1)S(1)}, bf16[512,512]{1,0:T(8,128)(2,1)S(1)}, u32[]{:S(2)}, u32[]{:S(2)}) %collective-permute-start.8) | collective-permute-done | bytes 524320 | tf_op jit(solution)/shard_map/ppermute | solution.py:844
  186.3 9.6 %collective-permute-done.4 = bf16[512,512]{1,0:T(8,128)(2,1)S(1)} collective-permute-done((bf16[512,512]{1,0:T(8,128)(2,1)S(1)}, bf16[512,512]{1,0:T(8,128)(2,1)S(1)}, u32[]{:S(2)}, u32[]{:S(2)}) %collective-permute-start.4) | collective-permute-done | bytes 524320 | tf_op jit(solution)/shard_map/ppermute | solution.py:844
  198.1 9.0 %collective-permute-done.10 = bf16[512,512]{1,0:T(8,128)(2,1)S(1)} collective-permute-done((bf16[512,512]{1,0:T(8,128)(2,1)S(1)}, bf16[512,512]{1,0:T(8,128)(2,1)S(1)}, u32[]{:S(2)}, u32[]{:S(2)}) %collective-permute-start.10) | collective-permute-done | bytes 524320 | tf_op jit(solution)/shard_map/ppermute | solution.py:844
  212.2 32.4 %shard_map.251 = (bf16[2048,2048]{1,0:T(8,128)(2,1)}, f32[1,512,2048]{2,1,0:T(8,128)}) custom-call(s32[2]{0:T(128)} %pad_add_fusion.place_ref, bf16[1024,2048]{1,0:T(8,128)(2,1)} %get-tuple-element.219.refs_0_, bf16[1024,2048]{1,0:T(8,128)(2,1)} %get-tuple-element.220.refs_0_.refs_1_, bf16[1024,512]{1,0:T(8,128)(2,1)} %get-tuple-element.124.refs_2_.out_ref.refs_3_, ...), custom_call_target="tpu_custom_call" | custom-call | flops 7469508096 | bytes 6710886 | tf_op jit(solution)/shard_map/pallas_call | solution.py:667
  244.6 3.6 collective-permute-done.16
  249.8 2.3 slice.118
  255.6 3.2 constant_dynamic-update-slice_fusion.9
  258.9 3.2 constant_dynamic-update-slice_fusion.8
  262.0 25.3 %shard_map.252 = (bf16[2048,2048]{1,0:T(8,128)(2,1)}, bf16[2048,2048]{1,0:T(8,128)(2,1)}) custom-call(bf16[2048,2048]{1,0:T(8,128)(2,1)} %get-tuple-element.145.x_ref, bf16[2048,3072]{1,0:T(8,128)(2,1)} %all-gather.6.cloned.1.call-done.w_ref.refs_2_), custom_call_target="tpu_custom_call" | custom-call | flops 5453926912 | bytes 5033164 | tf_op jit(solution)/shard_map/pallas_call | solution.py:525
  287.3 2.3 constant_dynamic-update-slice_fusion.7
  289.6 2.3 constant_dynamic-update-slice_fusion.6.dy_ref
  292.0 15.2 %shard_map.253.refs_0_ = bf16[2048,2048]{1,0:T(8,128)(2,1)} custom-call(bf16[2048,2048]{1,0:T(8,128)(2,1)} %constant_dynamic-update-slice_fusion.6.dy_ref, bf16[2048,2048]{1,0:T(8,128)(2,1)} %get-tuple-element.141.factors_ref, bf16[2048,3072]{1,0:T(8,128)(2,1)} %all-gather.6.cloned.1.call-done.w_ref.refs_2_), custom_call_target="tpu_custom_call" | custom-call | flops 2726963456 | bytes 5033164 | tf_op jit(solution)/shard_map/pallas_call | solution.py:557
  307.2 23.7 %convolution_convert_fusion.2 = bf16[2048,2048]{1,0:T(8,128)(2,1)} fusion(bf16[2048,2048]{1,0:T(8,128)(2,1)} %get-tuple-element.145.x_ref, bf16[2048,2048]{1,0:T(8,128)(2,1)} %shard_map.253.refs_0_), kind=kOutput, calls=%fused_computation.2 | convolution fusion | flops 17184063488 | bytes 25165824 | tf_op jit(solution)/shard_map/dot_general | solution.py:38
  331.0 2.7 constant_dynamic-slice_fusion
  335.6 36.0 %shard_map.254 = (bf16[2048,2048]{1,0:T(8,128)(2,1)}, bf16[2048,2048]{1,0:T(8,128)(2,1)}) custom-call(bf16[2048,2048]{1,0:T(8,128)(2,1)} %get-tuple-element.145.x_ref, bf16[2048,2048]{1,0:T(8,128)(2,1)} %constant_dynamic-update-slice_fusion.6.dy_ref, bf16[2048,3072]{1,0:T(8,128)(2,1)} %all-gather.8.cloned.1.call-done.w_ref.refs_3_, ...), custom_call_target="tpu_custom_call", output_to_operand_aliasing={{0}: (3, {})} | custom-call | flops 8180890112 | bytes 7549747 | tf_op jit(solution)/shard_map/pallas_call | solution.py:486
  375.7 23.9 %convolution_convert_fusion.1 = bf16[2048,2048]{1,0:T(8,128)(2,1)} fusion(bf16[2048,2048]{1,0:T(8,128)(2,1)} %get-tuple-element.145.x_ref, bf16[2048,2048]{1,0:T(8,128)(2,1)} %get-tuple-element.146.refs_1_), kind=kOutput, calls=%fused_computation.1 | convolution fusion | flops 17184063488 | bytes 25165824 | tf_op jit(solution)/shard_map/dot_general | solution.py:38
  399.6 24.1 %shard_map.255 = (f32[256,2048]{1,0:T(8,128)}, bf16[256,2048]{1,0:T(8,128)(2,1)}, bf16[256,2048]{1,0:T(8,128)(2,1)}, bf16[256,2048]{1,0:T(8,128)(2,1)}) custom-call(bf16[2048,2048]{1,0:T(8,128)(2,1)} %shard_map.253.refs_0_, bf16[2048,2048]{1,0:T(8,128)(2,1)} %get-tuple-element.146.refs_1_, bf16[2048,3072]{1,0:T(8,128)(2,1)} %all-gather.6.cloned.1.call-done.w_ref.refs_2_, ...), custom_call_target="tpu_custom_call" | custom-call | flops 844219584 | bytes 209715 | tf_op jit(solution)/shard_map/pallas_call | solution.py:608
  427.3 16.0 %shard_map.256 = (bf16[256,2048]{1,0:T(8,128)(2,1)}, f32[256,2048]{1,0:T(8,128)}) custom-call(bf16[2048,2048]{1,0:T(8,128)(2,1)} %shard_map.253.refs_0_, bf16[2048,2048]{1,0:T(8,128)(2,1)} %get-tuple-element.146.refs_1_, bf16[2048,3072]{1,0:T(8,128)(2,1)} %all-gather.6.cloned.1.call-done.w_ref.refs_2_, ...), custom_call_target="tpu_custom_call" | custom-call | flops 422109792 | bytes 104857 | tf_op jit(solution)/shard_map/pallas_call | solution.py:608
  443.5 4.7 collective-permute-done.24
  448.2 2.5 add_convert_fusion.3
  452.2 2.5 add_convert_fusion.2
  457.0 15.4 %shard_map.257 = (f32[256,2048]{1,0:T(8,128)}, f32[256,2048]{1,0:T(8,128)}) custom-call(bf16[2048,2048]{1,0:T(8,128)(2,1)} %shard_map.253.refs_0_, bf16[2048,2048]{1,0:T(8,128)(2,1)} %get-tuple-element.146.refs_1_, bf16[2048,3072]{1,0:T(8,128)(2,1)} %all-gather.6.cloned.1.call-done.w_ref.refs_2_, bf16[2048,3072]{1,0:T(8,128)(2,1)} %all-gather.8.cloned.1.call-done.w_ref.refs_3_), custom_call_target="tpu_custom_call" | custom-call | flops 422109792 | bytes 104857 | tf_op jit(solution)/shard_map/pallas_call | solution.py:608
  474.1 16.3 %collective-permute-done.25.refs_2_ = bf16[256,2048]{1,0:T(8,128)(2,1)S(1)} collective-permute-done((bf16[256,2048]{1,0:T(8,128)(2,1)}, bf16[256,2048]{1,0:T(8,128)(2,1)S(1)}, u32[]{:S(2)}, u32[]{:S(2)}) %collective-permute-start.25) | collective-permute-done | bytes 1048608 | tf_op jit(solution)/shard_map/ppermute | solution.py:844
  491.7 9.5 %shard_map.258 = (f32[2,256,2048]{2,1,0:T(8,128)}, bf16[2,256,2048]{2,1,0:T(8,128)(2,1)}, f32[8,2048]{1,0:T(8,128)}) custom-call(f32[256,2048]{1,0:T(8,128)} %get-tuple-element.154.refs_0_, bf16[256,2048]{1,0:T(8,128)(2,1)} %collective-permute-done.23.refs_1_, bf16[256,2048]{1,0:T(8,128)(2,1)} %copy-done.34, f32[256,2048]{1,0:T(8,128)} %get-tuple-element.156.refs_3_, ...), custom_call_target="tpu_custom_call" | custom-call | flops 1048576 | bytes 1048576 | tf_op jit(solution)/shard_map/pallas_call | solution.py:981
  501.2 9.3 %shard_map.259 = (bf16[512,512]{1,0:T(8,128)(2,1)}, bf16[512,512]{1,0:T(8,128)(2,1)}, bf16[512,512]{1,0:T(8,128)(2,1)}, bf16[512,512]{1,0:T(8,128)(2,1)}) custom-call(s32[1]{0:T(128)S(6)} %select_n.56.core_ref, bf16[512,2048]{1,0:T(8,128)(2,1)} %bitcast.43, bf16[2048,1280]{1,0:T(8,128)(2,1)} %all-gather.4.cloned.1.call-done.refs_2_.refs_10_.refs_0_.refs_4_, ...), custom_call_target="tpu_custom_call" | custom-call | flops 321720384 | bytes 209715 | tf_op jit(solution)/shard_map/pallas_call | solution.py:428
  514.0 24.1 %shard_map.260 = (f32[256,2048]{1,0:T(8,128)}, f32[256,2048]{1,0:T(8,128)}, bf16[256,2048]{1,0:T(8,128)(2,1)}, f32[256,2048]{1,0:T(8,128)}, f32[256,2048]{1,0:T(...) custom-call(bf16[2048,2048]{1,0:T(8,128)(2,1)} %get-tuple-element.161.refs_0_.refs_1_, ...), custom_call_target="tpu_custom_call" | custom-call | flops 844219584 | bytes 209715 | tf_op jit(solution)/shard_map/pallas_call | solution.py:608
  542.2 23.9 %convolution_convert_fusion = bf16[2048,2048]{1,0:T(8,128)(2,1)} fusion(bf16[2048,2048]{1,0:T(8,128)(2,1)} %constant_dynamic-update-slice_fusion.6.dy_ref, bf16[2048,2048]{1,0:T(8,128)(2,1)} %get-tuple-element.161.refs_0_.refs_1_), kind=kOutput, calls=%fused_computation | convolution fusion | flops 17184063488 | bytes 25165824 | tf_op jit(solution)/shard_map/dot_general | solution.py:38
  569.1 25.2 %shard_map.261 = (bf16[512,768]{1,0:T(8,128)(2,1)}, bf16[512,768]{1,0:T(8,128)(2,1)}, f32[8,128]{1,0:T(8,128)}, f32[8,128]{1,0:T(8,128)}) custom-call(s32[1]{0:T(128)S(6)} %select_n.55.inner_ref, bf16[1024,512]{1,0:T(8,128)(2,1)} %get-tuple-element.121.q_ref, bf16[1024,512]{1,0:T(8,128)(2,1)} %get-tuple-element.122.k_ref, ...), custom_call_target="tpu_custom_call" | custom-call | flops 5905580032 | bytes 10485760 | tf_op jit(solution)/shard_map/pallas_call | solution.py:258
  597.8 25.4 %shard_map.262 = (bf16[512,768]{1,0:T(8,128)(2,1)}, bf16[512,768]{1,0:T(8,128)(2,1)}, f32[8,128]{1,0:T(8,128)}, f32[8,128]{1,0:T(8,128)}) custom-call(s32[1]{0:T(128)S(6)} %select_n.55.inner_ref, bf16[1024,512]{1,0:T(8,128)(2,1)} %get-tuple-element.127.q_ref, bf16[1024,512]{1,0:T(8,128)(2,1)} %get-tuple-element.128.k_ref, ...), custom_call_target="tpu_custom_call" | custom-call | flops 5905580032 | bytes 10485760 | tf_op jit(solution)/shard_map/pallas_call | solution.py:258
  625.4 13.1 %shard_map.266 = bf16[2048,768]{1,0:T(8,128)(2,1)} custom-call(f32[1,2048]{1,0:T(1,128)} %bitcast.53, bf16[1024,2048]{1,0:T(8,128)(2,1)} %get-tuple-element.219.refs_0_, bf16[1024,2048]{1,0:T(8,128)(2,1)} %get-tuple-element.220.refs_0_.refs_1_, f32[1024,128]{1,0:T(8,128)} %get-tuple-element.221.refs_2_, f32[1024,128]{1,0:T(8,128)} %get-tuple-element.222.refs_3_, ...), custom_call_target="tpu_custom_call" | custom-call | flops 2996488704 | bytes 1677721 | tf_op jit(solution)/shard_map/pallas_call | solution.py:829
  638.5 10.9 %shard_map.265 = bf16[2048,512]{1,0:T(8,128)(2,1)} custom-call(s32[1]{0:T(128)S(6)} %select_n.55.inner_ref, bf16[512,2048]{1,0:T(8,128)(2,1)} %bitcast.44, bf16[256,2048]{1,0:T(8,128)(2,1)} %copy-done.30, bf16[256,2048]{1,0:T(8,128)(2,1)} %copy-done.32, bf16[1024,512]{1,0:T(8,128)(2,1)} %get-tuple-element.124.refs_2_.out_ref.refs_3_, ...), custom_call_target="tpu_custom_call" | custom-call | flops 2454267136 | bytes 1677721 | tf_op jit(solution)/shard_map/pallas_call | solution.py:795
  649.4 4.4 pad_maximum_fusion
  667.4 20.1 %shard_map.263 = (f32[512,2048]{1,0:T(8,128)}, f32[8,2048]{1,0:T(8,128)}) custom-call(s32[1]{0:T(128)S(6)} %select_n.56.core_ref, bf16[512,768]{1,0:T(8,128)(2,1)} %get-tuple-element.188.refs_0_.refs_4_, bf16[512,768]{1,0:T(8,128)(2,1)} %collective-permute-done.37.refs_1_, bf16[512,768]{1,0:T(8,128)(2,1)} %collective-permute-done.40.refs_2_, ...), custom_call_target="tpu_custom_call" | custom-call | flops 4601750528 | bytes 4194304 | tf_op jit(solution)/shard_map/pallas_call | solution.py:743
  687.5 2.6 add_convert_fusion.1
  691.7 2.5 add_convert_fusion
  698.8 3.1 collective-permute-done.49
  703.8 3.7 collective-permute-done.50
  708.1 21.8 %collective-permute-done.51 = f32[33,128]{1,0:T(8,128)S(1)} collective-permute-done((f32[33,128]{1,0:T(8,128)S(1)}, f32[33,128]{1,0:T(8,128)S(1)}, u32[]{:S(2)}, u32[]{:S(2)}) %collective-permute-start.51) | collective-permute-done | bytes 16928 | tf_op jit(solution)/shard_map/ppermute | solution.py:844
  731.4 2.3 collective-permute-done.52
  736.2 6.4 shard_map.264
  742.6 2.8 convert_element_type.91
  (284 shorter events, 103.1 us)
Async XLA Ops:
  7.2 81.5 %all-gather.4.cloned.1.call-start = ((), (), s32[]{:S(2)}) async-start(), calls=%async_computation.4 | async-start | bytes 5898240 | tf_op jit(solution)/shard_map/all_gather | solution.py:1034
  9.3 252.7 %all-gather.6.cloned.1.call-start = ((), (), s32[]{:S(2)}) async-start(), calls=%async_computation.5 | async-start | bytes 14155776 | tf_op jit(solution)/shard_map/all_gather | solution.py:1034
  13.3 322.3 %all-gather.8.cloned.1.call-start = ((), (), s32[]{:S(2)}) async-start(), calls=%async_computation.6 | async-start | bytes 14155776 | tf_op jit(solution)/shard_map/all_gather | solution.py:1034
  14.6 409.1 %reduce-scatter.5.cloned.1.call-start = ((), (), s32[]{:S(2)}) async-start(), calls=%async_computation.7 | async-start | bytes 9437184 | tf_op jit(solution)/shard_map/reduce_scatter | solution.py:1038
  90.9 33.8 %collective-permute-start.2 = (bf16[1024,512]{1,0:T(8,128)(2,1)}, bf16[1024,512]{1,0:T(8,128)(2,1)S(1)}, u32[]{:S(2)}, u32[]{:S(2)}) collective-permute-start(bf16[1024,512]{1,0:T(8,128)(2,1)} %constant_dynamic-slice_fusion.1), channel_id=1, source_target_pairs={{0,2},{1,3},{2,0},{3,1},{4,6},{5,7},{6,4},{7,5},{8,10},{9,11},{10,... | collective-permute-start | bytes 3145736 | tf_op jit(solution)/shard_map/ppermute | solution.py:844
  91.5 33.3 %collective-permute-start.1 = (bf16[1024,512]{1,0:T(8,128)(2,1)}, bf16[1024,512]{1,0:T(8,128)(2,1)S(1)}, u32[]{:S(2)}, u32[]{:S(2)}) collective-permute-start(bf16[1024,512]{1,0:T(8,128)(2,1)} %constant_dynamic-slice_fusion.1), channel_id=1, source_target_pairs={{0,1},{1,0},{2,3},{3,2},{4,5},{5,4},{6,7},{7,6},{8,9},{9,8},{10,11... | collective-permute-start | bytes 3145736 | tf_op jit(solution)/shard_map/ppermute | solution.py:844
  122.7 25.9 %collective-permute-start.7 = (bf16[1024,512]{1,0:T(8,128)(2,1)}, bf16[1024,512]{1,0:T(8,128)(2,1)S(1)}, u32[]{:S(2)}, u32[]{:S(2)}) collective-permute-start(bf16[1024,512]{1,0:T(8,128)(2,1)} %get-tuple-element.124.refs_2_.out_ref.refs_3_), channel_id=1, source_target_pairs={{0,2},{1,3},{2,0},{3,1},{4,6},{5,7},{6,4},{7,5},{8,10},{9,11},{10,... | collective-permute-start | bytes 3145736 | tf_op jit(solution)/shard_map/ppermute | solution.py:844
  123.3 25.9 %collective-permute-start = (bf16[1024,512]{1,0:T(8,128)(2,1)}, bf16[1024,512]{1,0:T(8,128)(2,1)}, u32[]{:S(2)}, u32[]{:S(2)}) collective-permute-start(bf16[1024,512]{1,0:T(8,128)(2,1)} %get-tuple-element.124.refs_2_.out_ref.refs_3_), channel_id=1, source_target_pairs={{0,1},{1,0},{2,3},{3,2},{4,5},{5,4},{6,7},{7,6},{8,9},{9,8},{10,11... | collective-permute-start | bytes 3145736 | tf_op jit(solution)/shard_map/ppermute | solution.py:844
  146.5 26.4 %collective-permute-start.3 = (bf16[1024,512]{1,0:T(8,128)(2,1)}, bf16[1024,512]{1,0:T(8,128)(2,1)S(1)}, u32[]{:S(2)}, u32[]{:S(2)}) collective-permute-start(bf16[1024,512]{1,0:T(8,128)(2,1)} %get-tuple-element.130.refs_6_.out_ref.refs_8_), channel_id=1, source_target_pairs={{0,2},{1,3},{2,0},{3,1},{4,6},{5,7},{6,4},{7,5},{8,10},{9,11},{10,... | collective-permute-start | bytes 3145736 | tf_op jit(solution)/shard_map/ppermute | solution.py:844
  147.1 26.5 %collective-permute-start.5 = (bf16[1024,512]{1,0:T(8,128)(2,1)}, bf16[1024,512]{1,0:T(8,128)(2,1)S(1)}, u32[]{:S(2)}, u32[]{:S(2)}) collective-permute-start(bf16[1024,512]{1,0:T(8,128)(2,1)} %get-tuple-element.130.refs_6_.out_ref.refs_8_), channel_id=1, source_target_pairs={{0,1},{1,0},{2,3},{3,2},{4,5},{5,4},{6,7},{7,6},{8,9},{9,8},{10,11... | collective-permute-start | bytes 3145736 | tf_op jit(solution)/shard_map/ppermute | solution.py:844
  148.6 36.0 %collective-permute-start.8 = (bf16[512,512]{1,0:T(8,128)(2,1)S(1)}, bf16[512,512]{1,0:T(8,128)(2,1)S(1)}, u32[]{:S(2)}, u32[]{:S(2)}) collective-permute-start(bf16[512,512]{1,0:T(8,128)(2,1)S(1)} %slice.150), channel_id=1, source_target_pairs={{0,1},{1,0},{2,3},{3,2},{4,5},{5,4},{6,7},{7,6},{8,9},{9,8},{10,11... | collective-permute-start | bytes 1572872 | tf_op jit(solution)/shard_map/ppermute | solution.py:844
  150.3 35.9 %collective-permute-start.9 = (bf16[512,512]{1,0:T(8,128)(2,1)S(1)}, bf16[512,512]{1,0:T(8,128)(2,1)S(1)}, u32[]{:S(2)}, u32[]{:S(2)}) collective-permute-start(bf16[512,512]{1,0:T(8,128)(2,1)S(1)} %slice.151), channel_id=1, source_target_pairs={{0,2},{1,3},{2,0},{3,1},{4,6},{5,7},{6,4},{7,5},{8,10},{9,11},{10,... | collective-permute-start | bytes 1572872 | tf_op jit(solution)/shard_map/ppermute | solution.py:844
  175.2 31.9 %collective-permute-start.10 = (bf16[512,512]{1,0:T(8,128)(2,1)S(1)}, bf16[512,512]{1,0:T(8,128)(2,1)S(1)}, u32[]{:S(2)}, u32[]{:S(2)}) collective-permute-start(bf16[512,512]{1,0:T(8,128)(2,1)S(1)} %slice.116), channel_id=1, source_target_pairs={{0,1},{1,0},{2,3},{3,2},{4,5},{5,4},{6,7},{7,6},{8,9},{9,8},{10,11... | collective-permute-start | bytes 1572872 | tf_op jit(solution)/shard_map/ppermute | solution.py:844
  196.0 52.3 %collective-permute-start.16 = (bf16[512,2048]{1,0:T(8,128)(2,1)S(1)}, bf16[512,2048]{1,0:T(8,128)(2,1)}, u32[]{:S(2)}, u32[]{:S(2)}) collective-permute-start(bf16[512,2048]{1,0:T(8,128)(2,1)S(1)} %copy-done.2), channel_id=1, source_target_pairs={{0,2},{1,3},{2,0},{3,1},{4,6},{5,7},{6,4},{7,5},{8,10},{9,11},{10,... | collective-permute-start | bytes 6291464 | tf_op jit(solution)/shard_map/ppermute | solution.py:844
  197.6 50.9 %collective-permute-start.15 = (bf16[512,2048]{1,0:T(8,128)(2,1)S(1)}, bf16[512,2048]{1,0:T(8,128)(2,1)}, u32[]{:S(2)}, u32[]{:S(2)}) collective-permute-start(bf16[512,2048]{1,0:T(8,128)(2,1)S(1)} %copy-done.2), channel_id=1, source_target_pairs={{0,1},{1,0},{2,3},{3,2},{4,5},{5,4},{6,7},{7,6},{8,9},{9,8},{10,11... | collective-permute-start | bytes 6291464 | tf_op jit(solution)/shard_map/ppermute | solution.py:844
  252.1 35.3 %collective-permute-start.17 = (bf16[256,2048]{1,0:T(8,128)(2,1)}, bf16[256,2048]{1,0:T(8,128)(2,1)}, u32[]{:S(2)}, u32[]{:S(2)}) collective-permute-start(bf16[256,2048]{1,0:T(8,128)(2,1)} %slice.118), channel_id=1, source_target_pairs={{0,1},{1,0},{2,3},{3,2},{4,5},{5,4},{6,7},{7,6},{8,9},{9,8},{10,11... | collective-permute-start | bytes 3145736 | tf_op jit(solution)/shard_map/ppermute | solution.py:844
  253.6 33.7 %collective-permute-start.18 = (bf16[256,2048]{1,0:T(8,128)(2,1)S(1)}, bf16[256,2048]{1,0:T(8,128)(2,1)}, u32[]{:S(2)}, u32[]{:S(2)}) collective-permute-start(bf16[256,2048]{1,0:T(8,128)(2,1)S(1)} %slice.119), channel_id=1, source_target_pairs={{0,2},{1,3},{2,0},{3,1},{4,6},{5,7},{6,4},{7,5},{8,10},{9,11},{10,... | collective-permute-start | bytes 3145736 | tf_op jit(solution)/shard_map/ppermute | solution.py:844
  330.9 211.2 %reduce-scatter.7.cloned.1.call-start = ((), (), s32[]{:S(2)}) async-start(), calls=%async_computation.8 | async-start | bytes 9437184 | tf_op jit(solution)/shard_map/reduce_scatter | solution.py:1038
  333.6 38.0 %collective-permute-start.20 = (bf16[1024,768]{1,0:T(8,128)(2,1)}, bf16[1024,768]{1,0:T(8,128)(2,1)S(1)}, u32[]{:S(2)}, u32[]{:S(2)}) collective-permute-start(bf16[1024,768]{1,0:T(8,128)(2,1)} %constant_dynamic-slice_fusion), channel_id=1, source_target_pairs={{0,2},{1,3},{2,0},{3,1},{4,6},{5,7},{6,4},{7,5},{8,10},{9,11},{10,... | collective-permute-start | bytes 4718600 | tf_op jit(solution)/shard_map/ppermute | solution.py:844
  335.2 39.1 %collective-permute-start.19 = (bf16[1024,768]{1,0:T(8,128)(2,1)}, bf16[1024,768]{1,0:T(8,128)(2,1)S(1)}, u32[]{:S(2)}, u32[]{:S(2)}) collective-permute-start(bf16[1024,768]{1,0:T(8,128)(2,1)} %constant_dynamic-slice_fusion), channel_id=1, source_target_pairs={{0,1},{1,0},{2,3},{3,2},{4,5},{5,4},{6,7},{7,6},{8,9},{9,8},{10,11... | collective-permute-start | bytes 4718600 | tf_op jit(solution)/shard_map/ppermute | solution.py:844
  372.7 27.0 %collective-permute-start.21 = (bf16[512,768]{1,0:T(8,128)(2,1)}, bf16[512,768]{1,0:T(8,128)(2,1)}, u32[]{:S(2)}, u32[]{:S(2)}) collective-permute-start(bf16[512,768]{1,0:T(8,128)(2,1)} %slice.152), channel_id=1, source_target_pairs={{0,1},{1,0},{2,3},{3,2},{4,5},{5,4},{6,7},{7,6},{8,9},{9,8},{10,11... | collective-permute-start | bytes 2359304 | tf_op jit(solution)/shard_map/ppermute | solution.py:844
  375.2 24.4 %collective-permute-start.22 = (bf16[512,768]{1,0:T(8,128)(2,1)}, bf16[512,768]{1,0:T(8,128)(2,1)}, u32[]{:S(2)}, u32[]{:S(2)}) collective-permute-start(bf16[512,768]{1,0:T(8,128)(2,1)} %slice.153), channel_id=1, source_target_pairs={{0,2},{1,3},{2,0},{3,1},{4,6},{5,7},{6,4},{7,5},{8,10},{9,11},{10,... | collective-permute-start | bytes 2359304 | tf_op jit(solution)/shard_map/ppermute | solution.py:844
  423.7 231.9 %reduce-scatter.9.cloned.1.call-start = ((), (), s32[]{:S(2)}) async-start(), calls=%async_computation.9 | async-start | bytes 9437184 | tf_op jit(solution)/shard_map/reduce_scatter | solution.py:1038
  423.8 24.5 %collective-permute-start.24 = (bf16[256,2048]{1,0:T(8,128)(2,1)}, bf16[256,2048]{1,0:T(8,128)(2,1)}, u32[]{:S(2)}, u32[]{:S(2)}) collective-permute-start(bf16[256,2048]{1,0:T(8,128)(2,1)} %get-tuple-element.148), channel_id=1, source_target_pairs={{0,1},{1,0},{2,3},{3,2},{4,5},{5,4},{6,7},{7,6},{8,9},{9,8},{10,11... | collective-permute-start | bytes 3145736 | tf_op jit(solution)/shard_map/ppermute | solution.py:844
  425.3 26.9 %collective-permute-start.26 = (bf16[256,2048]{1,0:T(8,128)(2,1)}, bf16[256,2048]{1,0:T(8,128)(2,1)}, u32[]{:S(2)}, u32[]{:S(2)}) collective-permute-start(bf16[256,2048]{1,0:T(8,128)(2,1)} %get-tuple-element.149), channel_id=1, source_target_pairs={{0,2},{1,3},{2,0},{3,1},{4,6},{5,7},{6,4},{7,5},{8,10},{9,11},{10,... | collective-permute-start | bytes 3145736 | tf_op jit(solution)/shard_map/ppermute | solution.py:844
  425.8 48.3 %collective-permute-start.28 = (bf16[256,2048]{1,0:T(8,128)(2,1)}, bf16[256,2048]{1,0:T(8,128)(2,1)S(1)}, u32[]{:S(2)}, u32[]{:S(2)}) collective-permute-start(bf16[256,2048]{1,0:T(8,128)(2,1)} %get-tuple-element.157), channel_id=1, source_target_pairs={{0,2},{1,3},{2,0},{3,1},{4,6},{5,7},{6,4},{7,5},{8,10},{9,11},{10,... | collective-permute-start | bytes 3145736 | tf_op jit(solution)/shard_map/ppermute | solution.py:844
  443.4 30.7 %collective-permute-start.23 = (bf16[256,2048]{1,0:T(8,128)(2,1)}, bf16[256,2048]{1,0:T(8,128)(2,1)}, u32[]{:S(2)}, u32[]{:S(2)}) collective-permute-start(bf16[256,2048]{1,0:T(8,128)(2,1)} %get-tuple-element.151), channel_id=1, source_target_pairs={{0,1},{1,0},{2,3},{3,2},{4,5},{5,4},{6,7},{7,6},{8,9},{9,8},{10,11... | collective-permute-start | bytes 3145736 | tf_op jit(solution)/shard_map/ppermute | solution.py:844
  450.8 39.6 %collective-permute-start.25 = (bf16[256,2048]{1,0:T(8,128)(2,1)}, bf16[256,2048]{1,0:T(8,128)(2,1)S(1)}, u32[]{:S(2)}, u32[]{:S(2)}) collective-permute-start(bf16[256,2048]{1,0:T(8,128)(2,1)} %add_convert_fusion.3), channel_id=1, source_target_pairs={{0,2},{1,3},{2,0},{3,1},{4,6},{5,7},{6,4},{7,5},{8,10},{9,11},{10,... | collective-permute-start | bytes 3145736 | tf_op jit(solution)/shard_map/ppermute | solution.py:844
  454.7 35.6 %collective-permute-start.27 = (bf16[256,2048]{1,0:T(8,128)(2,1)}, bf16[256,2048]{1,0:T(8,128)(2,1)S(1)}, u32[]{:S(2)}, u32[]{:S(2)}) collective-permute-start(bf16[256,2048]{1,0:T(8,128)(2,1)} %add_convert_fusion.2), channel_id=1, source_target_pairs={{0,1},{1,0},{2,3},{3,2},{4,5},{5,4},{6,7},{7,6},{8,9},{9,8},{10,11... | collective-permute-start | bytes 3145736 | tf_op jit(solution)/shard_map/ppermute | solution.py:844
  510.5 28.7 %collective-permute-start.32 = (bf16[512,512]{1,0:T(8,128)(2,1)}, bf16[512,512]{1,0:T(8,128)(2,1)}, u32[]{:S(2)}, u32[]{:S(2)}) collective-permute-start(bf16[512,512]{1,0:T(8,128)(2,1)} %get-tuple-element.169), channel_id=1, source_target_pairs={{0,1},{1,0},{2,3},{3,2},{4,5},{5,4},{6,7},{7,6},{8,9},{9,8},{10,11... | collective-permute-start | bytes 1572872 | tf_op jit(solution)/shard_map/ppermute | solution.py:844
  511.1 28.1 %collective-permute-start.33 = (bf16[512,512]{1,0:T(8,128)(2,1)}, bf16[512,512]{1,0:T(8,128)(2,1)S(1)}, u32[]{:S(2)}, u32[]{:S(2)}) collective-permute-start(bf16[512,512]{1,0:T(8,128)(2,1)} %get-tuple-element.170), channel_id=1, source_target_pairs={{0,2},{1,3},{2,0},{3,1},{4,6},{5,7},{6,4},{7,5},{8,10},{9,11},{10,... | collective-permute-start | bytes 1572872 | tf_op jit(solution)/shard_map/ppermute | solution.py:844
  512.6 26.6 %collective-permute-start.34 = (bf16[512,512]{1,0:T(8,128)(2,1)}, bf16[512,512]{1,0:T(8,128)(2,1)}, u32[]{:S(2)}, u32[]{:S(2)}) collective-permute-start(bf16[512,512]{1,0:T(8,128)(2,1)} %get-tuple-element.171), channel_id=1, source_target_pairs={{0,3},{1,2},{2,1},{3,0},{4,7},{5,6},{6,5},{7,4},{8,11},{9,10},{10,... | collective-permute-start | bytes 1572872 | tf_op jit(solution)/shard_map/ppermute | solution.py:844
  540.0 26.1 %collective-permute-start.36 = (bf16[256,2048]{1,0:T(8,128)(2,1)S(1)}, bf16[256,2048]{1,0:T(8,128)(2,1)S(1)}, u32[]{:S(2)}, u32[]{:S(2)}) collective-permute-start(bf16[256,2048]{1,0:T(8,128)(2,1)S(1)} %get-tuple-element.175), channel_id=1, source_target_pairs={{0,2},{1,3},{2,0},{3,1},{4,6},{5,7},{6,4},{7,5},{8,10},{9,11},{10,... | collective-permute-start | bytes 3145736 | tf_op jit(solution)/shard_map/ppermute | solution.py:844
  541.5 24.6 %collective-permute-start.35 = (bf16[256,2048]{1,0:T(8,128)(2,1)S(1)}, bf16[256,2048]{1,0:T(8,128)(2,1)S(1)}, u32[]{:S(2)}, u32[]{:S(2)}) collective-permute-start(bf16[256,2048]{1,0:T(8,128)(2,1)S(1)} %get-tuple-element.175), channel_id=1, source_target_pairs={{0,1},{1,0},{2,3},{3,2},{4,5},{5,4},{6,7},{7,6},{8,9},{9,8},{10,11... | collective-permute-start | bytes 3145736 | tf_op jit(solution)/shard_map/ppermute | solution.py:844
  567.2 178.2 %reduce-scatter.11.cloned.1.call-start = ((), (), s32[]{:S(2)}) async-start(), calls=%async_computation.10 | async-start | bytes 5898240 | tf_op jit(solution)/shard_map/reduce_scatter | solution.py:1038
  567.2 27.1 %collective-permute-start.39 = (bf16[256,2048]{1,0:T(8,128)(2,1)}, bf16[256,2048]{1,0:T(8,128)(2,1)S(1)}, u32[]{:S(2)}, u32[]{:S(2)}) collective-permute-start(bf16[256,2048]{1,0:T(8,128)(2,1)} %get-tuple-element.183), channel_id=1, source_target_pairs={{0,2},{1,3},{2,0},{3,1},{4,6},{5,7},{6,4},{7,5},{8,10},{9,11},{10,... | collective-permute-start | bytes 3145736 | tf_op jit(solution)/shard_map/ppermute | solution.py:844
  567.8 26.6 %collective-permute-start.38 = (bf16[256,2048]{1,0:T(8,128)(2,1)}, bf16[256,2048]{1,0:T(8,128)(2,1)S(1)}, u32[]{:S(2)}, u32[]{:S(2)}) collective-permute-start(bf16[256,2048]{1,0:T(8,128)(2,1)} %get-tuple-element.183), channel_id=1, source_target_pairs={{0,1},{1,0},{2,3},{3,2},{4,5},{5,4},{6,7},{7,6},{8,9},{9,8},{10,11... | collective-permute-start | bytes 3145736 | tf_op jit(solution)/shard_map/ppermute | solution.py:844
  594.3 31.1 %collective-permute-start.53 = (bf16[256,2048]{1,0:T(8,128)(2,1)S(1)}, bf16[256,2048]{1,0:T(8,128)(2,1)}, u32[]{:S(2)}, u32[]{:S(2)}) collective-permute-start(bf16[256,2048]{1,0:T(8,128)(2,1)S(1)} %collective-permute-done.36.refs_4_), channel_id=1, source_target_pairs={{0,1},{1,0},{2,3},{3,2},{4,5},{5,4},{6,7},{7,6},{8,9},{9,8},{10,11... | collective-permute-start | bytes 3145736 | tf_op jit(solution)/shard_map/ppermute | solution.py:844
  595.0 30.4 %collective-permute-start.54 = (bf16[256,2048]{1,0:T(8,128)(2,1)S(1)}, bf16[256,2048]{1,0:T(8,128)(2,1)}, u32[]{:S(2)}, u32[]{:S(2)}) collective-permute-start(bf16[256,2048]{1,0:T(8,128)(2,1)S(1)} %collective-permute-done.38.refs_2_), channel_id=1, source_target_pairs={{0,2},{1,3},{2,0},{3,1},{4,6},{5,7},{6,4},{7,5},{8,10},{9,11},{10,... | collective-permute-start | bytes 3145736 | tf_op jit(solution)/shard_map/ppermute | solution.py:844
  596.4 57.3 %collective-permute-start.37 = (bf16[512,768]{1,0:T(8,128)(2,1)}, bf16[512,768]{1,0:T(8,128)(2,1)}, u32[]{:S(2)}, u32[]{:S(2)}) collective-permute-start(bf16[512,768]{1,0:T(8,128)(2,1)} %get-tuple-element.179.refs_5_), channel_id=1, source_target_pairs={{0,1},{1,0},{2,3},{3,2},{4,5},{5,4},{6,7},{7,6},{8,9},{9,8},{10,11... | collective-permute-start | bytes 2359304 | tf_op jit(solution)/shard_map/ppermute | solution.py:844
  623.2 30.6 %collective-permute-start.40 = (bf16[512,768]{1,0:T(8,128)(2,1)}, bf16[512,768]{1,0:T(8,128)(2,1)}, u32[]{:S(2)}, u32[]{:S(2)}) collective-permute-start(bf16[512,768]{1,0:T(8,128)(2,1)} %get-tuple-element.186.refs_6_), channel_id=1, source_target_pairs={{0,2},{1,3},{2,0},{3,1},{4,6},{5,7},{6,4},{7,5},{8,10},{9,11},{10,... | collective-permute-start | bytes 2359304 | tf_op jit(solution)/shard_map/ppermute | solution.py:844
  624.0 29.8 %collective-permute-start.41 = (bf16[512,768]{1,0:T(8,128)(2,1)}, bf16[512,768]{1,0:T(8,128)(2,1)}, u32[]{:S(2)}, u32[]{:S(2)}) collective-permute-start(bf16[512,768]{1,0:T(8,128)(2,1)} %get-tuple-element.187.refs_7_), channel_id=1, source_target_pairs={{0,3},{1,2},{2,1},{3,0},{4,7},{5,6},{6,5},{7,4},{8,11},{9,10},{10,... | collective-permute-start | bytes 2359304 | tf_op jit(solution)/shard_map/ppermute | solution.py:844
  658.8 28.7 %collective-permute-start.30 = (bf16[256,2048]{1,0:T(8,128)(2,1)}, bf16[256,2048]{1,0:T(8,128)(2,1)}, u32[]{:S(2)}, u32[]{:S(2)}) collective-permute-start(bf16[256,2048]{1,0:T(8,128)(2,1)} %get-tuple-element.165), channel_id=1, source_target_pairs={{0,1},{1,0},{2,3},{3,2},{4,5},{5,4},{6,7},{7,6},{8,9},{9,8},{10,11... | collective-permute-start | bytes 3145736 | tf_op jit(solution)/shard_map/ppermute | solution.py:844
  660.3 27.2 %collective-permute-start.31 = (bf16[256,2048]{1,0:T(8,128)(2,1)}, bf16[256,2048]{1,0:T(8,128)(2,1)}, u32[]{:S(2)}, u32[]{:S(2)}) collective-permute-start(bf16[256,2048]{1,0:T(8,128)(2,1)} %get-tuple-element.166), channel_id=1, source_target_pairs={{0,2},{1,3},{2,0},{3,1},{4,6},{5,7},{6,4},{7,5},{8,10},{9,11},{10,... | collective-permute-start | bytes 3145736 | tf_op jit(solution)/shard_map/ppermute | solution.py:844
  665.0 69.8 %collective-permute-start.29 = (bf16[256,2048]{1,0:T(8,128)(2,1)}, bf16[256,2048]{1,0:T(8,128)(2,1)}, u32[]{:S(2)}, u32[]{:S(2)}) collective-permute-start(bf16[256,2048]{1,0:T(8,128)(2,1)} %get-tuple-element.163), channel_id=1, source_target_pairs={{0,1},{1,0},{2,3},{3,2},{4,5},{5,4},{6,7},{7,6},{8,9},{9,8},{10,11... | collective-permute-start | bytes 3145736 | tf_op jit(solution)/shard_map/ppermute | solution.py:844
  665.6 69.3 %collective-permute-start.47 = (bf16[256,2048]{1,0:T(8,128)(2,1)}, bf16[256,2048]{1,0:T(8,128)(2,1)S(1)}, u32[]{:S(2)}, u32[]{:S(2)}) collective-permute-start(bf16[256,2048]{1,0:T(8,128)(2,1)} %get-tuple-element.197), channel_id=1, source_target_pairs={{0,2},{1,3},{2,0},{3,1},{4,6},{5,7},{6,4},{7,5},{8,10},{9,11},{10,... | collective-permute-start | bytes 3145736 | tf_op jit(solution)/shard_map/ppermute | solution.py:844
  690.2 44.7 %collective-permute-start.45 = (bf16[256,2048]{1,0:T(8,128)(2,1)}, bf16[256,2048]{1,0:T(8,128)(2,1)S(1)}, u32[]{:S(2)}, u32[]{:S(2)}) collective-permute-start(bf16[256,2048]{1,0:T(8,128)(2,1)} %add_convert_fusion.1), channel_id=1, source_target_pairs={{0,2},{1,3},{2,0},{3,1},{4,6},{5,7},{6,4},{7,5},{8,10},{9,11},{10,... | collective-permute-start | bytes 3145736 | tf_op jit(solution)/shard_map/ppermute | solution.py:844
  694.3 40.7 %collective-permute-start.46 = (bf16[256,2048]{1,0:T(8,128)(2,1)}, bf16[256,2048]{1,0:T(8,128)(2,1)}, u32[]{:S(2)}, u32[]{:S(2)}) collective-permute-start(bf16[256,2048]{1,0:T(8,128)(2,1)} %add_convert_fusion), channel_id=1, source_target_pairs={{0,1},{1,0},{2,3},{3,2},{4,5},{5,4},{6,7},{7,6},{8,9},{9,8},{10,11... | collective-permute-start | bytes 3145736 | tf_op jit(solution)/shard_map/ppermute | solution.py:844
  (64 other events, 862.3 us)
Sparse Core Ops, SparseCore 0:
  10.2 58.7 all-gather.3
  71.2 115.4 all-gather.5
  189.0 114.9 all-gather.7
  331.1 90.0 reduce-scatter.4
  423.8 89.9 reduce-scatter.6
  566.3 89.2 reduce-scatter.8
  657.9 59.1 reduce-scatter.10

commit v3 on v2

--- a/solution.py
+++ b/solution.py
@@ -1149,9 +1149,15 @@
         sent = ()
         two.update(two_parts([0], after(grads_a, two[1])))
         two_rest = sum_rest(two, None, count)
+    distances = list(range(count))
+    out_act = after(act, two[0])
+    out = rows_out(
+        distances, [(out_act, units, 0), (out_act, units, 1)], w_mlp, [(units, 2), (units, 2)], chunk_rows
+    )
+    out_first = sum_first(out, count)
     grad_resid, branch_low, gain_mlp = own_rows_call(
         resid_back_kernel,
-        two_rest,
+        after(two_rest, out[0]),
         [out_grad.reshape(2, half, width), resid],
         [norm_mlp[None, :]],
         [
@@ -1161,33 +1167,27 @@
         True,
     )
     branch_low = branch_low.reshape(chunk_rows, width)
-    distances = list(range(count))
     heads_out = grad_heads(core, branch_low, w_attn, out_others, q_width, count)
     heads_in = exchange(heads_out, distances, count)
     scattered_a = scatter_weights(grad_a)
     scattered_b = scatter_weights(after(grad_b, scattered_a, two[count - 1]))
-    out_act = after(act, heads_out[0])
-    out = rows_out(
-        distances, [(out_act, units, 0), (out_act, units, 1)], w_mlp, [(units, 2), (units, 2)], chunk_rows
-    )
-    grad_down = contract_rows(after(grad_rows, out[0], scattered_b, heads_in), act).astype(jnp.bfloat16)
+    grad_down = contract_rows(
+        after(grad_rows, heads_out[0], scattered_b, out_first), act
+    ).astype(jnp.bfloat16)
     tops = bottoms = relays = []
     if count == 4:
-        top, bottom = after((branch_low[:half], branch_low[half:]), heads_in, out[0])
+        top, bottom = after((branch_low[:half], branch_low[half:]), heads_in, grad_down)
         tops = [shift(top, 1, count), shift(top, 2, count)]
     sums, raw_grads = [], []
     for sequence in range(2):
         pieces = heads_in[sequence * inner_count : (sequence + 1) * inner_count]
         if sequence == 0:
-            pieces = after(pieces, heads_in, grad_down, tops)
+            pieces = after(pieces, heads_in, grad_down)
+        else:
+            pieces = after(pieces, tops, raw_grads)
             if count == 4:
-                bottom = after(bottom, tops)
+                bottom = after(bottom, tops, raw_grads)
                 bottoms = [shift(bottom, 1, count), shift(bottom, 2, count)]
-        else:
-            pieces = after(pieces, bottoms, raw_grads)
-            if count == 4:
-                near_bottom, near_top = after((bottoms[0], tops[1]), bottoms, raw_grads)
-                relays = [shift(near_top, 1, count), shift(near_bottom, 2, count)]
         results = attend_back(
             inner, sequence, queries[sequence], key_sides[sequence], value_sides[sequence],
             segments[sequence], attended[sequence], inv_total[sequence], pieces, raw[sequence], tables,
@@ -1197,6 +1197,8 @@
         sums.append(results[inner_count:])
     raw_in = exchange(raw_grads, distances, count)
     if count == 4:
+        near_bottom, near_top = after((bottoms[0], tops[1]), bottoms, raw_grads)
+        relays = [shift(near_top, 1, count), shift(near_bottom, 2, count)]
         branch = (
             [branch_low, tops[0], bottoms[0]],
             [tops[1], bottoms[1], *relays],
@@ -1204,11 +1206,10 @@
     else:
         branch_near = gather_near(branch_low, count)
         branch = (branch_near[:inner_count], branch_near[inner_count:])
-    out_first = sum_first(out, count)
-    grad_w_out = out_weights(inner, after(branch, raw_grads), attended)
-    grad_qkv = projection_weights(after(rows_in, raw_grads, relays), inv_rows, norm_attn, raw_grads)
-
-    scattered_down = scatter_weights(after(grad_down, scattered_b, tops))
+    grad_qkv = projection_weights(after(rows_in, raw_grads, bottoms), inv_rows, norm_attn, raw_grads)
+    grad_w_out = out_weights(inner, after(branch, raw_grads, grad_qkv), attended)
+
+    scattered_down = scatter_weights(after(grad_down, scattered_b, heads_in))
     scattered_attn = scatter_weights(
         after(
             jnp.concatenate([grad_w_out, grad_qkv], axis=1),
@@ -1224,7 +1225,7 @@
     ).astype(jnp.float32)
     grad_w_down = scattered_down.astype(jnp.float32)
     grad_tokens, gain_attn = input_back(
-        core, after(raw_in, grad_w_gate, grad_w_up), w_attn, in_others, tokens, grad_resid.reshape(chunk_rows, width), norm_attn
+        core, after(raw_in, grad_w_gate, grad_w_up, grad_w_down), w_attn, in_others, tokens, grad_resid.reshape(chunk_rows, width), norm_attn
     )
     out_rest = sum_rest(out, after(out_first, gain_attn) if count == 4 else None, count)
     if count == 4:

time: 767 us -> 756 us (0.986)
  waiting for transfers between devices: 112 us -> 101 us
    ppermute x55, waiting for transfers between devices: 110 us -> 101 us  [shift(): return lax.ppermute(values, axis, [(i, i ^ distance) for i in range(count)])]
  transfers between devices with their start and end apart: 62 -> 62, of which waited for: 17 -> 16; matrix products, arithmetic and copies ran while one was open for 18% -> 18% of each run, Pallas kernels for 56% -> 57%
where the time goes in v3:
time: 756 us; the launch traced here: 745 us
  Pallas kernels  423 us (56%)
  waiting for transfers between devices  101 us (13%)
  matrix products  71.6 us (9%)
  starting transfers between devices  56.1 us (7%)
  local copies, waits for them, and re-layouts  44.4 us (6%)
  other arithmetic  33.1 us (4%)
  between operations  15.4 us (2%)
    ppermute x55, waiting for transfers between devices, shift(): return lax.ppermute(values, axis, [(i, i ^ distance) for i in range(count)])  101 us
    pallas_call x4, Pallas kernels, rows_out(): pl.pallas_call(functools.partial(rows_out_kernel, len(lefts)), grid=(widt...  79.4 us
    pallas_call x1, Pallas kernels, gather_rows(): pl.pallas_call(gather_kernel, in_specs=[place], out_specs=[place] * 2, ou...  72.8 us
    dot_general x3, matrix products, contract_rows(): lax.dot_general(left, right, (((0,), (0,)), ((), ())), preferred_element_...  71.6 us
    ppermute x55, starting transfers between devices, shift(): return lax.ppermute(values, axis, [(i, i ^ distance) for i in range(count)])  55.9 us
    pallas_call x2, Pallas kernels, attend_back(): pl.pallas_call(functools.partial(attend_back_kernel, chunks), grid_spec=p...  51.2 us
    pallas_call x1, Pallas kernels, hidden_units(): pl.pallas_call(hidden_kernel, grid=(rows // block,), in_specs=[pl.BlockSp...  36 us
    pallas_call x1, Pallas kernels, residual(): pl.pallas_call(functools.partial(resid_kernel, count), grid_spec=pltpu.Pr...  32.4 us
  transfers between devices with their start and end apart: 62, of which 16 were waited for; matrix products, arithmetic and copies ran while one was open for 18% of the time, Pallas kernels for 57%

profile of v3, /device:TPU:0, one launch (start us, length us, event | category | flops | bytes accessed | tf_op | source)
XLA Modules:
  0.0 745.5 jit_solution(3019990852915819163)
XLA Ops:
  15.0 72.8 %shard_map.246 = (bf16[1024,2048]{1,0:T(8,128)(2,1)}, bf16[1024,2048]{1,0:T(8,128)(2,1)}) custom-call(bf16[512,2048]{1,0:T(8,128)(2,1)} %refs_11_.1), custom_call_target="tpu_custom_call" | custom-call | bytes 12582912 | tf_op jit(solution)/shard_map/pallas_call | solution.py:892
  96.3 5.8 fusion
  102.1 11.1 %shard_map.247 = (f32[1024,128]{1,0:T(8,128)}, bf16[1024,512]{1,0:T(8,128)(2,1)}, bf16[1024,512]{1,0:T(8,128)(2,1)}, bf16[1024,512]{1,0:T(8,128)(2,1)}, f32[1024,640]{1,0:T(8,128)}) custom-call(s32[1]{0:T(128)S(6)} %select_n.55.inner_ref, bf16[1024,2048]{1,0:T(8,128)(2,1)} %get-tuple-element.225.refs_0_, f32[1,2048]{1,0:T(1,128)} %bitcast.51, ...), custom_call_target="tpu_custom_call" | custom-call | flops 2928386816 | bytes 2516582 | tf_op jit(solution)/shard_map/pallas_call | solution.py:376
  113.2 9.5 %shard_map.248 = (bf16[1024,512]{1,0:T(8,128)(2,1)}, f32[1024,512]{1,0:T(8,128)}) custom-call(bf16[1024,512]{1,0:T(8,128)(2,1)} %get-tuple-element.127.q_ref, bf16[1024,512]{1,0:T(8,128)(2,1)} %get-tuple-element.128.k_ref, bf16[1024,512]{1,0:T(8,128)(2,1)} %get-tuple-element.129.v_ref, s32[1024,1]{1,0:T(8,128)} %copy.29.segc_ref, ...), custom_call_target="tpu_custom_call" | custom-call | flops 2254857728 | bytes 6291456 | tf_op jit(solution)/shard_map/pallas_call | solution.py:225
  124.8 11.8 %shard_map.249 = (f32[1024,128]{1,0:T(8,128)}, bf16[1024,512]{1,0:T(8,128)(2,1)}, bf16[1024,512]{1,0:T(8,128)(2,1)}, bf16[1024,512]{1,0:T(8,128)(2,1)}, f32[1024,640]{1,0:T(8,128)}) custom-call(s32[1]{0:T(128)S(6)} %select_n.55.inner_ref, bf16[1024,2048]{1,0:T(8,128)(2,1)} %get-tuple-element.226.refs_0_.refs_1_, f32[1,2048]{1,0:T(1,128)} %bitcast.52, ...), custom_call_target="tpu_custom_call" | custom-call | flops 2928386816 | bytes 2516582 | tf_op jit(solution)/shard_map/pallas_call | solution.py:376
  136.6 10.0 %shard_map.250 = (bf16[1024,512]{1,0:T(8,128)(2,1)}, f32[1024,512]{1,0:T(8,128)}) custom-call(bf16[1024,512]{1,0:T(8,128)(2,1)} %get-tuple-element.133.q_ref, bf16[1024,512]{1,0:T(8,128)(2,1)} %get-tuple-element.134.k_ref, bf16[1024,512]{1,0:T(8,128)(2,1)} %get-tuple-element.135.v_ref, s32[1024,1]{1,0:T(8,128)} %copy.30.segc_ref, ...), custom_call_target="tpu_custom_call" | custom-call | flops 2254857728 | bytes 6291456 | tf_op jit(solution)/shard_map/pallas_call | solution.py:225
  151.9 21.0 %collective-permute-done.3.refs_4_ = bf16[1024,512]{1,0:T(8,128)(2,1)S(1)} collective-permute-done((bf16[1024,512]{1,0:T(8,128)(2,1)}, bf16[1024,512]{1,0:T(8,128)(2,1)S(1)}, u32[]{:S(2)}, u32[]{:S(2)}) %collective-permute-start.3) | collective-permute-done | bytes 1048608 | tf_op jit(solution)/shard_map/ppermute | solution.py:844
  175.8 8.8 %collective-permute-done.8 = bf16[512,512]{1,0:T(8,128)(2,1)S(1)} collective-permute-done((bf16[512,512]{1,0:T(8,128)(2,1)S(1)}, bf16[512,512]{1,0:T(8,128)(2,1)S(1)}, u32[]{:S(2)}, u32[]{:S(2)}) %collective-permute-start.8) | collective-permute-done | bytes 524320 | tf_op jit(solution)/shard_map/ppermute | solution.py:844
  186.3 9.6 %collective-permute-done.4 = bf16[512,512]{1,0:T(8,128)(2,1)S(1)} collective-permute-done((bf16[512,512]{1,0:T(8,128)(2,1)S(1)}, bf16[512,512]{1,0:T(8,128)(2,1)S(1)}, u32[]{:S(2)}, u32[]{:S(2)}) %collective-permute-start.4) | collective-permute-done | bytes 524320 | tf_op jit(solution)/shard_map/ppermute | solution.py:844
  198.1 9.0 %collective-permute-done.10 = bf16[512,512]{1,0:T(8,128)(2,1)S(1)} collective-permute-done((bf16[512,512]{1,0:T(8,128)(2,1)S(1)}, bf16[512,512]{1,0:T(8,128)(2,1)S(1)}, u32[]{:S(2)}, u32[]{:S(2)}) %collective-permute-start.10) | collective-permute-done | bytes 524320 | tf_op jit(solution)/shard_map/ppermute | solution.py:844
  212.3 32.4 %shard_map.251 = (bf16[2048,2048]{1,0:T(8,128)(2,1)}, f32[1,512,2048]{2,1,0:T(8,128)}) custom-call(s32[2]{0:T(128)} %pad_add_fusion.place_ref, bf16[1024,2048]{1,0:T(8,128)(2,1)} %get-tuple-element.225.refs_0_, bf16[1024,2048]{1,0:T(8,128)(2,1)} %get-tuple-element.226.refs_0_.refs_1_, bf16[1024,512]{1,0:T(8,128)(2,1)} %get-tuple-element.130.refs_2_.out_ref.refs_3_, ...), custom_call_target="tpu_custom_call" | custom-call | flops 7469508096 | bytes 6710886 | tf_op jit(solution)/shard_map/pallas_call | solution.py:667
  244.6 3.9 collective-permute-done.15
  256.7 3.2 constant_dynamic-update-slice_fusion.9
  259.9 3.2 constant_dynamic-update-slice_fusion.8
  263.0 25.3 %shard_map.252 = (bf16[2048,2048]{1,0:T(8,128)(2,1)}, bf16[2048,2048]{1,0:T(8,128)(2,1)}) custom-call(bf16[2048,2048]{1,0:T(8,128)(2,1)} %get-tuple-element.151.x_ref, bf16[2048,3072]{1,0:T(8,128)(2,1)} %all-gather.6.cloned.1.call-done.w_ref.refs_2_), custom_call_target="tpu_custom_call" | custom-call | flops 5453926912 | bytes 5033164 | tf_op jit(solution)/shard_map/pallas_call | solution.py:525
  289.3 2.3 constant_dynamic-update-slice_fusion.6.dy_ref
  291.7 15.2 %shard_map.253.refs_0_ = bf16[2048,2048]{1,0:T(8,128)(2,1)} custom-call(bf16[2048,2048]{1,0:T(8,128)(2,1)} %constant_dynamic-update-slice_fusion.6.dy_ref, bf16[2048,2048]{1,0:T(8,128)(2,1)} %get-tuple-element.147.factors_ref, bf16[2048,3072]{1,0:T(8,128)(2,1)} %all-gather.6.cloned.1.call-done.w_ref.refs_2_), custom_call_target="tpu_custom_call" | custom-call | flops 2726963456 | bytes 5033164 | tf_op jit(solution)/shard_map/pallas_call | solution.py:557
  306.9 23.8 %convolution_convert_fusion.2 = bf16[2048,2048]{1,0:T(8,128)(2,1)} fusion(bf16[2048,2048]{1,0:T(8,128)(2,1)} %get-tuple-element.151.x_ref, bf16[2048,2048]{1,0:T(8,128)(2,1)} %shard_map.253.refs_0_), kind=kOutput, calls=%fused_computation.2 | convolution fusion | flops 17184063488 | bytes 25165824 | tf_op jit(solution)/shard_map/dot_general | solution.py:38
  330.7 2.7 constant_dynamic-slice_fusion
  335.5 36.0 %shard_map.254 = (bf16[2048,2048]{1,0:T(8,128)(2,1)}, bf16[2048,2048]{1,0:T(8,128)(2,1)}) custom-call(bf16[2048,2048]{1,0:T(8,128)(2,1)} %get-tuple-element.151.x_ref, bf16[2048,2048]{1,0:T(8,128)(2,1)} %constant_dynamic-update-slice_fusion.6.dy_ref, bf16[2048,3072]{1,0:T(8,128)(2,1)} %all-gather.8.cloned.1.call-done.w_ref.refs_3_, ...), custom_call_target="tpu_custom_call", output_to_operand_aliasing={{0}: (3, {})} | custom-call | flops 8180890112 | bytes 7549747 | tf_op jit(solution)/shard_map/pallas_call | solution.py:486
  375.5 23.9 %convolution_convert_fusion.1 = bf16[2048,2048]{1,0:T(8,128)(2,1)} fusion(bf16[2048,2048]{1,0:T(8,128)(2,1)} %get-tuple-element.151.x_ref, bf16[2048,2048]{1,0:T(8,128)(2,1)} %get-tuple-element.152.refs_1_), kind=kOutput, calls=%fused_computation.1 | convolution fusion | flops 17184063488 | bytes 25165824 | tf_op jit(solution)/shard_map/dot_general | solution.py:38
  399.4 24.1 %shard_map.255 = (f32[256,2048]{1,0:T(8,128)}, bf16[256,2048]{1,0:T(8,128)(2,1)}, bf16[256,2048]{1,0:T(8,128)(2,1)}, bf16[256,2048]{1,0:T(8,128)(2,1)}) custom-call(bf16[2048,2048]{1,0:T(8,128)(2,1)} %shard_map.253.refs_0_, bf16[2048,2048]{1,0:T(8,128)(2,1)} %get-tuple-element.152.refs_1_, bf16[2048,3072]{1,0:T(8,128)(2,1)} %all-gather.6.cloned.1.call-done.w_ref.refs_2_, ...), custom_call_target="tpu_custom_call" | custom-call | flops 844219584 | bytes 209715 | tf_op jit(solution)/shard_map/pallas_call | solution.py:608
  425.7 15.7 %shard_map.256 = (bf16[256,2048]{1,0:T(8,128)(2,1)}, f32[256,2048]{1,0:T(8,128)}) custom-call(bf16[2048,2048]{1,0:T(8,128)(2,1)} %shard_map.253.refs_0_, bf16[2048,2048]{1,0:T(8,128)(2,1)} %get-tuple-element.152.refs_1_, bf16[2048,3072]{1,0:T(8,128)(2,1)} %all-gather.6.cloned.1.call-done.w_ref.refs_2_, ...), custom_call_target="tpu_custom_call" | custom-call | flops 422109792 | bytes 104857 | tf_op jit(solution)/shard_map/pallas_call | solution.py:608
  442.9 15.5 %shard_map.257 = (f32[256,2048]{1,0:T(8,128)}, f32[256,2048]{1,0:T(8,128)}) custom-call(bf16[2048,2048]{1,0:T(8,128)(2,1)} %shard_map.253.refs_0_, bf16[2048,2048]{1,0:T(8,128)(2,1)} %get-tuple-element.152.refs_1_, bf16[2048,3072]{1,0:T(8,128)(2,1)} %all-gather.6.cloned.1.call-done.w_ref.refs_2_, bf16[2048,3072]{1,0:T(8,128)(2,1)} %all-gather.8.cloned.1.call-done.w_ref.refs_3_), custom_call_target="tpu_custom_call" | custom-call | flops 422109792 | bytes 104857 | tf_op jit(solution)/shard_map/pallas_call | solution.py:608
  459.5 2.5 add_convert_fusion.2
  463.1 2.6 add_convert_fusion.3
  466.2 24.1 %shard_map.258 = (f32[256,2048]{1,0:T(8,128)}, f32[256,2048]{1,0:T(8,128)}, bf16[256,2048]{1,0:T(8,128)(2,1)}, f32[256,2048]{1,0:T(8,128)}, f32[256,2048]{1,0:T(...) custom-call(bf16[2048,2048]{1,0:T(8,128)(2,1)} %get-tuple-element.162.refs_0_.refs_1_, ...), custom_call_target="tpu_custom_call" | custom-call | flops 844219584 | bytes 209715 | tf_op jit(solution)/shard_map/pallas_call | solution.py:608
  492.9 14.4 %collective-permute-done.28.refs_2_ = bf16[256,2048]{1,0:T(8,128)(2,1)S(1)} collective-permute-done((bf16[256,2048]{1,0:T(8,128)(2,1)}, bf16[256,2048]{1,0:T(8,128)(2,1)S(1)}, u32[]{:S(2)}, u32[]{:S(2)}) %collective-permute-start.28) | collective-permute-done | bytes 1048608 | tf_op jit(solution)/shard_map/ppermute | solution.py:844
  508.2 9.5 %shard_map.259 = (f32[2,256,2048]{2,1,0:T(8,128)}, bf16[2,256,2048]{2,1,0:T(8,128)(2,1)}, f32[8,2048]{1,0:T(8,128)}) custom-call(f32[256,2048]{1,0:T(8,128)} %get-tuple-element.173.refs_0_, bf16[256,2048]{1,0:T(8,128)(2,1)} %copy-done.31, bf16[256,2048]{1,0:T(8,128)(2,1)} %copy-done.34, f32[256,2048]{1,0:T(8,128)} %get-tuple-element.176.refs_3_, ...), custom_call_target="tpu_custom_call" | custom-call | flops 1048576 | bytes 1048576 | tf_op jit(solution)/shard_map/pallas_call | solution.py:981
  517.7 9.3 %shard_map.260 = (bf16[512,512]{1,0:T(8,128)(2,1)}, bf16[512,512]{1,0:T(8,128)(2,1)}, bf16[512,512]{1,0:T(8,128)(2,1)}, bf16[512,512]{1,0:T(8,128)(2,1)}) custom-call(s32[1]{0:T(128)S(6)} %select_n.56.core_ref, bf16[512,2048]{1,0:T(8,128)(2,1)} %bitcast.43, bf16[2048,1280]{1,0:T(8,128)(2,1)} %all-gather.4.cloned.1.call-done.refs_2_.refs_10_.refs_0_.refs_4_, ...), custom_call_target="tpu_custom_call" | custom-call | flops 321720384 | bytes 209715 | tf_op jit(solution)/shard_map/pallas_call | solution.py:428
  530.5 2.3 collective-permute-done.25
  532.8 23.9 %convolution_convert_fusion = bf16[2048,2048]{1,0:T(8,128)(2,1)} fusion(bf16[2048,2048]{1,0:T(8,128)(2,1)} %constant_dynamic-update-slice_fusion.6.dy_ref, bf16[2048,2048]{1,0:T(8,128)(2,1)} %get-tuple-element.162.refs_0_.refs_1_), kind=kOutput, calls=%fused_computation | convolution fusion | flops 17184063488 | bytes 25165824 | tf_op jit(solution)/shard_map/dot_general | solution.py:38
  559.9 2.7 collective-permute-start.36
  563.4 25.8 %shard_map.261 = (bf16[512,768]{1,0:T(8,128)(2,1)}, bf16[512,768]{1,0:T(8,128)(2,1)}, f32[8,128]{1,0:T(8,128)}, f32[8,128]{1,0:T(8,128)}) custom-call(s32[1]{0:T(128)S(6)} %select_n.55.inner_ref, bf16[1024,512]{1,0:T(8,128)(2,1)} %get-tuple-element.127.q_ref, bf16[1024,512]{1,0:T(8,128)(2,1)} %get-tuple-element.128.k_ref, ...), custom_call_target="tpu_custom_call" | custom-call | flops 5905580032 | bytes 10485760 | tf_op jit(solution)/shard_map/pallas_call | solution.py:258
  590.7 25.4 %shard_map.262 = (bf16[512,768]{1,0:T(8,128)(2,1)}, bf16[512,768]{1,0:T(8,128)(2,1)}, f32[8,128]{1,0:T(8,128)}, f32[8,128]{1,0:T(8,128)}) custom-call(s32[1]{0:T(128)S(6)} %select_n.55.inner_ref, bf16[1024,512]{1,0:T(8,128)(2,1)} %get-tuple-element.133.q_ref, bf16[1024,512]{1,0:T(8,128)(2,1)} %get-tuple-element.134.k_ref, ...), custom_call_target="tpu_custom_call" | custom-call | flops 5905580032 | bytes 10485760 | tf_op jit(solution)/shard_map/pallas_call | solution.py:258
  622.3 13.0 %shard_map.265 = bf16[2048,768]{1,0:T(8,128)(2,1)} custom-call(f32[1,2048]{1,0:T(1,128)} %bitcast.53, bf16[1024,2048]{1,0:T(8,128)(2,1)} %get-tuple-element.225.refs_0_, bf16[1024,2048]{1,0:T(8,128)(2,1)} %get-tuple-element.226.refs_0_.refs_1_, f32[1024,128]{1,0:T(8,128)} %get-tuple-element.227.refs_2_, f32[1024,128]{1,0:T(8,128)} %get-tuple-element.228.refs_3_, ...), custom_call_target="tpu_custom_call" | custom-call | flops 2996488704 | bytes 1677721 | tf_op jit(solution)/shard_map/pallas_call | solution.py:829
  635.3 7.3 collective-permute-done.53.refs_6_
  642.6 10.7 %shard_map.266 = bf16[2048,512]{1,0:T(8,128)(2,1)} custom-call(s32[1]{0:T(128)S(6)} %select_n.55.inner_ref, bf16[512,2048]{1,0:T(8,128)(2,1)} %bitcast.44, bf16[256,2048]{1,0:T(8,128)(2,1)} %copy-done.30, bf16[256,2048]{1,0:T(8,128)(2,1)} %collective-permute-done.51.refs_2_, bf16[1024,512]{1,0:T(8,128)(2,1)} %get-tuple-element.130.refs_2_.out_ref.refs_3_, ...), custom_call_target="tpu_custom_call" | custom-call | flops 2454267136 | bytes 1677721 | tf_op jit(solution)/shard_map/pallas_call | solution.py:795
  653.3 4.3 pad_maximum_fusion
  657.6 3.5 collective-permute-done.39.refs_3_
  673.9 20.0 %shard_map.263 = (f32[512,2048]{1,0:T(8,128)}, f32[8,2048]{1,0:T(8,128)}) custom-call(s32[1]{0:T(128)S(6)} %select_n.56.core_ref, bf16[512,768]{1,0:T(8,128)(2,1)} %get-tuple-element.199.refs_0_.refs_4_, bf16[512,768]{1,0:T(8,128)(2,1)} %collective-permute-done.35.refs_1_, bf16[512,768]{1,0:T(8,128)(2,1)} %collective-permute-done.38.refs_2_, ...), custom_call_target="tpu_custom_call" | custom-call | flops 4601750528 | bytes 4194304 | tf_op jit(solution)/shard_map/pallas_call | solution.py:743
  695.9 2.5 add_convert_fusion.1
  703.1 2.8 collective-permute-done.47
  705.9 2.4 collective-permute-start.48
  708.3 3.3 collective-permute-done.48
  713.0 8.1 %collective-permute-done.49 = f32[33,128]{1,0:T(8,128)S(1)} collective-permute-done((f32[33,128]{1,0:T(8,128)S(1)}, f32[33,128]{1,0:T(8,128)S(1)}, u32[]{:S(2)}, u32[]{:S(2)}) %collective-permute-start.49) | collective-permute-done | bytes 16928 | tf_op jit(solution)/shard_map/ppermute | solution.py:844
  721.8 3.0 collective-permute-done.50
  728.1 6.4 shard_map.264
  (284 shorter events, 103.7 us)
Async XLA Ops:
  7.2 81.5 %all-gather.4.cloned.1.call-start = ((), (), s32[]{:S(2)}) async-start(), calls=%async_computation.4 | async-start | bytes 5898240 | tf_op jit(solution)/shard_map/all_gather | solution.py:1034
  9.3 253.7 %all-gather.6.cloned.1.call-start = ((), (), s32[]{:S(2)}) async-start(), calls=%async_computation.5 | async-start | bytes 14155776 | tf_op jit(solution)/shard_map/all_gather | solution.py:1034
  13.3 322.2 %all-gather.8.cloned.1.call-start = ((), (), s32[]{:S(2)}) async-start(), calls=%async_computation.6 | async-start | bytes 14155776 | tf_op jit(solution)/shard_map/all_gather | solution.py:1034
  14.6 408.8 %reduce-scatter.5.cloned.1.call-start = ((), (), s32[]{:S(2)}) async-start(), calls=%async_computation.7 | async-start | bytes 9437184 | tf_op jit(solution)/shard_map/reduce_scatter | solution.py:1038
  91.0 33.8 %collective-permute-start.1 = (bf16[1024,512]{1,0:T(8,128)(2,1)}, bf16[1024,512]{1,0:T(8,128)(2,1)S(1)}, u32[]{:S(2)}, u32[]{:S(2)}) collective-permute-start(bf16[1024,512]{1,0:T(8,128)(2,1)} %constant_dynamic-slice_fusion.1), channel_id=1, source_target_pairs={{0,1},{1,0},{2,3},{3,2},{4,5},{5,4},{6,7},{7,6},{8,9},{9,8},{10,11... | collective-permute-start | bytes 3145736 | tf_op jit(solution)/shard_map/ppermute | solution.py:844
  91.5 33.2 %collective-permute-start.2 = (bf16[1024,512]{1,0:T(8,128)(2,1)}, bf16[1024,512]{1,0:T(8,128)(2,1)S(1)}, u32[]{:S(2)}, u32[]{:S(2)}) collective-permute-start(bf16[1024,512]{1,0:T(8,128)(2,1)} %constant_dynamic-slice_fusion.1), channel_id=1, source_target_pairs={{0,2},{1,3},{2,0},{3,1},{4,6},{5,7},{6,4},{7,5},{8,10},{9,11},{10,... | collective-permute-start | bytes 3145736 | tf_op jit(solution)/shard_map/ppermute | solution.py:844
  122.7 25.9 %collective-permute-start.7 = (bf16[1024,512]{1,0:T(8,128)(2,1)}, bf16[1024,512]{1,0:T(8,128)(2,1)S(1)}, u32[]{:S(2)}, u32[]{:S(2)}) collective-permute-start(bf16[1024,512]{1,0:T(8,128)(2,1)} %get-tuple-element.130.refs_2_.out_ref.refs_3_), channel_id=1, source_target_pairs={{0,2},{1,3},{2,0},{3,1},{4,6},{5,7},{6,4},{7,5},{8,10},{9,11},{10,... | collective-permute-start | bytes 3145736 | tf_op jit(solution)/shard_map/ppermute | solution.py:844
  123.2 26.0 %collective-permute-start = (bf16[1024,512]{1,0:T(8,128)(2,1)}, bf16[1024,512]{1,0:T(8,128)(2,1)}, u32[]{:S(2)}, u32[]{:S(2)}) collective-permute-start(bf16[1024,512]{1,0:T(8,128)(2,1)} %get-tuple-element.130.refs_2_.out_ref.refs_3_), channel_id=1, source_target_pairs={{0,1},{1,0},{2,3},{3,2},{4,5},{5,4},{6,7},{7,6},{8,9},{9,8},{10,11... | collective-permute-start | bytes 3145736 | tf_op jit(solution)/shard_map/ppermute | solution.py:844
  146.6 26.4 %collective-permute-start.3 = (bf16[1024,512]{1,0:T(8,128)(2,1)}, bf16[1024,512]{1,0:T(8,128)(2,1)S(1)}, u32[]{:S(2)}, u32[]{:S(2)}) collective-permute-start(bf16[1024,512]{1,0:T(8,128)(2,1)} %get-tuple-element.136.refs_6_.out_ref.refs_8_), channel_id=1, source_target_pairs={{0,2},{1,3},{2,0},{3,1},{4,6},{5,7},{6,4},{7,5},{8,10},{9,11},{10,... | collective-permute-start | bytes 3145736 | tf_op jit(solution)/shard_map/ppermute | solution.py:844
  147.1 26.4 %collective-permute-start.5 = (bf16[1024,512]{1,0:T(8,128)(2,1)}, bf16[1024,512]{1,0:T(8,128)(2,1)S(1)}, u32[]{:S(2)}, u32[]{:S(2)}) collective-permute-start(bf16[1024,512]{1,0:T(8,128)(2,1)} %get-tuple-element.136.refs_6_.out_ref.refs_8_), channel_id=1, source_target_pairs={{0,1},{1,0},{2,3},{3,2},{4,5},{5,4},{6,7},{7,6},{8,9},{9,8},{10,11... | collective-permute-start | bytes 3145736 | tf_op jit(solution)/shard_map/ppermute | solution.py:844
  148.6 36.0 %collective-permute-start.8 = (bf16[512,512]{1,0:T(8,128)(2,1)S(1)}, bf16[512,512]{1,0:T(8,128)(2,1)S(1)}, u32[]{:S(2)}, u32[]{:S(2)}) collective-permute-start(bf16[512,512]{1,0:T(8,128)(2,1)S(1)} %slice.150), channel_id=1, source_target_pairs={{0,1},{1,0},{2,3},{3,2},{4,5},{5,4},{6,7},{7,6},{8,9},{9,8},{10,11... | collective-permute-start | bytes 1572872 | tf_op jit(solution)/shard_map/ppermute | solution.py:844
  150.3 35.9 %collective-permute-start.9 = (bf16[512,512]{1,0:T(8,128)(2,1)S(1)}, bf16[512,512]{1,0:T(8,128)(2,1)S(1)}, u32[]{:S(2)}, u32[]{:S(2)}) collective-permute-start(bf16[512,512]{1,0:T(8,128)(2,1)S(1)} %slice.151), channel_id=1, source_target_pairs={{0,2},{1,3},{2,0},{3,1},{4,6},{5,7},{6,4},{7,5},{8,10},{9,11},{10,... | collective-permute-start | bytes 1572872 | tf_op jit(solution)/shard_map/ppermute | solution.py:844
  175.2 32.0 %collective-permute-start.10 = (bf16[512,512]{1,0:T(8,128)(2,1)S(1)}, bf16[512,512]{1,0:T(8,128)(2,1)S(1)}, u32[]{:S(2)}, u32[]{:S(2)}) collective-permute-start(bf16[512,512]{1,0:T(8,128)(2,1)S(1)} %slice.116), channel_id=1, source_target_pairs={{0,1},{1,0},{2,3},{3,2},{4,5},{5,4},{6,7},{7,6},{8,9},{9,8},{10,11... | collective-permute-start | bytes 1572872 | tf_op jit(solution)/shard_map/ppermute | solution.py:844
  196.0 52.5 %collective-permute-start.15 = (bf16[512,2048]{1,0:T(8,128)(2,1)S(1)}, bf16[512,2048]{1,0:T(8,128)(2,1)}, u32[]{:S(2)}, u32[]{:S(2)}) collective-permute-start(bf16[512,2048]{1,0:T(8,128)(2,1)S(1)} %copy-done.2), channel_id=1, source_target_pairs={{0,1},{1,0},{2,3},{3,2},{4,5},{5,4},{6,7},{7,6},{8,9},{9,8},{10,11... | collective-permute-start | bytes 6291464 | tf_op jit(solution)/shard_map/ppermute | solution.py:844
  197.5 51.0 %collective-permute-start.16 = (bf16[512,2048]{1,0:T(8,128)(2,1)S(1)}, bf16[512,2048]{1,0:T(8,128)(2,1)}, u32[]{:S(2)}, u32[]{:S(2)}) collective-permute-start(bf16[512,2048]{1,0:T(8,128)(2,1)S(1)} %copy-done.2), channel_id=1, source_target_pairs={{0,2},{1,3},{2,0},{3,1},{4,6},{5,7},{6,4},{7,5},{8,10},{9,11},{10,... | collective-permute-start | bytes 6291464 | tf_op jit(solution)/shard_map/ppermute | solution.py:844
  250.8 37.5 %collective-permute-start.17 = (bf16[256,2048]{1,0:T(8,128)(2,1)}, bf16[256,2048]{1,0:T(8,128)(2,1)S(1)}, u32[]{:S(2)}, u32[]{:S(2)}) collective-permute-start(bf16[256,2048]{1,0:T(8,128)(2,1)} %slice.118), channel_id=1, source_target_pairs={{0,1},{1,0},{2,3},{3,2},{4,5},{5,4},{6,7},{7,6},{8,9},{9,8},{10,11... | collective-permute-start | bytes 3145736 | tf_op jit(solution)/shard_map/ppermute | solution.py:844
  254.7 33.6 %collective-permute-start.18 = (bf16[256,2048]{1,0:T(8,128)(2,1)}, bf16[256,2048]{1,0:T(8,128)(2,1)}, u32[]{:S(2)}, u32[]{:S(2)}) collective-permute-start(bf16[256,2048]{1,0:T(8,128)(2,1)} %slice.119), channel_id=1, source_target_pairs={{0,2},{1,3},{2,0},{3,1},{4,6},{5,7},{6,4},{7,5},{8,10},{9,11},{10,... | collective-permute-start | bytes 3145736 | tf_op jit(solution)/shard_map/ppermute | solution.py:844
  330.7 202.2 %reduce-scatter.7.cloned.1.call-start = ((), (), s32[]{:S(2)}) async-start(), calls=%async_computation.8 | async-start | bytes 9437184 | tf_op jit(solution)/shard_map/reduce_scatter | solution.py:1038
  333.4 38.2 %collective-permute-start.19 = (bf16[1024,768]{1,0:T(8,128)(2,1)}, bf16[1024,768]{1,0:T(8,128)(2,1)S(1)}, u32[]{:S(2)}, u32[]{:S(2)}) collective-permute-start(bf16[1024,768]{1,0:T(8,128)(2,1)} %constant_dynamic-slice_fusion), channel_id=1, source_target_pairs={{0,1},{1,0},{2,3},{3,2},{4,5},{5,4},{6,7},{7,6},{8,9},{9,8},{10,11... | collective-permute-start | bytes 4718600 | tf_op jit(solution)/shard_map/ppermute | solution.py:844
  334.9 36.7 %collective-permute-start.20 = (bf16[1024,768]{1,0:T(8,128)(2,1)}, bf16[1024,768]{1,0:T(8,128)(2,1)S(1)}, u32[]{:S(2)}, u32[]{:S(2)}) collective-permute-start(bf16[1024,768]{1,0:T(8,128)(2,1)} %constant_dynamic-slice_fusion), channel_id=1, source_target_pairs={{0,2},{1,3},{2,0},{3,1},{4,6},{5,7},{6,4},{7,5},{8,10},{9,11},{10,... | collective-permute-start | bytes 4718600 | tf_op jit(solution)/shard_map/ppermute | solution.py:844
  372.6 26.8 %collective-permute-start.21 = (bf16[512,768]{1,0:T(8,128)(2,1)}, bf16[512,768]{1,0:T(8,128)(2,1)}, u32[]{:S(2)}, u32[]{:S(2)}) collective-permute-start(bf16[512,768]{1,0:T(8,128)(2,1)} %slice.152), channel_id=1, source_target_pairs={{0,1},{1,0},{2,3},{3,2},{4,5},{5,4},{6,7},{7,6},{8,9},{9,8},{10,11... | collective-permute-start | bytes 2359304 | tf_op jit(solution)/shard_map/ppermute | solution.py:844
  375.0 24.4 %collective-permute-start.22 = (bf16[512,768]{1,0:T(8,128)(2,1)}, bf16[512,768]{1,0:T(8,128)(2,1)}, u32[]{:S(2)}, u32[]{:S(2)}) collective-permute-start(bf16[512,768]{1,0:T(8,128)(2,1)} %slice.153), channel_id=1, source_target_pairs={{0,2},{1,3},{2,0},{3,1},{4,6},{5,7},{6,4},{7,5},{8,10},{9,11},{10,... | collective-permute-start | bytes 2359304 | tf_op jit(solution)/shard_map/ppermute | solution.py:844
  423.5 237.7 %reduce-scatter.9.cloned.1.call-start = ((), (), s32[]{:S(2)}) async-start(), calls=%async_computation.9 | async-start | bytes 9437184 | tf_op jit(solution)/shard_map/reduce_scatter | solution.py:1038
  423.5 35.9 %collective-permute-start.29 = (bf16[256,2048]{1,0:T(8,128)(2,1)}, bf16[256,2048]{1,0:T(8,128)(2,1)}, u32[]{:S(2)}, u32[]{:S(2)}) collective-permute-start(bf16[256,2048]{1,0:T(8,128)(2,1)} %get-tuple-element.155), channel_id=1, source_target_pairs={{0,2},{1,3},{2,0},{3,1},{4,6},{5,7},{6,4},{7,5},{8,10},{9,11},{10,... | collective-permute-start | bytes 3145736 | tf_op jit(solution)/shard_map/ppermute | solution.py:844
  425.1 37.9 %collective-permute-start.27 = (bf16[256,2048]{1,0:T(8,128)(2,1)}, bf16[256,2048]{1,0:T(8,128)(2,1)}, u32[]{:S(2)}, u32[]{:S(2)}) collective-permute-start(bf16[256,2048]{1,0:T(8,128)(2,1)} %get-tuple-element.154), channel_id=1, source_target_pairs={{0,1},{1,0},{2,3},{3,2},{4,5},{5,4},{6,7},{7,6},{8,9},{9,8},{10,11... | collective-permute-start | bytes 3145736 | tf_op jit(solution)/shard_map/ppermute | solution.py:844
  441.4 50.4 %collective-permute-start.26 = (bf16[256,2048]{1,0:T(8,128)(2,1)}, bf16[256,2048]{1,0:T(8,128)(2,1)S(1)}, u32[]{:S(2)}, u32[]{:S(2)}) collective-permute-start(bf16[256,2048]{1,0:T(8,128)(2,1)} %get-tuple-element.157), channel_id=1, source_target_pairs={{0,1},{1,0},{2,3},{3,2},{4,5},{5,4},{6,7},{7,6},{8,9},{9,8},{10,11... | collective-permute-start | bytes 3145736 | tf_op jit(solution)/shard_map/ppermute | solution.py:844
  458.5 34.4 %collective-permute-start.31 = (bf16[256,2048]{1,0:T(8,128)(2,1)}, bf16[256,2048]{1,0:T(8,128)(2,1)}, u32[]{:S(2)}, u32[]{:S(2)}) collective-permute-start(bf16[256,2048]{1,0:T(8,128)(2,1)} %get-tuple-element.171), channel_id=1, source_target_pairs={{0,2},{1,3},{2,0},{3,1},{4,6},{5,7},{6,4},{7,5},{8,10},{9,11},{10,... | collective-permute-start | bytes 3145736 | tf_op jit(solution)/shard_map/ppermute | solution.py:844
  462.0 30.8 %collective-permute-start.30 = (bf16[256,2048]{1,0:T(8,128)(2,1)}, bf16[256,2048]{1,0:T(8,128)(2,1)S(1)}, u32[]{:S(2)}, u32[]{:S(2)}) collective-permute-start(bf16[256,2048]{1,0:T(8,128)(2,1)} %add_convert_fusion.2), channel_id=1, source_target_pairs={{0,1},{1,0},{2,3},{3,2},{4,5},{5,4},{6,7},{7,6},{8,9},{9,8},{10,11... | collective-permute-start | bytes 3145736 | tf_op jit(solution)/shard_map/ppermute | solution.py:844
  465.6 41.6 %collective-permute-start.28 = (bf16[256,2048]{1,0:T(8,128)(2,1)}, bf16[256,2048]{1,0:T(8,128)(2,1)S(1)}, u32[]{:S(2)}, u32[]{:S(2)}) collective-permute-start(bf16[256,2048]{1,0:T(8,128)(2,1)} %add_convert_fusion.3), channel_id=1, source_target_pairs={{0,2},{1,3},{2,0},{3,1},{4,6},{5,7},{6,4},{7,5},{8,10},{9,11},{10,... | collective-permute-start | bytes 3145736 | tf_op jit(solution)/shard_map/ppermute | solution.py:844
  490.4 40.1 %collective-permute-start.24 = (bf16[256,2048]{1,0:T(8,128)(2,1)}, bf16[256,2048]{1,0:T(8,128)(2,1)}, u32[]{:S(2)}, u32[]{:S(2)}) collective-permute-start(bf16[256,2048]{1,0:T(8,128)(2,1)} %get-tuple-element.166), channel_id=1, source_target_pairs={{0,1},{1,0},{2,3},{3,2},{4,5},{5,4},{6,7},{7,6},{8,9},{9,8},{10,11... | collective-permute-start | bytes 3145736 | tf_op jit(solution)/shard_map/ppermute | solution.py:844
  491.8 41.0 %collective-permute-start.25 = (bf16[256,2048]{1,0:T(8,128)(2,1)}, bf16[256,2048]{1,0:T(8,128)(2,1)}, u32[]{:S(2)}, u32[]{:S(2)}) collective-permute-start(bf16[256,2048]{1,0:T(8,128)(2,1)} %get-tuple-element.167), channel_id=1, source_target_pairs={{0,2},{1,3},{2,0},{3,1},{4,6},{5,7},{6,4},{7,5},{8,10},{9,11},{10,... | collective-permute-start | bytes 3145736 | tf_op jit(solution)/shard_map/ppermute | solution.py:844
  527.0 29.7 %collective-permute-start.32 = (bf16[512,512]{1,0:T(8,128)(2,1)}, bf16[512,512]{1,0:T(8,128)(2,1)}, u32[]{:S(2)}, u32[]{:S(2)}) collective-permute-start(bf16[512,512]{1,0:T(8,128)(2,1)} %get-tuple-element.182), channel_id=1, source_target_pairs={{0,1},{1,0},{2,3},{3,2},{4,5},{5,4},{6,7},{7,6},{8,9},{9,8},{10,11... | collective-permute-start | bytes 1572872 | tf_op jit(solution)/shard_map/ppermute | solution.py:844
  527.7 29.1 %collective-permute-start.33 = (bf16[512,512]{1,0:T(8,128)(2,1)}, bf16[512,512]{1,0:T(8,128)(2,1)S(1)}, u32[]{:S(2)}, u32[]{:S(2)}) collective-permute-start(bf16[512,512]{1,0:T(8,128)(2,1)} %get-tuple-element.183), channel_id=1, source_target_pairs={{0,2},{1,3},{2,0},{3,1},{4,6},{5,7},{6,4},{7,5},{8,10},{9,11},{10,... | collective-permute-start | bytes 1572872 | tf_op jit(solution)/shard_map/ppermute | solution.py:844
  529.2 27.6 %collective-permute-start.34 = (bf16[512,512]{1,0:T(8,128)(2,1)}, bf16[512,512]{1,0:T(8,128)(2,1)S(1)}, u32[]{:S(2)}, u32[]{:S(2)}) collective-permute-start(bf16[512,512]{1,0:T(8,128)(2,1)} %get-tuple-element.184), channel_id=1, source_target_pairs={{0,3},{1,2},{2,1},{3,0},{4,7},{5,6},{6,5},{7,4},{8,11},{9,10},{10,... | collective-permute-start | bytes 1572872 | tf_op jit(solution)/shard_map/ppermute | solution.py:844
  557.8 176.6 %reduce-scatter.11.cloned.1.call-start = ((), (), s32[]{:S(2)}) async-start(), calls=%async_computation.10 | async-start | bytes 5898240 | tf_op jit(solution)/shard_map/reduce_scatter | solution.py:1038
  559.9 29.3 %collective-permute-start.36 = (bf16[256,2048]{1,0:T(8,128)(2,1)}, bf16[256,2048]{1,0:T(8,128)(2,1)S(1)}, u32[]{:S(2)}, u32[]{:S(2)}) collective-permute-start(bf16[256,2048]{1,0:T(8,128)(2,1)} %get-tuple-element.193), channel_id=1, source_target_pairs={{0,1},{1,0},{2,3},{3,2},{4,5},{5,4},{6,7},{7,6},{8,9},{9,8},{10,11... | collective-permute-start | bytes 3145736 | tf_op jit(solution)/shard_map/ppermute | solution.py:844
  562.6 26.6 %collective-permute-start.37 = (bf16[256,2048]{1,0:T(8,128)(2,1)}, bf16[256,2048]{1,0:T(8,128)(2,1)}, u32[]{:S(2)}, u32[]{:S(2)}) collective-permute-start(bf16[256,2048]{1,0:T(8,128)(2,1)} %get-tuple-element.193), channel_id=1, source_target_pairs={{0,2},{1,3},{2,0},{3,1},{4,6},{5,7},{6,4},{7,5},{8,10},{9,11},{10,... | collective-permute-start | bytes 3145736 | tf_op jit(solution)/shard_map/ppermute | solution.py:844
  589.2 26.9 %collective-permute-start.51 = (bf16[256,2048]{1,0:T(8,128)(2,1)S(1)}, bf16[256,2048]{1,0:T(8,128)(2,1)}, u32[]{:S(2)}, u32[]{:S(2)}) collective-permute-start(bf16[256,2048]{1,0:T(8,128)(2,1)S(1)} %get-tuple-element.222), channel_id=1, source_target_pairs={{0,1},{1,0},{2,3},{3,2},{4,5},{5,4},{6,7},{7,6},{8,9},{9,8},{10,11... | collective-permute-start | bytes 3145736 | tf_op jit(solution)/shard_map/ppermute | solution.py:844
  589.3 26.8 %collective-permute-start.52 = (bf16[256,2048]{1,0:T(8,128)(2,1)S(1)}, bf16[256,2048]{1,0:T(8,128)(2,1)S(1)}, u32[]{:S(2)}, u32[]{:S(2)}) collective-permute-start(bf16[256,2048]{1,0:T(8,128)(2,1)S(1)} %get-tuple-element.222), channel_id=1, source_target_pairs={{0,2},{1,3},{2,0},{3,1},{4,6},{5,7},{6,4},{7,5},{8,10},{9,11},{10,... | collective-permute-start | bytes 3145736 | tf_op jit(solution)/shard_map/ppermute | solution.py:844
  616.1 26.5 %collective-permute-start.53 = (bf16[256,2048]{1,0:T(8,128)(2,1)}, bf16[256,2048]{1,0:T(8,128)(2,1)}, u32[]{:S(2)}, u32[]{:S(2)}) collective-permute-start(bf16[256,2048]{1,0:T(8,128)(2,1)} %collective-permute-done.37.refs_4_), channel_id=1, source_target_pairs={{0,1},{1,0},{2,3},{3,2},{4,5},{5,4},{6,7},{7,6},{8,9},{9,8},{10,11... | collective-permute-start | bytes 3145736 | tf_op jit(solution)/shard_map/ppermute | solution.py:844
  618.1 24.5 %collective-permute-start.54 = (bf16[256,2048]{1,0:T(8,128)(2,1)}, bf16[256,2048]{1,0:T(8,128)(2,1)}, u32[]{:S(2)}, u32[]{:S(2)}) collective-permute-start(bf16[256,2048]{1,0:T(8,128)(2,1)} %collective-permute-done.51.refs_2_), channel_id=1, source_target_pairs={{0,2},{1,3},{2,0},{3,1},{4,6},{5,7},{6,4},{7,5},{8,10},{9,11},{10,... | collective-permute-start | bytes 3145736 | tf_op jit(solution)/shard_map/ppermute | solution.py:844
  618.8 38.8 %collective-permute-start.35 = (bf16[512,768]{1,0:T(8,128)(2,1)}, bf16[512,768]{1,0:T(8,128)(2,1)}, u32[]{:S(2)}, u32[]{:S(2)}) collective-permute-start(bf16[512,768]{1,0:T(8,128)(2,1)} %get-tuple-element.190.refs_5_), channel_id=1, source_target_pairs={{0,1},{1,0},{2,3},{3,2},{4,5},{5,4},{6,7},{7,6},{8,9},{9,8},{10,11... | collective-permute-start | bytes 2359304 | tf_op jit(solution)/shard_map/ppermute | solution.py:844
  618.9 38.7 %collective-permute-start.38 = (bf16[512,768]{1,0:T(8,128)(2,1)}, bf16[512,768]{1,0:T(8,128)(2,1)}, u32[]{:S(2)}, u32[]{:S(2)}) collective-permute-start(bf16[512,768]{1,0:T(8,128)(2,1)} %get-tuple-element.196.refs_6_), channel_id=1, source_target_pairs={{0,2},{1,3},{2,0},{3,1},{4,6},{5,7},{6,4},{7,5},{8,10},{9,11},{10,... | collective-permute-start | bytes 2359304 | tf_op jit(solution)/shard_map/ppermute | solution.py:844
  620.2 40.9 %collective-permute-start.39 = (bf16[512,768]{1,0:T(8,128)(2,1)}, bf16[512,768]{1,0:T(8,128)(2,1)}, u32[]{:S(2)}, u32[]{:S(2)}) collective-permute-start(bf16[512,768]{1,0:T(8,128)(2,1)} %get-tuple-element.197.refs_7_), channel_id=1, source_target_pairs={{0,3},{1,2},{2,1},{3,0},{4,7},{5,6},{6,5},{7,4},{8,11},{9,10},{10,... | collective-permute-start | bytes 2359304 | tf_op jit(solution)/shard_map/ppermute | solution.py:844
  664.3 61.8 %collective-permute-start.23 = (bf16[256,2048]{1,0:T(8,128)(2,1)}, bf16[256,2048]{1,0:T(8,128)(2,1)}, u32[]{:S(2)}, u32[]{:S(2)}) collective-permute-start(bf16[256,2048]{1,0:T(8,128)(2,1)} %get-tuple-element.164), channel_id=1, source_target_pairs={{0,1},{1,0},{2,3},{3,2},{4,5},{5,4},{6,7},{7,6},{8,9},{9,8},{10,11... | collective-permute-start | bytes 3145736 | tf_op jit(solution)/shard_map/ppermute | solution.py:844
  665.6 60.5 %collective-permute-start.45 = (bf16[256,2048]{1,0:T(8,128)(2,1)}, bf16[256,2048]{1,0:T(8,128)(2,1)}, u32[]{:S(2)}, u32[]{:S(2)}) collective-permute-start(bf16[256,2048]{1,0:T(8,128)(2,1)} %get-tuple-element.208), channel_id=1, source_target_pairs={{0,2},{1,3},{2,0},{3,1},{4,6},{5,7},{6,4},{7,5},{8,10},{9,11},{10,... | collective-permute-start | bytes 3145736 | tf_op jit(solution)/shard_map/ppermute | solution.py:844
  695.7 30.3 %collective-permute-start.44 = (bf16[256,2048]{1,0:T(8,128)(2,1)S(1)}, bf16[256,2048]{1,0:T(8,128)(2,1)S(1)}, u32[]{:S(2)}, u32[]{:S(2)}) collective-permute-start(bf16[256,2048]{1,0:T(8,128)(2,1)S(1)} %add_convert_fusion), channel_id=1, source_target_pairs={{0,1},{1,0},{2,3},{3,2},{4,5},{5,4},{6,7},{7,6},{8,9},{9,8},{10,11... | collective-permute-start | bytes 3145736 | tf_op jit(solution)/shard_map/ppermute | solution.py:844
  698.4 27.7 %collective-permute-start.43 = (bf16[256,2048]{1,0:T(8,128)(2,1)}, bf16[256,2048]{1,0:T(8,128)(2,1)S(1)}, u32[]{:S(2)}, u32[]{:S(2)}) collective-permute-start(bf16[256,2048]{1,0:T(8,128)(2,1)} %add_convert_fusion.1), channel_id=1, source_target_pairs={{0,2},{1,3},{2,0},{3,1},{4,6},{5,7},{6,4},{7,5},{8,10},{9,11},{10,... | collective-permute-start | bytes 3145736 | tf_op jit(solution)/shard_map/ppermute | solution.py:844
  (64 other events, 845.5 us)
Sparse Core Ops, SparseCore 0:
  10.2 58.7 all-gather.3
  71.2 115.4 all-gather.5
  189.0 114.9 all-gather.7
  330.8 90.0 reduce-scatter.4
  423.6 90.0 reduce-scatter.6
  557.0 90.9 reduce-scatter.8
  661.3 61.3 reduce-scatter.10

commit v4 on v3

--- a/solution.py
+++ b/solution.py
@@ -763,9 +763,10 @@
     )(core, *grads, own, *others, inputs, grad_resid, norm[None, :])
 
 
-def attention_weights_kernel(inner_ref, *refs):
+def attention_weights_kernel(inner_ref, beside_ref, *refs):
     out_ref = refs[-1]
-    total = jnp.zeros(out_ref.shape, jnp.float32)
+    q_width = refs[-2].shape[1]
+    total = jnp.zeros((out_ref.shape[0], q_width), jnp.float32)
     pieces, at = [], 0
     chunk_rows = refs[0].shape[0]
     for ref in refs[:-1]:
@@ -782,13 +783,15 @@
             )
             at += rows
         pieces = []
-    out_ref[...] = total.astype(jnp.bfloat16)
-
-
-def out_weights(inner, pieces, attended):
+    out_ref[:, :q_width] = total.astype(jnp.bfloat16)
+    out_ref[:, q_width:] = beside_ref[...]
+
+
+def out_weights(inner, beside, pieces, attended):
     width, q_width = pieces[0][0].shape[1], attended[0].shape[1]
     whole = lambda n, inner: (0, 0)
-    in_specs = []
+    columns = q_width + beside.shape[1]
+    in_specs = [pl.BlockSpec((256, beside.shape[1]), lambda n, inner: (n, 0))]
     for rows in range(2):
         in_specs += [pl.BlockSpec((piece.shape[0], 256), lambda n, inner: (0, n)) for piece in pieces[rows]]
         in_specs.append(pl.BlockSpec((SEQ, q_width), whole))
@@ -798,12 +801,12 @@
             num_scalar_prefetch=1,
             grid=(width // 256,),
             in_specs=in_specs,
-            out_specs=pl.BlockSpec((256, q_width), lambda n, inner: (n, 0)),
+            out_specs=pl.BlockSpec((256, columns), lambda n, inner: (n, 0)),
         ),
-        out_shape=jax.ShapeDtypeStruct((width, q_width), jnp.bfloat16),
+        out_shape=jax.ShapeDtypeStruct((width, columns), jnp.bfloat16),
         compiler_params=pltpu.CompilerParams(vmem_limit_bytes=60 * 2**20),
         cost_estimate=cost(4 * SEQ * q_width * width, SEQ * width * 4, 0.35),
-    )(inner, *pieces[0], attended[0], *pieces[1], attended[1])
+    )(inner, beside, *pieces[0], attended[0], *pieces[1], attended[1])
 
 
 def projection_weights_kernel(norm_ref, *refs):
@@ -944,7 +947,15 @@
     return shift(parts[3][0], 1, count), shift(parts[3][1], 2, count)
 
 
-def sum_rest(parts, first, count):
+def sum_adds(parts, first):
+    far_top, far_bottom = first
+    return (
+        (parts[2][0] + far_top.astype(jnp.float32)).astype(jnp.bfloat16),
+        (parts[1][1] + far_bottom.astype(jnp.float32)).astype(jnp.bfloat16),
+    )
+
+
+def sum_rest(parts, near, adds, count):
     if count != 4:
         mine = lax.axis_index("tensor")
         half, width = parts[0][0].shape
@@ -957,12 +968,15 @@
         ).astype(jnp.float32)
         none = jnp.zeros((half, width), jnp.bfloat16)
         return [[total[:half], none, none], [total[half:], none, none]]
-    far_top, far_bottom = first
-    x_top = shift(parts[1][0], 1, count)
-    y_bottom = shift(parts[2][1], 2, count)
-    y_top = shift((parts[2][0] + far_top.astype(jnp.float32)).astype(jnp.bfloat16), 2, count)
-    x_bottom = shift((parts[1][1] + far_bottom.astype(jnp.float32)).astype(jnp.bfloat16), 1, count)
-    return [[None, x_top, y_top], [None, x_bottom, y_bottom]]
+    x_top, y_bottom = near
+    y_top, x_bottom = shift(adds[0], 2, count), shift(adds[1], 1, count)
+    return [[parts[0][0], x_top, y_top], [parts[0][1], x_bottom, y_bottom]]
+
+
+def sum_near(parts, count):
+    if count != 4:
+        return ()
+    return shift(parts[1][0], 1, count), shift(parts[2][1], 2, count)
 
 
 def added(own_ref, x_ref, y_ref):
@@ -1140,24 +1154,20 @@
     two_first = sum_first(two, count)
     for k in range(1, inner_count):
         two.update(two_parts([k], after(grads_a, two[count - 1])))
-    if count == 4:
-        two_rest = sum_rest(two, two_first, count)
-        sent = (two_rest[0][1], two_rest[1][2])
-        two.update(two_parts([0], after(grads_a, two[1])))
-        two_rest[0][0], two_rest[1][0] = two[0]
-    else:
-        sent = ()
-        two.update(two_parts([0], after(grads_a, two[1])))
-        two_rest = sum_rest(two, None, count)
+    two_near = sum_near(two, count)
+    two_adds = sum_adds(two, two_first) if count == 4 else ()
+    two.update(two_parts([0], after(grads_a, two[1], two_adds)))
+    two_rest = sum_rest(two, two_near, two_adds, count)
     distances = list(range(count))
     out_act = after(act, two[0])
     out = rows_out(
         distances, [(out_act, units, 0), (out_act, units, 1)], w_mlp, [(units, 2), (units, 2)], chunk_rows
     )
     out_first = sum_first(out, count)
+    out_near = sum_near(out, count)
     grad_resid, branch_low, gain_mlp = own_rows_call(
         resid_back_kernel,
-        after(two_rest, out[0]),
+        after(two_rest, out[0], in_others),
         [out_grad.reshape(2, half, width), resid],
         [norm_mlp[None, :]],
         [
@@ -1172,7 +1182,7 @@
     scattered_a = scatter_weights(grad_a)
     scattered_b = scatter_weights(after(grad_b, scattered_a, two[count - 1]))
     grad_down = contract_rows(
-        after(grad_rows, heads_out[0], scattered_b, out_first), act
+        after(grad_rows, heads_out[0], scattered_b, out_first, out_near), act
     ).astype(jnp.bfloat16)
     tops = bottoms = relays = []
     if count == 4:
@@ -1207,29 +1217,27 @@
         branch_near = gather_near(branch_low, count)
         branch = (branch_near[:inner_count], branch_near[inner_count:])
     grad_qkv = projection_weights(after(rows_in, raw_grads, bottoms), inv_rows, norm_attn, raw_grads)
-    grad_w_out = out_weights(inner, after(branch, raw_grads, grad_qkv), attended)
-
-    scattered_down = scatter_weights(after(grad_down, scattered_b, heads_in))
-    scattered_attn = scatter_weights(
-        after(
-            jnp.concatenate([grad_w_out, grad_qkv], axis=1),
-            scattered_down, raw_in,
-        )
-    )
-
     grad_w_gate = jnp.concatenate(
         [scattered_a[:, :units], scattered_b[:, :units]], axis=1
     ).astype(jnp.float32)
     grad_w_up = jnp.concatenate(
         [scattered_a[:, units:], scattered_b[:, units:]], axis=1
     ).astype(jnp.float32)
+    grad_attn = out_weights(inner, grad_qkv, after(branch, raw_grads, grad_w_gate, grad_w_up), attended)
+
+    out_adds = sum_adds(out, after(out_first, grad_attn)) if count == 4 else ()
+    scattered_down = scatter_weights(after(grad_down, scattered_b, heads_in))
+    scattered_attn = scatter_weights(
+        after(
+            grad_attn, scattered_down, raw_in,
+        )
+    )
+
     grad_w_down = scattered_down.astype(jnp.float32)
     grad_tokens, gain_attn = input_back(
-        core, after(raw_in, grad_w_gate, grad_w_up, grad_w_down), w_attn, in_others, tokens, grad_resid.reshape(chunk_rows, width), norm_attn
-    )
-    out_rest = sum_rest(out, after(out_first, gain_attn) if count == 4 else None, count)
-    if count == 4:
-        out_rest[0][0], out_rest[1][0] = out[0]
+        core, after(raw_in, grad_w_down, out_adds), w_attn, in_others, tokens, grad_resid.reshape(chunk_rows, width), norm_attn
+    )
+    out_rest = sum_rest(out, out_near, out_adds, count)
     gains = [
         jnp.sum(gain_attn, axis=0),
         jnp.sum(gain_mlp, axis=0),

time: 756 us -> 772 us (1.021)
  waiting for transfers between devices: 101 us -> 120 us
    ppermute x55, waiting for transfers between devices: 101 us -> 117 us  [shift(): return lax.ppermute(values, axis, [(i, i ^ distance) for i in range(count)])]
    unnamed x109 -> x93, local copies, waits for them, and re-layouts: 18.4 us -> 18.9 us
  transfers between devices with their start and end apart: 62 -> 62, of which waited for: 16 -> 19; matrix products, arithmetic and copies ran while one was open for 18% -> 17% of each run, Pallas kernels for 57% -> 56%
where the time goes in v4:
time: 772 us; the launch traced here: 761 us
  Pallas kernels  424 us (55%)
  waiting for transfers between devices  120 us (16%)
  matrix products  71.8 us (9%)
  starting transfers between devices  55.6 us (7%)
  local copies, waits for them, and re-layouts  43.5 us (6%)
  other arithmetic  31.6 us (4%)
  between operations  15.1 us (2%)
    ppermute x55, waiting for transfers between devices, shift(): return lax.ppermute(values, axis, [(i, i ^ distance) for i in range(count)])  117 us
    pallas_call x4, Pallas kernels, rows_out(): pl.pallas_call(functools.partial(rows_out_kernel, len(lefts)), grid=(widt...  78.8 us
    pallas_call x1, Pallas kernels, gather_rows(): pl.pallas_call(gather_kernel, in_specs=[place], out_specs=[place] * 2, ou...  72.8 us
    dot_general x3, matrix products, contract_rows(): lax.dot_general(left, right, (((0,), (0,)), ((), ())), preferred_element_...  71.8 us
    ppermute x55, starting transfers between devices, shift(): return lax.ppermute(values, axis, [(i, i ^ distance) for i in range(count)])  55.1 us
    pallas_call x2, Pallas kernels, attend_back(): pl.pallas_call(functools.partial(attend_back_kernel, chunks), grid_spec=p...  51.5 us
    pallas_call x1, Pallas kernels, hidden_units(): pl.pallas_call(hidden_kernel, grid=(rows // block,), in_specs=[pl.BlockSp...  36 us
    pallas_call x1, Pallas kernels, residual(): pl.pallas_call(functools.partial(resid_kernel, count), grid_spec=pltpu.Pr...  32.4 us
  transfers between devices with their start and end apart: 62, of which 19 were waited for; matrix products, arithmetic and copies ran while one was open for 17% of the time, Pallas kernels for 56%

profile of v4, /device:TPU:0, one launch (start us, length us, event | category | flops | bytes accessed | tf_op | source)
XLA Modules:
  0.0 761.4 jit_solution(17463328218059377231)
XLA Ops:
  13.8 72.8 %shard_map.246 = (bf16[1024,2048]{1,0:T(8,128)(2,1)}, bf16[1024,2048]{1,0:T(8,128)(2,1)}) custom-call(bf16[512,2048]{1,0:T(8,128)(2,1)} %refs_11_.1), custom_call_target="tpu_custom_call" | custom-call | bytes 12582912 | tf_op jit(solution)/shard_map/pallas_call | solution.py:895
  95.1 5.8 fusion
  101.0 11.1 %shard_map.247 = (f32[1024,128]{1,0:T(8,128)}, bf16[1024,512]{1,0:T(8,128)(2,1)}, bf16[1024,512]{1,0:T(8,128)(2,1)}, bf16[1024,512]{1,0:T(8,128)(2,1)}, f32[1024,640]{1,0:T(8,128)}) custom-call(s32[1]{0:T(128)S(6)} %select_n.55.inner_ref, bf16[1024,2048]{1,0:T(8,128)(2,1)} %get-tuple-element.201.refs_0_, f32[1,2048]{1,0:T(1,128)} %bitcast.51, ...), custom_call_target="tpu_custom_call" | custom-call | flops 2928386816 | bytes 2516582 | tf_op jit(solution)/shard_map/pallas_call | solution.py:376
  112.1 9.5 %shard_map.248 = (bf16[1024,512]{1,0:T(8,128)(2,1)}, f32[1024,512]{1,0:T(8,128)}) custom-call(bf16[1024,512]{1,0:T(8,128)(2,1)} %get-tuple-element.127.q_ref, bf16[1024,512]{1,0:T(8,128)(2,1)} %get-tuple-element.128.k_ref, bf16[1024,512]{1,0:T(8,128)(2,1)} %get-tuple-element.129.v_ref, s32[1024,1]{1,0:T(8,128)} %copy.29.segc_ref, ...), custom_call_target="tpu_custom_call" | custom-call | flops 2254857728 | bytes 6291456 | tf_op jit(solution)/shard_map/pallas_call | solution.py:225
  123.5 11.7 %shard_map.249 = (f32[1024,128]{1,0:T(8,128)}, bf16[1024,512]{1,0:T(8,128)(2,1)}, bf16[1024,512]{1,0:T(8,128)(2,1)}, bf16[1024,512]{1,0:T(8,128)(2,1)}, f32[1024,640]{1,0:T(8,128)}) custom-call(s32[1]{0:T(128)S(6)} %select_n.55.inner_ref, bf16[1024,2048]{1,0:T(8,128)(2,1)} %get-tuple-element.202.refs_0_.refs_1_, f32[1,2048]{1,0:T(1,128)} %bitcast.52, ...), custom_call_target="tpu_custom_call" | custom-call | flops 2928386816 | bytes 2516582 | tf_op jit(solution)/shard_map/pallas_call | solution.py:376
  135.3 9.7 %shard_map.250 = (bf16[1024,512]{1,0:T(8,128)(2,1)}, f32[1024,512]{1,0:T(8,128)}) custom-call(bf16[1024,512]{1,0:T(8,128)(2,1)} %get-tuple-element.133.q_ref, bf16[1024,512]{1,0:T(8,128)(2,1)} %get-tuple-element.134.k_ref, bf16[1024,512]{1,0:T(8,128)(2,1)} %get-tuple-element.135.v_ref, s32[1024,1]{1,0:T(8,128)} %copy.30.segc_ref, ...), custom_call_target="tpu_custom_call" | custom-call | flops 2254857728 | bytes 6291456 | tf_op jit(solution)/shard_map/pallas_call | solution.py:225
  150.3 21.0 %collective-permute-done.3.refs_4_ = bf16[1024,512]{1,0:T(8,128)(2,1)S(1)} collective-permute-done((bf16[1024,512]{1,0:T(8,128)(2,1)}, bf16[1024,512]{1,0:T(8,128)(2,1)S(1)}, u32[]{:S(2)}, u32[]{:S(2)}) %collective-permute-start.3) | collective-permute-done | bytes 1048608 | tf_op jit(solution)/shard_map/ppermute | solution.py:847
  174.2 8.8 %collective-permute-done.8 = bf16[512,512]{1,0:T(8,128)(2,1)S(1)} collective-permute-done((bf16[512,512]{1,0:T(8,128)(2,1)S(1)}, bf16[512,512]{1,0:T(8,128)(2,1)S(1)}, u32[]{:S(2)}, u32[]{:S(2)}) %collective-permute-start.8) | collective-permute-done | bytes 524320 | tf_op jit(solution)/shard_map/ppermute | solution.py:847
  184.7 9.6 %collective-permute-done.4 = bf16[512,512]{1,0:T(8,128)(2,1)S(1)} collective-permute-done((bf16[512,512]{1,0:T(8,128)(2,1)S(1)}, bf16[512,512]{1,0:T(8,128)(2,1)S(1)}, u32[]{:S(2)}, u32[]{:S(2)}) %collective-permute-start.4) | collective-permute-done | bytes 524320 | tf_op jit(solution)/shard_map/ppermute | solution.py:847
  196.5 9.0 %collective-permute-done.10 = bf16[512,512]{1,0:T(8,128)(2,1)S(1)} collective-permute-done((bf16[512,512]{1,0:T(8,128)(2,1)S(1)}, bf16[512,512]{1,0:T(8,128)(2,1)S(1)}, u32[]{:S(2)}, u32[]{:S(2)}) %collective-permute-start.10) | collective-permute-done | bytes 524320 | tf_op jit(solution)/shard_map/ppermute | solution.py:847
  210.7 32.4 %shard_map.251 = (bf16[2048,2048]{1,0:T(8,128)(2,1)}, f32[1,512,2048]{2,1,0:T(8,128)}) custom-call(s32[2]{0:T(128)} %pad_add_fusion.place_ref, bf16[1024,2048]{1,0:T(8,128)(2,1)} %get-tuple-element.201.refs_0_, bf16[1024,2048]{1,0:T(8,128)(2,1)} %get-tuple-element.202.refs_0_.refs_1_, bf16[1024,512]{1,0:T(8,128)(2,1)} %get-tuple-element.130.refs_2_.out_ref.refs_3_, ...), custom_call_target="tpu_custom_call" | custom-call | flops 7469508096 | bytes 6710886 | tf_op jit(solution)/shard_map/pallas_call | solution.py:667
  243.1 3.9 collective-permute-done.15
  247.0 2.3 slice.118
  250.9 2.3 slice.119
  255.2 3.2 constant_dynamic-update-slice_fusion.9
  258.5 3.1 constant_dynamic-update-slice_fusion.8
  261.6 25.6 %shard_map.252 = (bf16[2048,2048]{1,0:T(8,128)(2,1)}, bf16[2048,2048]{1,0:T(8,128)(2,1)}) custom-call(bf16[2048,2048]{1,0:T(8,128)(2,1)} %get-tuple-element.151.x_ref, bf16[2048,3072]{1,0:T(8,128)(2,1)} %all-gather.6.cloned.1.call-done.w_ref.refs_2_), custom_call_target="tpu_custom_call" | custom-call | flops 5453926912 | bytes 5033164 | tf_op jit(solution)/shard_map/pallas_call | solution.py:525
  290.6 15.2 %shard_map.253.refs_0_ = bf16[2048,2048]{1,0:T(8,128)(2,1)} custom-call(bf16[2048,2048]{1,0:T(8,128)(2,1)} %constant_dynamic-update-slice_fusion.6.dy_ref, bf16[2048,2048]{1,0:T(8,128)(2,1)} %get-tuple-element.147.factors_ref, bf16[2048,3072]{1,0:T(8,128)(2,1)} %all-gather.6.cloned.1.call-done.w_ref.refs_2_), custom_call_target="tpu_custom_call" | custom-call | flops 2726963456 | bytes 5033164 | tf_op jit(solution)/shard_map/pallas_call | solution.py:557
  305.8 23.7 %convolution_convert_fusion.2 = bf16[2048,2048]{1,0:T(8,128)(2,1)} fusion(bf16[2048,2048]{1,0:T(8,128)(2,1)} %get-tuple-element.151.x_ref, bf16[2048,2048]{1,0:T(8,128)(2,1)} %shard_map.253.refs_0_), kind=kOutput, calls=%fused_computation.2 | convolution fusion | flops 17184063488 | bytes 25165824 | tf_op jit(solution)/shard_map/dot_general | solution.py:38
  329.6 2.7 constant_dynamic-slice_fusion
  334.3 36.0 %shard_map.254 = (bf16[2048,2048]{1,0:T(8,128)(2,1)}, bf16[2048,2048]{1,0:T(8,128)(2,1)}) custom-call(bf16[2048,2048]{1,0:T(8,128)(2,1)} %get-tuple-element.151.x_ref, bf16[2048,2048]{1,0:T(8,128)(2,1)} %constant_dynamic-update-slice_fusion.6.dy_ref, bf16[2048,3072]{1,0:T(8,128)(2,1)} %all-gather.8.cloned.1.call-done.w_ref.refs_3_, ...), custom_call_target="tpu_custom_call", output_to_operand_aliasing={{0}: (3, {})} | custom-call | flops 8180890112 | bytes 7549747 | tf_op jit(solution)/shard_map/pallas_call | solution.py:486
  374.3 23.9 %convolution_convert_fusion.1 = bf16[2048,2048]{1,0:T(8,128)(2,1)} fusion(bf16[2048,2048]{1,0:T(8,128)(2,1)} %get-tuple-element.151.x_ref, bf16[2048,2048]{1,0:T(8,128)(2,1)} %get-tuple-element.152.refs_1_), kind=kOutput, calls=%fused_computation.1 | convolution fusion | flops 17184063488 | bytes 25165824 | tf_op jit(solution)/shard_map/dot_general | solution.py:38
  398.2 24.1 %shard_map.255 = (f32[256,2048]{1,0:T(8,128)}, bf16[256,2048]{1,0:T(8,128)(2,1)}, bf16[256,2048]{1,0:T(8,128)(2,1)}, bf16[256,2048]{1,0:T(8,128)(2,1)}) custom-call(bf16[2048,2048]{1,0:T(8,128)(2,1)} %shard_map.253.refs_0_, bf16[2048,2048]{1,0:T(8,128)(2,1)} %get-tuple-element.152.refs_1_, bf16[2048,3072]{1,0:T(8,128)(2,1)} %all-gather.6.cloned.1.call-done.w_ref.refs_2_, ...), custom_call_target="tpu_custom_call" | custom-call | flops 844219584 | bytes 209715 | tf_op jit(solution)/shard_map/pallas_call | solution.py:608
  429.4 15.3 %shard_map.256 = (bf16[256,2048]{1,0:T(8,128)(2,1)}, f32[256,2048]{1,0:T(8,128)}) custom-call(bf16[2048,2048]{1,0:T(8,128)(2,1)} %shard_map.253.refs_0_, bf16[2048,2048]{1,0:T(8,128)(2,1)} %get-tuple-element.152.refs_1_, bf16[2048,3072]{1,0:T(8,128)(2,1)} %all-gather.6.cloned.1.call-done.w_ref.refs_2_, ...), custom_call_target="tpu_custom_call" | custom-call | flops 422109792 | bytes 104857 | tf_op jit(solution)/shard_map/pallas_call | solution.py:608
  450.0 3.3 add_convert_fusion.2
  453.9 2.5 add_convert_fusion.3
  456.4 15.4 %shard_map.257 = (f32[256,2048]{1,0:T(8,128)}, f32[256,2048]{1,0:T(8,128)}) custom-call(bf16[2048,2048]{1,0:T(8,128)(2,1)} %shard_map.253.refs_0_, bf16[2048,2048]{1,0:T(8,128)(2,1)} %get-tuple-element.152.refs_1_, bf16[2048,3072]{1,0:T(8,128)(2,1)} %all-gather.6.cloned.1.call-done.w_ref.refs_2_, bf16[2048,3072]{1,0:T(8,128)(2,1)} %all-gather.8.cloned.1.call-done.w_ref.refs_3_), custom_call_target="tpu_custom_call" | custom-call | flops 422109792 | bytes 104857 | tf_op jit(solution)/shard_map/pallas_call | solution.py:608
  473.3 24.1 %shard_map.258 = (f32[256,2048]{1,0:T(8,128)}, f32[256,2048]{1,0:T(8,128)}, bf16[256,2048]{1,0:T(8,128)(2,1)}, f32[256,2048]{1,0:T(8,128)}, f32[256,2048]{1,0:T(...) custom-call(bf16[2048,2048]{1,0:T(8,128)(2,1)} %get-tuple-element.163.refs_0_.refs_1_, ...), custom_call_target="tpu_custom_call" | custom-call | flops 844219584 | bytes 209715 | tf_op jit(solution)/shard_map/pallas_call | solution.py:608
  501.6 9.4 %shard_map.259 = (f32[2,256,2048]{2,1,0:T(8,128)}, bf16[2,256,2048]{2,1,0:T(8,128)(2,1)}, f32[8,2048]{1,0:T(8,128)}) custom-call(f32[256,2048]{1,0:T(8,128)} %get-tuple-element.173.refs_0_, bf16[256,2048]{1,0:T(8,128)(2,1)} %copy-done.23, bf16[256,2048]{1,0:T(8,128)(2,1)} %collective-permute-done.29.refs_2_, f32[256,2048]{1,0:T(8,128)} %get-tuple-element.176.refs_3_, ...), custom_call_target="tpu_custom_call" | custom-call | flops 1048576 | bytes 1048576 | tf_op jit(solution)/shard_map/pallas_call | solution.py:995
  511.0 9.4 %shard_map.260 = (bf16[512,512]{1,0:T(8,128)(2,1)}, bf16[512,512]{1,0:T(8,128)(2,1)}, bf16[512,512]{1,0:T(8,128)(2,1)}, bf16[512,512]{1,0:T(8,128)(2,1)}) custom-call(s32[1]{0:T(128)S(6)} %select_n.56.core_ref, bf16[512,2048]{1,0:T(8,128)(2,1)} %bitcast.43, bf16[2048,1280]{1,0:T(8,128)(2,1)} %all-gather.4.cloned.1.call-done.refs_2_.refs_10_.refs_0_.refs_4_, ...), custom_call_target="tpu_custom_call" | custom-call | flops 321720384 | bytes 209715 | tf_op jit(solution)/shard_map/pallas_call | solution.py:428
  521.2 2.6 collective-permute-done.25.refs_1_
  524.4 22.0 %collective-permute-done.26 = bf16[256,2048]{1,0:T(8,128)(2,1)} collective-permute-done((bf16[256,2048]{1,0:T(8,128)(2,1)}, bf16[256,2048]{1,0:T(8,128)(2,1)}, u32[]{:S(2)}, u32[]{:S(2)}) %collective-permute-start.26) | collective-permute-done | bytes 1048608 | tf_op jit(solution)/shard_map/ppermute | solution.py:847
  548.4 24.2 %convolution_convert_fusion = bf16[2048,2048]{1,0:T(8,128)(2,1)} fusion(bf16[2048,2048]{1,0:T(8,128)(2,1)} %constant_dynamic-update-slice_fusion.6.dy_ref, bf16[2048,2048]{1,0:T(8,128)(2,1)} %get-tuple-element.163.refs_0_.refs_1_), kind=kOutput, calls=%fused_computation | convolution fusion | flops 17184063488 | bytes 25165824 | tf_op jit(solution)/shard_map/dot_general | solution.py:38
  577.4 26.0 %shard_map.261 = (bf16[512,768]{1,0:T(8,128)(2,1)}, bf16[512,768]{1,0:T(8,128)(2,1)}, f32[8,128]{1,0:T(8,128)}, f32[8,128]{1,0:T(8,128)}) custom-call(s32[1]{0:T(128)S(6)} %select_n.55.inner_ref, bf16[1024,512]{1,0:T(8,128)(2,1)} %get-tuple-element.127.q_ref, bf16[1024,512]{1,0:T(8,128)(2,1)} %get-tuple-element.128.k_ref, ...), custom_call_target="tpu_custom_call" | custom-call | flops 5905580032 | bytes 10485760 | tf_op jit(solution)/shard_map/pallas_call | solution.py:258
  605.7 25.5 %shard_map.262 = (bf16[512,768]{1,0:T(8,128)(2,1)}, bf16[512,768]{1,0:T(8,128)(2,1)}, f32[8,128]{1,0:T(8,128)}, f32[8,128]{1,0:T(8,128)}) custom-call(s32[1]{0:T(128)S(6)} %select_n.55.inner_ref, bf16[1024,512]{1,0:T(8,128)(2,1)} %get-tuple-element.133.q_ref, bf16[1024,512]{1,0:T(8,128)(2,1)} %get-tuple-element.134.k_ref, ...), custom_call_target="tpu_custom_call" | custom-call | flops 5905580032 | bytes 10485760 | tf_op jit(solution)/shard_map/pallas_call | solution.py:258
  640.0 13.0 %shard_map.263.beside_ref = bf16[2048,768]{1,0:T(8,128)(2,1)} custom-call(f32[1,2048]{1,0:T(1,128)} %bitcast.53, bf16[1024,2048]{1,0:T(8,128)(2,1)} %get-tuple-element.201.refs_0_, bf16[1024,2048]{1,0:T(8,128)(2,1)} %get-tuple-element.202.refs_0_.refs_1_, f32[1024,128]{1,0:T(8,128)} %get-tuple-element.203.refs_2_, f32[1024,128]{1,0:T(8,128)} %get-tuple-element.204.refs_3_, ...), custom_call_target="tpu_custom_call" | custom-call | flops 2996488704 | bytes 1677721 | tf_op jit(solution)/shard_map/pallas_call | solution.py:832
  653.0 16.0 %collective-permute-done.43.refs_6_ = bf16[256,2048]{1,0:T(8,128)(2,1)S(1)} collective-permute-done((bf16[256,2048]{1,0:T(8,128)(2,1)}, bf16[256,2048]{1,0:T(8,128)(2,1)S(1)}, u32[]{:S(2)}, u32[]{:S(2)}) %collective-permute-start.43) | collective-permute-done | bytes 1048608 | tf_op jit(solution)/shard_map/ppermute | solution.py:847
  669.9 11.8 %shard_map.264 = bf16[2048,1280]{1,0:T(8,128)(2,1)} custom-call(s32[1]{0:T(128)S(6)} %select_n.55.inner_ref, bf16[2048,768]{1,0:T(8,128)(2,1)} %shard_map.263.beside_ref, bf16[512,2048]{1,0:T(8,128)(2,1)} %bitcast.44, bf16[256,2048]{1,0:T(8,128)(2,1)} %copy-done.30, bf16[256,2048]{1,0:T(8,128)(2,1)} %collective-permute-done.41.refs_2_, ...), custom_call_target="tpu_custom_call" | custom-call | flops 2454267136 | bytes 1677721 | tf_op jit(solution)/shard_map/pallas_call | solution.py:798
  681.8 6.3 collective-permute-done.48.refs_2_
  689.0 2.7 add_convert_fusion
  693.4 2.6 add_convert_fusion.1
  699.0 19.8 %shard_map.265 = (f32[512,2048]{1,0:T(8,128)}, f32[8,2048]{1,0:T(8,128)}) custom-call(s32[1]{0:T(128)S(6)} %select_n.56.core_ref, bf16[512,768]{1,0:T(8,128)(2,1)} %get-tuple-element.218.refs_4_.refs_0_, bf16[512,768]{1,0:T(8,128)(2,1)} %collective-permute-done.47.refs_1_, bf16[512,768]{1,0:T(8,128)(2,1)} %copy-done.32, ...), custom_call_target="tpu_custom_call" | custom-call | flops 4601750528 | bytes 4194304 | tf_op jit(solution)/shard_map/pallas_call | solution.py:743
  722.7 2.8 collective-permute-done.51
  725.5 2.7 collective-permute-start.52
  728.2 3.0 collective-permute-done.52
  736.2 2.5 collective-permute-done.54
  740.1 6.4 shard_map.266
  747.7 2.9 reduce-scatter.11.cloned.1.call-done
  (267 shorter events, 106.6 us)
Async XLA Ops:
  7.2 80.3 %all-gather.4.cloned.1.call-start = ((), (), s32[]{:S(2)}) async-start(), calls=%async_computation.4 | async-start | bytes 5898240 | tf_op jit(solution)/shard_map/all_gather | solution.py:1048
  9.4 252.2 %all-gather.6.cloned.1.call-start = ((), (), s32[]{:S(2)}) async-start(), calls=%async_computation.5 | async-start | bytes 14155776 | tf_op jit(solution)/shard_map/all_gather | solution.py:1048
  12.1 322.1 %all-gather.8.cloned.1.call-start = ((), (), s32[]{:S(2)}) async-start(), calls=%async_computation.6 | async-start | bytes 14155776 | tf_op jit(solution)/shard_map/all_gather | solution.py:1048
  13.5 408.8 %reduce-scatter.5.cloned.1.call-start = ((), (), s32[]{:S(2)}) async-start(), calls=%async_computation.7 | async-start | bytes 9437184 | tf_op jit(solution)/shard_map/reduce_scatter | solution.py:1052
  89.8 33.7 %collective-permute-start.1 = (bf16[1024,512]{1,0:T(8,128)(2,1)}, bf16[1024,512]{1,0:T(8,128)(2,1)S(1)}, u32[]{:S(2)}, u32[]{:S(2)}) collective-permute-start(bf16[1024,512]{1,0:T(8,128)(2,1)} %constant_dynamic-slice_fusion.1), channel_id=1, source_target_pairs={{0,1},{1,0},{2,3},{3,2},{4,5},{5,4},{6,7},{7,6},{8,9},{9,8},{10,11... | collective-permute-start | bytes 3145736 | tf_op jit(solution)/shard_map/ppermute | solution.py:847
  90.4 33.1 %collective-permute-start.2 = (bf16[1024,512]{1,0:T(8,128)(2,1)}, bf16[1024,512]{1,0:T(8,128)(2,1)S(1)}, u32[]{:S(2)}, u32[]{:S(2)}) collective-permute-start(bf16[1024,512]{1,0:T(8,128)(2,1)} %constant_dynamic-slice_fusion.1), channel_id=1, source_target_pairs={{0,2},{1,3},{2,0},{3,1},{4,6},{5,7},{6,4},{7,5},{8,10},{9,11},{10,... | collective-permute-start | bytes 3145736 | tf_op jit(solution)/shard_map/ppermute | solution.py:847
  122.1 25.6 %collective-permute-start = (bf16[1024,512]{1,0:T(8,128)(2,1)}, bf16[1024,512]{1,0:T(8,128)(2,1)}, u32[]{:S(2)}, u32[]{:S(2)}) collective-permute-start(bf16[1024,512]{1,0:T(8,128)(2,1)} %get-tuple-element.130.refs_2_.out_ref.refs_3_), channel_id=1, source_target_pairs={{0,1},{1,0},{2,3},{3,2},{4,5},{5,4},{6,7},{7,6},{8,9},{9,8},{10,11... | collective-permute-start | bytes 3145736 | tf_op jit(solution)/shard_map/ppermute | solution.py:847
  144.9 26.4 %collective-permute-start.3 = (bf16[1024,512]{1,0:T(8,128)(2,1)}, bf16[1024,512]{1,0:T(8,128)(2,1)S(1)}, u32[]{:S(2)}, u32[]{:S(2)}) collective-permute-start(bf16[1024,512]{1,0:T(8,128)(2,1)} %get-tuple-element.136.refs_6_.out_ref.refs_8_), channel_id=1, source_target_pairs={{0,2},{1,3},{2,0},{3,1},{4,6},{5,7},{6,4},{7,5},{8,10},{9,11},{10,... | collective-permute-start | bytes 3145736 | tf_op jit(solution)/shard_map/ppermute | solution.py:847
  145.5 26.4 %collective-permute-start.5 = (bf16[1024,512]{1,0:T(8,128)(2,1)}, bf16[1024,512]{1,0:T(8,128)(2,1)S(1)}, u32[]{:S(2)}, u32[]{:S(2)}) collective-permute-start(bf16[1024,512]{1,0:T(8,128)(2,1)} %get-tuple-element.136.refs_6_.out_ref.refs_8_), channel_id=1, source_target_pairs={{0,1},{1,0},{2,3},{3,2},{4,5},{5,4},{6,7},{7,6},{8,9},{9,8},{10,11... | collective-permute-start | bytes 3145736 | tf_op jit(solution)/shard_map/ppermute | solution.py:847
  147.1 35.9 %collective-permute-start.8 = (bf16[512,512]{1,0:T(8,128)(2,1)S(1)}, bf16[512,512]{1,0:T(8,128)(2,1)S(1)}, u32[]{:S(2)}, u32[]{:S(2)}) collective-permute-start(bf16[512,512]{1,0:T(8,128)(2,1)S(1)} %slice.150), channel_id=1, source_target_pairs={{0,1},{1,0},{2,3},{3,2},{4,5},{5,4},{6,7},{7,6},{8,9},{9,8},{10,11... | collective-permute-start | bytes 1572872 | tf_op jit(solution)/shard_map/ppermute | solution.py:847
  148.7 35.9 %collective-permute-start.9 = (bf16[512,512]{1,0:T(8,128)(2,1)S(1)}, bf16[512,512]{1,0:T(8,128)(2,1)S(1)}, u32[]{:S(2)}, u32[]{:S(2)}) collective-permute-start(bf16[512,512]{1,0:T(8,128)(2,1)S(1)} %slice.151), channel_id=1, source_target_pairs={{0,2},{1,3},{2,0},{3,1},{4,6},{5,7},{6,4},{7,5},{8,10},{9,11},{10,... | collective-permute-start | bytes 1572872 | tf_op jit(solution)/shard_map/ppermute | solution.py:847
  173.7 31.9 %collective-permute-start.10 = (bf16[512,512]{1,0:T(8,128)(2,1)S(1)}, bf16[512,512]{1,0:T(8,128)(2,1)S(1)}, u32[]{:S(2)}, u32[]{:S(2)}) collective-permute-start(bf16[512,512]{1,0:T(8,128)(2,1)S(1)} %slice.116), channel_id=1, source_target_pairs={{0,1},{1,0},{2,3},{3,2},{4,5},{5,4},{6,7},{7,6},{8,9},{9,8},{10,11... | collective-permute-start | bytes 1572872 | tf_op jit(solution)/shard_map/ppermute | solution.py:847
  194.4 52.6 %collective-permute-start.15 = (bf16[512,2048]{1,0:T(8,128)(2,1)S(1)}, bf16[512,2048]{1,0:T(8,128)(2,1)}, u32[]{:S(2)}, u32[]{:S(2)}) collective-permute-start(bf16[512,2048]{1,0:T(8,128)(2,1)S(1)} %copy-done.1), channel_id=1, source_target_pairs={{0,1},{1,0},{2,3},{3,2},{4,5},{5,4},{6,7},{7,6},{8,9},{9,8},{10,11... | collective-permute-start | bytes 6291464 | tf_op jit(solution)/shard_map/ppermute | solution.py:847
  196.1 51.0 %collective-permute-start.16 = (bf16[512,2048]{1,0:T(8,128)(2,1)S(1)}, bf16[512,2048]{1,0:T(8,128)(2,1)}, u32[]{:S(2)}, u32[]{:S(2)}) collective-permute-start(bf16[512,2048]{1,0:T(8,128)(2,1)S(1)} %copy-done.1), channel_id=1, source_target_pairs={{0,2},{1,3},{2,0},{3,1},{4,6},{5,7},{6,4},{7,5},{8,10},{9,11},{10,... | collective-permute-start | bytes 6291464 | tf_op jit(solution)/shard_map/ppermute | solution.py:847
  249.4 37.9 %collective-permute-start.17 = (bf16[256,2048]{1,0:T(8,128)(2,1)}, bf16[256,2048]{1,0:T(8,128)(2,1)S(1)}, u32[]{:S(2)}, u32[]{:S(2)}) collective-permute-start(bf16[256,2048]{1,0:T(8,128)(2,1)} %slice.118), channel_id=1, source_target_pairs={{0,1},{1,0},{2,3},{3,2},{4,5},{5,4},{6,7},{7,6},{8,9},{9,8},{10,11... | collective-permute-start | bytes 3145736 | tf_op jit(solution)/shard_map/ppermute | solution.py:847
  253.2 34.0 %collective-permute-start.18 = (bf16[256,2048]{1,0:T(8,128)(2,1)}, bf16[256,2048]{1,0:T(8,128)(2,1)}, u32[]{:S(2)}, u32[]{:S(2)}) collective-permute-start(bf16[256,2048]{1,0:T(8,128)(2,1)} %slice.119), channel_id=1, source_target_pairs={{0,2},{1,3},{2,0},{3,1},{4,6},{5,7},{6,4},{7,5},{8,10},{9,11},{10,... | collective-permute-start | bytes 3145736 | tf_op jit(solution)/shard_map/ppermute | solution.py:847
  329.5 218.9 %reduce-scatter.7.cloned.1.call-start = ((), (), s32[]{:S(2)}) async-start(), calls=%async_computation.8 | async-start | bytes 9437184 | tf_op jit(solution)/shard_map/reduce_scatter | solution.py:1052
  332.3 38.0 %collective-permute-start.19 = (bf16[1024,768]{1,0:T(8,128)(2,1)}, bf16[1024,768]{1,0:T(8,128)(2,1)S(1)}, u32[]{:S(2)}, u32[]{:S(2)}) collective-permute-start(bf16[1024,768]{1,0:T(8,128)(2,1)} %constant_dynamic-slice_fusion), channel_id=1, source_target_pairs={{0,1},{1,0},{2,3},{3,2},{4,5},{5,4},{6,7},{7,6},{8,9},{9,8},{10,11... | collective-permute-start | bytes 4718600 | tf_op jit(solution)/shard_map/ppermute | solution.py:847
  333.7 36.6 %collective-permute-start.20 = (bf16[1024,768]{1,0:T(8,128)(2,1)}, bf16[1024,768]{1,0:T(8,128)(2,1)S(1)}, u32[]{:S(2)}, u32[]{:S(2)}) collective-permute-start(bf16[1024,768]{1,0:T(8,128)(2,1)} %constant_dynamic-slice_fusion), channel_id=1, source_target_pairs={{0,2},{1,3},{2,0},{3,1},{4,6},{5,7},{6,4},{7,5},{8,10},{9,11},{10,... | collective-permute-start | bytes 4718600 | tf_op jit(solution)/shard_map/ppermute | solution.py:847
  371.3 26.8 %collective-permute-start.21 = (bf16[512,768]{1,0:T(8,128)(2,1)}, bf16[512,768]{1,0:T(8,128)(2,1)}, u32[]{:S(2)}, u32[]{:S(2)}) collective-permute-start(bf16[512,768]{1,0:T(8,128)(2,1)} %slice.152), channel_id=1, source_target_pairs={{0,1},{1,0},{2,3},{3,2},{4,5},{5,4},{6,7},{7,6},{8,9},{9,8},{10,11... | collective-permute-start | bytes 2359304 | tf_op jit(solution)/shard_map/ppermute | solution.py:847
  422.3 265.8 %reduce-scatter.9.cloned.1.call-start = ((), (), s32[]{:S(2)}) async-start(), calls=%async_computation.9 | async-start | bytes 9437184 | tf_op jit(solution)/shard_map/reduce_scatter | solution.py:1052
  422.6 25.9 %collective-permute-start.24 = (bf16[256,2048]{1,0:T(8,128)(2,1)}, bf16[256,2048]{1,0:T(8,128)(2,1)}, u32[]{:S(2)}, u32[]{:S(2)}) collective-permute-start(bf16[256,2048]{1,0:T(8,128)(2,1)} %get-tuple-element.155), channel_id=1, source_target_pairs={{0,2},{1,3},{2,0},{3,1},{4,6},{5,7},{6,4},{7,5},{8,10},{9,11},{10,... | collective-permute-start | bytes 3145736 | tf_op jit(solution)/shard_map/ppermute | solution.py:847
  424.2 29.2 %collective-permute-start.23 = (bf16[256,2048]{1,0:T(8,128)(2,1)}, bf16[256,2048]{1,0:T(8,128)(2,1)}, u32[]{:S(2)}, u32[]{:S(2)}) collective-permute-start(bf16[256,2048]{1,0:T(8,128)(2,1)} %get-tuple-element.154), channel_id=1, source_target_pairs={{0,1},{1,0},{2,3},{3,2},{4,5},{5,4},{6,7},{7,6},{8,9},{9,8},{10,11... | collective-permute-start | bytes 3145736 | tf_op jit(solution)/shard_map/ppermute | solution.py:847
  424.7 47.1 %collective-permute-start.33 = (bf16[1024,768]{1,0:T(8,128)(2,1)S(1)}, bf16[1024,768]{1,0:T(8,128)(2,1)}, u32[]{:S(2)}, u32[]{:S(2)}) collective-permute-start(bf16[1024,768]{1,0:T(8,128)(2,1)S(1)} %collective-permute-done.20.refs_6_), channel_id=1, source_target_pairs={{0,4},{4,0},{8,12},{12,8},{16,20},{20,16},{24,28},{28,24},{1,5},{5... | collective-permute-start | bytes 4718600 | tf_op jit(solution)/shard_map/ppermute | solution.py:847
  428.9 70.7 %collective-permute-start.34 = (bf16[1024,768]{1,0:T(8,128)(2,1)}, bf16[1024,768]{1,0:T(8,128)(2,1)}, u32[]{:S(2)}, u32[]{:S(2)}) collective-permute-start(bf16[1024,768]{1,0:T(8,128)(2,1)} %constant_dynamic-update-slice_fusion.11.refs_7_), channel_id=1, source_target_pairs={{0,4},{4,0},{8,12},{12,8},{16,20},{20,16},{24,28},{28,24},{1,5},{5... | collective-permute-start | bytes 4718600 | tf_op jit(solution)/shard_map/ppermute | solution.py:847
  444.6 52.8 %collective-permute-start.28 = (bf16[256,2048]{1,0:T(8,128)(2,1)}, bf16[256,2048]{1,0:T(8,128)(2,1)S(1)}, u32[]{:S(2)}, u32[]{:S(2)}) collective-permute-start(bf16[256,2048]{1,0:T(8,128)(2,1)} %get-tuple-element.157), channel_id=1, source_target_pairs={{0,1},{1,0},{2,3},{3,2},{4,5},{5,4},{6,7},{7,6},{8,9},{9,8},{10,11... | collective-permute-start | bytes 3145736 | tf_op jit(solution)/shard_map/ppermute | solution.py:847
  448.5 49.7 %collective-permute-start.31 = (bf16[256,2048]{1,0:T(8,128)(2,1)}, bf16[256,2048]{1,0:T(8,128)(2,1)S(1)}, u32[]{:S(2)}, u32[]{:S(2)}) collective-permute-start(bf16[256,2048]{1,0:T(8,128)(2,1)} %get-tuple-element.171), channel_id=1, source_target_pairs={{0,2},{1,3},{2,0},{3,1},{4,6},{5,7},{6,4},{7,5},{8,10},{9,11},{10,... | collective-permute-start | bytes 3145736 | tf_op jit(solution)/shard_map/ppermute | solution.py:847
  453.3 46.8 %collective-permute-start.30 = (bf16[256,2048]{1,0:T(8,128)(2,1)}, bf16[256,2048]{1,0:T(8,128)(2,1)}, u32[]{:S(2)}, u32[]{:S(2)}) collective-permute-start(bf16[256,2048]{1,0:T(8,128)(2,1)} %add_convert_fusion.2), channel_id=1, source_target_pairs={{0,1},{1,0},{2,3},{3,2},{4,5},{5,4},{6,7},{7,6},{8,9},{9,8},{10,11... | collective-permute-start | bytes 3145736 | tf_op jit(solution)/shard_map/ppermute | solution.py:847
  471.8 29.8 %collective-permute-start.29 = (bf16[256,2048]{1,0:T(8,128)(2,1)}, bf16[256,2048]{1,0:T(8,128)(2,1)}, u32[]{:S(2)}, u32[]{:S(2)}) collective-permute-start(bf16[256,2048]{1,0:T(8,128)(2,1)} %add_convert_fusion.3), channel_id=1, source_target_pairs={{0,2},{1,3},{2,0},{3,1},{4,6},{5,7},{6,4},{7,5},{8,10},{9,11},{10,... | collective-permute-start | bytes 3145736 | tf_op jit(solution)/shard_map/ppermute | solution.py:847
  497.4 26.4 %collective-permute-start.25 = (bf16[256,2048]{1,0:T(8,128)(2,1)}, bf16[256,2048]{1,0:T(8,128)(2,1)S(1)}, u32[]{:S(2)}, u32[]{:S(2)}) collective-permute-start(bf16[256,2048]{1,0:T(8,128)(2,1)} %get-tuple-element.165), channel_id=1, source_target_pairs={{0,1},{1,0},{2,3},{3,2},{4,5},{5,4},{6,7},{7,6},{8,9},{9,8},{10,11... | collective-permute-start | bytes 3145736 | tf_op jit(solution)/shard_map/ppermute | solution.py:847
  498.2 48.2 %collective-permute-start.26 = (bf16[256,2048]{1,0:T(8,128)(2,1)}, bf16[256,2048]{1,0:T(8,128)(2,1)}, u32[]{:S(2)}, u32[]{:S(2)}) collective-permute-start(bf16[256,2048]{1,0:T(8,128)(2,1)} %get-tuple-element.167), channel_id=1, source_target_pairs={{0,1},{1,0},{2,3},{3,2},{4,5},{5,4},{6,7},{7,6},{8,9},{9,8},{10,11... | collective-permute-start | bytes 3145736 | tf_op jit(solution)/shard_map/ppermute | solution.py:847
  499.5 48.4 %collective-permute-start.27 = (bf16[256,2048]{1,0:T(8,128)(2,1)}, bf16[256,2048]{1,0:T(8,128)(2,1)}, u32[]{:S(2)}, u32[]{:S(2)}) collective-permute-start(bf16[256,2048]{1,0:T(8,128)(2,1)} %get-tuple-element.168), channel_id=1, source_target_pairs={{0,2},{1,3},{2,0},{3,1},{4,6},{5,7},{6,4},{7,5},{8,10},{9,11},{10,... | collective-permute-start | bytes 3145736 | tf_op jit(solution)/shard_map/ppermute | solution.py:847
  500.1 48.3 %collective-permute-start.38 = (bf16[256,2048]{1,0:T(8,128)(2,1)}, bf16[256,2048]{1,0:T(8,128)(2,1)}, u32[]{:S(2)}, u32[]{:S(2)}) collective-permute-start(bf16[256,2048]{1,0:T(8,128)(2,1)} %get-tuple-element.186), channel_id=1, source_target_pairs={{0,2},{1,3},{2,0},{3,1},{4,6},{5,7},{6,4},{7,5},{8,10},{9,11},{10,... | collective-permute-start | bytes 3145736 | tf_op jit(solution)/shard_map/ppermute | solution.py:847
  520.4 52.2 %collective-permute-start.35 = (bf16[512,512]{1,0:T(8,128)(2,1)}, bf16[512,512]{1,0:T(8,128)(2,1)}, u32[]{:S(2)}, u32[]{:S(2)}) collective-permute-start(bf16[512,512]{1,0:T(8,128)(2,1)} %get-tuple-element.182), channel_id=1, source_target_pairs={{0,1},{1,0},{2,3},{3,2},{4,5},{5,4},{6,7},{7,6},{8,9},{9,8},{10,11... | collective-permute-start | bytes 1572872 | tf_op jit(solution)/shard_map/ppermute | solution.py:847
  523.8 48.8 %collective-permute-start.36 = (bf16[512,512]{1,0:T(8,128)(2,1)}, bf16[512,512]{1,0:T(8,128)(2,1)}, u32[]{:S(2)}, u32[]{:S(2)}) collective-permute-start(bf16[512,512]{1,0:T(8,128)(2,1)} %get-tuple-element.183), channel_id=1, source_target_pairs={{0,2},{1,3},{2,0},{3,1},{4,6},{5,7},{6,4},{7,5},{8,10},{9,11},{10,... | collective-permute-start | bytes 1572872 | tf_op jit(solution)/shard_map/ppermute | solution.py:847
  546.4 26.2 %collective-permute-start.37 = (bf16[512,512]{1,0:T(8,128)(2,1)}, bf16[512,512]{1,0:T(8,128)(2,1)}, u32[]{:S(2)}, u32[]{:S(2)}) collective-permute-start(bf16[512,512]{1,0:T(8,128)(2,1)} %get-tuple-element.184), channel_id=1, source_target_pairs={{0,3},{1,2},{2,1},{3,0},{4,7},{5,6},{6,5},{7,4},{8,11},{9,10},{10,... | collective-permute-start | bytes 1572872 | tf_op jit(solution)/shard_map/ppermute | solution.py:847
  572.7 177.9 %reduce-scatter.11.cloned.1.call-start = ((), (), s32[]{:S(2)}) async-start(), calls=%async_computation.10 | async-start | bytes 5898240 | tf_op jit(solution)/shard_map/reduce_scatter | solution.py:1052
  575.4 28.0 %collective-permute-start.39 = (bf16[256,2048]{1,0:T(8,128)(2,1)}, bf16[256,2048]{1,0:T(8,128)(2,1)S(1)}, u32[]{:S(2)}, u32[]{:S(2)}) collective-permute-start(bf16[256,2048]{1,0:T(8,128)(2,1)} %get-tuple-element.194), channel_id=1, source_target_pairs={{0,1},{1,0},{2,3},{3,2},{4,5},{5,4},{6,7},{7,6},{8,9},{9,8},{10,11... | collective-permute-start | bytes 3145736 | tf_op jit(solution)/shard_map/ppermute | solution.py:847
  576.1 27.3 %collective-permute-start.40 = (bf16[256,2048]{1,0:T(8,128)(2,1)}, bf16[256,2048]{1,0:T(8,128)(2,1)}, u32[]{:S(2)}, u32[]{:S(2)}) collective-permute-start(bf16[256,2048]{1,0:T(8,128)(2,1)} %get-tuple-element.194), channel_id=1, source_target_pairs={{0,2},{1,3},{2,0},{3,1},{4,6},{5,7},{6,4},{7,5},{8,10},{9,11},{10,... | collective-permute-start | bytes 3145736 | tf_op jit(solution)/shard_map/ppermute | solution.py:847
  603.4 27.8 %collective-permute-start.41 = (bf16[256,2048]{1,0:T(8,128)(2,1)S(1)}, bf16[256,2048]{1,0:T(8,128)(2,1)}, u32[]{:S(2)}, u32[]{:S(2)}) collective-permute-start(bf16[256,2048]{1,0:T(8,128)(2,1)S(1)} %get-tuple-element.200), channel_id=1, source_target_pairs={{0,1},{1,0},{2,3},{3,2},{4,5},{5,4},{6,7},{7,6},{8,9},{9,8},{10,11... | collective-permute-start | bytes 3145736 | tf_op jit(solution)/shard_map/ppermute | solution.py:847
  604.4 26.9 %collective-permute-start.42 = (bf16[256,2048]{1,0:T(8,128)(2,1)S(1)}, bf16[256,2048]{1,0:T(8,128)(2,1)}, u32[]{:S(2)}, u32[]{:S(2)}) collective-permute-start(bf16[256,2048]{1,0:T(8,128)(2,1)S(1)} %get-tuple-element.200), channel_id=1, source_target_pairs={{0,2},{1,3},{2,0},{3,1},{4,6},{5,7},{6,4},{7,5},{8,10},{9,11},{10,... | collective-permute-start | bytes 3145736 | tf_op jit(solution)/shard_map/ppermute | solution.py:847
  604.8 77.0 %collective-permute-start.47 = (bf16[512,768]{1,0:T(8,128)(2,1)}, bf16[512,768]{1,0:T(8,128)(2,1)}, u32[]{:S(2)}, u32[]{:S(2)}) collective-permute-start(bf16[512,768]{1,0:T(8,128)(2,1)} %get-tuple-element.191.refs_5_), channel_id=1, source_target_pairs={{0,1},{1,0},{2,3},{3,2},{4,5},{5,4},{6,7},{7,6},{8,9},{9,8},{10,11... | collective-permute-start | bytes 2359304 | tf_op jit(solution)/shard_map/ppermute | solution.py:847
  631.3 37.6 %collective-permute-start.43 = (bf16[256,2048]{1,0:T(8,128)(2,1)}, bf16[256,2048]{1,0:T(8,128)(2,1)S(1)}, u32[]{:S(2)}, u32[]{:S(2)}) collective-permute-start(bf16[256,2048]{1,0:T(8,128)(2,1)} %collective-permute-done.40.refs_4_), channel_id=1, source_target_pairs={{0,1},{1,0},{2,3},{3,2},{4,5},{5,4},{6,7},{7,6},{8,9},{9,8},{10,11... | collective-permute-start | bytes 3145736 | tf_op jit(solution)/shard_map/ppermute | solution.py:847
  632.5 36.4 %collective-permute-start.44 = (bf16[256,2048]{1,0:T(8,128)(2,1)}, bf16[256,2048]{1,0:T(8,128)(2,1)}, u32[]{:S(2)}, u32[]{:S(2)}) collective-permute-start(bf16[256,2048]{1,0:T(8,128)(2,1)} %collective-permute-done.41.refs_2_), channel_id=1, source_target_pairs={{0,2},{1,3},{2,0},{3,1},{4,6},{5,7},{6,4},{7,5},{8,10},{9,11},{10,... | collective-permute-start | bytes 3145736 | tf_op jit(solution)/shard_map/ppermute | solution.py:847
  635.8 52.2 %collective-permute-start.48 = (bf16[512,768]{1,0:T(8,128)(2,1)}, bf16[512,768]{1,0:T(8,128)(2,1)S(1)}, u32[]{:S(2)}, u32[]{:S(2)}) collective-permute-start(bf16[512,768]{1,0:T(8,128)(2,1)} %get-tuple-element.197.refs_6_), channel_id=1, source_target_pairs={{0,2},{1,3},{2,0},{3,1},{4,6},{5,7},{6,4},{7,5},{8,10},{9,11},{10,... | collective-permute-start | bytes 2359304 | tf_op jit(solution)/shard_map/ppermute | solution.py:847
  636.2 51.9 %collective-permute-start.49 = (bf16[512,768]{1,0:T(8,128)(2,1)}, bf16[512,768]{1,0:T(8,128)(2,1)}, u32[]{:S(2)}, u32[]{:S(2)}) collective-permute-start(bf16[512,768]{1,0:T(8,128)(2,1)} %get-tuple-element.198.refs_7_), channel_id=1, source_target_pairs={{0,3},{1,2},{2,1},{3,0},{4,7},{5,6},{6,5},{7,4},{8,11},{9,10},{10,... | collective-permute-start | bytes 2359304 | tf_op jit(solution)/shard_map/ppermute | solution.py:847
  691.7 47.1 %collective-permute-start.46 = (bf16[256,2048]{1,0:T(8,128)(2,1)}, bf16[256,2048]{1,0:T(8,128)(2,1)S(1)}, u32[]{:S(2)}, u32[]{:S(2)}) collective-permute-start(bf16[256,2048]{1,0:T(8,128)(2,1)} %add_convert_fusion), channel_id=1, source_target_pairs={{0,1},{1,0},{2,3},{3,2},{4,5},{5,4},{6,7},{7,6},{8,9},{9,8},{10,11... | collective-permute-start | bytes 3145736 | tf_op jit(solution)/shard_map/ppermute | solution.py:847
  696.0 42.7 %collective-permute-start.45 = (bf16[256,2048]{1,0:T(8,128)(2,1)}, bf16[256,2048]{1,0:T(8,128)(2,1)S(1)}, u32[]{:S(2)}, u32[]{:S(2)}) collective-permute-start(bf16[256,2048]{1,0:T(8,128)(2,1)} %add_convert_fusion.1), channel_id=1, source_target_pairs={{0,2},{1,3},{2,0},{3,1},{4,6},{5,7},{6,4},{7,5},{8,10},{9,11},{10,... | collective-permute-start | bytes 3145736 | tf_op jit(solution)/shard_map/ppermute | solution.py:847
  (56 other events, 922.6 us)
Sparse Core Ops, SparseCore 0:
  10.2 58.7 all-gather.3
  71.2 115.4 all-gather.5
  189.0 114.9 all-gather.7
  329.7 90.0 reduce-scatter.4
  422.4 89.9 reduce-scatter.6
  572.8 90.0 reduce-scatter.8
  688.2 62.2 reduce-scatter.10

commit v5 on v4

--- a/solution.py
+++ b/solution.py
@@ -1167,7 +1167,7 @@
     out_near = sum_near(out, count)
     grad_resid, branch_low, gain_mlp = own_rows_call(
         resid_back_kernel,
-        after(two_rest, out[0], in_others),
+        after(two_rest, out[0]),
         [out_grad.reshape(2, half, width), resid],
         [norm_mlp[None, :]],
         [
@@ -1182,7 +1182,7 @@
     scattered_a = scatter_weights(grad_a)
     scattered_b = scatter_weights(after(grad_b, scattered_a, two[count - 1]))
     grad_down = contract_rows(
-        after(grad_rows, heads_out[0], scattered_b, out_first, out_near), act
+        after(grad_rows, heads_out[0], scattered_b, out_first), act
     ).astype(jnp.bfloat16)
     tops = bottoms = relays = []
     if count == 4:
@@ -1216,6 +1216,7 @@
     else:
         branch_near = gather_near(branch_low, count)
         branch = (branch_near[:inner_count], branch_near[inner_count:])
+    scattered_down = scatter_weights(after(grad_down, scattered_b, heads_in))
     grad_qkv = projection_weights(after(rows_in, raw_grads, bottoms), inv_rows, norm_attn, raw_grads)
     grad_w_gate = jnp.concatenate(
         [scattered_a[:, :units], scattered_b[:, :units]], axis=1
@@ -1223,10 +1224,9 @@
     grad_w_up = jnp.concatenate(
         [scattered_a[:, units:], scattered_b[:, units:]], axis=1
     ).astype(jnp.float32)
-    grad_attn = out_weights(inner, grad_qkv, after(branch, raw_grads, grad_w_gate, grad_w_up), attended)
+    grad_attn = out_weights(inner, grad_qkv, after(branch, raw_grads, grad_w_gate, grad_w_up, in_others), attended)
 
     out_adds = sum_adds(out, after(out_first, grad_attn)) if count == 4 else ()
-    scattered_down = scatter_weights(after(grad_down, scattered_b, heads_in))
     scattered_attn = scatter_weights(
         after(
             grad_attn, scattered_down, raw_in,

time: 772 us -> 750 us (0.972)
  waiting for transfers between devices: 120 us -> 99.8 us
    ppermute x55, waiting for transfers between devices: 117 us -> 99.7 us  [shift(): return lax.ppermute(values, axis, [(i, i ^ distance) for i in range(count)])]
    unnamed x93 -> x97, local copies, waits for them, and re-layouts: 18.9 us -> 16.5 us
  transfers between devices with their start and end apart: 62 -> 62, of which waited for: 19 -> 18; matrix products, arithmetic and copies ran while one was open for 17% -> 18% of each run, Pallas kernels for 56% -> 57%
where the time goes in v5:
time: 750 us; the launch traced here: 739 us
  Pallas kernels  425 us (57%)
  waiting for transfers between devices  99.8 us (13%)
  matrix products  71.8 us (10%)
  starting transfers between devices  55.1 us (7%)
  local copies, waits for them, and re-layouts  39.6 us (5%)
  other arithmetic  32.6 us (4%)
  between operations  15.2 us (2%)
    ppermute x55, waiting for transfers between devices, shift(): return lax.ppermute(values, axis, [(i, i ^ distance) for i in range(count)])  99.7 us
    pallas_call x4, Pallas kernels, rows_out(): pl.pallas_call(functools.partial(rows_out_kernel, len(lefts)), grid=(widt...  79.6 us
    pallas_call x1, Pallas kernels, gather_rows(): pl.pallas_call(gather_kernel, in_specs=[place], out_specs=[place] * 2, ou...  72.8 us
    dot_general x3, matrix products, contract_rows(): lax.dot_general(left, right, (((0,), (0,)), ((), ())), preferred_element_...  71.8 us
    ppermute x55, starting transfers between devices, shift(): return lax.ppermute(values, axis, [(i, i ^ distance) for i in range(count)])  54.9 us
    pallas_call x2, Pallas kernels, attend_back(): pl.pallas_call(functools.partial(attend_back_kernel, chunks), grid_spec=p...  51.2 us
    pallas_call x1, Pallas kernels, hidden_units(): pl.pallas_call(hidden_kernel, grid=(rows // block,), in_specs=[pl.BlockSp...  36 us
    pallas_call x1, Pallas kernels, residual(): pl.pallas_call(functools.partial(resid_kernel, count), grid_spec=pltpu.Pr...  32.3 us
  transfers between devices with their start and end apart: 62, of which 18 were waited for; matrix products, arithmetic and copies ran while one was open for 18% of the time, Pallas kernels for 57%

profile of v5, /device:TPU:0, one launch (start us, length us, event | category | flops | bytes accessed | tf_op | source)
XLA Modules:
  0.0 739.1 jit_solution(5951524969045276981)
XLA Ops:
  13.8 72.8 %shard_map.246 = (bf16[1024,2048]{1,0:T(8,128)(2,1)}, bf16[1024,2048]{1,0:T(8,128)(2,1)}) custom-call(bf16[512,2048]{1,0:T(8,128)(2,1)} %refs_11_.1), custom_call_target="tpu_custom_call" | custom-call | bytes 12582912 | tf_op jit(solution)/shard_map/pallas_call | solution.py:895
  95.2 5.9 fusion
  101.1 11.1 %shard_map.247 = (f32[1024,128]{1,0:T(8,128)}, bf16[1024,512]{1,0:T(8,128)(2,1)}, bf16[1024,512]{1,0:T(8,128)(2,1)}, bf16[1024,512]{1,0:T(8,128)(2,1)}, f32[1024,640]{1,0:T(8,128)}) custom-call(s32[1]{0:T(128)S(6)} %select_n.55.inner_ref, bf16[1024,2048]{1,0:T(8,128)(2,1)} %get-tuple-element.200.refs_0_, f32[1,2048]{1,0:T(1,128)} %bitcast.51, ...), custom_call_target="tpu_custom_call" | custom-call | flops 2928386816 | bytes 2516582 | tf_op jit(solution)/shard_map/pallas_call | solution.py:376
  112.2 9.5 %shard_map.248 = (bf16[1024,512]{1,0:T(8,128)(2,1)}, f32[1024,512]{1,0:T(8,128)}) custom-call(bf16[1024,512]{1,0:T(8,128)(2,1)} %get-tuple-element.127.q_ref, bf16[1024,512]{1,0:T(8,128)(2,1)} %get-tuple-element.128.k_ref, bf16[1024,512]{1,0:T(8,128)(2,1)} %get-tuple-element.129.v_ref, s32[1024,1]{1,0:T(8,128)} %copy.29.segc_ref, ...), custom_call_target="tpu_custom_call" | custom-call | flops 2254857728 | bytes 6291456 | tf_op jit(solution)/shard_map/pallas_call | solution.py:225
  123.7 11.8 %shard_map.249 = (f32[1024,128]{1,0:T(8,128)}, bf16[1024,512]{1,0:T(8,128)(2,1)}, bf16[1024,512]{1,0:T(8,128)(2,1)}, bf16[1024,512]{1,0:T(8,128)(2,1)}, f32[1024,640]{1,0:T(8,128)}) custom-call(s32[1]{0:T(128)S(6)} %select_n.55.inner_ref, bf16[1024,2048]{1,0:T(8,128)(2,1)} %get-tuple-element.201.refs_0_.refs_1_, f32[1,2048]{1,0:T(1,128)} %bitcast.52, ...), custom_call_target="tpu_custom_call" | custom-call | flops 2928386816 | bytes 2516582 | tf_op jit(solution)/shard_map/pallas_call | solution.py:376
  135.4 9.7 %shard_map.250 = (bf16[1024,512]{1,0:T(8,128)(2,1)}, f32[1024,512]{1,0:T(8,128)}) custom-call(bf16[1024,512]{1,0:T(8,128)(2,1)} %get-tuple-element.133.q_ref, bf16[1024,512]{1,0:T(8,128)(2,1)} %get-tuple-element.134.k_ref, bf16[1024,512]{1,0:T(8,128)(2,1)} %get-tuple-element.135.v_ref, s32[1024,1]{1,0:T(8,128)} %copy.30.segc_ref, ...), custom_call_target="tpu_custom_call" | custom-call | flops 2254857728 | bytes 6291456 | tf_op jit(solution)/shard_map/pallas_call | solution.py:225
  150.5 21.0 %collective-permute-done.3.refs_4_ = bf16[1024,512]{1,0:T(8,128)(2,1)S(1)} collective-permute-done((bf16[1024,512]{1,0:T(8,128)(2,1)}, bf16[1024,512]{1,0:T(8,128)(2,1)S(1)}, u32[]{:S(2)}, u32[]{:S(2)}) %collective-permute-start.3) | collective-permute-done | bytes 1048608 | tf_op jit(solution)/shard_map/ppermute | solution.py:847
  174.4 8.8 %collective-permute-done.8 = bf16[512,512]{1,0:T(8,128)(2,1)S(1)} collective-permute-done((bf16[512,512]{1,0:T(8,128)(2,1)S(1)}, bf16[512,512]{1,0:T(8,128)(2,1)S(1)}, u32[]{:S(2)}, u32[]{:S(2)}) %collective-permute-start.8) | collective-permute-done | bytes 524320 | tf_op jit(solution)/shard_map/ppermute | solution.py:847
  184.8 9.6 %collective-permute-done.4 = bf16[512,512]{1,0:T(8,128)(2,1)S(1)} collective-permute-done((bf16[512,512]{1,0:T(8,128)(2,1)S(1)}, bf16[512,512]{1,0:T(8,128)(2,1)S(1)}, u32[]{:S(2)}, u32[]{:S(2)}) %collective-permute-start.4) | collective-permute-done | bytes 524320 | tf_op jit(solution)/shard_map/ppermute | solution.py:847
  196.6 9.1 %collective-permute-done.10 = bf16[512,512]{1,0:T(8,128)(2,1)S(1)} collective-permute-done((bf16[512,512]{1,0:T(8,128)(2,1)S(1)}, bf16[512,512]{1,0:T(8,128)(2,1)S(1)}, u32[]{:S(2)}, u32[]{:S(2)}) %collective-permute-start.10) | collective-permute-done | bytes 524320 | tf_op jit(solution)/shard_map/ppermute | solution.py:847
  210.9 32.3 %shard_map.251 = (bf16[2048,2048]{1,0:T(8,128)(2,1)}, f32[1,512,2048]{2,1,0:T(8,128)}) custom-call(s32[2]{0:T(128)} %pad_add_fusion.place_ref, bf16[1024,2048]{1,0:T(8,128)(2,1)} %get-tuple-element.200.refs_0_, bf16[1024,2048]{1,0:T(8,128)(2,1)} %get-tuple-element.201.refs_0_.refs_1_, bf16[1024,512]{1,0:T(8,128)(2,1)} %get-tuple-element.130.refs_2_.out_ref.refs_3_, ...), custom_call_target="tpu_custom_call" | custom-call | flops 7469508096 | bytes 6710886 | tf_op jit(solution)/shard_map/pallas_call | solution.py:667
  243.2 3.9 collective-permute-done.15
  247.1 2.3 slice.118
  255.2 3.2 constant_dynamic-update-slice_fusion.9
  258.5 3.1 constant_dynamic-update-slice_fusion.8
  261.6 25.6 %shard_map.252 = (bf16[2048,2048]{1,0:T(8,128)(2,1)}, bf16[2048,2048]{1,0:T(8,128)(2,1)}) custom-call(bf16[2048,2048]{1,0:T(8,128)(2,1)} %get-tuple-element.151.x_ref, bf16[2048,3072]{1,0:T(8,128)(2,1)} %all-gather.6.cloned.1.call-done.w_ref.refs_2_), custom_call_target="tpu_custom_call" | custom-call | flops 5453926912 | bytes 5033164 | tf_op jit(solution)/shard_map/pallas_call | solution.py:525
  288.3 2.4 constant_dynamic-update-slice_fusion.6.dy_ref
  290.6 15.2 %shard_map.253.refs_0_ = bf16[2048,2048]{1,0:T(8,128)(2,1)} custom-call(bf16[2048,2048]{1,0:T(8,128)(2,1)} %constant_dynamic-update-slice_fusion.6.dy_ref, bf16[2048,2048]{1,0:T(8,128)(2,1)} %get-tuple-element.147.factors_ref, bf16[2048,3072]{1,0:T(8,128)(2,1)} %all-gather.6.cloned.1.call-done.w_ref.refs_2_), custom_call_target="tpu_custom_call" | custom-call | flops 2726963456 | bytes 5033164 | tf_op jit(solution)/shard_map/pallas_call | solution.py:557
  305.8 23.7 %convolution_convert_fusion.2 = bf16[2048,2048]{1,0:T(8,128)(2,1)} fusion(bf16[2048,2048]{1,0:T(8,128)(2,1)} %get-tuple-element.151.x_ref, bf16[2048,2048]{1,0:T(8,128)(2,1)} %shard_map.253.refs_0_), kind=kOutput, calls=%fused_computation.2 | convolution fusion | flops 17184063488 | bytes 25165824 | tf_op jit(solution)/shard_map/dot_general | solution.py:38
  333.3 36.0 %shard_map.254 = (bf16[2048,2048]{1,0:T(8,128)(2,1)}, bf16[2048,2048]{1,0:T(8,128)(2,1)}) custom-call(bf16[2048,2048]{1,0:T(8,128)(2,1)} %get-tuple-element.151.x_ref, bf16[2048,2048]{1,0:T(8,128)(2,1)} %constant_dynamic-update-slice_fusion.6.dy_ref, bf16[2048,3072]{1,0:T(8,128)(2,1)} %all-gather.8.cloned.1.call-done.w_ref.refs_3_, ...), custom_call_target="tpu_custom_call", output_to_operand_aliasing={{0}: (3, {})} | custom-call | flops 8180890112 | bytes 7549747 | tf_op jit(solution)/shard_map/pallas_call | solution.py:486
  373.8 23.9 %convolution_convert_fusion.1 = bf16[2048,2048]{1,0:T(8,128)(2,1)} fusion(bf16[2048,2048]{1,0:T(8,128)(2,1)} %get-tuple-element.151.x_ref, bf16[2048,2048]{1,0:T(8,128)(2,1)} %get-tuple-element.152.refs_1_), kind=kOutput, calls=%fused_computation.1 | convolution fusion | flops 17184063488 | bytes 25165824 | tf_op jit(solution)/shard_map/dot_general | solution.py:38
  397.7 24.6 %shard_map.255 = (f32[256,2048]{1,0:T(8,128)}, bf16[256,2048]{1,0:T(8,128)(2,1)}, bf16[256,2048]{1,0:T(8,128)(2,1)}, bf16[256,2048]{1,0:T(8,128)(2,1)}) custom-call(bf16[2048,2048]{1,0:T(8,128)(2,1)} %shard_map.253.refs_0_, bf16[2048,2048]{1,0:T(8,128)(2,1)} %get-tuple-element.152.refs_1_, bf16[2048,3072]{1,0:T(8,128)(2,1)} %all-gather.6.cloned.1.call-done.w_ref.refs_2_, ...), custom_call_target="tpu_custom_call" | custom-call | flops 844219584 | bytes 209715 | tf_op jit(solution)/shard_map/pallas_call | solution.py:608
  424.6 15.5 %shard_map.256 = (bf16[256,2048]{1,0:T(8,128)(2,1)}, f32[256,2048]{1,0:T(8,128)}) custom-call(bf16[2048,2048]{1,0:T(8,128)(2,1)} %shard_map.253.refs_0_, bf16[2048,2048]{1,0:T(8,128)(2,1)} %get-tuple-element.152.refs_1_, bf16[2048,3072]{1,0:T(8,128)(2,1)} %all-gather.6.cloned.1.call-done.w_ref.refs_2_, ...), custom_call_target="tpu_custom_call" | custom-call | flops 422109792 | bytes 104857 | tf_op jit(solution)/shard_map/pallas_call | solution.py:608
  442.2 4.9 collective-permute-done.24
  447.1 3.1 add_convert_fusion.2
  451.6 2.6 add_convert_fusion.3
  456.5 15.3 %shard_map.257 = (f32[256,2048]{1,0:T(8,128)}, f32[256,2048]{1,0:T(8,128)}) custom-call(bf16[2048,2048]{1,0:T(8,128)(2,1)} %shard_map.253.refs_0_, bf16[2048,2048]{1,0:T(8,128)(2,1)} %get-tuple-element.152.refs_1_, bf16[2048,3072]{1,0:T(8,128)(2,1)} %all-gather.6.cloned.1.call-done.w_ref.refs_2_, bf16[2048,3072]{1,0:T(8,128)(2,1)} %all-gather.8.cloned.1.call-done.w_ref.refs_3_), custom_call_target="tpu_custom_call" | custom-call | flops 422109792 | bytes 104857 | tf_op jit(solution)/shard_map/pallas_call | solution.py:608
  471.8 24.2 %shard_map.258 = (f32[256,2048]{1,0:T(8,128)}, f32[256,2048]{1,0:T(8,128)}, bf16[256,2048]{1,0:T(8,128)(2,1)}, f32[256,2048]{1,0:T(8,128)}, f32[256,2048]{1,0:T(...) custom-call(bf16[2048,2048]{1,0:T(8,128)(2,1)} %get-tuple-element.163.refs_0_.refs_1_, ...), custom_call_target="tpu_custom_call" | custom-call | flops 844219584 | bytes 209715 | tf_op jit(solution)/shard_map/pallas_call | solution.py:608
  498.3 9.5 %shard_map.259 = (f32[2,256,2048]{2,1,0:T(8,128)}, bf16[2,256,2048]{2,1,0:T(8,128)(2,1)}, f32[8,2048]{1,0:T(8,128)}) custom-call(f32[256,2048]{1,0:T(8,128)} %get-tuple-element.173.refs_0_, bf16[256,2048]{1,0:T(8,128)(2,1)} %copy-done.21, bf16[256,2048]{1,0:T(8,128)(2,1)} %collective-permute-done.29.refs_2_, f32[256,2048]{1,0:T(8,128)} %get-tuple-element.176.refs_3_, ...), custom_call_target="tpu_custom_call" | custom-call | flops 1048576 | bytes 1048576 | tf_op jit(solution)/shard_map/pallas_call | solution.py:995
  507.8 9.4 %shard_map.260 = (bf16[512,512]{1,0:T(8,128)(2,1)}, bf16[512,512]{1,0:T(8,128)(2,1)}, bf16[512,512]{1,0:T(8,128)(2,1)}, bf16[512,512]{1,0:T(8,128)(2,1)}) custom-call(s32[1]{0:T(128)S(6)} %select_n.56.core_ref, bf16[512,2048]{1,0:T(8,128)(2,1)} %bitcast.43, bf16[2048,1280]{1,0:T(8,128)(2,1)} %all-gather.4.cloned.1.call-done.refs_2_.refs_10_.refs_0_.refs_4_, ...), custom_call_target="tpu_custom_call" | custom-call | flops 321720384 | bytes 209715 | tf_op jit(solution)/shard_map/pallas_call | solution.py:428
  520.7 24.2 %convolution_convert_fusion = bf16[2048,2048]{1,0:T(8,128)(2,1)} fusion(bf16[2048,2048]{1,0:T(8,128)(2,1)} %constant_dynamic-update-slice_fusion.6.dy_ref, bf16[2048,2048]{1,0:T(8,128)(2,1)} %get-tuple-element.163.refs_0_.refs_1_), kind=kOutput, calls=%fused_computation | convolution fusion | flops 17184063488 | bytes 25165824 | tf_op jit(solution)/shard_map/dot_general | solution.py:38
  551.7 25.4 %shard_map.261 = (bf16[512,768]{1,0:T(8,128)(2,1)}, bf16[512,768]{1,0:T(8,128)(2,1)}, f32[8,128]{1,0:T(8,128)}, f32[8,128]{1,0:T(8,128)}) custom-call(s32[1]{0:T(128)S(6)} %select_n.55.inner_ref, bf16[1024,512]{1,0:T(8,128)(2,1)} %get-tuple-element.127.q_ref, bf16[1024,512]{1,0:T(8,128)(2,1)} %get-tuple-element.128.k_ref, ...), custom_call_target="tpu_custom_call" | custom-call | flops 5905580032 | bytes 10485760 | tf_op jit(solution)/shard_map/pallas_call | solution.py:258
  579.9 25.8 %shard_map.262 = (bf16[512,768]{1,0:T(8,128)(2,1)}, bf16[512,768]{1,0:T(8,128)(2,1)}, f32[8,128]{1,0:T(8,128)}, f32[8,128]{1,0:T(8,128)}) custom-call(s32[1]{0:T(128)S(6)} %select_n.55.inner_ref, bf16[1024,512]{1,0:T(8,128)(2,1)} %get-tuple-element.133.q_ref, bf16[1024,512]{1,0:T(8,128)(2,1)} %get-tuple-element.134.k_ref, ...), custom_call_target="tpu_custom_call" | custom-call | flops 5905580032 | bytes 10485760 | tf_op jit(solution)/shard_map/pallas_call | solution.py:258
  615.2 13.0 %shard_map.263.beside_ref = bf16[2048,768]{1,0:T(8,128)(2,1)} custom-call(f32[1,2048]{1,0:T(1,128)} %bitcast.53, bf16[1024,2048]{1,0:T(8,128)(2,1)} %get-tuple-element.200.refs_0_, bf16[1024,2048]{1,0:T(8,128)(2,1)} %get-tuple-element.201.refs_0_.refs_1_, f32[1024,128]{1,0:T(8,128)} %get-tuple-element.202.refs_2_, f32[1024,128]{1,0:T(8,128)} %get-tuple-element.203.refs_3_, ...), custom_call_target="tpu_custom_call" | custom-call | flops 2996488704 | bytes 1677721 | tf_op jit(solution)/shard_map/pallas_call | solution.py:832
  628.2 3.9 collective-permute-done.39.refs_6_
  633.8 11.9 %shard_map.264 = bf16[2048,1280]{1,0:T(8,128)(2,1)} custom-call(s32[1]{0:T(128)S(6)} %select_n.55.inner_ref, bf16[2048,768]{1,0:T(8,128)(2,1)} %shard_map.263.beside_ref, bf16[512,2048]{1,0:T(8,128)(2,1)} %bitcast.44, bf16[256,2048]{1,0:T(8,128)(2,1)} %collective-permute-done.35.refs_1_, bf16[256,2048]{1,0:T(8,128)(2,1)} %collective-permute-done.37.refs_2_, ...), custom_call_target="tpu_custom_call" | custom-call | flops 2454267136 | bytes 1677721 | tf_op jit(solution)/shard_map/pallas_call | solution.py:798
  645.7 3.3 collective-permute-done.47.refs_1_
  649.0 15.9 %collective-permute-done.48.refs_2_ = bf16[512,768]{1,0:T(8,128)(2,1)} collective-permute-done((bf16[512,768]{1,0:T(8,128)(2,1)}, bf16[512,768]{1,0:T(8,128)(2,1)}, u32[]{:S(2)}, u32[]{:S(2)}) %collective-permute-start.48) | collective-permute-done | bytes 786464 | tf_op jit(solution)/shard_map/ppermute | solution.py:847
  668.6 2.7 add_convert_fusion
  672.2 2.7 add_convert_fusion.1
  676.3 2.8 convert_element_type.87
  679.1 19.9 %shard_map.265 = (f32[512,2048]{1,0:T(8,128)}, f32[8,2048]{1,0:T(8,128)}) custom-call(s32[1]{0:T(128)S(6)} %select_n.56.core_ref, bf16[512,768]{1,0:T(8,128)(2,1)} %get-tuple-element.218.refs_4_.refs_0_, bf16[512,768]{1,0:T(8,128)(2,1)} %collective-permute-done.47.refs_1_, bf16[512,768]{1,0:T(8,128)(2,1)} %collective-permute-done.48.refs_2_, ...), custom_call_target="tpu_custom_call" | custom-call | flops 4601750528 | bytes 4194304 | tf_op jit(solution)/shard_map/pallas_call | solution.py:743
  702.8 2.8 collective-permute-done.51
  705.6 2.4 collective-permute-start.52
  708.1 3.2 collective-permute-done.52
  712.0 3.1 collective-permute-done.53
  716.0 2.8 collective-permute-done.54
  720.6 6.5 shard_map.266
  (271 shorter events, 101.7 us)
Async XLA Ops:
  7.2 80.3 %all-gather.4.cloned.1.call-start = ((), (), s32[]{:S(2)}) async-start(), calls=%async_computation.4 | async-start | bytes 5898240 | tf_op jit(solution)/shard_map/all_gather | solution.py:1048
  9.4 252.2 %all-gather.6.cloned.1.call-start = ((), (), s32[]{:S(2)}) async-start(), calls=%async_computation.5 | async-start | bytes 14155776 | tf_op jit(solution)/shard_map/all_gather | solution.py:1048
  12.1 321.2 %all-gather.8.cloned.1.call-start = ((), (), s32[]{:S(2)}) async-start(), calls=%async_computation.6 | async-start | bytes 14155776 | tf_op jit(solution)/shard_map/all_gather | solution.py:1048
  13.5 408.8 %reduce-scatter.5.cloned.1.call-start = ((), (), s32[]{:S(2)}) async-start(), calls=%async_computation.7 | async-start | bytes 9437184 | tf_op jit(solution)/shard_map/reduce_scatter | solution.py:1052
  89.8 33.8 %collective-permute-start.1 = (bf16[1024,512]{1,0:T(8,128)(2,1)}, bf16[1024,512]{1,0:T(8,128)(2,1)S(1)}, u32[]{:S(2)}, u32[]{:S(2)}) collective-permute-start(bf16[1024,512]{1,0:T(8,128)(2,1)} %constant_dynamic-slice_fusion.1), channel_id=1, source_target_pairs={{0,1},{1,0},{2,3},{3,2},{4,5},{5,4},{6,7},{7,6},{8,9},{9,8},{10,11... | collective-permute-start | bytes 3145736 | tf_op jit(solution)/shard_map/ppermute | solution.py:847
  90.4 33.2 %collective-permute-start.2 = (bf16[1024,512]{1,0:T(8,128)(2,1)}, bf16[1024,512]{1,0:T(8,128)(2,1)S(1)}, u32[]{:S(2)}, u32[]{:S(2)}) collective-permute-start(bf16[1024,512]{1,0:T(8,128)(2,1)} %constant_dynamic-slice_fusion.1), channel_id=1, source_target_pairs={{0,2},{1,3},{2,0},{3,1},{4,6},{5,7},{6,4},{7,5},{8,10},{9,11},{10,... | collective-permute-start | bytes 3145736 | tf_op jit(solution)/shard_map/ppermute | solution.py:847
  121.7 25.5 %collective-permute-start.7 = (bf16[1024,512]{1,0:T(8,128)(2,1)}, bf16[1024,512]{1,0:T(8,128)(2,1)S(1)}, u32[]{:S(2)}, u32[]{:S(2)}) collective-permute-start(bf16[1024,512]{1,0:T(8,128)(2,1)} %get-tuple-element.130.refs_2_.out_ref.refs_3_), channel_id=1, source_target_pairs={{0,2},{1,3},{2,0},{3,1},{4,6},{5,7},{6,4},{7,5},{8,10},{9,11},{10,... | collective-permute-start | bytes 3145736 | tf_op jit(solution)/shard_map/ppermute | solution.py:847
  122.2 25.6 %collective-permute-start = (bf16[1024,512]{1,0:T(8,128)(2,1)}, bf16[1024,512]{1,0:T(8,128)(2,1)}, u32[]{:S(2)}, u32[]{:S(2)}) collective-permute-start(bf16[1024,512]{1,0:T(8,128)(2,1)} %get-tuple-element.130.refs_2_.out_ref.refs_3_), channel_id=1, source_target_pairs={{0,1},{1,0},{2,3},{3,2},{4,5},{5,4},{6,7},{7,6},{8,9},{9,8},{10,11... | collective-permute-start | bytes 3145736 | tf_op jit(solution)/shard_map/ppermute | solution.py:847
  145.1 26.4 %collective-permute-start.3 = (bf16[1024,512]{1,0:T(8,128)(2,1)}, bf16[1024,512]{1,0:T(8,128)(2,1)S(1)}, u32[]{:S(2)}, u32[]{:S(2)}) collective-permute-start(bf16[1024,512]{1,0:T(8,128)(2,1)} %get-tuple-element.136.refs_6_.out_ref.refs_8_), channel_id=1, source_target_pairs={{0,2},{1,3},{2,0},{3,1},{4,6},{5,7},{6,4},{7,5},{8,10},{9,11},{10,... | collective-permute-start | bytes 3145736 | tf_op jit(solution)/shard_map/ppermute | solution.py:847
  145.7 26.4 %collective-permute-start.5 = (bf16[1024,512]{1,0:T(8,128)(2,1)}, bf16[1024,512]{1,0:T(8,128)(2,1)S(1)}, u32[]{:S(2)}, u32[]{:S(2)}) collective-permute-start(bf16[1024,512]{1,0:T(8,128)(2,1)} %get-tuple-element.136.refs_6_.out_ref.refs_8_), channel_id=1, source_target_pairs={{0,1},{1,0},{2,3},{3,2},{4,5},{5,4},{6,7},{7,6},{8,9},{9,8},{10,11... | collective-permute-start | bytes 3145736 | tf_op jit(solution)/shard_map/ppermute | solution.py:847
  147.2 36.0 %collective-permute-start.8 = (bf16[512,512]{1,0:T(8,128)(2,1)S(1)}, bf16[512,512]{1,0:T(8,128)(2,1)S(1)}, u32[]{:S(2)}, u32[]{:S(2)}) collective-permute-start(bf16[512,512]{1,0:T(8,128)(2,1)S(1)} %slice.150), channel_id=1, source_target_pairs={{0,1},{1,0},{2,3},{3,2},{4,5},{5,4},{6,7},{7,6},{8,9},{9,8},{10,11... | collective-permute-start | bytes 1572872 | tf_op jit(solution)/shard_map/ppermute | solution.py:847
  148.9 35.9 %collective-permute-start.9 = (bf16[512,512]{1,0:T(8,128)(2,1)S(1)}, bf16[512,512]{1,0:T(8,128)(2,1)S(1)}, u32[]{:S(2)}, u32[]{:S(2)}) collective-permute-start(bf16[512,512]{1,0:T(8,128)(2,1)S(1)} %slice.151), channel_id=1, source_target_pairs={{0,2},{1,3},{2,0},{3,1},{4,6},{5,7},{6,4},{7,5},{8,10},{9,11},{10,... | collective-permute-start | bytes 1572872 | tf_op jit(solution)/shard_map/ppermute | solution.py:847
  173.8 31.9 %collective-permute-start.10 = (bf16[512,512]{1,0:T(8,128)(2,1)S(1)}, bf16[512,512]{1,0:T(8,128)(2,1)S(1)}, u32[]{:S(2)}, u32[]{:S(2)}) collective-permute-start(bf16[512,512]{1,0:T(8,128)(2,1)S(1)} %slice.116), channel_id=1, source_target_pairs={{0,1},{1,0},{2,3},{3,2},{4,5},{5,4},{6,7},{7,6},{8,9},{9,8},{10,11... | collective-permute-start | bytes 1572872 | tf_op jit(solution)/shard_map/ppermute | solution.py:847
  194.6 52.6 %collective-permute-start.15 = (bf16[512,2048]{1,0:T(8,128)(2,1)S(1)}, bf16[512,2048]{1,0:T(8,128)(2,1)}, u32[]{:S(2)}, u32[]{:S(2)}) collective-permute-start(bf16[512,2048]{1,0:T(8,128)(2,1)S(1)} %copy-done.1), channel_id=1, source_target_pairs={{0,1},{1,0},{2,3},{3,2},{4,5},{5,4},{6,7},{7,6},{8,9},{9,8},{10,11... | collective-permute-start | bytes 6291464 | tf_op jit(solution)/shard_map/ppermute | solution.py:847
  196.2 51.0 %collective-permute-start.16 = (bf16[512,2048]{1,0:T(8,128)(2,1)S(1)}, bf16[512,2048]{1,0:T(8,128)(2,1)}, u32[]{:S(2)}, u32[]{:S(2)}) collective-permute-start(bf16[512,2048]{1,0:T(8,128)(2,1)S(1)} %copy-done.1), channel_id=1, source_target_pairs={{0,2},{1,3},{2,0},{3,1},{4,6},{5,7},{6,4},{7,5},{8,10},{9,11},{10,... | collective-permute-start | bytes 6291464 | tf_op jit(solution)/shard_map/ppermute | solution.py:847
  249.5 37.7 %collective-permute-start.17 = (bf16[256,2048]{1,0:T(8,128)(2,1)}, bf16[256,2048]{1,0:T(8,128)(2,1)S(1)}, u32[]{:S(2)}, u32[]{:S(2)}) collective-permute-start(bf16[256,2048]{1,0:T(8,128)(2,1)} %slice.118), channel_id=1, source_target_pairs={{0,1},{1,0},{2,3},{3,2},{4,5},{5,4},{6,7},{7,6},{8,9},{9,8},{10,11... | collective-permute-start | bytes 3145736 | tf_op jit(solution)/shard_map/ppermute | solution.py:847
  253.3 33.9 %collective-permute-start.18 = (bf16[256,2048]{1,0:T(8,128)(2,1)}, bf16[256,2048]{1,0:T(8,128)(2,1)}, u32[]{:S(2)}, u32[]{:S(2)}) collective-permute-start(bf16[256,2048]{1,0:T(8,128)(2,1)} %slice.119), channel_id=1, source_target_pairs={{0,2},{1,3},{2,0},{3,1},{4,6},{5,7},{6,4},{7,5},{8,10},{9,11},{10,... | collective-permute-start | bytes 3145736 | tf_op jit(solution)/shard_map/ppermute | solution.py:847
  329.6 191.2 %reduce-scatter.7.cloned.1.call-start = ((), (), s32[]{:S(2)}) async-start(), calls=%async_computation.8 | async-start | bytes 9437184 | tf_op jit(solution)/shard_map/reduce_scatter | solution.py:1052
  331.1 38.2 %collective-permute-start.19 = (bf16[1024,768]{1,0:T(8,128)(2,1)S(1)}, bf16[1024,768]{1,0:T(8,128)(2,1)}, u32[]{:S(2)}, u32[]{:S(2)}) collective-permute-start(bf16[1024,768]{1,0:T(8,128)(2,1)S(1)} %constant_dynamic-slice_fusion), channel_id=1, source_target_pairs={{0,1},{1,0},{2,3},{3,2},{4,5},{5,4},{6,7},{7,6},{8,9},{9,8},{10,11... | collective-permute-start | bytes 4718600 | tf_op jit(solution)/shard_map/ppermute | solution.py:847
  332.7 36.6 %collective-permute-start.20 = (bf16[1024,768]{1,0:T(8,128)(2,1)S(1)}, bf16[1024,768]{1,0:T(8,128)(2,1)}, u32[]{:S(2)}, u32[]{:S(2)}) collective-permute-start(bf16[1024,768]{1,0:T(8,128)(2,1)S(1)} %constant_dynamic-slice_fusion), channel_id=1, source_target_pairs={{0,2},{1,3},{2,0},{3,1},{4,6},{5,7},{6,4},{7,5},{8,10},{9,11},{10,... | collective-permute-start | bytes 4718600 | tf_op jit(solution)/shard_map/ppermute | solution.py:847
  370.5 27.1 %collective-permute-start.21 = (bf16[512,768]{1,0:T(8,128)(2,1)S(1)}, bf16[512,768]{1,0:T(8,128)(2,1)S(1)}, u32[]{:S(2)}, u32[]{:S(2)}) collective-permute-start(bf16[512,768]{1,0:T(8,128)(2,1)S(1)} %slice.152), channel_id=1, source_target_pairs={{0,1},{1,0},{2,3},{3,2},{4,5},{5,4},{6,7},{7,6},{8,9},{9,8},{10,11... | collective-permute-start | bytes 2359304 | tf_op jit(solution)/shard_map/ppermute | solution.py:847
  422.3 244.0 %reduce-scatter.9.cloned.1.call-start = ((), (), s32[]{:S(2)}) async-start(), calls=%async_computation.9 | async-start | bytes 9437184 | tf_op jit(solution)/shard_map/reduce_scatter | solution.py:1052
  422.4 24.8 %collective-permute-start.24 = (bf16[256,2048]{1,0:T(8,128)(2,1)}, bf16[256,2048]{1,0:T(8,128)(2,1)S(1)}, u32[]{:S(2)}, u32[]{:S(2)}) collective-permute-start(bf16[256,2048]{1,0:T(8,128)(2,1)} %get-tuple-element.155), channel_id=1, source_target_pairs={{0,2},{1,3},{2,0},{3,1},{4,6},{5,7},{6,4},{7,5},{8,10},{9,11},{10,... | collective-permute-start | bytes 3145736 | tf_op jit(solution)/shard_map/ppermute | solution.py:847
  423.9 27.6 %collective-permute-start.23 = (bf16[256,2048]{1,0:T(8,128)(2,1)}, bf16[256,2048]{1,0:T(8,128)(2,1)}, u32[]{:S(2)}, u32[]{:S(2)}) collective-permute-start(bf16[256,2048]{1,0:T(8,128)(2,1)} %get-tuple-element.154), channel_id=1, source_target_pairs={{0,1},{1,0},{2,3},{3,2},{4,5},{5,4},{6,7},{7,6},{8,9},{9,8},{10,11... | collective-permute-start | bytes 3145736 | tf_op jit(solution)/shard_map/ppermute | solution.py:847
  440.1 56.5 %collective-permute-start.28 = (bf16[256,2048]{1,0:T(8,128)(2,1)}, bf16[256,2048]{1,0:T(8,128)(2,1)S(1)}, u32[]{:S(2)}, u32[]{:S(2)}) collective-permute-start(bf16[256,2048]{1,0:T(8,128)(2,1)} %get-tuple-element.157), channel_id=1, source_target_pairs={{0,1},{1,0},{2,3},{3,2},{4,5},{5,4},{6,7},{7,6},{8,9},{9,8},{10,11... | collective-permute-start | bytes 3145736 | tf_op jit(solution)/shard_map/ppermute | solution.py:847
  441.6 55.0 %collective-permute-start.31 = (bf16[256,2048]{1,0:T(8,128)(2,1)}, bf16[256,2048]{1,0:T(8,128)(2,1)S(1)}, u32[]{:S(2)}, u32[]{:S(2)}) collective-permute-start(bf16[256,2048]{1,0:T(8,128)(2,1)} %get-tuple-element.171), channel_id=1, source_target_pairs={{0,2},{1,3},{2,0},{3,1},{4,6},{5,7},{6,4},{7,5},{8,10},{9,11},{10,... | collective-permute-start | bytes 3145736 | tf_op jit(solution)/shard_map/ppermute | solution.py:847
  450.2 46.5 %collective-permute-start.30 = (bf16[256,2048]{1,0:T(8,128)(2,1)}, bf16[256,2048]{1,0:T(8,128)(2,1)S(1)}, u32[]{:S(2)}, u32[]{:S(2)}) collective-permute-start(bf16[256,2048]{1,0:T(8,128)(2,1)} %add_convert_fusion.2), channel_id=1, source_target_pairs={{0,1},{1,0},{2,3},{3,2},{4,5},{5,4},{6,7},{7,6},{8,9},{9,8},{10,11... | collective-permute-start | bytes 3145736 | tf_op jit(solution)/shard_map/ppermute | solution.py:847
  454.1 42.6 %collective-permute-start.29 = (bf16[256,2048]{1,0:T(8,128)(2,1)}, bf16[256,2048]{1,0:T(8,128)(2,1)}, u32[]{:S(2)}, u32[]{:S(2)}) collective-permute-start(bf16[256,2048]{1,0:T(8,128)(2,1)} %add_convert_fusion.3), channel_id=1, source_target_pairs={{0,2},{1,3},{2,0},{3,1},{4,6},{5,7},{6,4},{7,5},{8,10},{9,11},{10,... | collective-permute-start | bytes 3145736 | tf_op jit(solution)/shard_map/ppermute | solution.py:847
  496.0 24.8 %collective-permute-start.26 = (bf16[256,2048]{1,0:T(8,128)(2,1)}, bf16[256,2048]{1,0:T(8,128)(2,1)}, u32[]{:S(2)}, u32[]{:S(2)}) collective-permute-start(bf16[256,2048]{1,0:T(8,128)(2,1)} %get-tuple-element.167), channel_id=1, source_target_pairs={{0,1},{1,0},{2,3},{3,2},{4,5},{5,4},{6,7},{7,6},{8,9},{9,8},{10,11... | collective-permute-start | bytes 3145736 | tf_op jit(solution)/shard_map/ppermute | solution.py:847
  517.2 27.7 %collective-permute-start.32 = (bf16[512,512]{1,0:T(8,128)(2,1)}, bf16[512,512]{1,0:T(8,128)(2,1)}, u32[]{:S(2)}, u32[]{:S(2)}) collective-permute-start(bf16[512,512]{1,0:T(8,128)(2,1)} %get-tuple-element.182), channel_id=1, source_target_pairs={{0,1},{1,0},{2,3},{3,2},{4,5},{5,4},{6,7},{7,6},{8,9},{9,8},{10,11... | collective-permute-start | bytes 1572872 | tf_op jit(solution)/shard_map/ppermute | solution.py:847
  518.7 26.3 %collective-permute-start.33 = (bf16[512,512]{1,0:T(8,128)(2,1)}, bf16[512,512]{1,0:T(8,128)(2,1)S(1)}, u32[]{:S(2)}, u32[]{:S(2)}) collective-permute-start(bf16[512,512]{1,0:T(8,128)(2,1)} %get-tuple-element.183), channel_id=1, source_target_pairs={{0,2},{1,3},{2,0},{3,1},{4,6},{5,7},{6,4},{7,5},{8,10},{9,11},{10,... | collective-permute-start | bytes 1572872 | tf_op jit(solution)/shard_map/ppermute | solution.py:847
  545.9 182.3 %reduce-scatter.11.cloned.1.call-start = ((), (), s32[]{:S(2)}) async-start(), calls=%async_computation.10 | async-start | bytes 5898240 | tf_op jit(solution)/shard_map/reduce_scatter | solution.py:1052
  548.1 29.0 %collective-permute-start.35 = (bf16[256,2048]{1,0:T(8,128)(2,1)S(1)}, bf16[256,2048]{1,0:T(8,128)(2,1)}, u32[]{:S(2)}, u32[]{:S(2)}) collective-permute-start(bf16[256,2048]{1,0:T(8,128)(2,1)S(1)} %get-tuple-element.193), channel_id=1, source_target_pairs={{0,1},{1,0},{2,3},{3,2},{4,5},{5,4},{6,7},{7,6},{8,9},{9,8},{10,11... | collective-permute-start | bytes 3145736 | tf_op jit(solution)/shard_map/ppermute | solution.py:847
  549.5 27.6 %collective-permute-start.36 = (bf16[256,2048]{1,0:T(8,128)(2,1)S(1)}, bf16[256,2048]{1,0:T(8,128)(2,1)}, u32[]{:S(2)}, u32[]{:S(2)}) collective-permute-start(bf16[256,2048]{1,0:T(8,128)(2,1)S(1)} %get-tuple-element.193), channel_id=1, source_target_pairs={{0,2},{1,3},{2,0},{3,1},{4,6},{5,7},{6,4},{7,5},{8,10},{9,11},{10,... | collective-permute-start | bytes 3145736 | tf_op jit(solution)/shard_map/ppermute | solution.py:847
  551.1 59.0 %collective-permute-start.41 = (bf16[1024,768]{1,0:T(8,128)(2,1)}, bf16[1024,768]{1,0:T(8,128)(2,1)}, u32[]{:S(2)}, u32[]{:S(2)}) collective-permute-start(bf16[1024,768]{1,0:T(8,128)(2,1)} %collective-permute-done.19.refs_5_), channel_id=1, source_target_pairs={{0,4},{4,0},{8,12},{12,8},{16,20},{20,16},{24,28},{28,24},{1,5},{5... | collective-permute-start | bytes 4718600 | tf_op jit(solution)/shard_map/ppermute | solution.py:847
  551.1 60.2 %collective-permute-start.42 = (bf16[1024,768]{1,0:T(8,128)(2,1)}, bf16[1024,768]{1,0:T(8,128)(2,1)}, u32[]{:S(2)}, u32[]{:S(2)}) collective-permute-start(bf16[1024,768]{1,0:T(8,128)(2,1)} %collective-permute-done.20.refs_6_), channel_id=1, source_target_pairs={{0,4},{4,0},{8,12},{12,8},{16,20},{20,16},{24,28},{28,24},{1,5},{5... | collective-permute-start | bytes 4718600 | tf_op jit(solution)/shard_map/ppermute | solution.py:847
  577.1 28.7 %collective-permute-start.37 = (bf16[256,2048]{1,0:T(8,128)(2,1)}, bf16[256,2048]{1,0:T(8,128)(2,1)}, u32[]{:S(2)}, u32[]{:S(2)}) collective-permute-start(bf16[256,2048]{1,0:T(8,128)(2,1)} %get-tuple-element.199), channel_id=1, source_target_pairs={{0,1},{1,0},{2,3},{3,2},{4,5},{5,4},{6,7},{7,6},{8,9},{9,8},{10,11... | collective-permute-start | bytes 3145736 | tf_op jit(solution)/shard_map/ppermute | solution.py:847
  578.3 27.4 %collective-permute-start.38 = (bf16[256,2048]{1,0:T(8,128)(2,1)}, bf16[256,2048]{1,0:T(8,128)(2,1)}, u32[]{:S(2)}, u32[]{:S(2)}) collective-permute-start(bf16[256,2048]{1,0:T(8,128)(2,1)} %get-tuple-element.199), channel_id=1, source_target_pairs={{0,2},{1,3},{2,0},{3,1},{4,6},{5,7},{6,4},{7,5},{8,10},{9,11},{10,... | collective-permute-start | bytes 3145736 | tf_op jit(solution)/shard_map/ppermute | solution.py:847
  579.7 31.8 %collective-permute-start.43 = (bf16[1024,768]{1,0:T(8,128)(2,1)S(1)}, bf16[1024,768]{1,0:T(8,128)(2,1)}, u32[]{:S(2)}, u32[]{:S(2)}) collective-permute-start(bf16[1024,768]{1,0:T(8,128)(2,1)S(1)} %constant_dynamic-update-slice_fusion.11.refs_7_), channel_id=1, source_target_pairs={{0,4},{4,0},{8,12},{12,8},{16,20},{20,16},{24,28},{28,24},{1,5},{5... | collective-permute-start | bytes 4718600 | tf_op jit(solution)/shard_map/ppermute | solution.py:847
  605.7 26.4 %collective-permute-start.39 = (bf16[256,2048]{1,0:T(8,128)(2,1)}, bf16[256,2048]{1,0:T(8,128)(2,1)}, u32[]{:S(2)}, u32[]{:S(2)}) collective-permute-start(bf16[256,2048]{1,0:T(8,128)(2,1)} %collective-permute-done.36.refs_4_), channel_id=1, source_target_pairs={{0,1},{1,0},{2,3},{3,2},{4,5},{5,4},{6,7},{7,6},{8,9},{9,8},{10,11... | collective-permute-start | bytes 3145736 | tf_op jit(solution)/shard_map/ppermute | solution.py:847
  607.4 26.4 %collective-permute-start.40 = (bf16[256,2048]{1,0:T(8,128)(2,1)}, bf16[256,2048]{1,0:T(8,128)(2,1)}, u32[]{:S(2)}, u32[]{:S(2)}) collective-permute-start(bf16[256,2048]{1,0:T(8,128)(2,1)} %collective-permute-done.37.refs_2_), channel_id=1, source_target_pairs={{0,2},{1,3},{2,0},{3,1},{4,6},{5,7},{6,4},{7,5},{8,10},{9,11},{10,... | collective-permute-start | bytes 3145736 | tf_op jit(solution)/shard_map/ppermute | solution.py:847
  610.1 38.8 %collective-permute-start.47 = (bf16[512,768]{1,0:T(8,128)(2,1)S(1)}, bf16[512,768]{1,0:T(8,128)(2,1)}, u32[]{:S(2)}, u32[]{:S(2)}) collective-permute-start(bf16[512,768]{1,0:T(8,128)(2,1)S(1)} %copy-done.29), channel_id=1, source_target_pairs={{0,1},{1,0},{2,3},{3,2},{4,5},{5,4},{6,7},{7,6},{8,9},{9,8},{10,11... | collective-permute-start | bytes 2359304 | tf_op jit(solution)/shard_map/ppermute | solution.py:847
  611.3 53.6 %collective-permute-start.48 = (bf16[512,768]{1,0:T(8,128)(2,1)}, bf16[512,768]{1,0:T(8,128)(2,1)}, u32[]{:S(2)}, u32[]{:S(2)}) collective-permute-start(bf16[512,768]{1,0:T(8,128)(2,1)} %get-tuple-element.196.refs_6_), channel_id=1, source_target_pairs={{0,2},{1,3},{2,0},{3,1},{4,6},{5,7},{6,4},{7,5},{8,10},{9,11},{10,... | collective-permute-start | bytes 2359304 | tf_op jit(solution)/shard_map/ppermute | solution.py:847
  611.5 54.8 %collective-permute-start.49 = (bf16[512,768]{1,0:T(8,128)(2,1)}, bf16[512,768]{1,0:T(8,128)(2,1)}, u32[]{:S(2)}, u32[]{:S(2)}) collective-permute-start(bf16[512,768]{1,0:T(8,128)(2,1)} %get-tuple-element.197.refs_7_), channel_id=1, source_target_pairs={{0,3},{1,2},{2,1},{3,0},{4,7},{5,6},{6,5},{7,4},{8,11},{9,10},{10,... | collective-permute-start | bytes 2359304 | tf_op jit(solution)/shard_map/ppermute | solution.py:847
  666.3 52.6 %collective-permute-start.25 = (bf16[256,2048]{1,0:T(8,128)(2,1)}, bf16[256,2048]{1,0:T(8,128)(2,1)S(1)}, u32[]{:S(2)}, u32[]{:S(2)}) collective-permute-start(bf16[256,2048]{1,0:T(8,128)(2,1)} %get-tuple-element.165), channel_id=1, source_target_pairs={{0,1},{1,0},{2,3},{3,2},{4,5},{5,4},{6,7},{7,6},{8,9},{9,8},{10,11... | collective-permute-start | bytes 3145736 | tf_op jit(solution)/shard_map/ppermute | solution.py:847
  667.2 51.7 %collective-permute-start.46 = (bf16[256,2048]{1,0:T(8,128)(2,1)}, bf16[256,2048]{1,0:T(8,128)(2,1)}, u32[]{:S(2)}, u32[]{:S(2)}) collective-permute-start(bf16[256,2048]{1,0:T(8,128)(2,1)} %get-tuple-element.216), channel_id=1, source_target_pairs={{0,2},{1,3},{2,0},{3,1},{4,6},{5,7},{6,4},{7,5},{8,10},{9,11},{10,... | collective-permute-start | bytes 3145736 | tf_op jit(solution)/shard_map/ppermute | solution.py:847
  671.3 47.6 %collective-permute-start.45 = (bf16[256,2048]{1,0:T(8,128)(2,1)}, bf16[256,2048]{1,0:T(8,128)(2,1)S(1)}, u32[]{:S(2)}, u32[]{:S(2)}) collective-permute-start(bf16[256,2048]{1,0:T(8,128)(2,1)} %add_convert_fusion), channel_id=1, source_target_pairs={{0,1},{1,0},{2,3},{3,2},{4,5},{5,4},{6,7},{7,6},{8,9},{9,8},{10,11... | collective-permute-start | bytes 3145736 | tf_op jit(solution)/shard_map/ppermute | solution.py:847
  674.9 44.1 %collective-permute-start.44 = (bf16[256,2048]{1,0:T(8,128)(2,1)}, bf16[256,2048]{1,0:T(8,128)(2,1)S(1)}, u32[]{:S(2)}, u32[]{:S(2)}) collective-permute-start(bf16[256,2048]{1,0:T(8,128)(2,1)} %add_convert_fusion.1), channel_id=1, source_target_pairs={{0,2},{1,3},{2,0},{3,1},{4,6},{5,7},{6,4},{7,5},{8,10},{9,11},{10,... | collective-permute-start | bytes 3145736 | tf_op jit(solution)/shard_map/ppermute | solution.py:847
  (58 other events, 834.6 us)
Sparse Core Ops, SparseCore 0:
  10.2 58.7 all-gather.3
  71.2 115.4 all-gather.5
  189.0 114.9 all-gather.7
  329.7 90.0 reduce-scatter.4
  422.4 90.0 reduce-scatter.6
  545.1 90.3 reduce-scatter.8
  666.4 60.6 reduce-scatter.10

commit v6 on v5

--- a/solution.py
+++ b/solution.py
@@ -1194,7 +1194,7 @@
         if sequence == 0:
             pieces = after(pieces, heads_in, grad_down)
         else:
-            pieces = after(pieces, tops, raw_grads)
+            pieces = after(pieces, tops, raw_grads, in_others)
             if count == 4:
                 bottom = after(bottom, tops, raw_grads)
                 bottoms = [shift(bottom, 1, count), shift(bottom, 2, count)]
@@ -1217,7 +1217,8 @@
         branch_near = gather_near(branch_low, count)
         branch = (branch_near[:inner_count], branch_near[inner_count:])
     scattered_down = scatter_weights(after(grad_down, scattered_b, heads_in))
-    grad_qkv = projection_weights(after(rows_in, raw_grads, bottoms), inv_rows, norm_attn, raw_grads)
+    out_adds = sum_adds(out, after(out_first, raw_grads)) if count == 4 else ()
+    grad_qkv = projection_weights(after(rows_in, raw_grads, bottoms, out_adds), inv_rows, norm_attn, raw_grads)
     grad_w_gate = jnp.concatenate(
         [scattered_a[:, :units], scattered_b[:, :units]], axis=1
     ).astype(jnp.float32)
@@ -1226,7 +1227,6 @@
     ).astype(jnp.float32)
     grad_attn = out_weights(inner, grad_qkv, after(branch, raw_grads, grad_w_gate, grad_w_up, in_others), attended)
 
-    out_adds = sum_adds(out, after(out_first, grad_attn)) if count == 4 else ()
     scattered_attn = scatter_weights(
         after(
             grad_attn, scattered_down, raw_in,
@@ -1235,7 +1235,7 @@
 
     grad_w_down = scattered_down.astype(jnp.float32)
     grad_tokens, gain_attn = input_back(
-        core, after(raw_in, grad_w_down, out_adds), w_attn, in_others, tokens, grad_resid.reshape(chunk_rows, width), norm_attn
+        core, after(raw_in, grad_w_down), w_attn, in_others, tokens, grad_resid.reshape(chunk_rows, width), norm_attn
     )
     out_rest = sum_rest(out, out_near, out_adds, count)
     gains = [

time: 750 us -> 764 us (1.019)
  waiting for transfers between devices: 99.8 us -> 112 us
    ppermute x55, waiting for transfers between devices: 99.7 us -> 111 us  [shift(): return lax.ppermute(values, axis, [(i, i ^ distance) for i in range(count)])]
    unnamed x97 -> x95, local copies, waits for them, and re-layouts: 16.5 us -> 17.6 us
  transfers between devices with their start and end apart: 62 -> 62, of which waited for: 18 -> 16; matrix products, arithmetic and copies ran while one was open for 18% -> 18% of each run, Pallas kernels for 57% -> 56%
where the time goes in v6:
time: 764 us; the launch traced here: 754 us
  Pallas kernels  424 us (55%)
  waiting for transfers between devices  112 us (15%)
  matrix products  71.7 us (9%)
  starting transfers between devices  56.2 us (7%)
  local copies, waits for them, and re-layouts  42.3 us (6%)
  other arithmetic  32.4 us (4%)
  between operations  15.2 us (2%)
    ppermute x55, waiting for transfers between devices, shift(): return lax.ppermute(values, axis, [(i, i ^ distance) for i in range(count)])  111 us
    pallas_call x4, Pallas kernels, rows_out(): pl.pallas_call(functools.partial(rows_out_kernel, len(lefts)), grid=(widt...  79.1 us
    pallas_call x1, Pallas kernels, gather_rows(): pl.pallas_call(gather_kernel, in_specs=[place], out_specs=[place] * 2, ou...  72.8 us
    dot_general x3, matrix products, contract_rows(): lax.dot_general(left, right, (((0,), (0,)), ((), ())), preferred_element_...  71.7 us
    ppermute x55, starting transfers between devices, shift(): return lax.ppermute(values, axis, [(i, i ^ distance) for i in range(count)])  55.9 us
    pallas_call x2, Pallas kernels, attend_back(): pl.pallas_call(functools.partial(attend_back_kernel, chunks), grid_spec=p...  51.1 us
    pallas_call x1, Pallas kernels, hidden_units(): pl.pallas_call(hidden_kernel, grid=(rows // block,), in_specs=[pl.BlockSp...  36 us
    pallas_call x1, Pallas kernels, residual(): pl.pallas_call(functools.partial(resid_kernel, count), grid_spec=pltpu.Pr...  32.4 us
  transfers between devices with their start and end apart: 62, of which 16 were waited for; matrix products, arithmetic and copies ran while one was open for 18% of the time, Pallas kernels for 56%

profile of v6, /device:TPU:0, one launch (start us, length us, event | category | flops | bytes accessed | tf_op | source)
XLA Modules:
  0.0 753.7 jit_solution(10396755776393911010)
XLA Ops:
  13.8 72.8 %shard_map.246 = (bf16[1024,2048]{1,0:T(8,128)(2,1)}, bf16[1024,2048]{1,0:T(8,128)(2,1)}) custom-call(bf16[512,2048]{1,0:T(8,128)(2,1)} %refs_11_.1), custom_call_target="tpu_custom_call" | custom-call | bytes 12582912 | tf_op jit(solution)/shard_map/pallas_call | solution.py:895
  95.1 5.8 fusion
  101.0 11.1 %shard_map.247 = (f32[1024,128]{1,0:T(8,128)}, bf16[1024,512]{1,0:T(8,128)(2,1)}, bf16[1024,512]{1,0:T(8,128)(2,1)}, bf16[1024,512]{1,0:T(8,128)(2,1)}, f32[1024,640]{1,0:T(8,128)}) custom-call(s32[1]{0:T(128)S(6)} %select_n.55.inner_ref, bf16[1024,2048]{1,0:T(8,128)(2,1)} %get-tuple-element.223.refs_0_, f32[1,2048]{1,0:T(1,128)} %bitcast.51, ...), custom_call_target="tpu_custom_call" | custom-call | flops 2928386816 | bytes 2516582 | tf_op jit(solution)/shard_map/pallas_call | solution.py:376
  112.1 9.5 %shard_map.248 = (bf16[1024,512]{1,0:T(8,128)(2,1)}, f32[1024,512]{1,0:T(8,128)}) custom-call(bf16[1024,512]{1,0:T(8,128)(2,1)} %get-tuple-element.127.q_ref, bf16[1024,512]{1,0:T(8,128)(2,1)} %get-tuple-element.128.k_ref, bf16[1024,512]{1,0:T(8,128)(2,1)} %get-tuple-element.129.v_ref, s32[1024,1]{1,0:T(8,128)} %copy.29.segc_ref, ...), custom_call_target="tpu_custom_call" | custom-call | flops 2254857728 | bytes 6291456 | tf_op jit(solution)/shard_map/pallas_call | solution.py:225
  123.5 11.8 %shard_map.249 = (f32[1024,128]{1,0:T(8,128)}, bf16[1024,512]{1,0:T(8,128)(2,1)}, bf16[1024,512]{1,0:T(8,128)(2,1)}, bf16[1024,512]{1,0:T(8,128)(2,1)}, f32[1024,640]{1,0:T(8,128)}) custom-call(s32[1]{0:T(128)S(6)} %select_n.55.inner_ref, bf16[1024,2048]{1,0:T(8,128)(2,1)} %get-tuple-element.224.refs_0_.refs_1_, f32[1,2048]{1,0:T(1,128)} %bitcast.52, ...), custom_call_target="tpu_custom_call" | custom-call | flops 2928386816 | bytes 2516582 | tf_op jit(solution)/shard_map/pallas_call | solution.py:376
  135.3 9.7 %shard_map.250 = (bf16[1024,512]{1,0:T(8,128)(2,1)}, f32[1024,512]{1,0:T(8,128)}) custom-call(bf16[1024,512]{1,0:T(8,128)(2,1)} %get-tuple-element.133.q_ref, bf16[1024,512]{1,0:T(8,128)(2,1)} %get-tuple-element.134.k_ref, bf16[1024,512]{1,0:T(8,128)(2,1)} %get-tuple-element.135.v_ref, s32[1024,1]{1,0:T(8,128)} %copy.30.segc_ref, ...), custom_call_target="tpu_custom_call" | custom-call | flops 2254857728 | bytes 6291456 | tf_op jit(solution)/shard_map/pallas_call | solution.py:225
  150.4 21.0 %collective-permute-done.3.refs_4_ = bf16[1024,512]{1,0:T(8,128)(2,1)S(1)} collective-permute-done((bf16[1024,512]{1,0:T(8,128)(2,1)}, bf16[1024,512]{1,0:T(8,128)(2,1)S(1)}, u32[]{:S(2)}, u32[]{:S(2)}) %collective-permute-start.3) | collective-permute-done | bytes 1048608 | tf_op jit(solution)/shard_map/ppermute | solution.py:847
  174.3 8.8 %collective-permute-done.8 = bf16[512,512]{1,0:T(8,128)(2,1)S(1)} collective-permute-done((bf16[512,512]{1,0:T(8,128)(2,1)S(1)}, bf16[512,512]{1,0:T(8,128)(2,1)S(1)}, u32[]{:S(2)}, u32[]{:S(2)}) %collective-permute-start.8) | collective-permute-done | bytes 524320 | tf_op jit(solution)/shard_map/ppermute | solution.py:847
  184.7 9.6 %collective-permute-done.4 = bf16[512,512]{1,0:T(8,128)(2,1)S(1)} collective-permute-done((bf16[512,512]{1,0:T(8,128)(2,1)S(1)}, bf16[512,512]{1,0:T(8,128)(2,1)S(1)}, u32[]{:S(2)}, u32[]{:S(2)}) %collective-permute-start.4) | collective-permute-done | bytes 524320 | tf_op jit(solution)/shard_map/ppermute | solution.py:847
  196.5 9.1 %collective-permute-done.10 = bf16[512,512]{1,0:T(8,128)(2,1)S(1)} collective-permute-done((bf16[512,512]{1,0:T(8,128)(2,1)S(1)}, bf16[512,512]{1,0:T(8,128)(2,1)S(1)}, u32[]{:S(2)}, u32[]{:S(2)}) %collective-permute-start.10) | collective-permute-done | bytes 524320 | tf_op jit(solution)/shard_map/ppermute | solution.py:847
  210.7 32.4 %shard_map.251 = (bf16[2048,2048]{1,0:T(8,128)(2,1)}, f32[1,512,2048]{2,1,0:T(8,128)}) custom-call(s32[2]{0:T(128)} %pad_add_fusion.place_ref, bf16[1024,2048]{1,0:T(8,128)(2,1)} %get-tuple-element.223.refs_0_, bf16[1024,2048]{1,0:T(8,128)(2,1)} %get-tuple-element.224.refs_0_.refs_1_, bf16[1024,512]{1,0:T(8,128)(2,1)} %get-tuple-element.130.refs_2_.out_ref.refs_3_, ...), custom_call_target="tpu_custom_call" | custom-call | flops 7469508096 | bytes 6710886 | tf_op jit(solution)/shard_map/pallas_call | solution.py:667
  243.1 4.0 collective-permute-done.15
  250.8 2.3 slice.119
  255.2 3.2 constant_dynamic-update-slice_fusion.9
  258.4 3.1 constant_dynamic-update-slice_fusion.8
  261.6 25.6 %shard_map.252 = (bf16[2048,2048]{1,0:T(8,128)(2,1)}, bf16[2048,2048]{1,0:T(8,128)(2,1)}) custom-call(bf16[2048,2048]{1,0:T(8,128)(2,1)} %get-tuple-element.151.x_ref, bf16[2048,3072]{1,0:T(8,128)(2,1)} %all-gather.6.cloned.1.call-done.w_ref.refs_2_), custom_call_target="tpu_custom_call" | custom-call | flops 5453926912 | bytes 5033164 | tf_op jit(solution)/shard_map/pallas_call | solution.py:525
  288.2 2.3 constant_dynamic-update-slice_fusion.6.dy_ref
  290.6 15.2 %shard_map.253.refs_0_ = bf16[2048,2048]{1,0:T(8,128)(2,1)} custom-call(bf16[2048,2048]{1,0:T(8,128)(2,1)} %constant_dynamic-update-slice_fusion.6.dy_ref, bf16[2048,2048]{1,0:T(8,128)(2,1)} %get-tuple-element.147.factors_ref, bf16[2048,3072]{1,0:T(8,128)(2,1)} %all-gather.6.cloned.1.call-done.w_ref.refs_2_), custom_call_target="tpu_custom_call" | custom-call | flops 2726963456 | bytes 5033164 | tf_op jit(solution)/shard_map/pallas_call | solution.py:557
  305.8 23.8 %convolution_convert_fusion.2 = bf16[2048,2048]{1,0:T(8,128)(2,1)} fusion(bf16[2048,2048]{1,0:T(8,128)(2,1)} %get-tuple-element.151.x_ref, bf16[2048,2048]{1,0:T(8,128)(2,1)} %shard_map.253.refs_0_), kind=kOutput, calls=%fused_computation.2 | convolution fusion | flops 17184063488 | bytes 25165824 | tf_op jit(solution)/shard_map/dot_general | solution.py:38
  329.7 2.7 constant_dynamic-slice_fusion
  334.4 36.0 %shard_map.254 = (bf16[2048,2048]{1,0:T(8,128)(2,1)}, bf16[2048,2048]{1,0:T(8,128)(2,1)}) custom-call(bf16[2048,2048]{1,0:T(8,128)(2,1)} %get-tuple-element.151.x_ref, bf16[2048,2048]{1,0:T(8,128)(2,1)} %constant_dynamic-update-slice_fusion.6.dy_ref, bf16[2048,3072]{1,0:T(8,128)(2,1)} %all-gather.8.cloned.1.call-done.w_ref.refs_3_, ...), custom_call_target="tpu_custom_call", output_to_operand_aliasing={{0}: (3, {})} | custom-call | flops 8180890112 | bytes 7549747 | tf_op jit(solution)/shard_map/pallas_call | solution.py:486
  374.3 23.9 %convolution_convert_fusion.1 = bf16[2048,2048]{1,0:T(8,128)(2,1)} fusion(bf16[2048,2048]{1,0:T(8,128)(2,1)} %get-tuple-element.151.x_ref, bf16[2048,2048]{1,0:T(8,128)(2,1)} %get-tuple-element.152.refs_1_), kind=kOutput, calls=%fused_computation.1 | convolution fusion | flops 17184063488 | bytes 25165824 | tf_op jit(solution)/shard_map/dot_general | solution.py:38
  398.2 24.1 %shard_map.255 = (f32[256,2048]{1,0:T(8,128)}, bf16[256,2048]{1,0:T(8,128)(2,1)}, bf16[256,2048]{1,0:T(8,128)(2,1)}, bf16[256,2048]{1,0:T(8,128)(2,1)}) custom-call(bf16[2048,2048]{1,0:T(8,128)(2,1)} %shard_map.253.refs_0_, bf16[2048,2048]{1,0:T(8,128)(2,1)} %get-tuple-element.152.refs_1_, bf16[2048,3072]{1,0:T(8,128)(2,1)} %all-gather.6.cloned.1.call-done.w_ref.refs_2_, ...), custom_call_target="tpu_custom_call" | custom-call | flops 844219584 | bytes 209715 | tf_op jit(solution)/shard_map/pallas_call | solution.py:608
  424.6 15.5 %shard_map.256 = (bf16[256,2048]{1,0:T(8,128)(2,1)}, f32[256,2048]{1,0:T(8,128)}) custom-call(bf16[2048,2048]{1,0:T(8,128)(2,1)} %shard_map.253.refs_0_, bf16[2048,2048]{1,0:T(8,128)(2,1)} %get-tuple-element.152.refs_1_, bf16[2048,3072]{1,0:T(8,128)(2,1)} %all-gather.6.cloned.1.call-done.w_ref.refs_2_, ...), custom_call_target="tpu_custom_call" | custom-call | flops 422109792 | bytes 104857 | tf_op jit(solution)/shard_map/pallas_call | solution.py:608
  442.3 4.9 collective-permute-done.24
  447.2 3.1 add_convert_fusion.2
  451.6 2.5 add_convert_fusion.3
  456.4 15.3 %shard_map.257 = (f32[256,2048]{1,0:T(8,128)}, f32[256,2048]{1,0:T(8,128)}) custom-call(bf16[2048,2048]{1,0:T(8,128)(2,1)} %shard_map.253.refs_0_, bf16[2048,2048]{1,0:T(8,128)(2,1)} %get-tuple-element.152.refs_1_, bf16[2048,3072]{1,0:T(8,128)(2,1)} %all-gather.6.cloned.1.call-done.w_ref.refs_2_, bf16[2048,3072]{1,0:T(8,128)(2,1)} %all-gather.8.cloned.1.call-done.w_ref.refs_3_), custom_call_target="tpu_custom_call" | custom-call | flops 422109792 | bytes 104857 | tf_op jit(solution)/shard_map/pallas_call | solution.py:608
  471.8 24.2 %shard_map.258 = (f32[256,2048]{1,0:T(8,128)}, f32[256,2048]{1,0:T(8,128)}, bf16[256,2048]{1,0:T(8,128)(2,1)}, f32[256,2048]{1,0:T(8,128)}, f32[256,2048]{1,0:T(...) custom-call(bf16[2048,2048]{1,0:T(8,128)(2,1)} %get-tuple-element.163.refs_0_.refs_1_, ...), custom_call_target="tpu_custom_call" | custom-call | flops 844219584 | bytes 209715 | tf_op jit(solution)/shard_map/pallas_call | solution.py:608
  498.2 9.5 %shard_map.259 = (f32[2,256,2048]{2,1,0:T(8,128)}, bf16[2,256,2048]{2,1,0:T(8,128)(2,1)}, f32[8,2048]{1,0:T(8,128)}) custom-call(f32[256,2048]{1,0:T(8,128)} %get-tuple-element.173.refs_0_, bf16[256,2048]{1,0:T(8,128)(2,1)} %copy-done.22, bf16[256,2048]{1,0:T(8,128)(2,1)} %collective-permute-done.29.refs_2_, f32[256,2048]{1,0:T(8,128)} %get-tuple-element.176.refs_3_, ...), custom_call_target="tpu_custom_call" | custom-call | flops 1048576 | bytes 1048576 | tf_op jit(solution)/shard_map/pallas_call | solution.py:995
  507.7 9.4 %shard_map.260 = (bf16[512,512]{1,0:T(8,128)(2,1)}, bf16[512,512]{1,0:T(8,128)(2,1)}, bf16[512,512]{1,0:T(8,128)(2,1)}, bf16[512,512]{1,0:T(8,128)(2,1)}) custom-call(s32[1]{0:T(128)S(6)} %select_n.56.core_ref, bf16[512,2048]{1,0:T(8,128)(2,1)} %bitcast.43, bf16[2048,1280]{1,0:T(8,128)(2,1)} %all-gather.4.cloned.1.call-done.refs_2_.refs_10_.refs_0_.refs_4_, ...), custom_call_target="tpu_custom_call" | custom-call | flops 321720384 | bytes 209715 | tf_op jit(solution)/shard_map/pallas_call | solution.py:428
  520.6 24.0 %convolution_convert_fusion = bf16[2048,2048]{1,0:T(8,128)(2,1)} fusion(bf16[2048,2048]{1,0:T(8,128)(2,1)} %constant_dynamic-update-slice_fusion.6.dy_ref, bf16[2048,2048]{1,0:T(8,128)(2,1)} %get-tuple-element.163.refs_0_.refs_1_), kind=kOutput, calls=%fused_computation | convolution fusion | flops 17184063488 | bytes 25165824 | tf_op jit(solution)/shard_map/dot_general | solution.py:38
  555.2 25.6 %shard_map.261 = (bf16[512,768]{1,0:T(8,128)(2,1)}, bf16[512,768]{1,0:T(8,128)(2,1)}, f32[8,128]{1,0:T(8,128)}, f32[8,128]{1,0:T(8,128)}) custom-call(s32[1]{0:T(128)S(6)} %select_n.55.inner_ref, bf16[1024,512]{1,0:T(8,128)(2,1)} %get-tuple-element.127.q_ref, bf16[1024,512]{1,0:T(8,128)(2,1)} %get-tuple-element.128.k_ref, ...), custom_call_target="tpu_custom_call" | custom-call | flops 5905580032 | bytes 10485760 | tf_op jit(solution)/shard_map/pallas_call | solution.py:258
  586.3 25.5 %shard_map.262 = (bf16[512,768]{1,0:T(8,128)(2,1)}, bf16[512,768]{1,0:T(8,128)(2,1)}, f32[8,128]{1,0:T(8,128)}, f32[8,128]{1,0:T(8,128)}) custom-call(s32[1]{0:T(128)S(6)} %select_n.55.inner_ref, bf16[1024,512]{1,0:T(8,128)(2,1)} %get-tuple-element.133.q_ref, bf16[1024,512]{1,0:T(8,128)(2,1)} %get-tuple-element.134.k_ref, ...), custom_call_target="tpu_custom_call" | custom-call | flops 5905580032 | bytes 10485760 | tf_op jit(solution)/shard_map/pallas_call | solution.py:258
  617.1 2.6 add_convert_fusion
  619.7 2.5 add_convert_fusion.1
  622.2 13.0 %shard_map.265.beside_ref = bf16[2048,768]{1,0:T(8,128)(2,1)} custom-call(f32[1,2048]{1,0:T(1,128)} %bitcast.53, bf16[1024,2048]{1,0:T(8,128)(2,1)} %get-tuple-element.223.refs_0_, bf16[1024,2048]{1,0:T(8,128)(2,1)} %get-tuple-element.224.refs_0_.refs_1_, f32[1024,128]{1,0:T(8,128)} %get-tuple-element.225.refs_2_, f32[1024,128]{1,0:T(8,128)} %get-tuple-element.226.refs_3_, ...), custom_call_target="tpu_custom_call" | custom-call | flops 2996488704 | bytes 1677721 | tf_op jit(solution)/shard_map/pallas_call | solution.py:832
  635.3 26.8 %collective-permute-done.53.refs_6_ = bf16[256,2048]{1,0:T(8,128)(2,1)S(1)} collective-permute-done((bf16[256,2048]{1,0:T(8,128)(2,1)}, bf16[256,2048]{1,0:T(8,128)(2,1)S(1)}, u32[]{:S(2)}, u32[]{:S(2)}) %collective-permute-start.53) | collective-permute-done | bytes 1048608 | tf_op jit(solution)/shard_map/ppermute | solution.py:847
  662.0 8.1 %collective-permute-done.54.refs_7_ = bf16[256,2048]{1,0:T(8,128)(2,1)} collective-permute-done((bf16[256,2048]{1,0:T(8,128)(2,1)}, bf16[256,2048]{1,0:T(8,128)(2,1)}, u32[]{:S(2)}, u32[]{:S(2)}) %collective-permute-start.54) | collective-permute-done | bytes 1048608 | tf_op jit(solution)/shard_map/ppermute | solution.py:847
  670.2 11.8 %shard_map.266 = bf16[2048,1280]{1,0:T(8,128)(2,1)} custom-call(s32[1]{0:T(128)S(6)} %select_n.55.inner_ref, bf16[2048,768]{1,0:T(8,128)(2,1)} %shard_map.265.beside_ref, bf16[512,2048]{1,0:T(8,128)(2,1)} %bitcast.44, bf16[256,2048]{1,0:T(8,128)(2,1)} %collective-permute-done.35.refs_1_, bf16[256,2048]{1,0:T(8,128)(2,1)} %collective-permute-done.51.refs_2_, ...), custom_call_target="tpu_custom_call" | custom-call | flops 2454267136 | bytes 1677721 | tf_op jit(solution)/shard_map/pallas_call | solution.py:798
  686.5 2.8 convert_element_type.85
  689.3 19.8 %shard_map.263 = (f32[512,2048]{1,0:T(8,128)}, f32[8,2048]{1,0:T(8,128)}) custom-call(s32[1]{0:T(128)S(6)} %select_n.56.core_ref, bf16[512,768]{1,0:T(8,128)(2,1)} %get-tuple-element.203.refs_0_.refs_4_, bf16[512,768]{1,0:T(8,128)(2,1)} %collective-permute-done.43.refs_1_, bf16[512,768]{1,0:T(8,128)(2,1)} %collective-permute-done.44.refs_2_, ...), custom_call_target="tpu_custom_call" | custom-call | flops 4601750528 | bytes 4194304 | tf_op jit(solution)/shard_map/pallas_call | solution.py:743
  713.3 2.7 collective-permute-done.47
  716.0 2.5 collective-permute-start.48
  718.5 3.0 collective-permute-done.48
  723.0 6.0 collective-permute-done.49
  730.1 2.7 collective-permute-done.50
  734.5 6.5 shard_map.264
  (269 shorter events, 100.4 us)
Async XLA Ops:
  7.2 80.3 %all-gather.4.cloned.1.call-start = ((), (), s32[]{:S(2)}) async-start(), calls=%async_computation.4 | async-start | bytes 5898240 | tf_op jit(solution)/shard_map/all_gather | solution.py:1048
  9.4 252.2 %all-gather.6.cloned.1.call-start = ((), (), s32[]{:S(2)}) async-start(), calls=%async_computation.5 | async-start | bytes 14155776 | tf_op jit(solution)/shard_map/all_gather | solution.py:1048
  12.1 322.3 %all-gather.8.cloned.1.call-start = ((), (), s32[]{:S(2)}) async-start(), calls=%async_computation.6 | async-start | bytes 14155776 | tf_op jit(solution)/shard_map/all_gather | solution.py:1048
  13.5 408.8 %reduce-scatter.5.cloned.1.call-start = ((), (), s32[]{:S(2)}) async-start(), calls=%async_computation.7 | async-start | bytes 9437184 | tf_op jit(solution)/shard_map/reduce_scatter | solution.py:1052
  89.8 33.7 %collective-permute-start.1 = (bf16[1024,512]{1,0:T(8,128)(2,1)}, bf16[1024,512]{1,0:T(8,128)(2,1)S(1)}, u32[]{:S(2)}, u32[]{:S(2)}) collective-permute-start(bf16[1024,512]{1,0:T(8,128)(2,1)} %constant_dynamic-slice_fusion.1), channel_id=1, source_target_pairs={{0,1},{1,0},{2,3},{3,2},{4,5},{5,4},{6,7},{7,6},{8,9},{9,8},{10,11... | collective-permute-start | bytes 3145736 | tf_op jit(solution)/shard_map/ppermute | solution.py:847
  90.4 33.1 %collective-permute-start.2 = (bf16[1024,512]{1,0:T(8,128)(2,1)}, bf16[1024,512]{1,0:T(8,128)(2,1)S(1)}, u32[]{:S(2)}, u32[]{:S(2)}) collective-permute-start(bf16[1024,512]{1,0:T(8,128)(2,1)} %constant_dynamic-slice_fusion.1), channel_id=1, source_target_pairs={{0,2},{1,3},{2,0},{3,1},{4,6},{5,7},{6,4},{7,5},{8,10},{9,11},{10,... | collective-permute-start | bytes 3145736 | tf_op jit(solution)/shard_map/ppermute | solution.py:847
  121.6 25.5 %collective-permute-start.7 = (bf16[1024,512]{1,0:T(8,128)(2,1)}, bf16[1024,512]{1,0:T(8,128)(2,1)S(1)}, u32[]{:S(2)}, u32[]{:S(2)}) collective-permute-start(bf16[1024,512]{1,0:T(8,128)(2,1)} %get-tuple-element.130.refs_2_.out_ref.refs_3_), channel_id=1, source_target_pairs={{0,2},{1,3},{2,0},{3,1},{4,6},{5,7},{6,4},{7,5},{8,10},{9,11},{10,... | collective-permute-start | bytes 3145736 | tf_op jit(solution)/shard_map/ppermute | solution.py:847
  122.1 25.6 %collective-permute-start = (bf16[1024,512]{1,0:T(8,128)(2,1)}, bf16[1024,512]{1,0:T(8,128)(2,1)}, u32[]{:S(2)}, u32[]{:S(2)}) collective-permute-start(bf16[1024,512]{1,0:T(8,128)(2,1)} %get-tuple-element.130.refs_2_.out_ref.refs_3_), channel_id=1, source_target_pairs={{0,1},{1,0},{2,3},{3,2},{4,5},{5,4},{6,7},{7,6},{8,9},{9,8},{10,11... | collective-permute-start | bytes 3145736 | tf_op jit(solution)/shard_map/ppermute | solution.py:847
  145.0 26.4 %collective-permute-start.3 = (bf16[1024,512]{1,0:T(8,128)(2,1)}, bf16[1024,512]{1,0:T(8,128)(2,1)S(1)}, u32[]{:S(2)}, u32[]{:S(2)}) collective-permute-start(bf16[1024,512]{1,0:T(8,128)(2,1)} %get-tuple-element.136.refs_6_.out_ref.refs_8_), channel_id=1, source_target_pairs={{0,2},{1,3},{2,0},{3,1},{4,6},{5,7},{6,4},{7,5},{8,10},{9,11},{10,... | collective-permute-start | bytes 3145736 | tf_op jit(solution)/shard_map/ppermute | solution.py:847
  145.6 26.3 %collective-permute-start.5 = (bf16[1024,512]{1,0:T(8,128)(2,1)}, bf16[1024,512]{1,0:T(8,128)(2,1)S(1)}, u32[]{:S(2)}, u32[]{:S(2)}) collective-permute-start(bf16[1024,512]{1,0:T(8,128)(2,1)} %get-tuple-element.136.refs_6_.out_ref.refs_8_), channel_id=1, source_target_pairs={{0,1},{1,0},{2,3},{3,2},{4,5},{5,4},{6,7},{7,6},{8,9},{9,8},{10,11... | collective-permute-start | bytes 3145736 | tf_op jit(solution)/shard_map/ppermute | solution.py:847
  147.1 36.0 %collective-permute-start.8 = (bf16[512,512]{1,0:T(8,128)(2,1)S(1)}, bf16[512,512]{1,0:T(8,128)(2,1)S(1)}, u32[]{:S(2)}, u32[]{:S(2)}) collective-permute-start(bf16[512,512]{1,0:T(8,128)(2,1)S(1)} %slice.150), channel_id=1, source_target_pairs={{0,1},{1,0},{2,3},{3,2},{4,5},{5,4},{6,7},{7,6},{8,9},{9,8},{10,11... | collective-permute-start | bytes 1572872 | tf_op jit(solution)/shard_map/ppermute | solution.py:847
  148.8 35.9 %collective-permute-start.9 = (bf16[512,512]{1,0:T(8,128)(2,1)S(1)}, bf16[512,512]{1,0:T(8,128)(2,1)S(1)}, u32[]{:S(2)}, u32[]{:S(2)}) collective-permute-start(bf16[512,512]{1,0:T(8,128)(2,1)S(1)} %slice.151), channel_id=1, source_target_pairs={{0,2},{1,3},{2,0},{3,1},{4,6},{5,7},{6,4},{7,5},{8,10},{9,11},{10,... | collective-permute-start | bytes 1572872 | tf_op jit(solution)/shard_map/ppermute | solution.py:847
  173.6 32.0 %collective-permute-start.10 = (bf16[512,512]{1,0:T(8,128)(2,1)S(1)}, bf16[512,512]{1,0:T(8,128)(2,1)S(1)}, u32[]{:S(2)}, u32[]{:S(2)}) collective-permute-start(bf16[512,512]{1,0:T(8,128)(2,1)S(1)} %slice.116), channel_id=1, source_target_pairs={{0,1},{1,0},{2,3},{3,2},{4,5},{5,4},{6,7},{7,6},{8,9},{9,8},{10,11... | collective-permute-start | bytes 1572872 | tf_op jit(solution)/shard_map/ppermute | solution.py:847
  194.4 52.6 %collective-permute-start.15 = (bf16[512,2048]{1,0:T(8,128)(2,1)S(1)}, bf16[512,2048]{1,0:T(8,128)(2,1)}, u32[]{:S(2)}, u32[]{:S(2)}) collective-permute-start(bf16[512,2048]{1,0:T(8,128)(2,1)S(1)} %copy-done.1), channel_id=1, source_target_pairs={{0,1},{1,0},{2,3},{3,2},{4,5},{5,4},{6,7},{7,6},{8,9},{9,8},{10,11... | collective-permute-start | bytes 6291464 | tf_op jit(solution)/shard_map/ppermute | solution.py:847
  196.0 51.1 %collective-permute-start.16 = (bf16[512,2048]{1,0:T(8,128)(2,1)S(1)}, bf16[512,2048]{1,0:T(8,128)(2,1)}, u32[]{:S(2)}, u32[]{:S(2)}) collective-permute-start(bf16[512,2048]{1,0:T(8,128)(2,1)S(1)} %copy-done.1), channel_id=1, source_target_pairs={{0,2},{1,3},{2,0},{3,1},{4,6},{5,7},{6,4},{7,5},{8,10},{9,11},{10,... | collective-permute-start | bytes 6291464 | tf_op jit(solution)/shard_map/ppermute | solution.py:847
  249.4 37.8 %collective-permute-start.17 = (bf16[256,2048]{1,0:T(8,128)(2,1)}, bf16[256,2048]{1,0:T(8,128)(2,1)S(1)}, u32[]{:S(2)}, u32[]{:S(2)}) collective-permute-start(bf16[256,2048]{1,0:T(8,128)(2,1)} %slice.118), channel_id=1, source_target_pairs={{0,1},{1,0},{2,3},{3,2},{4,5},{5,4},{6,7},{7,6},{8,9},{9,8},{10,11... | collective-permute-start | bytes 3145736 | tf_op jit(solution)/shard_map/ppermute | solution.py:847
  253.2 34.0 %collective-permute-start.18 = (bf16[256,2048]{1,0:T(8,128)(2,1)}, bf16[256,2048]{1,0:T(8,128)(2,1)}, u32[]{:S(2)}, u32[]{:S(2)}) collective-permute-start(bf16[256,2048]{1,0:T(8,128)(2,1)} %slice.119), channel_id=1, source_target_pairs={{0,2},{1,3},{2,0},{3,1},{4,6},{5,7},{6,4},{7,5},{8,10},{9,11},{10,... | collective-permute-start | bytes 3145736 | tf_op jit(solution)/shard_map/ppermute | solution.py:847
  329.6 191.0 %reduce-scatter.7.cloned.1.call-start = ((), (), s32[]{:S(2)}) async-start(), calls=%async_computation.8 | async-start | bytes 9437184 | tf_op jit(solution)/shard_map/reduce_scatter | solution.py:1052
  332.3 38.1 %collective-permute-start.19 = (bf16[1024,768]{1,0:T(8,128)(2,1)}, bf16[1024,768]{1,0:T(8,128)(2,1)S(1)}, u32[]{:S(2)}, u32[]{:S(2)}) collective-permute-start(bf16[1024,768]{1,0:T(8,128)(2,1)} %constant_dynamic-slice_fusion), channel_id=1, source_target_pairs={{0,1},{1,0},{2,3},{3,2},{4,5},{5,4},{6,7},{7,6},{8,9},{9,8},{10,11... | collective-permute-start | bytes 4718600 | tf_op jit(solution)/shard_map/ppermute | solution.py:847
  333.8 36.6 %collective-permute-start.20 = (bf16[1024,768]{1,0:T(8,128)(2,1)}, bf16[1024,768]{1,0:T(8,128)(2,1)S(1)}, u32[]{:S(2)}, u32[]{:S(2)}) collective-permute-start(bf16[1024,768]{1,0:T(8,128)(2,1)} %constant_dynamic-slice_fusion), channel_id=1, source_target_pairs={{0,2},{1,3},{2,0},{3,1},{4,6},{5,7},{6,4},{7,5},{8,10},{9,11},{10,... | collective-permute-start | bytes 4718600 | tf_op jit(solution)/shard_map/ppermute | solution.py:847
  371.5 26.7 %collective-permute-start.21 = (bf16[512,768]{1,0:T(8,128)(2,1)}, bf16[512,768]{1,0:T(8,128)(2,1)}, u32[]{:S(2)}, u32[]{:S(2)}) collective-permute-start(bf16[512,768]{1,0:T(8,128)(2,1)} %slice.152), channel_id=1, source_target_pairs={{0,1},{1,0},{2,3},{3,2},{4,5},{5,4},{6,7},{7,6},{8,9},{9,8},{10,11... | collective-permute-start | bytes 2359304 | tf_op jit(solution)/shard_map/ppermute | solution.py:847
  422.4 259.8 %reduce-scatter.9.cloned.1.call-start = ((), (), s32[]{:S(2)}) async-start(), calls=%async_computation.9 | async-start | bytes 9437184 | tf_op jit(solution)/shard_map/reduce_scatter | solution.py:1052
  422.4 24.8 %collective-permute-start.24 = (bf16[256,2048]{1,0:T(8,128)(2,1)}, bf16[256,2048]{1,0:T(8,128)(2,1)S(1)}, u32[]{:S(2)}, u32[]{:S(2)}) collective-permute-start(bf16[256,2048]{1,0:T(8,128)(2,1)} %get-tuple-element.155), channel_id=1, source_target_pairs={{0,2},{1,3},{2,0},{3,1},{4,6},{5,7},{6,4},{7,5},{8,10},{9,11},{10,... | collective-permute-start | bytes 3145736 | tf_op jit(solution)/shard_map/ppermute | solution.py:847
  424.0 27.7 %collective-permute-start.23 = (bf16[256,2048]{1,0:T(8,128)(2,1)}, bf16[256,2048]{1,0:T(8,128)(2,1)}, u32[]{:S(2)}, u32[]{:S(2)}) collective-permute-start(bf16[256,2048]{1,0:T(8,128)(2,1)} %get-tuple-element.154), channel_id=1, source_target_pairs={{0,1},{1,0},{2,3},{3,2},{4,5},{5,4},{6,7},{7,6},{8,9},{9,8},{10,11... | collective-permute-start | bytes 3145736 | tf_op jit(solution)/shard_map/ppermute | solution.py:847
  440.1 56.5 %collective-permute-start.28 = (bf16[256,2048]{1,0:T(8,128)(2,1)}, bf16[256,2048]{1,0:T(8,128)(2,1)S(1)}, u32[]{:S(2)}, u32[]{:S(2)}) collective-permute-start(bf16[256,2048]{1,0:T(8,128)(2,1)} %get-tuple-element.157), channel_id=1, source_target_pairs={{0,1},{1,0},{2,3},{3,2},{4,5},{5,4},{6,7},{7,6},{8,9},{9,8},{10,11... | collective-permute-start | bytes 3145736 | tf_op jit(solution)/shard_map/ppermute | solution.py:847
  441.6 55.0 %collective-permute-start.31 = (bf16[256,2048]{1,0:T(8,128)(2,1)}, bf16[256,2048]{1,0:T(8,128)(2,1)S(1)}, u32[]{:S(2)}, u32[]{:S(2)}) collective-permute-start(bf16[256,2048]{1,0:T(8,128)(2,1)} %get-tuple-element.171), channel_id=1, source_target_pairs={{0,2},{1,3},{2,0},{3,1},{4,6},{5,7},{6,4},{7,5},{8,10},{9,11},{10,... | collective-permute-start | bytes 3145736 | tf_op jit(solution)/shard_map/ppermute | solution.py:847
  450.3 46.3 %collective-permute-start.30 = (bf16[256,2048]{1,0:T(8,128)(2,1)}, bf16[256,2048]{1,0:T(8,128)(2,1)S(1)}, u32[]{:S(2)}, u32[]{:S(2)}) collective-permute-start(bf16[256,2048]{1,0:T(8,128)(2,1)} %add_convert_fusion.2), channel_id=1, source_target_pairs={{0,1},{1,0},{2,3},{3,2},{4,5},{5,4},{6,7},{7,6},{8,9},{9,8},{10,11... | collective-permute-start | bytes 3145736 | tf_op jit(solution)/shard_map/ppermute | solution.py:847
  454.2 42.5 %collective-permute-start.29 = (bf16[256,2048]{1,0:T(8,128)(2,1)}, bf16[256,2048]{1,0:T(8,128)(2,1)}, u32[]{:S(2)}, u32[]{:S(2)}) collective-permute-start(bf16[256,2048]{1,0:T(8,128)(2,1)} %add_convert_fusion.3), channel_id=1, source_target_pairs={{0,2},{1,3},{2,0},{3,1},{4,6},{5,7},{6,4},{7,5},{8,10},{9,11},{10,... | collective-permute-start | bytes 3145736 | tf_op jit(solution)/shard_map/ppermute | solution.py:847
  495.9 24.7 %collective-permute-start.26 = (bf16[256,2048]{1,0:T(8,128)(2,1)}, bf16[256,2048]{1,0:T(8,128)(2,1)}, u32[]{:S(2)}, u32[]{:S(2)}) collective-permute-start(bf16[256,2048]{1,0:T(8,128)(2,1)} %get-tuple-element.167), channel_id=1, source_target_pairs={{0,1},{1,0},{2,3},{3,2},{4,5},{5,4},{6,7},{7,6},{8,9},{9,8},{10,11... | collective-permute-start | bytes 3145736 | tf_op jit(solution)/shard_map/ppermute | solution.py:847
  517.1 27.5 %collective-permute-start.32 = (bf16[512,512]{1,0:T(8,128)(2,1)}, bf16[512,512]{1,0:T(8,128)(2,1)S(1)}, u32[]{:S(2)}, u32[]{:S(2)}) collective-permute-start(bf16[512,512]{1,0:T(8,128)(2,1)} %get-tuple-element.182), channel_id=1, source_target_pairs={{0,1},{1,0},{2,3},{3,2},{4,5},{5,4},{6,7},{7,6},{8,9},{9,8},{10,11... | collective-permute-start | bytes 1572872 | tf_op jit(solution)/shard_map/ppermute | solution.py:847
  518.6 26.1 %collective-permute-start.33 = (bf16[512,512]{1,0:T(8,128)(2,1)}, bf16[512,512]{1,0:T(8,128)(2,1)S(1)}, u32[]{:S(2)}, u32[]{:S(2)}) collective-permute-start(bf16[512,512]{1,0:T(8,128)(2,1)} %get-tuple-element.183), channel_id=1, source_target_pairs={{0,2},{1,3},{2,0},{3,1},{4,6},{5,7},{6,4},{7,5},{8,10},{9,11},{10,... | collective-permute-start | bytes 1572872 | tf_op jit(solution)/shard_map/ppermute | solution.py:847
  545.9 197.1 %reduce-scatter.11.cloned.1.call-start = ((), (), s32[]{:S(2)}) async-start(), calls=%async_computation.10 | async-start | bytes 5898240 | tf_op jit(solution)/shard_map/reduce_scatter | solution.py:1052
  545.9 39.4 %collective-permute-start.37 = (bf16[1024,768]{1,0:T(8,128)(2,1)}, bf16[1024,768]{1,0:T(8,128)(2,1)}, u32[]{:S(2)}, u32[]{:S(2)}) collective-permute-start(bf16[1024,768]{1,0:T(8,128)(2,1)} %copy-done.9), channel_id=1, source_target_pairs={{0,4},{4,0},{8,12},{12,8},{16,20},{20,16},{24,28},{28,24},{1,5},{5... | collective-permute-start | bytes 4718600 | tf_op jit(solution)/shard_map/ppermute | solution.py:847
  546.0 40.3 %collective-permute-start.38 = (bf16[1024,768]{1,0:T(8,128)(2,1)}, bf16[1024,768]{1,0:T(8,128)(2,1)}, u32[]{:S(2)}, u32[]{:S(2)}) collective-permute-start(bf16[1024,768]{1,0:T(8,128)(2,1)} %copy-done.10), channel_id=1, source_target_pairs={{0,4},{4,0},{8,12},{12,8},{16,20},{20,16},{24,28},{28,24},{1,5},{5... | collective-permute-start | bytes 4718600 | tf_op jit(solution)/shard_map/ppermute | solution.py:847
  550.6 35.7 %collective-permute-start.39 = (bf16[1024,768]{1,0:T(8,128)(2,1)}, bf16[1024,768]{1,0:T(8,128)(2,1)}, u32[]{:S(2)}, u32[]{:S(2)}) collective-permute-start(bf16[1024,768]{1,0:T(8,128)(2,1)} %constant_dynamic-update-slice_fusion.11.refs_7_), channel_id=1, source_target_pairs={{0,4},{4,0},{8,12},{12,8},{16,20},{20,16},{24,28},{28,24},{1,5},{5... | collective-permute-start | bytes 4718600 | tf_op jit(solution)/shard_map/ppermute | solution.py:847
  551.9 28.9 %collective-permute-start.35 = (bf16[256,2048]{1,0:T(8,128)(2,1)}, bf16[256,2048]{1,0:T(8,128)(2,1)}, u32[]{:S(2)}, u32[]{:S(2)}) collective-permute-start(bf16[256,2048]{1,0:T(8,128)(2,1)} %get-tuple-element.193), channel_id=1, source_target_pairs={{0,1},{1,0},{2,3},{3,2},{4,5},{5,4},{6,7},{7,6},{8,9},{9,8},{10,11... | collective-permute-start | bytes 3145736 | tf_op jit(solution)/shard_map/ppermute | solution.py:847
  553.3 27.5 %collective-permute-start.36 = (bf16[256,2048]{1,0:T(8,128)(2,1)}, bf16[256,2048]{1,0:T(8,128)(2,1)}, u32[]{:S(2)}, u32[]{:S(2)}) collective-permute-start(bf16[256,2048]{1,0:T(8,128)(2,1)} %get-tuple-element.193), channel_id=1, source_target_pairs={{0,2},{1,3},{2,0},{3,1},{4,6},{5,7},{6,4},{7,5},{8,10},{9,11},{10,... | collective-permute-start | bytes 3145736 | tf_op jit(solution)/shard_map/ppermute | solution.py:847
  580.8 33.5 %collective-permute-start.51 = (bf16[256,2048]{1,0:T(8,128)(2,1)S(1)}, bf16[256,2048]{1,0:T(8,128)(2,1)}, u32[]{:S(2)}, u32[]{:S(2)}) collective-permute-start(bf16[256,2048]{1,0:T(8,128)(2,1)S(1)} %get-tuple-element.222), channel_id=1, source_target_pairs={{0,1},{1,0},{2,3},{3,2},{4,5},{5,4},{6,7},{7,6},{8,9},{9,8},{10,11... | collective-permute-start | bytes 3145736 | tf_op jit(solution)/shard_map/ppermute | solution.py:847
  581.4 32.9 %collective-permute-start.52 = (bf16[256,2048]{1,0:T(8,128)(2,1)S(1)}, bf16[256,2048]{1,0:T(8,128)(2,1)}, u32[]{:S(2)}, u32[]{:S(2)}) collective-permute-start(bf16[256,2048]{1,0:T(8,128)(2,1)S(1)} %get-tuple-element.222), channel_id=1, source_target_pairs={{0,2},{1,3},{2,0},{3,1},{4,6},{5,7},{6,4},{7,5},{8,10},{9,11},{10,... | collective-permute-start | bytes 3145736 | tf_op jit(solution)/shard_map/ppermute | solution.py:847
  585.3 96.8 %collective-permute-start.43 = (bf16[512,768]{1,0:T(8,128)(2,1)}, bf16[512,768]{1,0:T(8,128)(2,1)}, u32[]{:S(2)}, u32[]{:S(2)}) collective-permute-start(bf16[512,768]{1,0:T(8,128)(2,1)} %get-tuple-element.190.refs_5_), channel_id=1, source_target_pairs={{0,1},{1,0},{2,3},{3,2},{4,5},{5,4},{6,7},{7,6},{8,9},{9,8},{10,11... | collective-permute-start | bytes 2359304 | tf_op jit(solution)/shard_map/ppermute | solution.py:847
  611.8 70.3 %collective-permute-start.44 = (bf16[512,768]{1,0:T(8,128)(2,1)}, bf16[512,768]{1,0:T(8,128)(2,1)}, u32[]{:S(2)}, u32[]{:S(2)}) collective-permute-start(bf16[512,768]{1,0:T(8,128)(2,1)} %get-tuple-element.196.refs_6_), channel_id=1, source_target_pairs={{0,2},{1,3},{2,0},{3,1},{4,6},{5,7},{6,4},{7,5},{8,10},{9,11},{10,... | collective-permute-start | bytes 2359304 | tf_op jit(solution)/shard_map/ppermute | solution.py:847
  613.6 68.5 %collective-permute-start.45 = (bf16[512,768]{1,0:T(8,128)(2,1)}, bf16[512,768]{1,0:T(8,128)(2,1)}, u32[]{:S(2)}, u32[]{:S(2)}) collective-permute-start(bf16[512,768]{1,0:T(8,128)(2,1)} %get-tuple-element.197.refs_7_), channel_id=1, source_target_pairs={{0,3},{1,2},{2,1},{3,0},{4,7},{5,6},{6,5},{7,4},{8,11},{9,10},{10,... | collective-permute-start | bytes 2359304 | tf_op jit(solution)/shard_map/ppermute | solution.py:847
  614.3 47.7 %collective-permute-start.53 = (bf16[256,2048]{1,0:T(8,128)(2,1)}, bf16[256,2048]{1,0:T(8,128)(2,1)S(1)}, u32[]{:S(2)}, u32[]{:S(2)}) collective-permute-start(bf16[256,2048]{1,0:T(8,128)(2,1)} %collective-permute-done.36.refs_4_), channel_id=1, source_target_pairs={{0,1},{1,0},{2,3},{3,2},{4,5},{5,4},{6,7},{7,6},{8,9},{9,8},{10,11... | collective-permute-start | bytes 3145736 | tf_op jit(solution)/shard_map/ppermute | solution.py:847
  615.4 54.8 %collective-permute-start.54 = (bf16[256,2048]{1,0:T(8,128)(2,1)}, bf16[256,2048]{1,0:T(8,128)(2,1)}, u32[]{:S(2)}, u32[]{:S(2)}) collective-permute-start(bf16[256,2048]{1,0:T(8,128)(2,1)} %collective-permute-done.51.refs_2_), channel_id=1, source_target_pairs={{0,2},{1,3},{2,0},{3,1},{4,6},{5,7},{6,4},{7,5},{8,10},{9,11},{10,... | collective-permute-start | bytes 3145736 | tf_op jit(solution)/shard_map/ppermute | solution.py:847
  682.2 50.6 %collective-permute-start.25 = (bf16[256,2048]{1,0:T(8,128)(2,1)}, bf16[256,2048]{1,0:T(8,128)(2,1)S(1)}, u32[]{:S(2)}, u32[]{:S(2)}) collective-permute-start(bf16[256,2048]{1,0:T(8,128)(2,1)} %get-tuple-element.165), channel_id=1, source_target_pairs={{0,1},{1,0},{2,3},{3,2},{4,5},{5,4},{6,7},{7,6},{8,9},{9,8},{10,11... | collective-permute-start | bytes 3145736 | tf_op jit(solution)/shard_map/ppermute | solution.py:847
  683.7 49.1 %collective-permute-start.42 = (bf16[256,2048]{1,0:T(8,128)(2,1)}, bf16[256,2048]{1,0:T(8,128)(2,1)S(1)}, u32[]{:S(2)}, u32[]{:S(2)}) collective-permute-start(bf16[256,2048]{1,0:T(8,128)(2,1)} %get-tuple-element.201), channel_id=1, source_target_pairs={{0,2},{1,3},{2,0},{3,1},{4,6},{5,7},{6,4},{7,5},{8,10},{9,11},{10,... | collective-permute-start | bytes 3145736 | tf_op jit(solution)/shard_map/ppermute | solution.py:847
  684.3 48.5 %collective-permute-start.41 = (bf16[256,2048]{1,0:T(8,128)(2,1)}, bf16[256,2048]{1,0:T(8,128)(2,1)S(1)}, u32[]{:S(2)}, u32[]{:S(2)}) collective-permute-start(bf16[256,2048]{1,0:T(8,128)(2,1)} %add_convert_fusion), channel_id=1, source_target_pairs={{0,1},{1,0},{2,3},{3,2},{4,5},{5,4},{6,7},{7,6},{8,9},{9,8},{10,11... | collective-permute-start | bytes 3145736 | tf_op jit(solution)/shard_map/ppermute | solution.py:847
  685.8 47.1 %collective-permute-start.40 = (bf16[256,2048]{1,0:T(8,128)(2,1)}, bf16[256,2048]{1,0:T(8,128)(2,1)}, u32[]{:S(2)}, u32[]{:S(2)}) collective-permute-start(bf16[256,2048]{1,0:T(8,128)(2,1)} %add_convert_fusion.1), channel_id=1, source_target_pairs={{0,2},{1,3},{2,0},{3,1},{4,6},{5,7},{6,4},{7,5},{8,10},{9,11},{10,... | collective-permute-start | bytes 3145736 | tf_op jit(solution)/shard_map/ppermute | solution.py:847
  (57 other events, 809.3 us)
Sparse Core Ops, SparseCore 0:
  10.2 58.7 all-gather.3
  71.2 115.4 all-gather.5
  189.0 114.9 all-gather.7
  329.7 90.0 reduce-scatter.4
  422.5 90.0 reduce-scatter.6
  546.0 90.4 reduce-scatter.8
  682.3 60.5 reduce-scatter.10

commit v7 on v5

--- a/solution.py
+++ b/solution.py
@@ -1164,7 +1164,6 @@
         distances, [(out_act, units, 0), (out_act, units, 1)], w_mlp, [(units, 2), (units, 2)], chunk_rows
     )
     out_first = sum_first(out, count)
-    out_near = sum_near(out, count)
     grad_resid, branch_low, gain_mlp = own_rows_call(
         resid_back_kernel,
         after(two_rest, out[0]),
@@ -1229,7 +1228,7 @@
     out_adds = sum_adds(out, after(out_first, grad_attn)) if count == 4 else ()
     scattered_attn = scatter_weights(
         after(
-            grad_attn, scattered_down, raw_in,
+            grad_attn, scattered_down, raw_in[1:-1],
         )
     )
 
@@ -1237,7 +1236,8 @@
     grad_tokens, gain_attn = input_back(
         core, after(raw_in, grad_w_down, out_adds), w_attn, in_others, tokens, grad_resid.reshape(chunk_rows, width), norm_attn
     )
-    out_rest = sum_rest(out, out_near, out_adds, count)
+    out_near = sum_near(after(out, raw_in), count)
+    out_rest = sum_rest(out, out_near, after(out_adds, raw_in), count)
     gains = [
         jnp.sum(gain_attn, axis=0),
         jnp.sum(gain_mlp, axis=0),

time: 750 us -> 753 us (level)
    unnamed x97 -> x103, local copies, waits for them, and re-layouts: 16.5 us -> 19.2 us
where the time goes in v7:
time: 753 us; the launch traced here: 742 us
  Pallas kernels  425 us (56%)
  waiting for transfers between devices  100 us (13%)
  matrix products  71.9 us (10%)
  starting transfers between devices  55.5 us (7%)
  local copies, waits for them, and re-layouts  42.2 us (6%)
  other arithmetic  32.4 us (4%)
  between operations  15.2 us (2%)
    ppermute x55, waiting for transfers between devices, shift(): return lax.ppermute(values, axis, [(i, i ^ distance) for i in range(count)])  100 us
    pallas_call x4, Pallas kernels, rows_out(): pl.pallas_call(functools.partial(rows_out_kernel, len(lefts)), grid=(widt...  79.6 us
    pallas_call x1, Pallas kernels, gather_rows(): pl.pallas_call(gather_kernel, in_specs=[place], out_specs=[place] * 2, ou...  72.8 us
    dot_general x3, matrix products, contract_rows(): lax.dot_general(left, right, (((0,), (0,)), ((), ())), preferred_element_...  71.9 us
    ppermute x55, starting transfers between devices, shift(): return lax.ppermute(values, axis, [(i, i ^ distance) for i in range(count)])  55.3 us
    pallas_call x2, Pallas kernels, attend_back(): pl.pallas_call(functools.partial(attend_back_kernel, chunks), grid_spec=p...  51.1 us
    pallas_call x1, Pallas kernels, hidden_units(): pl.pallas_call(hidden_kernel, grid=(rows // block,), in_specs=[pl.BlockSp...  36 us
    pallas_call x1, Pallas kernels, residual(): pl.pallas_call(functools.partial(resid_kernel, count), grid_spec=pltpu.Pr...  32.5 us
  transfers between devices with their start and end apart: 62, of which 18 were waited for; matrix products, arithmetic and copies ran while one was open for 18% of the time, Pallas kernels for 57%

profile of v7, /device:TPU:0, one launch (start us, length us, event | category | flops | bytes accessed | tf_op | source)
XLA Modules:
  0.0 742.4 jit_solution(440451434500541454)
XLA Ops:
  13.8 72.8 %shard_map.246 = (bf16[1024,2048]{1,0:T(8,128)(2,1)}, bf16[1024,2048]{1,0:T(8,128)(2,1)}) custom-call(bf16[512,2048]{1,0:T(8,128)(2,1)} %refs_11_.1), custom_call_target="tpu_custom_call" | custom-call | bytes 12582912 | tf_op jit(solution)/shard_map/pallas_call | solution.py:895
  95.1 5.8 fusion
  101.0 11.1 %shard_map.247 = (f32[1024,128]{1,0:T(8,128)}, bf16[1024,512]{1,0:T(8,128)(2,1)}, bf16[1024,512]{1,0:T(8,128)(2,1)}, bf16[1024,512]{1,0:T(8,128)(2,1)}, f32[1024,640]{1,0:T(8,128)}) custom-call(s32[1]{0:T(128)S(6)} %select_n.55.inner_ref, bf16[1024,2048]{1,0:T(8,128)(2,1)} %get-tuple-element.207.refs_0_, f32[1,2048]{1,0:T(1,128)} %bitcast.51, ...), custom_call_target="tpu_custom_call" | custom-call | flops 2928386816 | bytes 2516582 | tf_op jit(solution)/shard_map/pallas_call | solution.py:376
  112.1 9.5 %shard_map.248 = (bf16[1024,512]{1,0:T(8,128)(2,1)}, f32[1024,512]{1,0:T(8,128)}) custom-call(bf16[1024,512]{1,0:T(8,128)(2,1)} %get-tuple-element.131.q_ref, bf16[1024,512]{1,0:T(8,128)(2,1)} %get-tuple-element.132.k_ref, bf16[1024,512]{1,0:T(8,128)(2,1)} %get-tuple-element.133.v_ref, s32[1024,1]{1,0:T(8,128)} %copy.29.segc_ref, ...), custom_call_target="tpu_custom_call" | custom-call | flops 2254857728 | bytes 6291456 | tf_op jit(solution)/shard_map/pallas_call | solution.py:225
  123.5 11.8 %shard_map.249 = (f32[1024,128]{1,0:T(8,128)}, bf16[1024,512]{1,0:T(8,128)(2,1)}, bf16[1024,512]{1,0:T(8,128)(2,1)}, bf16[1024,512]{1,0:T(8,128)(2,1)}, f32[1024,640]{1,0:T(8,128)}) custom-call(s32[1]{0:T(128)S(6)} %select_n.55.inner_ref, bf16[1024,2048]{1,0:T(8,128)(2,1)} %get-tuple-element.208.refs_0_.refs_1_, f32[1,2048]{1,0:T(1,128)} %bitcast.52, ...), custom_call_target="tpu_custom_call" | custom-call | flops 2928386816 | bytes 2516582 | tf_op jit(solution)/shard_map/pallas_call | solution.py:376
  135.3 9.7 %shard_map.250 = (bf16[1024,512]{1,0:T(8,128)(2,1)}, f32[1024,512]{1,0:T(8,128)}) custom-call(bf16[1024,512]{1,0:T(8,128)(2,1)} %get-tuple-element.137.q_ref, bf16[1024,512]{1,0:T(8,128)(2,1)} %get-tuple-element.138.k_ref, bf16[1024,512]{1,0:T(8,128)(2,1)} %get-tuple-element.139.v_ref, s32[1024,1]{1,0:T(8,128)} %copy.30.segc_ref, ...), custom_call_target="tpu_custom_call" | custom-call | flops 2254857728 | bytes 6291456 | tf_op jit(solution)/shard_map/pallas_call | solution.py:225
  150.4 21.0 %collective-permute-done.3.refs_4_ = bf16[1024,512]{1,0:T(8,128)(2,1)S(1)} collective-permute-done((bf16[1024,512]{1,0:T(8,128)(2,1)}, bf16[1024,512]{1,0:T(8,128)(2,1)S(1)}, u32[]{:S(2)}, u32[]{:S(2)}) %collective-permute-start.3) | collective-permute-done | bytes 1048608 | tf_op jit(solution)/shard_map/ppermute | solution.py:847
  174.3 8.8 %collective-permute-done.8 = bf16[512,512]{1,0:T(8,128)(2,1)S(1)} collective-permute-done((bf16[512,512]{1,0:T(8,128)(2,1)S(1)}, bf16[512,512]{1,0:T(8,128)(2,1)S(1)}, u32[]{:S(2)}, u32[]{:S(2)}) %collective-permute-start.8) | collective-permute-done | bytes 524320 | tf_op jit(solution)/shard_map/ppermute | solution.py:847
  184.8 9.6 %collective-permute-done.4 = bf16[512,512]{1,0:T(8,128)(2,1)S(1)} collective-permute-done((bf16[512,512]{1,0:T(8,128)(2,1)S(1)}, bf16[512,512]{1,0:T(8,128)(2,1)S(1)}, u32[]{:S(2)}, u32[]{:S(2)}) %collective-permute-start.4) | collective-permute-done | bytes 524320 | tf_op jit(solution)/shard_map/ppermute | solution.py:847
  196.5 9.1 %collective-permute-done.10 = bf16[512,512]{1,0:T(8,128)(2,1)S(1)} collective-permute-done((bf16[512,512]{1,0:T(8,128)(2,1)S(1)}, bf16[512,512]{1,0:T(8,128)(2,1)S(1)}, u32[]{:S(2)}, u32[]{:S(2)}) %collective-permute-start.10) | collective-permute-done | bytes 524320 | tf_op jit(solution)/shard_map/ppermute | solution.py:847
  210.7 32.5 %shard_map.251 = (bf16[2048,2048]{1,0:T(8,128)(2,1)}, f32[1,512,2048]{2,1,0:T(8,128)}) custom-call(s32[2]{0:T(128)} %pad_add_fusion.place_ref, bf16[1024,2048]{1,0:T(8,128)(2,1)} %get-tuple-element.207.refs_0_, bf16[1024,2048]{1,0:T(8,128)(2,1)} %get-tuple-element.208.refs_0_.refs_1_, bf16[1024,512]{1,0:T(8,128)(2,1)} %get-tuple-element.134.refs_2_.out_ref.refs_3_, ...), custom_call_target="tpu_custom_call" | custom-call | flops 7469508096 | bytes 6710886 | tf_op jit(solution)/shard_map/pallas_call | solution.py:667
  243.2 3.8 collective-permute-done.15
  247.1 2.3 slice.118
  250.8 2.3 slice.119
  255.2 3.3 constant_dynamic-update-slice_fusion.9
  258.4 3.1 constant_dynamic-update-slice_fusion.8
  261.6 25.6 %shard_map.252 = (bf16[2048,2048]{1,0:T(8,128)(2,1)}, bf16[2048,2048]{1,0:T(8,128)(2,1)}) custom-call(bf16[2048,2048]{1,0:T(8,128)(2,1)} %get-tuple-element.155.x_ref, bf16[2048,3072]{1,0:T(8,128)(2,1)} %all-gather.6.cloned.1.call-done.w_ref.refs_2_), custom_call_target="tpu_custom_call" | custom-call | flops 5453926912 | bytes 5033164 | tf_op jit(solution)/shard_map/pallas_call | solution.py:525
  288.3 2.4 constant_dynamic-update-slice_fusion.6.dy_ref
  290.6 15.2 %shard_map.253.refs_0_ = bf16[2048,2048]{1,0:T(8,128)(2,1)} custom-call(bf16[2048,2048]{1,0:T(8,128)(2,1)} %constant_dynamic-update-slice_fusion.6.dy_ref, bf16[2048,2048]{1,0:T(8,128)(2,1)} %get-tuple-element.151.factors_ref, bf16[2048,3072]{1,0:T(8,128)(2,1)} %all-gather.6.cloned.1.call-done.w_ref.refs_2_), custom_call_target="tpu_custom_call" | custom-call | flops 2726963456 | bytes 5033164 | tf_op jit(solution)/shard_map/pallas_call | solution.py:557
  305.8 23.8 %convolution_convert_fusion.2 = bf16[2048,2048]{1,0:T(8,128)(2,1)} fusion(bf16[2048,2048]{1,0:T(8,128)(2,1)} %get-tuple-element.155.x_ref, bf16[2048,2048]{1,0:T(8,128)(2,1)} %shard_map.253.refs_0_), kind=kOutput, calls=%fused_computation.2 | convolution fusion | flops 17184063488 | bytes 25165824 | tf_op jit(solution)/shard_map/dot_general | solution.py:38
  333.4 36.0 %shard_map.254 = (bf16[2048,2048]{1,0:T(8,128)(2,1)}, bf16[2048,2048]{1,0:T(8,128)(2,1)}) custom-call(bf16[2048,2048]{1,0:T(8,128)(2,1)} %get-tuple-element.155.x_ref, bf16[2048,2048]{1,0:T(8,128)(2,1)} %constant_dynamic-update-slice_fusion.6.dy_ref, bf16[2048,3072]{1,0:T(8,128)(2,1)} %all-gather.8.cloned.1.call-done.w_ref.refs_3_, ...), custom_call_target="tpu_custom_call", output_to_operand_aliasing={{0}: (3, {})} | custom-call | flops 8180890112 | bytes 7549747 | tf_op jit(solution)/shard_map/pallas_call | solution.py:486
  373.8 23.9 %convolution_convert_fusion.1 = bf16[2048,2048]{1,0:T(8,128)(2,1)} fusion(bf16[2048,2048]{1,0:T(8,128)(2,1)} %get-tuple-element.155.x_ref, bf16[2048,2048]{1,0:T(8,128)(2,1)} %get-tuple-element.156.refs_1_), kind=kOutput, calls=%fused_computation.1 | convolution fusion | flops 17184063488 | bytes 25165824 | tf_op jit(solution)/shard_map/dot_general | solution.py:38
  397.7 24.6 %shard_map.255 = (f32[256,2048]{1,0:T(8,128)}, bf16[256,2048]{1,0:T(8,128)(2,1)}, bf16[256,2048]{1,0:T(8,128)(2,1)}, bf16[256,2048]{1,0:T(8,128)(2,1)}) custom-call(bf16[2048,2048]{1,0:T(8,128)(2,1)} %shard_map.253.refs_0_, bf16[2048,2048]{1,0:T(8,128)(2,1)} %get-tuple-element.156.refs_1_, bf16[2048,3072]{1,0:T(8,128)(2,1)} %all-gather.6.cloned.1.call-done.w_ref.refs_2_, ...), custom_call_target="tpu_custom_call" | custom-call | flops 844219584 | bytes 209715 | tf_op jit(solution)/shard_map/pallas_call | solution.py:608
  424.6 15.5 %shard_map.256 = (bf16[256,2048]{1,0:T(8,128)(2,1)}, f32[256,2048]{1,0:T(8,128)}) custom-call(bf16[2048,2048]{1,0:T(8,128)(2,1)} %shard_map.253.refs_0_, bf16[2048,2048]{1,0:T(8,128)(2,1)} %get-tuple-element.156.refs_1_, bf16[2048,3072]{1,0:T(8,128)(2,1)} %all-gather.6.cloned.1.call-done.w_ref.refs_2_, ...), custom_call_target="tpu_custom_call" | custom-call | flops 422109792 | bytes 104857 | tf_op jit(solution)/shard_map/pallas_call | solution.py:608
  442.2 5.1 collective-permute-done.24
  447.3 3.1 add_convert_fusion.2
  451.6 2.6 add_convert_fusion.3
  454.2 2.3 collective-permute-start.26
  456.5 15.3 %shard_map.257 = (f32[256,2048]{1,0:T(8,128)}, f32[256,2048]{1,0:T(8,128)}) custom-call(bf16[2048,2048]{1,0:T(8,128)(2,1)} %shard_map.253.refs_0_, bf16[2048,2048]{1,0:T(8,128)(2,1)} %get-tuple-element.156.refs_1_, bf16[2048,3072]{1,0:T(8,128)(2,1)} %all-gather.6.cloned.1.call-done.w_ref.refs_2_, bf16[2048,3072]{1,0:T(8,128)(2,1)} %all-gather.8.cloned.1.call-done.w_ref.refs_3_), custom_call_target="tpu_custom_call" | custom-call | flops 422109792 | bytes 104857 | tf_op jit(solution)/shard_map/pallas_call | solution.py:608
  471.8 24.1 %shard_map.258 = (f32[256,2048]{1,0:T(8,128)}, f32[256,2048]{1,0:T(8,128)}, bf16[256,2048]{1,0:T(8,128)(2,1)}, f32[256,2048]{1,0:T(8,128)}, f32[256,2048]{1,0:T(...) custom-call(bf16[2048,2048]{1,0:T(8,128)(2,1)} %get-tuple-element.167.refs_0_.refs_1_, ...), custom_call_target="tpu_custom_call" | custom-call | flops 844219584 | bytes 209715 | tf_op jit(solution)/shard_map/pallas_call | solution.py:608
  498.3 9.5 %shard_map.259 = (f32[2,256,2048]{2,1,0:T(8,128)}, bf16[2,256,2048]{2,1,0:T(8,128)(2,1)}, f32[8,2048]{1,0:T(8,128)}) custom-call(f32[256,2048]{1,0:T(8,128)} %get-tuple-element.179.refs_0_, bf16[256,2048]{1,0:T(8,128)(2,1)} %copy-done.21, bf16[256,2048]{1,0:T(8,128)(2,1)} %collective-permute-done.26.refs_2_, f32[256,2048]{1,0:T(8,128)} %get-tuple-element.182.refs_3_, ...), custom_call_target="tpu_custom_call" | custom-call | flops 1048576 | bytes 1048576 | tf_op jit(solution)/shard_map/pallas_call | solution.py:995
  507.8 9.4 %shard_map.260 = (bf16[512,512]{1,0:T(8,128)(2,1)}, bf16[512,512]{1,0:T(8,128)(2,1)}, bf16[512,512]{1,0:T(8,128)(2,1)}, bf16[512,512]{1,0:T(8,128)(2,1)}) custom-call(s32[1]{0:T(128)S(6)} %select_n.56.core_ref, bf16[512,2048]{1,0:T(8,128)(2,1)} %bitcast.43, bf16[2048,1280]{1,0:T(8,128)(2,1)} %all-gather.4.cloned.1.call-done.refs_2_.refs_10_.refs_0_.refs_4_, ...), custom_call_target="tpu_custom_call" | custom-call | flops 321720384 | bytes 209715 | tf_op jit(solution)/shard_map/pallas_call | solution.py:428
  520.7 24.2 %convolution_convert_fusion = bf16[2048,2048]{1,0:T(8,128)(2,1)} fusion(bf16[2048,2048]{1,0:T(8,128)(2,1)} %constant_dynamic-update-slice_fusion.6.dy_ref, bf16[2048,2048]{1,0:T(8,128)(2,1)} %get-tuple-element.167.refs_0_.refs_1_), kind=kOutput, calls=%fused_computation | convolution fusion | flops 17184063488 | bytes 25165824 | tf_op jit(solution)/shard_map/dot_general | solution.py:38
  551.7 25.3 %shard_map.261 = (bf16[512,768]{1,0:T(8,128)(2,1)}, bf16[512,768]{1,0:T(8,128)(2,1)}, f32[8,128]{1,0:T(8,128)}, f32[8,128]{1,0:T(8,128)}) custom-call(s32[1]{0:T(128)S(6)} %select_n.55.inner_ref, bf16[1024,512]{1,0:T(8,128)(2,1)} %get-tuple-element.131.q_ref, bf16[1024,512]{1,0:T(8,128)(2,1)} %get-tuple-element.132.k_ref, ...), custom_call_target="tpu_custom_call" | custom-call | flops 5905580032 | bytes 10485760 | tf_op jit(solution)/shard_map/pallas_call | solution.py:258
  581.8 25.8 %shard_map.262 = (bf16[512,768]{1,0:T(8,128)(2,1)}, bf16[512,768]{1,0:T(8,128)(2,1)}, f32[8,128]{1,0:T(8,128)}, f32[8,128]{1,0:T(8,128)}) custom-call(s32[1]{0:T(128)S(6)} %select_n.55.inner_ref, bf16[1024,512]{1,0:T(8,128)(2,1)} %get-tuple-element.137.q_ref, bf16[1024,512]{1,0:T(8,128)(2,1)} %get-tuple-element.138.k_ref, ...), custom_call_target="tpu_custom_call" | custom-call | flops 5905580032 | bytes 10485760 | tf_op jit(solution)/shard_map/pallas_call | solution.py:258
  615.0 13.0 %shard_map.263.beside_ref = bf16[2048,768]{1,0:T(8,128)(2,1)} custom-call(f32[1,2048]{1,0:T(1,128)} %bitcast.53, bf16[1024,2048]{1,0:T(8,128)(2,1)} %get-tuple-element.207.refs_0_, bf16[1024,2048]{1,0:T(8,128)(2,1)} %get-tuple-element.208.refs_0_.refs_1_, f32[1024,128]{1,0:T(8,128)} %get-tuple-element.209.refs_2_, f32[1024,128]{1,0:T(8,128)} %get-tuple-element.210.refs_3_, ...), custom_call_target="tpu_custom_call" | custom-call | flops 2996488704 | bytes 1677721 | tf_op jit(solution)/shard_map/pallas_call | solution.py:832
  628.1 6.0 collective-permute-done.42.refs_6_
  634.9 11.9 %shard_map.264 = bf16[2048,1280]{1,0:T(8,128)(2,1)} custom-call(s32[1]{0:T(128)S(6)} %select_n.55.inner_ref, bf16[2048,768]{1,0:T(8,128)(2,1)} %shard_map.263.beside_ref, bf16[512,2048]{1,0:T(8,128)(2,1)} %bitcast.44, bf16[256,2048]{1,0:T(8,128)(2,1)} %copy-done.29, bf16[256,2048]{1,0:T(8,128)(2,1)} %collective-permute-done.40.refs_2_, ...), custom_call_target="tpu_custom_call" | custom-call | flops 2454267136 | bytes 1677721 | tf_op jit(solution)/shard_map/pallas_call | solution.py:798
  646.8 3.3 collective-permute-done.34.refs_1_
  652.9 17.9 %collective-permute-done.38.refs_3_ = bf16[512,768]{1,0:T(8,128)(2,1)S(1)} collective-permute-done((bf16[512,768]{1,0:T(8,128)(2,1)S(1)}, bf16[512,768]{1,0:T(8,128)(2,1)S(1)}, u32[]{:S(2)}, u32[]{:S(2)}) %collective-permute-start.38) | collective-permute-done | bytes 786464 | tf_op jit(solution)/shard_map/ppermute | solution.py:847
  674.0 2.5 add_convert_fusion
  676.6 2.6 add_convert_fusion.1
  681.2 2.8 convert_element_type.87
  684.0 19.9 %shard_map.265 = (f32[512,2048]{1,0:T(8,128)}, f32[8,2048]{1,0:T(8,128)}) custom-call(s32[1]{0:T(128)S(6)} %select_n.56.core_ref, bf16[512,768]{1,0:T(8,128)(2,1)} %get-tuple-element.226.refs_4_.refs_0_, bf16[512,768]{1,0:T(8,128)(2,1)} %collective-permute-done.34.refs_1_, bf16[512,768]{1,0:T(8,128)(2,1)} %collective-permute-done.37.refs_2_, ...), custom_call_target="tpu_custom_call" | custom-call | flops 4601750528 | bytes 4194304 | tf_op jit(solution)/shard_map/pallas_call | solution.py:743
  710.0 2.6 collective-permute-start.52
  715.6 2.9 collective-permute-done.53
  719.7 2.6 collective-permute-done.54
  724.0 6.4 shard_map.266
  (277 shorter events, 102.5 us)
Async XLA Ops:
  7.2 80.3 %all-gather.4.cloned.1.call-start = ((), (), s32[]{:S(2)}) async-start(), calls=%async_computation.4 | async-start | bytes 5898240 | tf_op jit(solution)/shard_map/all_gather | solution.py:1048
  9.4 252.2 %all-gather.6.cloned.1.call-start = ((), (), s32[]{:S(2)}) async-start(), calls=%async_computation.5 | async-start | bytes 14155776 | tf_op jit(solution)/shard_map/all_gather | solution.py:1048
  12.1 321.3 %all-gather.8.cloned.1.call-start = ((), (), s32[]{:S(2)}) async-start(), calls=%async_computation.6 | async-start | bytes 14155776 | tf_op jit(solution)/shard_map/all_gather | solution.py:1048
  13.5 408.9 %reduce-scatter.5.cloned.1.call-start = ((), (), s32[]{:S(2)}) async-start(), calls=%async_computation.7 | async-start | bytes 9437184 | tf_op jit(solution)/shard_map/reduce_scatter | solution.py:1052
  89.8 33.7 %collective-permute-start.1 = (bf16[1024,512]{1,0:T(8,128)(2,1)}, bf16[1024,512]{1,0:T(8,128)(2,1)S(1)}, u32[]{:S(2)}, u32[]{:S(2)}) collective-permute-start(bf16[1024,512]{1,0:T(8,128)(2,1)} %constant_dynamic-slice_fusion.1), channel_id=1, source_target_pairs={{0,1},{1,0},{2,3},{3,2},{4,5},{5,4},{6,7},{7,6},{8,9},{9,8},{10,11... | collective-permute-start | bytes 3145736 | tf_op jit(solution)/shard_map/ppermute | solution.py:847
  90.4 33.1 %collective-permute-start.2 = (bf16[1024,512]{1,0:T(8,128)(2,1)}, bf16[1024,512]{1,0:T(8,128)(2,1)S(1)}, u32[]{:S(2)}, u32[]{:S(2)}) collective-permute-start(bf16[1024,512]{1,0:T(8,128)(2,1)} %constant_dynamic-slice_fusion.1), channel_id=1, source_target_pairs={{0,2},{1,3},{2,0},{3,1},{4,6},{5,7},{6,4},{7,5},{8,10},{9,11},{10,... | collective-permute-start | bytes 3145736 | tf_op jit(solution)/shard_map/ppermute | solution.py:847
  121.6 25.4 %collective-permute-start.7 = (bf16[1024,512]{1,0:T(8,128)(2,1)}, bf16[1024,512]{1,0:T(8,128)(2,1)S(1)}, u32[]{:S(2)}, u32[]{:S(2)}) collective-permute-start(bf16[1024,512]{1,0:T(8,128)(2,1)} %get-tuple-element.134.refs_2_.out_ref.refs_3_), channel_id=1, source_target_pairs={{0,2},{1,3},{2,0},{3,1},{4,6},{5,7},{6,4},{7,5},{8,10},{9,11},{10,... | collective-permute-start | bytes 3145736 | tf_op jit(solution)/shard_map/ppermute | solution.py:847
  122.1 25.6 %collective-permute-start = (bf16[1024,512]{1,0:T(8,128)(2,1)}, bf16[1024,512]{1,0:T(8,128)(2,1)}, u32[]{:S(2)}, u32[]{:S(2)}) collective-permute-start(bf16[1024,512]{1,0:T(8,128)(2,1)} %get-tuple-element.134.refs_2_.out_ref.refs_3_), channel_id=1, source_target_pairs={{0,1},{1,0},{2,3},{3,2},{4,5},{5,4},{6,7},{7,6},{8,9},{9,8},{10,11... | collective-permute-start | bytes 3145736 | tf_op jit(solution)/shard_map/ppermute | solution.py:847
  145.0 26.4 %collective-permute-start.3 = (bf16[1024,512]{1,0:T(8,128)(2,1)}, bf16[1024,512]{1,0:T(8,128)(2,1)S(1)}, u32[]{:S(2)}, u32[]{:S(2)}) collective-permute-start(bf16[1024,512]{1,0:T(8,128)(2,1)} %get-tuple-element.140.refs_6_.out_ref.refs_8_), channel_id=1, source_target_pairs={{0,2},{1,3},{2,0},{3,1},{4,6},{5,7},{6,4},{7,5},{8,10},{9,11},{10,... | collective-permute-start | bytes 3145736 | tf_op jit(solution)/shard_map/ppermute | solution.py:847
  145.6 26.3 %collective-permute-start.5 = (bf16[1024,512]{1,0:T(8,128)(2,1)}, bf16[1024,512]{1,0:T(8,128)(2,1)S(1)}, u32[]{:S(2)}, u32[]{:S(2)}) collective-permute-start(bf16[1024,512]{1,0:T(8,128)(2,1)} %get-tuple-element.140.refs_6_.out_ref.refs_8_), channel_id=1, source_target_pairs={{0,1},{1,0},{2,3},{3,2},{4,5},{5,4},{6,7},{7,6},{8,9},{9,8},{10,11... | collective-permute-start | bytes 3145736 | tf_op jit(solution)/shard_map/ppermute | solution.py:847
  147.1 36.0 %collective-permute-start.8 = (bf16[512,512]{1,0:T(8,128)(2,1)S(1)}, bf16[512,512]{1,0:T(8,128)(2,1)S(1)}, u32[]{:S(2)}, u32[]{:S(2)}) collective-permute-start(bf16[512,512]{1,0:T(8,128)(2,1)S(1)} %slice.150), channel_id=1, source_target_pairs={{0,1},{1,0},{2,3},{3,2},{4,5},{5,4},{6,7},{7,6},{8,9},{9,8},{10,11... | collective-permute-start | bytes 1572872 | tf_op jit(solution)/shard_map/ppermute | solution.py:847
  148.8 35.9 %collective-permute-start.9 = (bf16[512,512]{1,0:T(8,128)(2,1)S(1)}, bf16[512,512]{1,0:T(8,128)(2,1)S(1)}, u32[]{:S(2)}, u32[]{:S(2)}) collective-permute-start(bf16[512,512]{1,0:T(8,128)(2,1)S(1)} %slice.151), channel_id=1, source_target_pairs={{0,2},{1,3},{2,0},{3,1},{4,6},{5,7},{6,4},{7,5},{8,10},{9,11},{10,... | collective-permute-start | bytes 1572872 | tf_op jit(solution)/shard_map/ppermute | solution.py:847
  173.6 32.0 %collective-permute-start.10 = (bf16[512,512]{1,0:T(8,128)(2,1)S(1)}, bf16[512,512]{1,0:T(8,128)(2,1)S(1)}, u32[]{:S(2)}, u32[]{:S(2)}) collective-permute-start(bf16[512,512]{1,0:T(8,128)(2,1)S(1)} %slice.116), channel_id=1, source_target_pairs={{0,1},{1,0},{2,3},{3,2},{4,5},{5,4},{6,7},{7,6},{8,9},{9,8},{10,11... | collective-permute-start | bytes 1572872 | tf_op jit(solution)/shard_map/ppermute | solution.py:847
  194.5 52.6 %collective-permute-start.15 = (bf16[512,2048]{1,0:T(8,128)(2,1)S(1)}, bf16[512,2048]{1,0:T(8,128)(2,1)}, u32[]{:S(2)}, u32[]{:S(2)}) collective-permute-start(bf16[512,2048]{1,0:T(8,128)(2,1)S(1)} %copy-done.1), channel_id=1, source_target_pairs={{0,1},{1,0},{2,3},{3,2},{4,5},{5,4},{6,7},{7,6},{8,9},{9,8},{10,11... | collective-permute-start | bytes 6291464 | tf_op jit(solution)/shard_map/ppermute | solution.py:847
  196.0 51.1 %collective-permute-start.16 = (bf16[512,2048]{1,0:T(8,128)(2,1)S(1)}, bf16[512,2048]{1,0:T(8,128)(2,1)}, u32[]{:S(2)}, u32[]{:S(2)}) collective-permute-start(bf16[512,2048]{1,0:T(8,128)(2,1)S(1)} %copy-done.1), channel_id=1, source_target_pairs={{0,2},{1,3},{2,0},{3,1},{4,6},{5,7},{6,4},{7,5},{8,10},{9,11},{10,... | collective-permute-start | bytes 6291464 | tf_op jit(solution)/shard_map/ppermute | solution.py:847
  249.4 37.8 %collective-permute-start.17 = (bf16[256,2048]{1,0:T(8,128)(2,1)}, bf16[256,2048]{1,0:T(8,128)(2,1)S(1)}, u32[]{:S(2)}, u32[]{:S(2)}) collective-permute-start(bf16[256,2048]{1,0:T(8,128)(2,1)} %slice.118), channel_id=1, source_target_pairs={{0,1},{1,0},{2,3},{3,2},{4,5},{5,4},{6,7},{7,6},{8,9},{9,8},{10,11... | collective-permute-start | bytes 3145736 | tf_op jit(solution)/shard_map/ppermute | solution.py:847
  253.2 34.0 %collective-permute-start.18 = (bf16[256,2048]{1,0:T(8,128)(2,1)}, bf16[256,2048]{1,0:T(8,128)(2,1)}, u32[]{:S(2)}, u32[]{:S(2)}) collective-permute-start(bf16[256,2048]{1,0:T(8,128)(2,1)} %slice.119), channel_id=1, source_target_pairs={{0,2},{1,3},{2,0},{3,1},{4,6},{5,7},{6,4},{7,5},{8,10},{9,11},{10,... | collective-permute-start | bytes 3145736 | tf_op jit(solution)/shard_map/ppermute | solution.py:847
  329.6 191.1 %reduce-scatter.7.cloned.1.call-start = ((), (), s32[]{:S(2)}) async-start(), calls=%async_computation.8 | async-start | bytes 9437184 | tf_op jit(solution)/shard_map/reduce_scatter | solution.py:1052
  331.2 38.2 %collective-permute-start.19 = (bf16[1024,768]{1,0:T(8,128)(2,1)S(1)}, bf16[1024,768]{1,0:T(8,128)(2,1)}, u32[]{:S(2)}, u32[]{:S(2)}) collective-permute-start(bf16[1024,768]{1,0:T(8,128)(2,1)S(1)} %constant_dynamic-slice_fusion), channel_id=1, source_target_pairs={{0,1},{1,0},{2,3},{3,2},{4,5},{5,4},{6,7},{7,6},{8,9},{9,8},{10,11... | collective-permute-start | bytes 4718600 | tf_op jit(solution)/shard_map/ppermute | solution.py:847
  332.7 36.7 %collective-permute-start.20 = (bf16[1024,768]{1,0:T(8,128)(2,1)S(1)}, bf16[1024,768]{1,0:T(8,128)(2,1)}, u32[]{:S(2)}, u32[]{:S(2)}) collective-permute-start(bf16[1024,768]{1,0:T(8,128)(2,1)S(1)} %constant_dynamic-slice_fusion), channel_id=1, source_target_pairs={{0,2},{1,3},{2,0},{3,1},{4,6},{5,7},{6,4},{7,5},{8,10},{9,11},{10,... | collective-permute-start | bytes 4718600 | tf_op jit(solution)/shard_map/ppermute | solution.py:847
  370.6 27.1 %collective-permute-start.21 = (bf16[512,768]{1,0:T(8,128)(2,1)S(1)}, bf16[512,768]{1,0:T(8,128)(2,1)S(1)}, u32[]{:S(2)}, u32[]{:S(2)}) collective-permute-start(bf16[512,768]{1,0:T(8,128)(2,1)S(1)} %slice.152), channel_id=1, source_target_pairs={{0,1},{1,0},{2,3},{3,2},{4,5},{5,4},{6,7},{7,6},{8,9},{9,8},{10,11... | collective-permute-start | bytes 2359304 | tf_op jit(solution)/shard_map/ppermute | solution.py:847
  422.4 228.3 %reduce-scatter.9.cloned.1.call-start = ((), (), s32[]{:S(2)}) async-start(), calls=%async_computation.9 | async-start | bytes 9437184 | tf_op jit(solution)/shard_map/reduce_scatter | solution.py:1052
  422.4 24.9 %collective-permute-start.24 = (bf16[256,2048]{1,0:T(8,128)(2,1)}, bf16[256,2048]{1,0:T(8,128)(2,1)S(1)}, u32[]{:S(2)}, u32[]{:S(2)}) collective-permute-start(bf16[256,2048]{1,0:T(8,128)(2,1)} %get-tuple-element.159), channel_id=1, source_target_pairs={{0,2},{1,3},{2,0},{3,1},{4,6},{5,7},{6,4},{7,5},{8,10},{9,11},{10,... | collective-permute-start | bytes 3145736 | tf_op jit(solution)/shard_map/ppermute | solution.py:847
  424.0 27.7 %collective-permute-start.23 = (bf16[256,2048]{1,0:T(8,128)(2,1)}, bf16[256,2048]{1,0:T(8,128)(2,1)}, u32[]{:S(2)}, u32[]{:S(2)}) collective-permute-start(bf16[256,2048]{1,0:T(8,128)(2,1)} %get-tuple-element.158), channel_id=1, source_target_pairs={{0,1},{1,0},{2,3},{3,2},{4,5},{5,4},{6,7},{7,6},{8,9},{9,8},{10,11... | collective-permute-start | bytes 3145736 | tf_op jit(solution)/shard_map/ppermute | solution.py:847
  440.2 56.5 %collective-permute-start.25 = (bf16[256,2048]{1,0:T(8,128)(2,1)}, bf16[256,2048]{1,0:T(8,128)(2,1)S(1)}, u32[]{:S(2)}, u32[]{:S(2)}) collective-permute-start(bf16[256,2048]{1,0:T(8,128)(2,1)} %get-tuple-element.161), channel_id=1, source_target_pairs={{0,1},{1,0},{2,3},{3,2},{4,5},{5,4},{6,7},{7,6},{8,9},{9,8},{10,11... | collective-permute-start | bytes 3145736 | tf_op jit(solution)/shard_map/ppermute | solution.py:847
  441.7 55.0 %collective-permute-start.28 = (bf16[256,2048]{1,0:T(8,128)(2,1)}, bf16[256,2048]{1,0:T(8,128)(2,1)S(1)}, u32[]{:S(2)}, u32[]{:S(2)}) collective-permute-start(bf16[256,2048]{1,0:T(8,128)(2,1)} %get-tuple-element.178), channel_id=1, source_target_pairs={{0,2},{1,3},{2,0},{3,1},{4,6},{5,7},{6,4},{7,5},{8,10},{9,11},{10,... | collective-permute-start | bytes 3145736 | tf_op jit(solution)/shard_map/ppermute | solution.py:847
  450.3 46.3 %collective-permute-start.27 = (bf16[256,2048]{1,0:T(8,128)(2,1)}, bf16[256,2048]{1,0:T(8,128)(2,1)S(1)}, u32[]{:S(2)}, u32[]{:S(2)}) collective-permute-start(bf16[256,2048]{1,0:T(8,128)(2,1)} %add_convert_fusion.2), channel_id=1, source_target_pairs={{0,1},{1,0},{2,3},{3,2},{4,5},{5,4},{6,7},{7,6},{8,9},{9,8},{10,11... | collective-permute-start | bytes 3145736 | tf_op jit(solution)/shard_map/ppermute | solution.py:847
  454.2 42.5 %collective-permute-start.26 = (bf16[256,2048]{1,0:T(8,128)(2,1)}, bf16[256,2048]{1,0:T(8,128)(2,1)}, u32[]{:S(2)}, u32[]{:S(2)}) collective-permute-start(bf16[256,2048]{1,0:T(8,128)(2,1)} %add_convert_fusion.3), channel_id=1, source_target_pairs={{0,2},{1,3},{2,0},{3,1},{4,6},{5,7},{6,4},{7,5},{8,10},{9,11},{10,... | collective-permute-start | bytes 3145736 | tf_op jit(solution)/shard_map/ppermute | solution.py:847
  496.0 24.8 %collective-permute-start.32 = (bf16[256,2048]{1,0:T(8,128)(2,1)}, bf16[256,2048]{1,0:T(8,128)(2,1)}, u32[]{:S(2)}, u32[]{:S(2)}) collective-permute-start(bf16[256,2048]{1,0:T(8,128)(2,1)} %get-tuple-element.174), channel_id=1, source_target_pairs={{0,1},{1,0},{2,3},{3,2},{4,5},{5,4},{6,7},{7,6},{8,9},{9,8},{10,11... | collective-permute-start | bytes 3145736 | tf_op jit(solution)/shard_map/ppermute | solution.py:847
  517.2 27.7 %collective-permute-start.29 = (bf16[512,512]{1,0:T(8,128)(2,1)}, bf16[512,512]{1,0:T(8,128)(2,1)}, u32[]{:S(2)}, u32[]{:S(2)}) collective-permute-start(bf16[512,512]{1,0:T(8,128)(2,1)} %get-tuple-element.188), channel_id=1, source_target_pairs={{0,1},{1,0},{2,3},{3,2},{4,5},{5,4},{6,7},{7,6},{8,9},{9,8},{10,11... | collective-permute-start | bytes 1572872 | tf_op jit(solution)/shard_map/ppermute | solution.py:847
  518.7 26.3 %collective-permute-start.30 = (bf16[512,512]{1,0:T(8,128)(2,1)}, bf16[512,512]{1,0:T(8,128)(2,1)S(1)}, u32[]{:S(2)}, u32[]{:S(2)}) collective-permute-start(bf16[512,512]{1,0:T(8,128)(2,1)} %get-tuple-element.189), channel_id=1, source_target_pairs={{0,2},{1,3},{2,0},{3,1},{4,6},{5,7},{6,4},{7,5},{8,10},{9,11},{10,... | collective-permute-start | bytes 1572872 | tf_op jit(solution)/shard_map/ppermute | solution.py:847
  520.3 24.7 %collective-permute-start.31 = (bf16[512,512]{1,0:T(8,128)(2,1)}, bf16[512,512]{1,0:T(8,128)(2,1)S(1)}, u32[]{:S(2)}, u32[]{:S(2)}) collective-permute-start(bf16[512,512]{1,0:T(8,128)(2,1)} %get-tuple-element.190), channel_id=1, source_target_pairs={{0,3},{1,2},{2,1},{3,0},{4,7},{5,6},{6,5},{7,4},{8,11},{9,10},{10,... | collective-permute-start | bytes 1572872 | tf_op jit(solution)/shard_map/ppermute | solution.py:847
  546.0 185.6 %reduce-scatter.11.cloned.1.call-start = ((), (), s32[]{:S(2)}) async-start(), calls=%async_computation.10 | async-start | bytes 5898240 | tf_op jit(solution)/shard_map/reduce_scatter | solution.py:1052
  548.1 28.9 %collective-permute-start.35 = (bf16[256,2048]{1,0:T(8,128)(2,1)S(1)}, bf16[256,2048]{1,0:T(8,128)(2,1)S(1)}, u32[]{:S(2)}, u32[]{:S(2)}) collective-permute-start(bf16[256,2048]{1,0:T(8,128)(2,1)S(1)} %get-tuple-element.199), channel_id=1, source_target_pairs={{0,1},{1,0},{2,3},{3,2},{4,5},{5,4},{6,7},{7,6},{8,9},{9,8},{10,11... | collective-permute-start | bytes 3145736 | tf_op jit(solution)/shard_map/ppermute | solution.py:847
  549.5 27.6 %collective-permute-start.36 = (bf16[256,2048]{1,0:T(8,128)(2,1)S(1)}, bf16[256,2048]{1,0:T(8,128)(2,1)S(1)}, u32[]{:S(2)}, u32[]{:S(2)}) collective-permute-start(bf16[256,2048]{1,0:T(8,128)(2,1)S(1)} %get-tuple-element.199), channel_id=1, source_target_pairs={{0,2},{1,3},{2,0},{3,1},{4,6},{5,7},{6,4},{7,5},{8,10},{9,11},{10,... | collective-permute-start | bytes 3145736 | tf_op jit(solution)/shard_map/ppermute | solution.py:847
  551.2 60.5 %collective-permute-start.44 = (bf16[1024,768]{1,0:T(8,128)(2,1)}, bf16[1024,768]{1,0:T(8,128)(2,1)}, u32[]{:S(2)}, u32[]{:S(2)}) collective-permute-start(bf16[1024,768]{1,0:T(8,128)(2,1)} %collective-permute-done.19.refs_5_), channel_id=1, source_target_pairs={{0,4},{4,0},{8,12},{12,8},{16,20},{20,16},{24,28},{28,24},{1,5},{5... | collective-permute-start | bytes 4718600 | tf_op jit(solution)/shard_map/ppermute | solution.py:847
  551.2 61.4 %collective-permute-start.45 = (bf16[1024,768]{1,0:T(8,128)(2,1)}, bf16[1024,768]{1,0:T(8,128)(2,1)}, u32[]{:S(2)}, u32[]{:S(2)}) collective-permute-start(bf16[1024,768]{1,0:T(8,128)(2,1)} %collective-permute-done.20.refs_6_), channel_id=1, source_target_pairs={{0,4},{4,0},{8,12},{12,8},{16,20},{20,16},{24,28},{28,24},{1,5},{5... | collective-permute-start | bytes 4718600 | tf_op jit(solution)/shard_map/ppermute | solution.py:847
  577.1 30.6 %collective-permute-start.40 = (bf16[256,2048]{1,0:T(8,128)(2,1)}, bf16[256,2048]{1,0:T(8,128)(2,1)}, u32[]{:S(2)}, u32[]{:S(2)}) collective-permute-start(bf16[256,2048]{1,0:T(8,128)(2,1)} %get-tuple-element.206), channel_id=1, source_target_pairs={{0,1},{1,0},{2,3},{3,2},{4,5},{5,4},{6,7},{7,6},{8,9},{9,8},{10,11... | collective-permute-start | bytes 3145736 | tf_op jit(solution)/shard_map/ppermute | solution.py:847
  578.4 29.3 %collective-permute-start.41 = (bf16[256,2048]{1,0:T(8,128)(2,1)}, bf16[256,2048]{1,0:T(8,128)(2,1)}, u32[]{:S(2)}, u32[]{:S(2)}) collective-permute-start(bf16[256,2048]{1,0:T(8,128)(2,1)} %get-tuple-element.206), channel_id=1, source_target_pairs={{0,2},{1,3},{2,0},{3,1},{4,6},{5,7},{6,4},{7,5},{8,10},{9,11},{10,... | collective-permute-start | bytes 3145736 | tf_op jit(solution)/shard_map/ppermute | solution.py:847
  581.7 46.4 %collective-permute-start.46 = (bf16[1024,768]{1,0:T(8,128)(2,1)S(1)}, bf16[1024,768]{1,0:T(8,128)(2,1)}, u32[]{:S(2)}, u32[]{:S(2)}) collective-permute-start(bf16[1024,768]{1,0:T(8,128)(2,1)S(1)} %constant_dynamic-update-slice_fusion.11.refs_7_), channel_id=1, source_target_pairs={{0,4},{4,0},{8,12},{12,8},{16,20},{20,16},{24,28},{28,24},{1,5},{5... | collective-permute-start | bytes 4718600 | tf_op jit(solution)/shard_map/ppermute | solution.py:847
  607.7 26.4 %collective-permute-start.42 = (bf16[256,2048]{1,0:T(8,128)(2,1)}, bf16[256,2048]{1,0:T(8,128)(2,1)}, u32[]{:S(2)}, u32[]{:S(2)}) collective-permute-start(bf16[256,2048]{1,0:T(8,128)(2,1)} %copy-done.30), channel_id=1, source_target_pairs={{0,1},{1,0},{2,3},{3,2},{4,5},{5,4},{6,7},{7,6},{8,9},{9,8},{10,11... | collective-permute-start | bytes 3145736 | tf_op jit(solution)/shard_map/ppermute | solution.py:847
  608.5 26.4 %collective-permute-start.43 = (bf16[256,2048]{1,0:T(8,128)(2,1)}, bf16[256,2048]{1,0:T(8,128)(2,1)}, u32[]{:S(2)}, u32[]{:S(2)}) collective-permute-start(bf16[256,2048]{1,0:T(8,128)(2,1)} %collective-permute-done.40.refs_2_), channel_id=1, source_target_pairs={{0,2},{1,3},{2,0},{3,1},{4,6},{5,7},{6,4},{7,5},{8,10},{9,11},{10,... | collective-permute-start | bytes 3145736 | tf_op jit(solution)/shard_map/ppermute | solution.py:847
  611.6 38.5 %collective-permute-start.34 = (bf16[512,768]{1,0:T(8,128)(2,1)S(1)}, bf16[512,768]{1,0:T(8,128)(2,1)}, u32[]{:S(2)}, u32[]{:S(2)}) collective-permute-start(bf16[512,768]{1,0:T(8,128)(2,1)S(1)} %copy-done.31), channel_id=1, source_target_pairs={{0,1},{1,0},{2,3},{3,2},{4,5},{5,4},{6,7},{7,6},{8,9},{9,8},{10,11... | collective-permute-start | bytes 2359304 | tf_op jit(solution)/shard_map/ppermute | solution.py:847
  612.6 38.1 %collective-permute-start.37 = (bf16[512,768]{1,0:T(8,128)(2,1)}, bf16[512,768]{1,0:T(8,128)(2,1)}, u32[]{:S(2)}, u32[]{:S(2)}) collective-permute-start(bf16[512,768]{1,0:T(8,128)(2,1)} %get-tuple-element.202.refs_6_), channel_id=1, source_target_pairs={{0,2},{1,3},{2,0},{3,1},{4,6},{5,7},{6,4},{7,5},{8,10},{9,11},{10,... | collective-permute-start | bytes 2359304 | tf_op jit(solution)/shard_map/ppermute | solution.py:847
  671.7 50.6 %collective-permute-start.39 = (bf16[256,2048]{1,0:T(8,128)(2,1)}, bf16[256,2048]{1,0:T(8,128)(2,1)S(1)}, u32[]{:S(2)}, u32[]{:S(2)}) collective-permute-start(bf16[256,2048]{1,0:T(8,128)(2,1)} %get-tuple-element.204), channel_id=1, source_target_pairs={{0,1},{1,0},{2,3},{3,2},{4,5},{5,4},{6,7},{7,6},{8,9},{9,8},{10,11... | collective-permute-start | bytes 3145736 | tf_op jit(solution)/shard_map/ppermute | solution.py:847
  672.6 49.7 %collective-permute-start.49 = (bf16[256,2048]{1,0:T(8,128)(2,1)}, bf16[256,2048]{1,0:T(8,128)(2,1)}, u32[]{:S(2)}, u32[]{:S(2)}) collective-permute-start(bf16[256,2048]{1,0:T(8,128)(2,1)} %get-tuple-element.224), channel_id=1, source_target_pairs={{0,2},{1,3},{2,0},{3,1},{4,6},{5,7},{6,4},{7,5},{8,10},{9,11},{10,... | collective-permute-start | bytes 3145736 | tf_op jit(solution)/shard_map/ppermute | solution.py:847
  679.2 43.2 %collective-permute-start.47 = (bf16[256,2048]{1,0:T(8,128)(2,1)}, bf16[256,2048]{1,0:T(8,128)(2,1)S(1)}, u32[]{:S(2)}, u32[]{:S(2)}) collective-permute-start(bf16[256,2048]{1,0:T(8,128)(2,1)} %add_convert_fusion.1), channel_id=1, source_target_pairs={{0,2},{1,3},{2,0},{3,1},{4,6},{5,7},{6,4},{7,5},{8,10},{9,11},{10,... | collective-permute-start | bytes 3145736 | tf_op jit(solution)/shard_map/ppermute | solution.py:847
  679.8 42.6 %collective-permute-start.48 = (bf16[256,2048]{1,0:T(8,128)(2,1)}, bf16[256,2048]{1,0:T(8,128)(2,1)S(1)}, u32[]{:S(2)}, u32[]{:S(2)}) collective-permute-start(bf16[256,2048]{1,0:T(8,128)(2,1)} %add_convert_fusion), channel_id=1, source_target_pairs={{0,1},{1,0},{2,3},{3,2},{4,5},{5,4},{6,7},{7,6},{8,9},{9,8},{10,11... | collective-permute-start | bytes 3145736 | tf_op jit(solution)/shard_map/ppermute | solution.py:847
  (61 other events, 837.5 us)
Sparse Core Ops, SparseCore 0:
  10.2 58.7 all-gather.3
  71.2 115.4 all-gather.5
  189.0 114.9 all-gather.7
  329.7 90.1 reduce-scatter.4
  422.5 90.1 reduce-scatter.6
  545.1 90.3 reduce-scatter.8
  650.8 60.3 reduce-scatter.10
